TPU v7x, 32 devices: a whole 2x2x4 slice. The times are simulated.
32 devices in a mesh: rep: 8 (over y, x, core), shard: 4 (over z).
Axes of the slice: x: 2, y: 2, z: 4, core: 2. Of those that a mesh axis runs over, the one named last changes fastest.
Arguments:
- latents: bfloat16 [64, 4096], P(('rep', 'shard')), may hold values from -6 to 6
- noise: bfloat16 [64, 4096], P(('rep', 'shard')), may hold values from -6 to 6
- labels: int32 [64], P(('rep', 'shard')), may hold values from 0 to 999
- t_index: int32 [64], P(('rep', 'shard')), may hold values from 0 to 999, as said below
- owner: int32 [234], replicated, may hold values from 0 to 479, as said below
- master: float32 [768, 480, 128], P(None, ('rep', 'shard'))
- first_moment: float32 [768, 480, 128], P(None, ('rep', 'shard'))
- second_moment: float32 [768, 480, 128], P(None, ('rep', 'shard'))
- small: float32 [1288, 768], replicated
- small_first: float32 [1288, 768], replicated
- small_second: float32 [1288, 768], replicated
Outputs:
- loss_sum: float32 [], replicated
- weight_total: float32 [], replicated
- new_master: float32 [768, 480, 128], P(None, ('rep', 'shard'))
- new_first: float32 [768, 480, 128], P(None, ('rep', 'shard'))
- new_second: float32 [768, 480, 128], P(None, ('rep', 'shard'))
- new_small: float32 [1288, 768], replicated
- new_small_first: float32 [1288, 768], replicated
- new_small_second: float32 [1288, 768], replicated
Inputs may be any that keep to these rules, and one draw needn't show every extreme that they name: `t_index`: image b's index lies between b * 1000 // 64 and ((b + 1) * 1000 - 1) // 64. `owner`: distinct slots; slot s belongs to device s // 15, devices in the order rep then shard; some device holds 15 blocks.
All inputs are finite; a program needn't handle non-finite values.
Results may differ from a plain program's by a relative error of at most 0.022.
Values may be sent and summed in bfloat16 or wider, within the bound.
A program may use at most 320 MiB of HBM per device.

v0:
```python
import jax
import jax.numpy as jnp
from jax import lax
from jax.sharding import PartitionSpec as P

D = 768
HEADS = 12
HEAD_DIM = 64
FF = 3072
FREQ = 256
CLASSES = 1000
CHANNELS = 16
GRID = 16
PATCHES = 256
LAYERS = 2
TSTEPS = 1000
STEP = 10
BLOCK = 128
LAYER_COLS = 13824
LAYER_UNITS = 108
UNITS = 234


beta_one = 0.5
beta_two = 0.5
adam_eps = 1e-08
decay_rate = 0.1
rate_factor = 0.5


def gelu_tanh(values):
    return jax.nn.gelu(values, approximate=True)


def norm_rows(hidden):
    centered = hidden - jnp.mean(hidden, -1, keepdims=True)
    return centered * lax.rsqrt(jnp.mean(centered * centered, -1, keepdims=True) + 1e-06)


def local_back(function, primal, upstream):
    return jax.vjp(function, primal)[1](upstream)[0]


def dot_low(pattern, left_side, right_side):
    return jnp.einsum(pattern, left_side, right_side, preferred_element_type=jnp.float32)


def positions():
    quarter = D // 4
    angular = jnp.exp(-jnp.log(10000.0) * jnp.arange(quarter, dtype=jnp.float32) / quarter)
    patch_idx = jnp.arange(PATCHES, dtype=jnp.int32)
    row_pos = (patch_idx // GRID).astype(jnp.float32)[:, None] * angular
    col_pos = (patch_idx % GRID).astype(jnp.float32)[:, None] * angular
    return jnp.concatenate(
        [jnp.sin(col_pos), jnp.cos(col_pos), jnp.sin(row_pos), jnp.cos(row_pos)], -1
    )


def frequencies(times):
    half_size = FREQ // 2
    spacing = jnp.exp(-jnp.log(10000.0) * jnp.arange(half_size, dtype=jnp.float32) / half_size)
    angles = 1000.0 * times[:, None] * spacing
    return jnp.concatenate([jnp.cos(angles), jnp.sin(angles)], -1)


def unit_scale(unit_ids):
    column = unit_ids % LAYER_UNITS * BLOCK
    in_layer = unit_ids < LAYERS * LAYER_UNITS
    is_output = in_layer & (column >= 9 * D) & (column < 10 * D)
    is_down = in_layer & (column >= 10 * D + FF)
    factor = jnp.where(is_output, 4.0, jnp.where(is_down, 1.5 * (D / FF) ** 0.5, 1.0))
    return factor / D**0.5


def table_scale(row_ids):
    return jnp.where(
        row_ids < CHANNELS,
        CHANNELS ** (-0.5),
        jnp.where(
            row_ids < CHANNELS + FREQ,
            FREQ ** (-0.5),
            jnp.where(row_ids < CHANNELS + FREQ + CLASSES, 0.5, D ** (-0.5)),
        ),
    )


def adam_update(weight, first_mom, second, gradient, rate):
    first_new = beta_one * first_mom + (1.0 - beta_one) * gradient
    second_new = beta_two * second + (1.0 - beta_two) * gradient * gradient
    ratio = (
        first_new
        / (1.0 - beta_one**STEP)
        / (jnp.sqrt(second_new / (1.0 - beta_two**STEP)) + adam_eps)
    )
    return (weight - rate * (ratio + decay_rate * weight), first_new, second_new)


def split_layer(weights):
    return (
        weights[:, : 6 * D],
        weights[:, 6 * D : 9 * D],
        weights[:, 9 * D : 10 * D],
        weights[:, 10 * D : 10 * D + FF],
        weights[:, 10 * D + FF :],
    )


def split_heads(qkv_all):
    groups, length = (qkv_all.shape[0], qkv_all.shape[1])
    return tuple(
        (
            qkv_all[..., part_idx * D : (part_idx + 1) * D].reshape(groups, length, HEADS, HEAD_DIM)
            for part_idx in range(3)
        )
    )


def modulate(normed, shift, scale):
    return normed * (1.0 + scale[:, None, :]) + shift[:, None, :]


def layer_forward(hidden, cond_act, weights):
    w_ada, w_qkv, w_out, w_up, w_down = split_layer(weights)
    groups = hidden.shape[0]
    modul = jnp.dot(cond_act, w_ada, preferred_element_type=jnp.float32)
    shift_a, scale_a, gate_a, shift_b, scale_b, gate_b = jnp.split(modul, 6, -1)
    attn_in = modulate(norm_rows(hidden), shift_a, scale_a).astype(jnp.bfloat16)
    qkv_all = dot_low("gpd,de->gpe", attn_in, w_qkv).astype(jnp.bfloat16)
    queries, keys_all, values = split_heads(qkv_all)
    scores = dot_low("gqhe,gkhe->ghqk", queries, keys_all) * HEAD_DIM ** (-0.5)
    top_score = jnp.max(scores, -1, keepdims=True)
    log_total = top_score + jnp.log(jnp.sum(jnp.exp(scores - top_score), -1, keepdims=True))
    attn_prob = jnp.exp(scores - log_total).astype(jnp.bfloat16)
    heads_out = (
        dot_low("ghqk,gkhe->gqhe", attn_prob, values).astype(jnp.bfloat16).reshape(groups, -1, D)
    )
    branch_a = dot_low("gpd,de->gpe", heads_out, w_out)
    middle = hidden + gate_a[:, None, :] * branch_a
    mlp_in = modulate(norm_rows(middle), shift_b, scale_b).astype(jnp.bfloat16)
    pre_act = dot_low("gpd,df->gpf", mlp_in, w_up)
    post_act = gelu_tanh(pre_act).astype(jnp.bfloat16)
    branch_b = dot_low("gpf,df->gpd", post_act, w_down)
    output = middle + gate_b[:, None, :] * branch_b
    return (
        output,
        (
            hidden,
            modul,
            attn_in,
            qkv_all,
            log_total,
            heads_out,
            branch_a,
            middle,
            mlp_in,
            pre_act,
            post_act,
            branch_b,
        ),
    )


def layer_backward(grad_out, cond_act, weights, saved):
    w_ada, w_qkv, w_out, w_up, w_down = split_layer(weights)
    (
        hidden,
        modul,
        attn_in,
        qkv_all,
        log_total,
        heads_out,
        branch_a,
        middle,
        mlp_in,
        pre_act,
        post_act,
        branch_b,
    ) = saved
    groups = hidden.shape[0]
    shift_a, scale_a, gate_a, shift_b, scale_b, gate_b = jnp.split(modul, 6, -1)
    grad_gate_b = jnp.sum(grad_out * branch_b, 1)
    grad_branch_b = (gate_b[:, None, :] * grad_out).astype(jnp.bfloat16)
    grad_down = dot_low("gpd,gpf->df", grad_branch_b, post_act)
    grad_post = dot_low("gpd,df->gpf", grad_branch_b, w_down)
    grad_pre = local_back(gelu_tanh, pre_act, grad_post).astype(jnp.bfloat16)
    grad_up = dot_low("gpd,gpf->df", mlp_in, grad_pre)
    grad_mlp_in = dot_low("gpf,df->gpd", grad_pre, w_up)
    normed_b = norm_rows(middle)
    grad_scale_b = jnp.sum(grad_mlp_in * normed_b, 1)
    grad_shift_b = jnp.sum(grad_mlp_in, 1)
    grad_middle = grad_out + local_back(
        norm_rows, middle, grad_mlp_in * (1.0 + scale_b[:, None, :])
    )
    grad_gate_a = jnp.sum(grad_middle * branch_a, 1)
    grad_branch_a = (gate_a[:, None, :] * grad_middle).astype(jnp.bfloat16)
    grad_out_w = dot_low("gpd,gpe->de", heads_out, grad_branch_a)
    grad_heads = (
        dot_low("gpe,de->gpd", grad_branch_a, w_out)
        .astype(jnp.bfloat16)
        .reshape(groups, -1, HEADS, HEAD_DIM)
    )
    queries, keys_all, values = split_heads(qkv_all)
    scores = dot_low("gqhe,gkhe->ghqk", queries, keys_all) * HEAD_DIM ** (-0.5)
    attn_prob = jnp.exp(scores - log_total)
    grad_prob = dot_low("gqhe,gkhe->ghqk", grad_heads, values)
    grad_values = dot_low("ghqk,gqhe->gkhe", attn_prob.astype(jnp.bfloat16), grad_heads)
    inner_sum = jnp.sum(attn_prob * grad_prob, -1, keepdims=True)
    grad_scores = (HEAD_DIM ** (-0.5) * attn_prob * (grad_prob - inner_sum)).astype(jnp.bfloat16)
    grad_queries = dot_low("ghqk,gkhe->gqhe", grad_scores, keys_all)
    grad_keys = dot_low("ghqk,gqhe->gkhe", grad_scores, queries)
    grad_qkv = jnp.concatenate(
        [
            grad_queries.reshape(groups, -1, D),
            grad_keys.reshape(groups, -1, D),
            grad_values.reshape(groups, -1, D),
        ],
        -1,
    ).astype(jnp.bfloat16)
    grad_qkv_w = dot_low("gpd,gpe->de", attn_in, grad_qkv)
    grad_attn_in = dot_low("gpe,de->gpd", grad_qkv, w_qkv)
    normed_a = norm_rows(hidden)
    grad_scale_a = jnp.sum(grad_attn_in * normed_a, 1)
    grad_shift_a = jnp.sum(grad_attn_in, 1)
    grad_in = grad_middle + local_back(
        norm_rows, hidden, grad_attn_in * (1.0 + scale_a[:, None, :])
    )
    grad_modul = jnp.concatenate(
        [grad_shift_a, grad_scale_a, grad_gate_a, grad_shift_b, grad_scale_b, grad_gate_b], -1
    ).astype(jnp.bfloat16)
    grad_ada = dot_low("gd,ge->de", cond_act, grad_modul)
    grad_cond = dot_low("ge,de->gd", grad_modul, w_ada)
    weight_grad = jnp.concatenate([grad_ada, grad_qkv_w, grad_out_w, grad_up, grad_down], 1)
    return (grad_in, grad_cond, weight_grad)


def on_device(
    latents,
    noise,
    labels,
    t_index,
    owner,
    master,
    first_moment,
    second_moment,
    small,
    small_first,
    small_second,
):
    shard_count = lax.axis_size("shard")
    rep_count = lax.axis_size("rep")
    rows_dev = master.shape[0] // shard_count
    slot_dev = master.shape[1]
    group_slots = shard_count * slot_dev
    spread = lax.all_to_all(
        master.astype(jnp.bfloat16), "shard", split_axis=0, concat_axis=1, tiled=True
    )
    every_slot = lax.all_gather(spread, "rep", axis=1, tiled=True)
    unit_rows = jnp.take(every_slot, owner, axis=1).reshape(rows_dev, UNITS * BLOCK)

    def full_columns(first_col, col_count):
        return lax.all_gather(
            unit_rows[:, first_col : first_col + col_count], "shard", axis=0, tiled=True
        )

    def shard_sum(weight_grad):
        return lax.psum_scatter(
            weight_grad.astype(jnp.bfloat16), "shard", scatter_dimension=0, tiled=True
        ).astype(jnp.float32)

    x_start = latents.astype(jnp.float32).reshape(-1, PATCHES, CHANNELS)
    noise_f = noise.astype(jnp.float32).reshape(-1, PATCHES, CHANNELS)
    times = (t_index.astype(jnp.float32) + 0.5) / TSTEPS
    noisy = (1.0 - times)[:, None, None] * x_start + times[:, None, None] * noise_f
    target = noise_f - x_start
    loss_weight = 1.0 + 3.0 * times
    small_low = small.astype(jnp.bfloat16)
    patch_w = small_low[:CHANNELS]
    time_w = small_low[CHANNELS : CHANNELS + FREQ]
    table = small[CHANNELS + FREQ : CHANNELS + FREQ + CLASSES]
    head_w = small_low[CHANNELS + FREQ + CLASSES :]
    tail_w = full_columns(LAYERS * LAYER_COLS, 3 * D)
    time_two = tail_w[:, :D]
    final_ada = tail_w[:, D:]
    noisy_low = noisy.astype(jnp.bfloat16)
    hidden = dot_low("gpc,cd->gpd", noisy_low, patch_w) + positions()
    freq_low = frequencies(times).astype(jnp.bfloat16)
    time_pre = jnp.dot(freq_low, time_w, preferred_element_type=jnp.float32)
    time_act = jax.nn.silu(time_pre).astype(jnp.bfloat16)
    cond = jnp.dot(time_act, time_two, preferred_element_type=jnp.float32) + jnp.take(
        table, labels, axis=0
    )
    cond_act = jax.nn.silu(cond).astype(jnp.bfloat16)
    kept_weights = []
    saved_all = []
    for layer_idx in range(LAYERS):
        weights = full_columns(layer_idx * LAYER_COLS, LAYER_COLS)
        hidden, saved = layer_forward(hidden, cond_act, weights)
        kept_weights.append(weights)
        saved_all.append(saved)
    modul_f = jnp.dot(cond_act, final_ada, preferred_element_type=jnp.float32)
    shift_f, scale_f = jnp.split(modul_f, 2, -1)
    normed_f = norm_rows(hidden)
    final_in = modulate(normed_f, shift_f, scale_f).astype(jnp.bfloat16)
    predict = dot_low("gpd,cd->gpc", final_in, head_w)
    error = predict - target
    loss_part = jnp.sum(loss_weight[:, None, None] * error * error) / CHANNELS
    weight_part = jnp.sum(loss_weight) * PATCHES
    grad_pred = (loss_weight[:, None, None] * 2.0 * error / CHANNELS).astype(jnp.bfloat16)
    grad_head = dot_low("gpc,gpd->cd", grad_pred, final_in)
    grad_final_in = dot_low("gpc,cd->gpd", grad_pred, head_w)
    grad_modul_f = jnp.concatenate(
        [jnp.sum(grad_final_in, 1), jnp.sum(grad_final_in * normed_f, 1)], -1
    ).astype(jnp.bfloat16)
    grad_final_ada = dot_low("gd,ge->de", cond_act, grad_modul_f)
    grad_cond_act = dot_low("ge,de->gd", grad_modul_f, final_ada)
    grad_hidden = local_back(norm_rows, hidden, grad_final_in * (1.0 + scale_f[:, None, :]))
    layer_grads = [None] * LAYERS
    for layer_idx in reversed(range(LAYERS)):
        weights = full_columns(layer_idx * LAYER_COLS, LAYER_COLS)
        grad_hidden, grad_cond_layer, weight_grad = layer_backward(
            grad_hidden, cond_act, weights, saved_all[layer_idx]
        )
        grad_cond_act = grad_cond_act + grad_cond_layer
        layer_grads[layer_idx] = shard_sum(weight_grad)
    grad_cond = local_back(jax.nn.silu, cond, grad_cond_act)
    grad_time_out = grad_cond.astype(jnp.bfloat16)
    grad_time_two = dot_low("gd,ge->de", time_act, grad_time_out)
    grad_time_act = dot_low("ge,de->gd", grad_time_out, time_two)
    grad_time_pre = local_back(jax.nn.silu, time_pre, grad_time_act).astype(jnp.bfloat16)
    grad_time_w = dot_low("gf,gd->fd", freq_low, grad_time_pre)
    one_hot = (labels[:, None] == jnp.arange(CLASSES, dtype=jnp.int32)[None, :]).astype(jnp.float32)
    grad_table = jnp.einsum("gk,gd->kd", one_hot, grad_cond, precision=lax.Precision.HIGHEST)
    grad_embed = grad_hidden.astype(jnp.bfloat16)
    grad_patch = dot_low("gpc,gpd->cd", noisy_low, grad_embed)
    tail_grad = shard_sum(jnp.concatenate([grad_time_two, grad_final_ada], 1))
    unit_grad_rows = jnp.concatenate(layer_grads + [tail_grad], 1)
    small_grad = jnp.concatenate([grad_patch, grad_time_w, grad_table, grad_head], 0)
    small_total, loss_sum, weight_total = lax.psum(
        (small_grad, loss_part, weight_part), ("rep", "shard")
    )
    slot_total = rep_count * group_slots
    unit_of_slot = (
        jnp.zeros((slot_total,), jnp.int32).at[owner].set(jnp.arange(UNITS, dtype=jnp.int32))
    )
    used_slot = jnp.zeros((slot_total,), jnp.int32).at[owner].set(1)
    summed = lax.psum(unit_grad_rows.astype(jnp.bfloat16), "rep").astype(jnp.float32)
    picked = lax.dynamic_slice_in_dim(
        unit_of_slot, lax.axis_index("rep") * group_slots, group_slots
    )
    group_grad = jnp.take(summed.reshape(rows_dev, UNITS, BLOCK), picked, axis=1)
    owned_grad = lax.all_to_all(
        group_grad.astype(jnp.bfloat16), "shard", split_axis=1, concat_axis=0, tiled=True
    ).astype(group_grad.dtype)
    my_start = (lax.axis_index("rep") * shard_count + lax.axis_index("shard")) * slot_dev
    my_units = lax.dynamic_slice_in_dim(unit_of_slot, my_start, slot_dev)
    my_used = (lax.dynamic_slice_in_dim(used_slot, my_start, slot_dev) > 0)[None, :, None]
    rate = rate_factor * unit_scale(my_units)[None, :, None]
    new_w, new_first, new_second = adam_update(
        master, first_moment, second_moment, owned_grad, rate
    )
    new_master = jnp.where(my_used, new_w, master)
    new_first = jnp.where(my_used, new_first, first_moment)
    new_second = jnp.where(my_used, new_second, second_moment)
    small_rate = rate_factor * table_scale(jnp.arange(small.shape[0], dtype=jnp.int32))[:, None]
    new_small, new_small_first, new_small_second = adam_update(
        small, small_first, small_second, small_total, small_rate
    )
    return (
        loss_sum,
        weight_total,
        new_master,
        new_first,
        new_second,
        new_small,
        new_small_first,
        new_small_second,
    )


def solution(mesh):
    return jax.shard_map(
        on_device,
        mesh=mesh,
        in_specs=(
            P(("rep", "shard"), None),
            P(("rep", "shard"), None),
            P(("rep", "shard")),
            P(("rep", "shard")),
            P(),
            P(None, ("rep", "shard"), None),
            P(None, ("rep", "shard"), None),
            P(None, ("rep", "shard"), None),
            P(),
            P(),
            P(),
        ),
        out_specs=(
            P(),
            P(),
            P(None, ("rep", "shard"), None),
            P(None, ("rep", "shard"), None),
            P(None, ("rep", "shard"), None),
            P(),
            P(),
            P(),
        ),
        check_vma=False,
    )
```

profile of v0, /device:TPU:3, one launch (start us, length us, event | category | flops | bytes accessed | tf_op | source)
XLA Modules:
  0.0 2386.8 jit_solution(12891831303949775527)
XLA Ops:
  12.4 74.2 %all_to_all.27 = bf16[768,15,128]{2,1,0:T(8,128)(2,1)S(1)} all-to-all(bf16[768,15,128]{2,1,0:T(8,128)(2,1)S(1)} %copy.202), channel_id=1, replica_groups=mesh['rep'=8,'shard'=4] {'shard'}, dimensions={0} | all-to-all | bytes 5898240 | tf_op jit(solution)/shard_map/all_to_all | solution.py:254
  89.7 118.9 %all-gather.5.cloned.1.call-done = bf16[192,480,128]{2,0,1:T(8,128)(2,1)} async-done(((bf16[192,60,128]{2,0,1:T(8,128)(2,1)}), bf16[192,480,128]{2,0,1:T(8,128)(2,1)}) %all-gather.5.cloned.1.call-update) | async-done | bytes 23592976 | tf_op jit(solution)/shard_map/all_gather | solution.py:257
  208.7 17.9 gather_fusion
  238.4 8.9 fusion.130
  259.5 48.5 %all-gather.7.cloned.1.call-done = bf16[768,2304]{1,0:T(8,128)(2,1)} async-done(((bf16[192,2304]{1,0:T(8,128)(2,1)}), bf16[768,2304]{1,0:T(8,128)(2,1)}) %all-gather.7.cloned.1.call-update) | async-done | bytes 3538960 | tf_op jit(solution)/shard_map/all_gather | solution.py:261
  311.7 358.3 %all-gather.9.cloned.1.call-done = bf16[768,13824]{1,0:T(8,128)(2,1)} async-done(((bf16[192,13824]{1,0:T(8,128)(2,1)}), bf16[768,13824]{1,0:T(8,128)(2,1)}) %all-gather.9.cloned.1.call-update) | async-done | bytes 21233680 | tf_op jit(solution)/shard_map/all_gather | solution.py:261
  703.2 7.7 fusion.128
  711.3 320.4 %all-gather.11.cloned.1.call-done = bf16[768,13824]{1,0:T(8,128)(2,1)} async-done(((bf16[192,13824]{1,0:T(8,128)(2,1)}), bf16[768,13824]{1,0:T(8,128)(2,1)}) %all-gather.11.cloned.1.call-update) | async-done | bytes 21233680 | tf_op jit(solution)/shard_map/all_gather | solution.py:261
  1055.4 7.1 fusion.41
  1062.5 9.3 fusion.126
  1077.0 8.6 fusion.15
  1098.0 7.5 multiply_reduce_fusion.1
  1131.0 9.0 fusion.8
  1154.8 7.5 multiply_reduce_fusion
  1241.6 23.4 reduce-scatter.8.cloned.1.call-done
  1265.0 353.9 %reduce-scatter.4.cloned.1.call-done = bf16[192,13824]{1,0:T(8,128)(2,1)} async-done(((bf16[768,13824]{1,0:T(8,128)(2,1)}), bf16[192,13824]{1,0:T(8,128)(2,1)}) %reduce-scatter.4.cloned.1.call-update) | async-done | bytes 5308432 | tf_op jit(solution)/shard_map/reduce_scatter | solution.py:266
  1618.9 355.4 %reduce-scatter.6.cloned.1.call-done = bf16[192,13824]{1,0:T(8,128)(2,1)} async-done(((bf16[768,13824]{1,0:T(8,128)(2,1)}), bf16[192,13824]{1,0:T(8,128)(2,1)}) %reduce-scatter.6.cloned.1.call-update) | async-done | bytes 5308432 | tf_op jit(solution)/shard_map/reduce_scatter | solution.py:266
  1974.3 10.4 copy_bitcast_fusion
  1993.6 153.6 %all-reduce.4.cloned.1.call-done = bf16[192,234,128]{2,0,1:T(8,128)(2,1)} async-done(((bf16[192,234,128]{2,0,1:T(8,128)(2,1)}), bf16[192,234,128]{2,0,1:T(8,128)(2,1)}) %all-reduce.4.cloned.1.call-update) | async-done | bytes 11501584 | tf_op jit(solution)/shard_map/psum | solution.py:346
  2147.2 6.8 gather_fusion.2
  2171.6 96.9 %all-reduce = (f32[]{:T(128)}, f32[]{:T(128)}) all-reduce(f32[]{:T(128)S(6)} %div.196, f32[]{:T(128)S(6)} %mul.754), channel_id=1, replica_groups=mesh['rep'=8,'shard'=4] {'rep','shard'}, use_global_device_ids=true, to_apply=%region_15.16 | all-reduce | flops 2 | bytes 16 | tf_op jit(solution)/shard_map/psum | solution.py:338
  2268.5 85.9 %all-reduce.6.cloned.1.call-done = f32[1288,768]{1,0:T(8,128)} async-done(((f32[1288,768]{1,0:T(8,128)}), f32[1288,768]{1,0:T(8,128)}) %all-reduce.6.cloned.1.call-update) | async-done | bytes 3956752 | tf_op jit(solution)/shard_map/psum | solution.py:338
  2354.4 10.0 multiply_subtract_fusion
  2368.6 11.4 fusion.32
  (399 shorter events, 258.3 us)
Async XLA Ops:
  7.2 201.5 %all-gather.5.cloned.1.call-start = ((), (), s32[]{:S(2)}) async-start(), calls=%async_computation.5 | async-start | bytes 26542080 | tf_op jit(solution)/shard_map/all_gather | solution.py:257
  89.0 219.0 %all-gather.7.cloned.1.call-start = ((), (), s32[]{:S(2)}) async-start(), calls=%async_computation.6 | async-start | bytes 4423680 | tf_op jit(solution)/shard_map/all_gather | solution.py:261
  238.3 431.6 %all-gather.9.cloned.1.call-start = ((), (), s32[]{:S(2)}) async-start(), calls=%async_computation.7 | async-start | bytes 26542080 | tf_op jit(solution)/shard_map/all_gather | solution.py:261
  247.3 784.4 %all-gather.11.cloned.1.call-start = ((), (), s32[]{:S(2)}) async-start(), calls=%async_computation.8 | async-start | bytes 26542080 | tf_op jit(solution)/shard_map/all_gather | solution.py:261
  247.9 1017.1 %reduce-scatter.8.cloned.1.call-start = ((), (), s32[]{:S(2)}) async-start(), calls=%async_computation.11 | async-start | bytes 4423680 | tf_op jit(solution)/shard_map/reduce_scatter | solution.py:266
  256.5 815.7 %copy-start.84 = (f32[2]{0:T(128)}, f32[2]{0:T(128)S(1)}, u32[]{:S(2)}) copy-start(f32[2]{0:T(128)S(1)} %get-tuple-element.39) | copy-start | bytes 28
  256.5 818.2 %copy-start.73 = (f32[2]{0:T(128)}, f32[2]{0:T(128)S(1)}, u32[]{:S(2)}) copy-start(f32[2]{0:T(128)S(1)} %get-tuple-element.38) | copy-start | bytes 28
  258.3 415.7 %copy-start.75 = (bf16[2,128]{1,0:T(2,128)(2,1)}, bf16[2,128]{1,0:T(2,128)(2,1)S(1)}, u32[]{:S(2)}) copy-start(bf16[2,128]{1,0:T(2,128)(2,1)S(1)} %get-tuple-element.78) | copy-start | bytes 1540
  258.3 415.7 %copy-start.77 = (bf16[2,128]{1,0:T(2,128)(2,1)}, bf16[2,128]{1,0:T(2,128)(2,1)S(1)}, u32[]{:S(2)}) copy-start(bf16[2,128]{1,0:T(2,128)(2,1)S(1)} %get-tuple-element.79) | copy-start | bytes 1540
  259.5 410.5 %copy-start.59 = (f32[2,768]{1,0:T(2,128)}, f32[2,768]{1,0:T(2,128)S(1)}, u32[]{:S(2)}) copy-start(f32[2,768]{1,0:T(2,128)S(1)} %fusion.69) | copy-start | bytes 18436
  311.6 760.5 %copy-start.65 = (f32[2,768]{1,0:T(2,128)}, f32[2,768]{1,0:T(2,128)S(1)}, u32[]{:S(2)}) copy-start(f32[2,768]{1,0:T(2,128)S(1)} %get-tuple-element.73) | copy-start | bytes 18436
  311.6 764.7 %copy-start.57 = (f32[2,768]{1,0:T(2,128)}, f32[2,768]{1,0:T(2,128)S(1)}, u32[]{:S(2)}) copy-start(f32[2,768]{1,0:T(2,128)S(1)} %get-tuple-element.72) | copy-start | bytes 18436
  710.9 324.8 %copy-start.5 = (f32[2,256,768]{2,1,0:T(8,128)}, f32[2,256,768]{2,1,0:T(8,128)S(1)}, u32[]{:S(2)}) copy-start(f32[2,256,768]{2,1,0:T(8,128)S(1)} %get-tuple-element.45) | copy-start | bytes 4718596
  1062.5 14.5 slice-start.7
  1062.5 14.5 slice-start.8
  1062.5 14.5 slice-start.9
  1062.5 14.5 slice-start.10
  1062.5 14.5 slice-start.11
  1131.0 16.2 copy-start.40
  1200.2 418.8 %reduce-scatter.4.cloned.1.call-start = ((), (), s32[]{:S(2)}) async-start(), calls=%async_computation.9 | async-start | bytes 26542080 | tf_op jit(solution)/shard_map/reduce_scatter | solution.py:266
  1220.7 753.6 %reduce-scatter.6.cloned.1.call-start = ((), (), s32[]{:S(2)}) async-start(), calls=%async_computation.10 | async-start | bytes 26542080 | tf_op jit(solution)/shard_map/reduce_scatter | solution.py:266
  1241.6 905.6 %all-reduce.4.cloned.1.call-start = ((), (), s32[]{:S(2)}) async-start(), calls=%async_computation.12 | async-start | bytes 23003136 | tf_op jit(solution)/shard_map/psum | solution.py:346
  2158.4 205.9 %all-to-all-start.1 = ((bf16[192,60,128]{2,0,1:T(8,128)(2,1)}), bf16[192,60,128]{2,0,1:T(8,128)(2,1)}, u32[]{:S(2)}, u32[]{:S(2)}) async-start(bf16[192,60,128]{2,0,1:T(8,128)(2,1)} %fusion.44), calls=%async_computation.4 | async-start | bytes 5898240 | tf_op jit(solution)/shard_map/all_to_all | solution.py:351
  2163.2 191.2 %all-reduce.6.cloned.1.call-start = ((), (), s32[]{:S(2)}) async-start(), calls=%async_computation.13 | async-start | bytes 7913472 | tf_op jit(solution)/shard_map/psum | solution.py:338
  (93 other events, 377.1 us)
Sparse Core Ops, SparseCore 0:
  89.1 119.5 all-gather.4
  238.4 69.5 all-gather.6
  310.2 359.7 all-gather.8
  672.0 359.6 all-gather.10
  1200.3 64.6 reduce-scatter.7
  1267.2 351.6 reduce-scatter.3
  1621.4 352.8 reduce-scatter.5
  1984.9 162.2 all-reduce.3
  2171.2 183.1 all-reduce.5
where the time goes:
time: 2400 us; the launch traced here: 2390 us
  waiting for transfers between devices  1820 us (76%)
  matrix products  201 us (8%)
  blocking collectives  171 us (7%)
  local copies, waits for them, and re-layouts  93.7 us (4%)
  other arithmetic  79.2 us (3%)
    reduce_scatter x3, waiting for transfers between devices, shard_sum(): lax.psum_scatter(weight_grad.astype(jnp.bfloat16), 'shard', scatter_dimen...  733 us
    all_gather x3, waiting for transfers between devices, full_columns(): lax.all_gather(unit_rows[:, first_col:first_col + col_count], 'shard', ax...  727 us
    dot_general x49, matrix products, dot_low(): jnp.einsum(pattern, left_side, right_side, preferred_element_type=jnp.flo...  185 us
    psum x1, waiting for transfers between devices, on_device(): lax.psum(unit_grad_rows.astype(jnp.bfloat16), 'rep').astype(jnp.float32)  154 us
    all_gather x1, waiting for transfers between devices, on_device(): every_slot = lax.all_gather(spread, 'rep', axis=1, tiled=True)  119 us
    psum x1, blocking collectives, on_device(): lax.psum((small_grad, loss_part, weight_part), ('rep', 'shard'))  96.9 us
    psum x1, waiting for transfers between devices, on_device(): lax.psum((small_grad, loss_part, weight_part), ('rep', 'shard'))  85.9 us
    all_to_all x1, blocking collectives, on_device(): lax.all_to_all(master.astype(jnp.bfloat16), 'shard', split_axis=0, concat...  74.2 us
  transfers between devices with their start and end apart: 10, of which 9 were waited for; matrix products, arithmetic and copies ran while one was open for 5% of the time, Pallas kernels for 0%

commit v1 on v0

--- a/solution.py
+++ b/solution.py
@@ -1,5 +1,6 @@
 import jax
 import jax.numpy as jnp
+import numpy as np
 from jax import lax
 from jax.sharding import PartitionSpec as P
 
@@ -20,6 +21,13 @@
 LAYER_UNITS = 108
 UNITS = 234
 
+ADA_UNITS = 6 * D // BLOCK
+DENSE_UNITS = LAYER_UNITS - ADA_UNITS
+DENSE_COLS = DENSE_UNITS * BLOCK
+TIME_UNITS = D // BLOCK
+TAIL_FIRST = LAYERS * LAYER_UNITS
+AXES = ("rep", "shard")
+
 
 beta_one = 0.5
 beta_two = 0.5
@@ -95,13 +103,12 @@
     return (weight - rate * (ratio + decay_rate * weight), first_new, second_new)
 
 
-def split_layer(weights):
+def split_dense(weights):
     return (
-        weights[:, : 6 * D],
-        weights[:, 6 * D : 9 * D],
-        weights[:, 9 * D : 10 * D],
-        weights[:, 10 * D : 10 * D + FF],
-        weights[:, 10 * D + FF :],
+        weights[:, : 3 * D],
+        weights[:, 3 * D : 4 * D],
+        weights[:, 4 * D : 4 * D + FF],
+        weights[:, 4 * D + FF :],
     )
 
 
@@ -119,10 +126,9 @@
     return normed * (1.0 + scale[:, None, :]) + shift[:, None, :]
 
 
-def layer_forward(hidden, cond_act, weights):
-    w_ada, w_qkv, w_out, w_up, w_down = split_layer(weights)
+def layer_forward(hidden, modul, weights):
+    w_qkv, w_out, w_up, w_down = split_dense(weights)
     groups = hidden.shape[0]
-    modul = jnp.dot(cond_act, w_ada, preferred_element_type=jnp.float32)
     shift_a, scale_a, gate_a, shift_b, scale_b, gate_b = jnp.split(modul, 6, -1)
     attn_in = modulate(norm_rows(hidden), shift_a, scale_a).astype(jnp.bfloat16)
     qkv_all = dot_low("gpd,de->gpe", attn_in, w_qkv).astype(jnp.bfloat16)
@@ -160,8 +166,8 @@
     )
 
 
-def layer_backward(grad_out, cond_act, weights, saved):
-    w_ada, w_qkv, w_out, w_up, w_down = split_layer(weights)
+def layer_backward(grad_out, weights, saved):
+    w_qkv, w_out, w_up, w_down = split_dense(weights)
     (
         hidden,
         modul,
@@ -227,10 +233,20 @@
     grad_modul = jnp.concatenate(
         [grad_shift_a, grad_scale_a, grad_gate_a, grad_shift_b, grad_scale_b, grad_gate_b], -1
     ).astype(jnp.bfloat16)
-    grad_ada = dot_low("gd,ge->de", cond_act, grad_modul)
-    grad_cond = dot_low("ge,de->gd", grad_modul, w_ada)
-    weight_grad = jnp.concatenate([grad_ada, grad_qkv_w, grad_out_w, grad_up, grad_down], 1)
-    return (grad_in, grad_cond, weight_grad)
+    weight_grad = jnp.concatenate([grad_qkv_w, grad_out_w, grad_up, grad_down], 1)
+    return (grad_in, grad_modul, weight_grad)
+
+
+def unit_lists():
+    dense = np.concatenate(
+        [np.arange(l * LAYER_UNITS + ADA_UNITS, (l + 1) * LAYER_UNITS) for l in range(LAYERS)]
+    )
+    time_units = np.arange(TAIL_FIRST, TAIL_FIRST + TIME_UNITS)
+    image_units = np.concatenate(
+        [np.arange(l * LAYER_UNITS, l * LAYER_UNITS + ADA_UNITS) for l in range(LAYERS)]
+        + [np.arange(TAIL_FIRST + TIME_UNITS, UNITS)]
+    )
+    return dense, time_units, image_units
 
 
 def on_device(
@@ -246,26 +262,39 @@
     small_first,
     small_second,
 ):
-    shard_count = lax.axis_size("shard")
-    rep_count = lax.axis_size("rep")
-    rows_dev = master.shape[0] // shard_count
+    count = lax.axis_size("rep") * lax.axis_size("shard")
+    me = lax.axis_index(AXES)
     slot_dev = master.shape[1]
-    group_slots = shard_count * slot_dev
-    spread = lax.all_to_all(
-        master.astype(jnp.bfloat16), "shard", split_axis=0, concat_axis=1, tiled=True
-    )
-    every_slot = lax.all_gather(spread, "rep", axis=1, tiled=True)
-    unit_rows = jnp.take(every_slot, owner, axis=1).reshape(rows_dev, UNITS * BLOCK)
-
-    def full_columns(first_col, col_count):
-        return lax.all_gather(
-            unit_rows[:, first_col : first_col + col_count], "shard", axis=0, tiled=True
+    slot_total = count * slot_dev
+    rows = D // count
+    images = latents.shape[0]
+    dense_units, time_units, image_units = unit_lists()
+
+    unit_of_slot = (
+        jnp.full((slot_total,), -1, jnp.int32).at[owner].set(jnp.arange(UNITS, dtype=jnp.int32))
+    )
+    my_unit = lax.dynamic_slice_in_dim(unit_of_slot, me * slot_dev, slot_dev)
+    low_slots = master.astype(jnp.bfloat16)
+
+    spread = lax.all_to_all(low_slots, AXES, split_axis=0, concat_axis=1, tiled=True)
+    moved = np.concatenate([dense_units, time_units])
+    unit_rows = jnp.take(spread, owner[moved], axis=1)
+    time_two = lax.all_gather(
+        unit_rows[:, len(dense_units) :].reshape(rows, D), AXES, axis=0, tiled=True
+    )
+    weights_all = [
+        lax.all_gather(
+            unit_rows[:, l * DENSE_UNITS : (l + 1) * DENSE_UNITS].reshape(rows, DENSE_COLS),
+            AXES,
+            axis=0,
+            tiled=True,
         )
-
-    def shard_sum(weight_grad):
-        return lax.psum_scatter(
-            weight_grad.astype(jnp.bfloat16), "shard", scatter_dimension=0, tiled=True
-        ).astype(jnp.float32)
+        for l in range(LAYERS)
+    ]
+
+    every_t = lax.all_gather(t_index, AXES, axis=0, tiled=True)
+    every_label = lax.all_gather(labels, AXES, axis=0, tiled=True)
+    all_images = every_t.shape[0]
 
     x_start = latents.astype(jnp.float32).reshape(-1, PATCHES, CHANNELS)
     noise_f = noise.astype(jnp.float32).reshape(-1, PATCHES, CHANNELS)
@@ -278,92 +307,113 @@
     time_w = small_low[CHANNELS : CHANNELS + FREQ]
     table = small[CHANNELS + FREQ : CHANNELS + FREQ + CLASSES]
     head_w = small_low[CHANNELS + FREQ + CLASSES :]
-    tail_w = full_columns(LAYERS * LAYER_COLS, 3 * D)
-    time_two = tail_w[:, :D]
-    final_ada = tail_w[:, D:]
     noisy_low = noisy.astype(jnp.bfloat16)
     hidden = dot_low("gpc,cd->gpd", noisy_low, patch_w) + positions()
-    freq_low = frequencies(times).astype(jnp.bfloat16)
+
+    every_time = (every_t.astype(jnp.float32) + 0.5) / TSTEPS
+    weight_total = jnp.sum(1.0 + 3.0 * every_time) * PATCHES
+    freq_low = frequencies(every_time).astype(jnp.bfloat16)
     time_pre = jnp.dot(freq_low, time_w, preferred_element_type=jnp.float32)
     time_act = jax.nn.silu(time_pre).astype(jnp.bfloat16)
     cond = jnp.dot(time_act, time_two, preferred_element_type=jnp.float32) + jnp.take(
-        table, labels, axis=0
+        table, every_label, axis=0
     )
     cond_act = jax.nn.silu(cond).astype(jnp.bfloat16)
-    kept_weights = []
+
+    slot_modul = dot_low("gd,dsc->gsc", cond_act, low_slots)
+    slot_modul = lax.all_to_all(slot_modul, AXES, split_axis=0, concat_axis=1, tiled=True)
+    modul_all = jnp.take(slot_modul, owner[image_units], axis=1).reshape(images, -1)
+
     saved_all = []
-    for layer_idx in range(LAYERS):
-        weights = full_columns(layer_idx * LAYER_COLS, LAYER_COLS)
-        hidden, saved = layer_forward(hidden, cond_act, weights)
-        kept_weights.append(weights)
+    for l in range(LAYERS):
+        hidden, saved = layer_forward(
+            hidden, modul_all[:, l * 6 * D : (l + 1) * 6 * D], weights_all[l]
+        )
         saved_all.append(saved)
-    modul_f = jnp.dot(cond_act, final_ada, preferred_element_type=jnp.float32)
-    shift_f, scale_f = jnp.split(modul_f, 2, -1)
+    shift_f, scale_f = jnp.split(modul_all[:, LAYERS * 6 * D :], 2, -1)
     normed_f = norm_rows(hidden)
     final_in = modulate(normed_f, shift_f, scale_f).astype(jnp.bfloat16)
     predict = dot_low("gpd,cd->gpc", final_in, head_w)
     error = predict - target
     loss_part = jnp.sum(loss_weight[:, None, None] * error * error) / CHANNELS
-    weight_part = jnp.sum(loss_weight) * PATCHES
     grad_pred = (loss_weight[:, None, None] * 2.0 * error / CHANNELS).astype(jnp.bfloat16)
     grad_head = dot_low("gpc,gpd->cd", grad_pred, final_in)
     grad_final_in = dot_low("gpc,cd->gpd", grad_pred, head_w)
     grad_modul_f = jnp.concatenate(
         [jnp.sum(grad_final_in, 1), jnp.sum(grad_final_in * normed_f, 1)], -1
     ).astype(jnp.bfloat16)
-    grad_final_ada = dot_low("gd,ge->de", cond_act, grad_modul_f)
-    grad_cond_act = dot_low("ge,de->gd", grad_modul_f, final_ada)
     grad_hidden = local_back(norm_rows, hidden, grad_final_in * (1.0 + scale_f[:, None, :]))
-    layer_grads = [None] * LAYERS
-    for layer_idx in reversed(range(LAYERS)):
-        weights = full_columns(layer_idx * LAYER_COLS, LAYER_COLS)
-        grad_hidden, grad_cond_layer, weight_grad = layer_backward(
-            grad_hidden, cond_act, weights, saved_all[layer_idx]
+    grad_rows = [None] * LAYERS
+    grad_moduls = [None] * LAYERS
+    for l in reversed(range(LAYERS)):
+        grad_hidden, grad_moduls[l], weight_grad = layer_backward(
+            grad_hidden, weights_all[l], saved_all[l]
         )
-        grad_cond_act = grad_cond_act + grad_cond_layer
-        layer_grads[layer_idx] = shard_sum(weight_grad)
+        grad_rows[l] = lax.psum_scatter(
+            weight_grad.astype(jnp.bfloat16), AXES, scatter_dimension=0, tiled=True
+        )
+    grad_embed = grad_hidden.astype(jnp.bfloat16)
+    grad_patch = dot_low("gpc,gpd->cd", noisy_low, grad_embed)
+
+    every_modul = lax.all_gather(
+        jnp.concatenate(grad_moduls + [grad_modul_f], -1), AXES, axis=0, tiled=True
+    ).reshape(all_images, len(image_units), BLOCK)
+    image_place = np.full((UNITS + 1,), -1, np.int32)
+    image_place[image_units] = np.arange(len(image_units))
+    my_place = jnp.asarray(image_place)[my_unit]
+    slot_grad_out = jnp.where(
+        (my_place >= 0)[None, :, None],
+        jnp.take(every_modul, jnp.maximum(my_place, 0), axis=1),
+        jnp.zeros((), jnp.bfloat16),
+    )
+    cond_part = dot_low("gsc,dsc->gd", slot_grad_out, low_slots)
+    small_part = jnp.concatenate([cond_part, grad_patch, grad_head], 0)
+    small_sum, loss_sum = lax.psum((small_part, loss_part), AXES)
+    grad_cond_act = small_sum[:all_images]
+    grad_patch = small_sum[all_images : all_images + CHANNELS]
+    grad_head = small_sum[all_images + CHANNELS :]
     grad_cond = local_back(jax.nn.silu, cond, grad_cond_act)
     grad_time_out = grad_cond.astype(jnp.bfloat16)
-    grad_time_two = dot_low("gd,ge->de", time_act, grad_time_out)
     grad_time_act = dot_low("ge,de->gd", grad_time_out, time_two)
     grad_time_pre = local_back(jax.nn.silu, time_pre, grad_time_act).astype(jnp.bfloat16)
     grad_time_w = dot_low("gf,gd->fd", freq_low, grad_time_pre)
-    one_hot = (labels[:, None] == jnp.arange(CLASSES, dtype=jnp.int32)[None, :]).astype(jnp.float32)
-    grad_table = jnp.einsum("gk,gd->kd", one_hot, grad_cond, precision=lax.Precision.HIGHEST)
-    grad_embed = grad_hidden.astype(jnp.bfloat16)
-    grad_patch = dot_low("gpc,gpd->cd", noisy_low, grad_embed)
-    tail_grad = shard_sum(jnp.concatenate([grad_time_two, grad_final_ada], 1))
-    unit_grad_rows = jnp.concatenate(layer_grads + [tail_grad], 1)
+    grad_table = jnp.zeros((CLASSES, D), jnp.float32).at[every_label].add(grad_cond)
     small_grad = jnp.concatenate([grad_patch, grad_time_w, grad_table, grad_head], 0)
-    small_total, loss_sum, weight_total = lax.psum(
-        (small_grad, loss_part, weight_part), ("rep", "shard")
-    )
-    slot_total = rep_count * group_slots
-    unit_of_slot = (
-        jnp.zeros((slot_total,), jnp.int32).at[owner].set(jnp.arange(UNITS, dtype=jnp.int32))
-    )
-    used_slot = jnp.zeros((slot_total,), jnp.int32).at[owner].set(1)
-    summed = lax.psum(unit_grad_rows.astype(jnp.bfloat16), "rep").astype(jnp.float32)
-    picked = lax.dynamic_slice_in_dim(
-        unit_of_slot, lax.axis_index("rep") * group_slots, group_slots
-    )
-    group_grad = jnp.take(summed.reshape(rows_dev, UNITS, BLOCK), picked, axis=1)
-    owned_grad = lax.all_to_all(
-        group_grad.astype(jnp.bfloat16), "shard", split_axis=1, concat_axis=0, tiled=True
-    ).astype(group_grad.dtype)
-    my_start = (lax.axis_index("rep") * shard_count + lax.axis_index("shard")) * slot_dev
-    my_units = lax.dynamic_slice_in_dim(unit_of_slot, my_start, slot_dev)
-    my_used = (lax.dynamic_slice_in_dim(used_slot, my_start, slot_dev) > 0)[None, :, None]
-    rate = rate_factor * unit_scale(my_units)[None, :, None]
+
+    my_time = jnp.clip(my_unit - TAIL_FIRST, 0, TIME_UNITS - 1)
+    is_time = (my_unit >= TAIL_FIRST) & (my_unit < TAIL_FIRST + TIME_UNITS)
+    time_cols = jnp.take(grad_time_out.reshape(all_images, TIME_UNITS, BLOCK), my_time, axis=1)
+    is_image = my_place >= 0
+    image_grad = dot_low("gd,gsc->dsc", cond_act, slot_grad_out)
+    time_grad = dot_low("gd,gsc->dsc", time_act, time_cols)
+
+    dense_place = np.full((UNITS + 1,), 0, np.int32)
+    dense_place[dense_units] = np.arange(len(dense_units))
+    slot_place = jnp.asarray(dense_place)[unit_of_slot]
+    all_rows = jnp.concatenate(
+        [rows_l.reshape(rows, DENSE_UNITS, BLOCK) for rows_l in grad_rows], 1
+    )
+    slot_rows = jnp.take(all_rows, slot_place, axis=1)
+    dense_grad = lax.all_to_all(
+        slot_rows, AXES, split_axis=1, concat_axis=0, tiled=True
+    ).astype(jnp.float32)
+
+    owned_grad = jnp.where(
+        is_image[None, :, None],
+        image_grad,
+        jnp.where(is_time[None, :, None], time_grad, dense_grad),
+    )
+    used = (my_unit >= 0)[None, :, None]
+    rate = rate_factor * unit_scale(jnp.maximum(my_unit, 0))[None, :, None]
     new_w, new_first, new_second = adam_update(
         master, first_moment, second_moment, owned_grad, rate
     )
-    new_master = jnp.where(my_used, new_w, master)
-    new_first = jnp.where(my_used, new_first, first_moment)
-    new_second = jnp.where(my_used, new_second, second_moment)
+    new_master = jnp.where(used, new_w, master)
+    new_first = jnp.where(used, new_first, first_moment)
+    new_second = jnp.where(used, new_second, second_moment)
     small_rate = rate_factor * table_scale(jnp.arange(small.shape[0], dtype=jnp.int32))[:, None]
     new_small, new_small_first, new_small_second = adam_update(
-        small, small_first, small_second, small_total, small_rate
+        small, small_first, small_second, small_grad, small_rate
     )
     return (
         loss_sum,

time: 2400 us -> 1120 us (0.47)
  waiting for transfers between devices: 1820 us -> 593 us
  blocking collectives: 171 us -> 128 us
    all_gather x4, waiting for transfers between devices: 846 us -> 147 us  [the longest x2 147 us: on_device(): lax.all_gather(unit_rows[:, l * DENSE_UNITS:(l + 1) * DENSE_UNITS].reshap...]
    reduce_scatter x3 -> x2, waiting for transfers between devices: 733 us -> 234 us  [on_device(): lax.psum_scatter(weight_grad.astype(jnp.bfloat16), AXES, scatter_dimensio...]
    psum x2 -> x1, waiting for transfers between devices: 240 us -> 122 us  [on_device(): small_sum, loss_sum = lax.psum((small_part, loss_part), AXES)]
    all_to_all x1 -> x3, waiting for transfers between devices: 0.01 us -> 89.6 us  [the longest x1 68.4 us: on_device(): lax.all_to_all(low_slots, AXES, split_axis=0, concat_axis=1, tiled=True)]
    all_to_all x1 -> x0, blocking collectives: 74.2 us -> none  [on_device(): lax.all_to_all(master.astype(jnp.bfloat16), 'shard', split_axis=0, concat...]
    unnamed x0 -> x1, blocking collectives: none -> 38.7 us
    dot_general x49 -> x46, matrix products: 185 us -> 183 us  [dot_low(): jnp.einsum(pattern, left_side, right_side, preferred_element_type=jnp.flo...]
  transfers between devices with their start and end apart: 10 -> 10, of which waited for: 9 -> 7; matrix products, arithmetic and copies ran while one was open for 5% -> 17% of each run, Pallas kernels for 0% -> 0%
where the time goes in v1:
time: 1120 us; the launch traced here: 1110 us
  waiting for transfers between devices  593 us (53%)
  matrix products  186 us (17%)
  blocking collectives  128 us (11%)
  local copies, waits for them, and re-layouts  95.8 us (9%)
  other arithmetic  70.1 us (6%)
  between operations  18.4 us (2%)
  starting transfers between devices  18 us (2%)
    reduce_scatter x2, waiting for transfers between devices, on_device(): lax.psum_scatter(weight_grad.astype(jnp.bfloat16), AXES, scatter_dimensio...  234 us
    dot_general x46, matrix products, dot_low(): jnp.einsum(pattern, left_side, right_side, preferred_element_type=jnp.flo...  183 us
    all_gather x2, waiting for transfers between devices, on_device(): lax.all_gather(unit_rows[:, l * DENSE_UNITS:(l + 1) * DENSE_UNITS].reshap...  147 us
    psum x1, waiting for transfers between devices, on_device(): small_sum, loss_sum = lax.psum((small_part, loss_part), AXES)  122 us
    psum x1, blocking collectives, on_device(): small_sum, loss_sum = lax.psum((small_part, loss_part), AXES)  89.7 us
    all_to_all x1, waiting for transfers between devices, on_device(): lax.all_to_all(low_slots, AXES, split_axis=0, concat_axis=1, tiled=True)  68.4 us
    unnamed x1, blocking collectives  38.7 us
  transfers between devices with their start and end apart: 10, of which 7 were waited for; matrix products, arithmetic and copies ran while one was open for 17% of the time, Pallas kernels for 0%

profile of v1, /device:TPU:3, one launch (start us, length us, event | category | flops | bytes accessed | tf_op | source)
XLA Modules:
  0.0 1108.8 jit_solution(12820731517129057808)
XLA Ops:
  14.0 6.5 all-to-all-start
  23.5 68.4 %all-to-all-done = bf16[768,15,128]{2,1,0:T(8,128)(2,1)} async-done(((bf16[768,15,128]{2,1,0:T(8,128)(2,1)}), bf16[768,15,128]{2,1,0:T(8,128)(2,1)}, u32[]{:S(2)}, u32[]{:S(2)}) %all-to-all-start) | async-done | bytes 2949152 | tf_op jit(solution)/shard_map/all_to_all | solution.py:279
  112.5 38.7 %all-reduce.2 = (s32[64]{0:T(128)S(1)}, s32[64]{0:T(128)S(1)}) all-reduce(s32[64]{0:T(128)S(1)} %dynamic-update-slice.1, s32[64]{0:T(128)S(1)} %dynamic-update-slice), channel_id=1, replica_groups=mesh['rep'=8,'shard'=4] {'rep','shard'}, use_global_device_ids=true, to_apply=%add.1 | all-reduce | flops 128 | bytes 1024
  170.7 21.2 %all-to-all-done.1 = f32[64,15,128]{2,1,0:T(8,128)S(1)} async-done(((f32[64,15,128]{2,1,0:T(8,128)}), f32[64,15,128]{2,1,0:T(8,128)S(1)}, u32[]{:S(2)}, u32[]{:S(2)}) %all-to-all-start.1) | async-done | bytes 491552 | tf_op jit(solution)/shard_map/all_to_all | solution.py:324
  193.0 76.2 %all-gather.8.cloned.1.call-done = bf16[768,9216]{1,0:T(8,128)(2,1)} async-done(((bf16[24,9216]{1,0:T(8,128)(2,1)}), bf16[768,9216]{1,0:T(8,128)(2,1)}) %all-gather.8.cloned.1.call-update) | async-done | bytes 14155792 | tf_op jit(solution)/shard_map/all_gather | solution.py:286
  293.2 9.6 fusion.106
  303.1 70.8 %all-gather.10.cloned.1.call-done = bf16[768,9216]{1,0:T(8,128)(2,1)} async-done(((bf16[24,9216]{1,0:T(8,128)(2,1)}), bf16[768,9216]{1,0:T(8,128)(2,1)}) %all-gather.10.cloned.1.call-update) | async-done | bytes 14155792 | tf_op jit(solution)/shard_map/all_gather | solution.py:286
  395.4 7.3 fusion.26
  402.8 6.7 fusion.104
  413.9 8.0 bitcast_convert_fusion
  421.9 8.0 fusion.13
  445.6 5.3 convolution_convert_fusion.6
  472.0 11.3 %pad_maximum_fusion.1 = bf16[768,9216]{1,0:T(8,128)(2,1)} fusion(bf16[768,3072]{1,0:T(8,128)(2,1)} %bitcast_convert_fusion, bf16[768,3072]{1,0:T(8,128)(2,1)} %bitcast_convert_fusion.1, bf16[768,768]{1,0:T(8,128)(2,1)S(1)} %copy-done.39, bf16[768,2304]{1,0:T(8,128)(2,1)S(1)} %bitcast_convert_fusion.4), kind=kLoop, calls=%fused_computation.13 | loop fusion | flops 56623104 | bytes 28311552 | tf_op jit(solution)/shard_map/concatenate | solution.py:236
  491.1 9.3 fusion.6
  500.5 6.6 multiply_reduce_fusion.14
  518.7 5.6 convolution_convert_fusion.2
  552.8 9.2 pad_maximum_fusion
  575.5 67.2 %reduce-scatter.5.cloned.1.call-done = bf16[24,9216]{1,0:T(8,128)(2,1)} async-done(((bf16[768,9216]{1,0:T(8,128)(2,1)}), bf16[24,9216]{1,0:T(8,128)(2,1)}) %reduce-scatter.5.cloned.1.call-update) | async-done | bytes 442384 | tf_op jit(solution)/shard_map/reduce_scatter | solution.py:352
  643.8 166.3 %reduce-scatter.3.cloned.1.call-done = bf16[24,9216]{1,0:T(8,128)(2,1)} async-done(((bf16[768,9216]{1,0:T(8,128)(2,1)}), bf16[24,9216]{1,0:T(8,128)(2,1)}) %reduce-scatter.3.cloned.1.call-update) | async-done | bytes 442384 | tf_op jit(solution)/shard_map/reduce_scatter | solution.py:352
  818.4 5.5 all-to-all-start.2
  827.8 89.7 %psum.14 = f32[]{:T(128)} all-reduce(f32[]{:T(128)S(6)} %div.198), channel_id=1, replica_groups=mesh['rep'=8,'shard'=4] {'rep','shard'}, use_global_device_ids=true, to_apply=%region_15.16 | all-reduce | flops 1 | bytes 8 | tf_op jit(solution)/shard_map/psum | solution.py:371
  935.2 122.3 %all-reduce.5.cloned.1.call-done = f32[96,768]{1,0:T(8,128)} async-done(((f32[96,768]{1,0:T(8,128)}), f32[96,768]{1,0:T(8,128)}) %all-reduce.5.cloned.1.call-update) | async-done | bytes 294928 | tf_op jit(solution)/shard_map/psum | solution.py:371
  1066.6 10.7 multiply_subtract_fusion
  1083.0 17.6 %fusion.17 = (f32[768,15,128]{2,0,1:T(8,128)}, f32[768,15,128]{2,0,1:T(8,128)}, f32[768,15,128]{2,0,1:T(8,128)}) fusion(f32[768,15,128]{2,0,1:T(8,128)} %param.24, pred[15]{0:T(512)(128)(4,1)S(1)} %copy-done.78, f32[768,15,128]{2,0,1:T(8,128)S(1)} %bitcast.264, f32[768,15,128]{2,0,1:T(8,128)} %param.23, f32[15]{0:T(128)S(1)} %copy-done.82, ...), kind=kOutput, calls=%fused_computation.64 | convolution fusion | flops 217128960 | bytes 47628408 | tf_op jit(solution)/shard_map/gd,gsc->dsc/dot_general | solution.py:53
  (410 shorter events, 242.5 us)
Async XLA Ops:
  10.4 152.4 %copy-start.6 = (bf16[768,15,128]{2,0,1:T(8,128)(2,1)}, bf16[768,15,128]{2,0,1:T(8,128)(2,1)S(1)}, u32[]{:S(2)}) copy-start(bf16[768,15,128]{2,0,1:T(8,128)(2,1)S(1)} %convert_element_type.157) | copy-start | bytes 8847364
  14.0 78.0 %all-to-all-start = ((bf16[768,15,128]{2,1,0:T(8,128)(2,1)}), bf16[768,15,128]{2,1,0:T(8,128)(2,1)}, u32[]{:S(2)}, u32[]{:S(2)}) async-start(bf16[768,15,128]{2,1,0:T(8,128)(2,1)} %copy.225), calls=%async_computation | async-start | bytes 6291456 | tf_op jit(solution)/shard_map/all_to_all | solution.py:279
  20.5 140.6 %all-gather.6.cloned.1.call-start = ((), (), s32[]{:S(2)}) async-start(), calls=%async_computation.5 | async-start | bytes 1216512 | tf_op jit(solution)/shard_map/all_gather | solution.py:282
  102.8 166.4 %all-gather.8.cloned.1.call-start = ((), (), s32[]{:S(2)}) async-start(), calls=%async_computation.6 | async-start | bytes 14598144 | tf_op jit(solution)/shard_map/all_gather | solution.py:286
  105.0 268.9 %all-gather.10.cloned.1.call-start = ((), (), s32[]{:S(2)}) async-start(), calls=%async_computation.7 | async-start | bytes 14598144 | tf_op jit(solution)/shard_map/all_gather | solution.py:286
  159.0 110.1 %copy-start.60 = (f32[2,256]{1,0:T(2,128)}, f32[2,256]{1,0:T(2,128)S(1)}, u32[]{:S(2)}) copy-start(f32[2,256]{1,0:T(2,128)S(1)} %broadcast_multiply_fusion.4) | copy-start | bytes 6148
  164.5 27.3 %all-to-all-start.1 = ((f32[64,15,128]{2,1,0:T(8,128)}), f32[64,15,128]{2,1,0:T(8,128)S(1)}, u32[]{:S(2)}, u32[]{:S(2)}) async-start(f32[64,15,128]{2,1,0:T(8,128)} %copy.229), calls=%async_computation.1 | async-start | bytes 1048576 | tf_op jit(solution)/shard_map/all_to_all | solution.py:324
  169.7 473.0 %reduce-scatter.5.cloned.1.call-start = ((), (), s32[]{:S(2)}) async-start(), calls=%async_computation.10 | async-start | bytes 14598144 | tf_op jit(solution)/shard_map/reduce_scatter | solution.py:352
  170.6 22.2 %copy-start.64 = (f32[2,256]{1,0:T(2,128)}, f32[2,256]{1,0:T(2,128)S(1)}, u32[]{:S(2)}) copy-start(f32[2,256]{1,0:T(2,128)S(1)} %multiply_reduce_fusion.22) | copy-start | bytes 6148
  170.6 102.7 %copy-start.62 = (f32[2,256]{1,0:T(2,128)}, f32[2,256]{1,0:T(2,128)S(1)}, u32[]{:S(2)}) copy-start(f32[2,256]{1,0:T(2,128)S(1)} %fusion.75) | copy-start | bytes 6148
  192.9 76.3 %copy-start.57 = (f32[2,768]{1,0:T(2,128)}, f32[2,768]{1,0:T(2,128)S(1)}, u32[]{:S(2)}) copy-start(f32[2,768]{1,0:T(2,128)S(1)} %get-tuple-element.76) | copy-start | bytes 18436
  192.9 80.4 %copy-start.70 = (f32[2,768]{1,0:T(2,128)}, f32[2,768]{1,0:T(2,128)S(1)}, u32[]{:S(2)}) copy-start(f32[2,768]{1,0:T(2,128)S(1)} %get-tuple-element.75) | copy-start | bytes 18436
  192.9 95.1 %copy-start.68 = (f32[2,768]{1,0:T(2,128)}, f32[2,768]{1,0:T(2,128)S(1)}, u32[]{:S(2)}) copy-start(f32[2,768]{1,0:T(2,128)S(1)} %get-tuple-element.72) | copy-start | bytes 18436
  302.8 89.9 %copy-start.17 = (f32[2,256,768]{2,1,0:T(8,128)}, f32[2,256,768]{2,1,0:T(8,128)S(1)}, u32[]{:S(2)}) copy-start(f32[2,256,768]{2,1,0:T(8,128)S(1)} %get-tuple-element.47) | copy-start | bytes 4718596
  483.3 326.8 %reduce-scatter.3.cloned.1.call-start = ((), (), s32[]{:S(2)}) async-start(), calls=%async_computation.9 | async-start | bytes 14598144 | tf_op jit(solution)/shard_map/reduce_scatter | solution.py:352
  491.1 16.9 %copy-start.36 = (f32[2,256,768]{2,1,0:T(8,128)}, f32[2,256,768]{2,1,0:T(8,128)S(1)}, u32[]{:S(2)}) copy-start(f32[2,256,768]{2,1,0:T(8,128)S(1)} %get-tuple-element.37) | copy-start | bytes 4718596
  562.0 358.5 %all-gather.12.cloned.1.call-start = ((), (), s32[]{:S(2)}) async-start(), calls=%async_computation.11 | async-start | bytes 1419264 | tf_op jit(solution)/shard_map/all_gather | solution.py:358
  818.4 99.0 %copy-start.13 = (f32[2,256,768]{2,1,0:T(8,128)S(1)}, f32[2,256,768]{2,1,0:T(8,128)}, u32[]{:S(2)}) copy-start(f32[2,256,768]{2,1,0:T(8,128)} %copy-done.12) | copy-start | bytes 4718596
  818.4 99.5 %copy-start.52 = (bf16[2,256,16]{1,2,0:T(8,128)(2,1)S(1)}, bf16[2,256,16]{1,2,0:T(8,128)(2,1)}, u32[]{:S(2)}) copy-start(bf16[2,256,16]{1,2,0:T(8,128)(2,1)} %copy-done.51) | copy-start | bytes 49156
  818.4 259.0 %all-to-all-start.2 = ((bf16[24,480,128]{2,0,1:T(8,128)(2,1)}), bf16[24,480,128]{2,0,1:T(8,128)(2,1)}, u32[]{:S(2)}, u32[]{:S(2)}) async-start(bf16[24,480,128]{2,0,1:T(8,128)(2,1)} %select_bitcast_fusion), calls=%async_computation.4 | async-start | bytes 5898240 | tf_op jit(solution)/shard_map/all_to_all | solution.py:397
  823.9 233.6 %all-reduce.5.cloned.1.call-start = ((), (), s32[]{:S(2)}) async-start(), calls=%async_computation.8 | async-start | bytes 589824 | tf_op jit(solution)/shard_map/psum | solution.py:371
  826.5 105.2 %copy-start.72 = (pred[15]{0:T(512)(128)(4,1)}, pred[15]{0:T(512)(128)(4,1)S(1)}, u32[]{:S(2)}) copy-start(pred[15]{0:T(512)(128)(4,1)S(1)} %get-tuple-element.88) | copy-start | bytes 49
  935.2 128.5 %copy-start.54 = (bf16[64,128]{1,0:T(8,128)(2,1)S(1)}, bf16[64,128]{1,0:T(8,128)(2,1)}, u32[]{:S(2)}) copy-start(bf16[64,128]{1,0:T(8,128)(2,1)} %copy-done.53) | copy-start | bytes 49156
  935.2 128.5 %copy-start.56 = (bf16[64,128]{1,0:T(8,128)(2,1)S(1)}, bf16[64,128]{1,0:T(8,128)(2,1)}, u32[]{:S(2)}) copy-start(bf16[64,128]{1,0:T(8,128)(2,1)} %copy-done.55) | copy-start | bytes 49156
  (84 other events, 355.6 us)
Sparse Core Ops, SparseCore 0:
  102.9 52.9 all-gather.5
  159.2 109.9 all-gather.7
  272.6 101.3 all-gather.9
  483.4 159.1 reduce-scatter.4
  648.5 161.5 reduce-scatter.2
  813.4 74.0 all-gather.11
  931.8 125.7 all-reduce.4

commit v2 on v1

--- a/solution.py
+++ b/solution.py
@@ -2,6 +2,8 @@
 import jax.numpy as jnp
 import numpy as np
 from jax import lax
+from jax.experimental import pallas as pl
+from jax.experimental.pallas import tpu as pltpu
 from jax.sharding import PartitionSpec as P
 
 D = 768
@@ -103,15 +105,6 @@
     return (weight - rate * (ratio + decay_rate * weight), first_new, second_new)
 
 
-def split_dense(weights):
-    return (
-        weights[:, : 3 * D],
-        weights[:, 3 * D : 4 * D],
-        weights[:, 4 * D : 4 * D + FF],
-        weights[:, 4 * D + FF :],
-    )
-
-
 def split_heads(qkv_all):
     groups, length = (qkv_all.shape[0], qkv_all.shape[1])
     return tuple(
@@ -127,7 +120,7 @@
 
 
 def layer_forward(hidden, modul, weights):
-    w_qkv, w_out, w_up, w_down = split_dense(weights)
+    w_qkv, w_out, w_up, w_down = weights
     groups = hidden.shape[0]
     shift_a, scale_a, gate_a, shift_b, scale_b, gate_b = jnp.split(modul, 6, -1)
     attn_in = modulate(norm_rows(hidden), shift_a, scale_a).astype(jnp.bfloat16)
@@ -167,7 +160,7 @@
 
 
 def layer_backward(grad_out, weights, saved):
-    w_qkv, w_out, w_up, w_down = split_dense(weights)
+    w_qkv, w_out, w_up, w_down = weights
     (
         hidden,
         modul,
@@ -186,10 +179,10 @@
     shift_a, scale_a, gate_a, shift_b, scale_b, gate_b = jnp.split(modul, 6, -1)
     grad_gate_b = jnp.sum(grad_out * branch_b, 1)
     grad_branch_b = (gate_b[:, None, :] * grad_out).astype(jnp.bfloat16)
-    grad_down = dot_low("gpd,gpf->df", grad_branch_b, post_act)
+    grad_down = row_product(grad_branch_b, post_act)
     grad_post = dot_low("gpd,df->gpf", grad_branch_b, w_down)
     grad_pre = local_back(gelu_tanh, pre_act, grad_post).astype(jnp.bfloat16)
-    grad_up = dot_low("gpd,gpf->df", mlp_in, grad_pre)
+    grad_up = row_product(mlp_in, grad_pre)
     grad_mlp_in = dot_low("gpf,df->gpd", grad_pre, w_up)
     normed_b = norm_rows(middle)
     grad_scale_b = jnp.sum(grad_mlp_in * normed_b, 1)
@@ -199,7 +192,7 @@
     )
     grad_gate_a = jnp.sum(grad_middle * branch_a, 1)
     grad_branch_a = (gate_a[:, None, :] * grad_middle).astype(jnp.bfloat16)
-    grad_out_w = dot_low("gpd,gpe->de", heads_out, grad_branch_a)
+    grad_out_w = row_product(heads_out, grad_branch_a)
     grad_heads = (
         dot_low("gpe,de->gpd", grad_branch_a, w_out)
         .astype(jnp.bfloat16)
@@ -222,7 +215,7 @@
         ],
         -1,
     ).astype(jnp.bfloat16)
-    grad_qkv_w = dot_low("gpd,gpe->de", attn_in, grad_qkv)
+    grad_qkv_w = row_product(attn_in, grad_qkv)
     grad_attn_in = dot_low("gpe,de->gpd", grad_qkv, w_qkv)
     normed_a = norm_rows(hidden)
     grad_scale_a = jnp.sum(grad_attn_in * normed_a, 1)
@@ -233,8 +226,448 @@
     grad_modul = jnp.concatenate(
         [grad_shift_a, grad_scale_a, grad_gate_a, grad_shift_b, grad_scale_b, grad_gate_b], -1
     ).astype(jnp.bfloat16)
-    weight_grad = jnp.concatenate([grad_qkv_w, grad_out_w, grad_up, grad_down], 1)
-    return (grad_in, grad_modul, weight_grad)
+    return (grad_in, grad_modul, [jnp.concatenate([grad_qkv_w, grad_out_w], 1), grad_up, grad_down])
+
+
+def swap_bit(values, bit, count):
+    return lax.ppermute(values, AXES, [(i, i ^ bit) for i in range(count)])
+
+
+def gather_small(values, count):
+    if count & (count - 1):
+        return lax.all_gather(values, AXES, axis=0, tiled=True)
+    me = lax.axis_index(AXES)
+    bit = 1
+    while bit < count:
+        other = swap_bit(values, bit, count)
+        upper = (me & bit) > 0
+        values = jnp.concatenate(
+            [jnp.where(upper, other, values), jnp.where(upper, values, other)], 0
+        )
+        bit *= 2
+    return values
+
+
+def scatter_small(values, count):
+    if count & (count - 1):
+        return lax.psum_scatter(values, AXES, scatter_dimension=0, tiled=False)
+    me = lax.axis_index(AXES)
+    bit = count // 2
+    while bit:
+        half = values.shape[0] // 2
+        upper = (me & bit) > 0
+        low, high = values[:half], values[half:]
+        other = swap_bit(jnp.where(upper, low, high), bit, count)
+        values = jnp.where(upper, high, low) + other
+        bit //= 2
+    return values[0]
+
+
+MESH = pl.DeviceIdType.MESH
+SCATTER_VMEM = 56 * 2**20
+
+
+def dot_rows(left_side, right_side):
+    return lax.dot_general(
+        left_side, right_side, (((0,), (0,)), ((), ())), preferred_element_type=jnp.float32
+    )
+
+
+def row_product(left_side, right_side):
+    left_side = left_side.reshape(-1, left_side.shape[-1])
+    right_side = right_side.reshape(-1, right_side.shape[-1])
+    return dot_rows(left_side, right_side).astype(jnp.bfloat16)
+
+
+def place_of():
+    rep = lax.axis_index("rep")
+    return rep // 4, (rep // 2) % 2, rep % 2, lax.axis_index("shard")
+
+
+def rep_of(y, x, c):
+    return (y * 2 + x) * 2 + c
+
+
+def meet(targets):
+    barrier = pltpu.get_barrier_semaphore()
+    for target in targets:
+        pl.semaphore_signal(barrier, inc=1, device_id=target, device_id_type=MESH)
+    pl.semaphore_wait(barrier, len(targets))
+
+
+def neighbours():
+    y, x, c, z = place_of()
+    to_x = (rep_of(y, 1 - x, c), z)
+    to_y = (rep_of(1 - y, x, c), z)
+    to_core = (rep_of(y, x, 1 - c), z)
+    to_z = [(rep_of(y, x, c), lax.rem(z + step, 4)) for step in (1, 2, 3)]
+    return to_x, to_y, to_core, to_z
+
+
+def gather_kernel(widths, *refs):
+    count = len(widths)
+    pieces, outs = refs[:count], refs[count : 2 * count]
+    own_sem, send_sem, recv_sem = refs[2 * count :]
+    y, x, c, z = place_of()
+    to_x, to_y, to_core, to_z = neighbours()
+    meet([to_x, to_y, to_core] + to_z)
+
+    def remote(k, number, source, dest, target):
+        return pltpu.make_async_remote_copy(
+            src_ref=source,
+            dst_ref=dest,
+            send_sem=send_sem.at[k, number],
+            recv_sem=recv_sem.at[k, number],
+            device_id=target,
+            device_id_type=MESH,
+        )
+
+    def own_copy(k):
+        return pltpu.make_async_copy(pieces[k], outs[k].at[c, y, x, z], own_sem.at[k])
+
+    def line_copies(k, arriving):
+        copies = []
+        for step in (1, 2, 3):
+            at_z = lax.rem(z + 4 - step, 4) if arriving else z
+            copies.append(
+                remote(k, step - 1, pieces[k], outs[k].at[c, y, x, at_z], to_z[step - 1])
+            )
+        return copies
+
+    def first_copies(k, arriving):
+        half = widths[k] // 2
+        left, right = pl.ds(0, half), pl.ds(half, half)
+        at_x = 1 - x if arriving else x
+        at_y = 1 - y if arriving else y
+        a_block = outs[k].at[c, y, at_x, :, :, left]
+        b_block = outs[k].at[c, at_y, x, :, :, right]
+        return [remote(k, 3, a_block, a_block, to_x), remote(k, 4, b_block, b_block, to_y)]
+
+    def second_copies(k, arriving):
+        half = widths[k] // 2
+        left, right = pl.ds(0, half), pl.ds(half, half)
+        at_x = 1 - x if arriving else x
+        at_y = 1 - y if arriving else y
+        a_block = outs[k].at[c, at_y, :, :, :, left]
+        b_block = outs[k].at[c, :, at_x, :, :, right]
+        return [remote(k, 5, a_block, a_block, to_y), remote(k, 6, b_block, b_block, to_x)]
+
+    def core_copies(k, arriving):
+        block = outs[k].at[1 - c if arriving else c]
+        return [remote(k, 7, block, block, to_core)]
+
+    def start(copies):
+        for copy in copies:
+            copy.start()
+
+    def arrived(copies):
+        for copy in copies:
+            copy.wait_recv()
+
+    for k in range(count):
+        own_copy(k).start()
+    start(line_copies(0, False))
+    for t in range(count + 2):
+        if t + 1 < count:
+            start(line_copies(t + 1, False))
+        if t < count:
+            own_copy(t).wait()
+            arrived(line_copies(t, True))
+            start(first_copies(t, False))
+        if 0 <= t - 1 < count:
+            arrived(first_copies(t - 1, True))
+            start(second_copies(t - 1, False))
+        if 0 <= t - 2 < count:
+            arrived(second_copies(t - 2, True))
+            start(core_copies(t - 2, False))
+    for k in range(count):
+        arrived(core_copies(k, True))
+    for k in range(count):
+        for copies in (line_copies, first_copies, second_copies, core_copies):
+            for copy in copies(k, False):
+                copy.wait_send()
+
+
+def scatter_kernel(widths, *refs):
+    count = len(widths)
+    grads, outs = refs[:count], refs[count : 2 * count]
+    scratch = refs[2 * count :]
+    own, core_in, first_in, second_in, line_in = (
+        scratch[i * count : (i + 1) * count] for i in range(5)
+    )
+    own_sem, send_sem, recv_sem = scratch[5 * count :]
+    y, x, c, z = place_of()
+    to_x, to_y, to_core, to_z = neighbours()
+    meet([to_x, to_y, to_core] + to_z)
+
+    def remote(k, number, source, dest, target):
+        return pltpu.make_async_remote_copy(
+            src_ref=source,
+            dst_ref=dest,
+            send_sem=send_sem.at[k, number],
+            recv_sem=recv_sem.at[k, number],
+            device_id=target,
+            device_id_type=MESH,
+        )
+
+    def own_copy(k):
+        return pltpu.make_async_copy(grads[k].at[c], own[k], own_sem.at[k])
+
+    def core_copies(k):
+        return [remote(k, 0, grads[k].at[1 - c], core_in[k], to_core)]
+
+    def first_copies(k):
+        half = widths[k] // 2
+        return [
+            remote(k, 1, own[k].at[:, 1 - x, :, :, pl.ds(0, half)], first_in[k].at[0], to_x),
+            remote(k, 2, own[k].at[1 - y, :, :, :, pl.ds(half, half)], first_in[k].at[1], to_y),
+        ]
+
+    def second_copies(k):
+        half = widths[k] // 2
+        return [
+            remote(k, 3, own[k].at[1 - y, x, :, :, pl.ds(0, half)], second_in[k].at[0], to_y),
+            remote(k, 4, own[k].at[y, 1 - x, :, :, pl.ds(half, half)], second_in[k].at[1], to_x),
+        ]
+
+    def line_copies(k):
+        return [
+            remote(
+                k,
+                4 + step,
+                own[k].at[y, x, lax.rem(z + step, 4)],
+                line_in[k].at[step - 1],
+                to_z[step - 1],
+            )
+            for step in (1, 2, 3)
+        ]
+
+    def start(copies):
+        for copy in copies:
+            copy.start()
+
+    def arrived(copies):
+        for copy in copies:
+            copy.wait_recv()
+
+    def core_sum(k):
+        @pl.loop(0, 16)
+        def _(i):
+            at = (i // 8, (i // 4) % 2, i % 4)
+            own[k][at] = own[k][at] + core_in[k][at]
+
+    def first_sum(k):
+        half = widths[k] // 2
+
+        @pl.loop(0, 8)
+        def _(i):
+            two, at_z = i // 4, i % 4
+            a_at = (two, x, at_z, slice(None), pl.ds(0, half))
+            b_at = (y, two, at_z, slice(None), pl.ds(half, half))
+            own[k][a_at] = own[k][a_at] + first_in[k][0, two, at_z]
+            own[k][b_at] = own[k][b_at] + first_in[k][1, two, at_z]
+
+    def second_sum(k):
+        half = widths[k] // 2
+
+        @pl.loop(0, 4)
+        def _(at_z):
+            a_at = (y, x, at_z, slice(None), pl.ds(0, half))
+            b_at = (y, x, at_z, slice(None), pl.ds(half, half))
+            own[k][a_at] = own[k][a_at] + second_in[k][0, at_z]
+            own[k][b_at] = own[k][b_at] + second_in[k][1, at_z]
+
+    for k in range(count):
+        start(core_copies(k))
+        own_copy(k).start()
+    for t in range(count + 3):
+        if t < count:
+            own_copy(t).wait()
+            arrived(core_copies(t))
+            core_sum(t)
+            start(first_copies(t))
+        if 0 <= t - 1 < count:
+            arrived(first_copies(t - 1))
+            first_sum(t - 1)
+            start(second_copies(t - 1))
+        if 0 <= t - 2 < count:
+            arrived(second_copies(t - 2))
+            second_sum(t - 2)
+            start(line_copies(t - 2))
+        if 0 <= t - 3 < count:
+            k = t - 3
+            arrived(line_copies(k))
+            total = own[k][y, x, z].astype(jnp.float32)
+            for step in (1, 2, 3):
+                total = total + line_in[k][step - 1].astype(jnp.float32)
+            outs[k][...] = total.astype(jnp.bfloat16)
+    for k in range(count):
+        for copies in (core_copies, first_copies, second_copies, line_copies):
+            for copy in copies(k):
+                copy.wait_send()
+
+
+def share_kernel(finish, parts, extra, out, landed, send_sem, recv_sem):
+    devices = parts.shape[0]
+    shards = lax.axis_size("shard")
+    me = lax.axis_index("rep") * shards + lax.axis_index("shard")
+
+    def target(j):
+        peer = lax.rem(me + j, devices)
+        return peer, (peer // shards, lax.rem(peer, shards))
+
+    barrier = pltpu.get_barrier_semaphore()
+
+    @pl.loop(1, devices)
+    def _(j):
+        pl.semaphore_signal(barrier, inc=1, device_id=target(j)[1], device_id_type=MESH)
+
+    pl.semaphore_wait(barrier, devices - 1)
+
+    def copy_part(j):
+        peer, where = target(j)
+        return pltpu.make_async_remote_copy(
+            src_ref=parts.at[peer],
+            dst_ref=landed.at[j],
+            send_sem=send_sem.at[0, j],
+            recv_sem=recv_sem.at[0, j],
+            device_id=where,
+            device_id_type=MESH,
+        )
+
+    def copy_sum(j, arriving):
+        owner = lax.rem(me + devices - j, devices) if arriving else me
+        return pltpu.make_async_remote_copy(
+            src_ref=out.at[owner],
+            dst_ref=out.at[owner],
+            send_sem=send_sem.at[1, j],
+            recv_sem=recv_sem.at[1, j],
+            device_id=target(j)[1],
+            device_id_type=MESH,
+        )
+
+    @pl.loop(1, devices)
+    def _(j):
+        copy_part(j).start()
+
+    landed[0] = parts[me]
+
+    @pl.loop(1, devices)
+    def _(j):
+        copy_part(j).wait_recv()
+
+    out[me] = finish(jnp.sum(landed[...], 0), extra[...])
+
+    @pl.loop(1, devices)
+    def _(j):
+        copy_sum(j, False).start()
+
+    @pl.loop(1, devices)
+    def _(j):
+        copy_sum(j, True).wait_recv()
+
+    @pl.loop(1, devices)
+    def _(j):
+        copy_part(j).wait_send()
+        copy_sum(j, False).wait_send()
+
+
+def share(finish, parts, extra, number):
+    devices = parts.shape[0]
+    return pl.pallas_call(
+        lambda *refs: share_kernel(finish, *refs),
+        out_shape=jax.ShapeDtypeStruct(parts.shape, jnp.float32),
+        in_specs=[pl.BlockSpec(memory_space=pltpu.VMEM)] * 2,
+        out_specs=pl.BlockSpec(memory_space=pltpu.VMEM),
+        scratch_shapes=[
+            pltpu.VMEM(parts.shape, jnp.float32),
+            pltpu.SemaphoreType.DMA((2, devices)),
+            pltpu.SemaphoreType.DMA((2, devices)),
+        ],
+        compiler_params=pltpu.CompilerParams(collective_id=number, has_side_effects=True),
+        cost_estimate=pl.CostEstimate(flops=0, bytes_accessed=20_000_000, transcendentals=0),
+    )(parts, extra)
+
+
+class RingPlan:
+    def order_rows(self, values):
+        shape = values.shape
+        split = values.reshape((2, 2, 2, 4, D // 32) + shape[1:])
+        return jnp.moveaxis(split, 0, 2).reshape(shape)
+
+    def restore_rows(self, values):
+        shape = values.shape
+        split = values.reshape((2, 2, 2, 4, D // 32) + shape[1:])
+        return jnp.moveaxis(split, 2, 0).reshape(shape)
+
+    def gather(self, pieces):
+        widths = tuple(piece.shape[1] for piece in pieces)
+        count, rows = len(pieces), D // 32
+        size = sum(4 * D * width for width in widths)
+        whole = pl.pallas_call(
+            lambda *refs: gather_kernel(widths, *refs),
+            out_shape=[
+                jax.ShapeDtypeStruct((2, 2, 2, 4, rows, width), jnp.bfloat16) for width in widths
+            ],
+            in_specs=[pl.BlockSpec(memory_space=pltpu.VMEM)] * count,
+            out_specs=[pl.BlockSpec(memory_space=pl.ANY)] * count,
+            scratch_shapes=[
+                pltpu.SemaphoreType.DMA((count,)),
+                pltpu.SemaphoreType.DMA((count, 8)),
+                pltpu.SemaphoreType.DMA((count, 8)),
+            ],
+            compiler_params=pltpu.CompilerParams(collective_id=0, has_side_effects=True),
+            cost_estimate=pl.CostEstimate(flops=0, bytes_accessed=size, transcendentals=0),
+        )(*pieces)
+        return [part.reshape(D, -1) for part in whole]
+
+    def scatter(self, grads):
+        widths = tuple(grad.shape[1] for grad in grads)
+        count, rows = len(grads), D // 32
+        size = sum(4 * D * width for width in widths)
+        scratch = [pltpu.VMEM((2, 2, 4, rows, width), jnp.bfloat16) for width in widths] * 2
+        scratch += [pltpu.VMEM((2, 2, 4, rows, width // 2), jnp.bfloat16) for width in widths]
+        scratch += [pltpu.VMEM((2, 4, rows, width // 2), jnp.bfloat16) for width in widths]
+        scratch += [pltpu.VMEM((3, rows, width), jnp.bfloat16) for width in widths]
+        return pl.pallas_call(
+            lambda *refs: scatter_kernel(widths, *refs),
+            out_shape=[jax.ShapeDtypeStruct((rows, width), jnp.bfloat16) for width in widths],
+            in_specs=[pl.BlockSpec(memory_space=pl.ANY)] * count,
+            out_specs=[pl.BlockSpec(memory_space=pltpu.VMEM)] * count,
+            scratch_shapes=scratch
+            + [
+                pltpu.SemaphoreType.DMA((count,)),
+                pltpu.SemaphoreType.DMA((count, 8)),
+                pltpu.SemaphoreType.DMA((count, 8)),
+            ],
+            compiler_params=pltpu.CompilerParams(
+                collective_id=1, has_side_effects=True, vmem_limit_bytes=SCATTER_VMEM
+            ),
+            cost_estimate=pl.CostEstimate(flops=0, bytes_accessed=size, transcendentals=0),
+        )(*[grad.reshape(2, 2, 2, 4, rows, -1) for grad in grads])
+
+    def share(self, finish, parts, extra, number):
+        return share(finish, parts, extra, number)
+
+
+class PlainPlan:
+    def order_rows(self, values):
+        return values
+
+    def restore_rows(self, values):
+        return values
+
+    def gather(self, pieces):
+        return [lax.all_gather(piece, AXES, axis=0, tiled=True) for piece in pieces]
+
+    def scatter(self, grads):
+        return [
+            lax.psum_scatter(grad, AXES, scatter_dimension=0, tiled=True) for grad in grads
+        ]
+
+    def share(self, finish, parts, extra, number):
+        own = finish(scatter_small(parts, parts.shape[0]), extra)
+        return gather_small(own[None], parts.shape[0])
 
 
 def unit_lists():
@@ -276,25 +709,27 @@
     my_unit = lax.dynamic_slice_in_dim(unit_of_slot, me * slot_dev, slot_dev)
     low_slots = master.astype(jnp.bfloat16)
 
-    spread = lax.all_to_all(low_slots, AXES, split_axis=0, concat_axis=1, tiled=True)
+    plan = RingPlan() if (lax.axis_size("rep"), lax.axis_size("shard")) == (8, 4) else PlainPlan()
+    every_int = gather_small(jnp.stack([t_index, labels], 1), count)
+    every_t, every_label = every_int[:, 0], every_int[:, 1]
+    all_images = every_t.shape[0]
+
+    spread = lax.all_to_all(
+        plan.order_rows(low_slots), AXES, split_axis=0, concat_axis=1, tiled=True
+    )
     moved = np.concatenate([dense_units, time_units])
-    unit_rows = jnp.take(spread, owner[moved], axis=1)
-    time_two = lax.all_gather(
-        unit_rows[:, len(dense_units) :].reshape(rows, D), AXES, axis=0, tiled=True
-    )
+    unit_rows = jnp.take(spread, owner[moved], axis=1).reshape(rows, -1)
+    pieces = []
+    for l in range(LAYERS):
+        base = l * DENSE_COLS
+        cuts = (base, base + 4 * D, base + 4 * D + FF, base + DENSE_COLS)
+        pieces += [unit_rows[:, cuts[i] : cuts[i + 1]] for i in range(3)]
+    whole = plan.gather(pieces)
     weights_all = [
-        lax.all_gather(
-            unit_rows[:, l * DENSE_UNITS : (l + 1) * DENSE_UNITS].reshape(rows, DENSE_COLS),
-            AXES,
-            axis=0,
-            tiled=True,
-        )
+        (whole[3 * l][:, : 3 * D], whole[3 * l][:, 3 * D :], whole[3 * l + 1], whole[3 * l + 2])
         for l in range(LAYERS)
     ]
-
-    every_t = lax.all_gather(t_index, AXES, axis=0, tiled=True)
-    every_label = lax.all_gather(labels, AXES, axis=0, tiled=True)
-    all_images = every_t.shape[0]
+    time_two = plan.restore_rows(gather_small(unit_rows[:, LAYERS * DENSE_COLS :], count))
 
     x_start = latents.astype(jnp.float32).reshape(-1, PATCHES, CHANNELS)
     noise_f = noise.astype(jnp.float32).reshape(-1, PATCHES, CHANNELS)
@@ -315,10 +750,17 @@
     freq_low = frequencies(every_time).astype(jnp.bfloat16)
     time_pre = jnp.dot(freq_low, time_w, preferred_element_type=jnp.float32)
     time_act = jax.nn.silu(time_pre).astype(jnp.bfloat16)
-    cond = jnp.dot(time_act, time_two, preferred_element_type=jnp.float32) + jnp.take(
-        table, every_label, axis=0
-    )
-    cond_act = jax.nn.silu(cond).astype(jnp.bfloat16)
+    slot_cond = dot_low("gd,dsc->gsc", time_act, low_slots)
+    time_place = owner[time_units] - me * slot_dev
+    is_here = (time_place >= 0) & (time_place < slot_dev)
+    cond_part = jnp.where(
+        is_here[None, :, None],
+        jnp.take(slot_cond, jnp.clip(time_place, 0, slot_dev - 1), axis=1),
+        0.0,
+    ).reshape(count, images, D)
+    cond_all = plan.share(lambda a, b: a + b, cond_part, jnp.take(table, labels, axis=0), 2)
+    cond = lax.dynamic_index_in_dim(cond_all, me, 0, False)
+    cond_act = jax.nn.silu(cond_all.reshape(all_images, D)).astype(jnp.bfloat16)
 
     slot_modul = dot_low("gd,dsc->gsc", cond_act, low_slots)
     slot_modul = lax.all_to_all(slot_modul, AXES, split_axis=0, concat_axis=1, tiled=True)
@@ -343,20 +785,22 @@
         [jnp.sum(grad_final_in, 1), jnp.sum(grad_final_in * normed_f, 1)], -1
     ).astype(jnp.bfloat16)
     grad_hidden = local_back(norm_rows, hidden, grad_final_in * (1.0 + scale_f[:, None, :]))
-    grad_rows = [None] * LAYERS
+    layer_grads = [None] * LAYERS
     grad_moduls = [None] * LAYERS
     for l in reversed(range(LAYERS)):
-        grad_hidden, grad_moduls[l], weight_grad = layer_backward(
+        grad_hidden, grad_moduls[l], layer_grads[l] = layer_backward(
             grad_hidden, weights_all[l], saved_all[l]
         )
-        grad_rows[l] = lax.psum_scatter(
-            weight_grad.astype(jnp.bfloat16), AXES, scatter_dimension=0, tiled=True
-        )
+    order = list(reversed(range(LAYERS)))
+    scattered = plan.scatter([grad for l in order for grad in reversed(layer_grads[l])])
+    grad_rows = {
+        (l, 2 - i): scattered[3 * n + i] for n, l in enumerate(order) for i in range(3)
+    }
     grad_embed = grad_hidden.astype(jnp.bfloat16)
     grad_patch = dot_low("gpc,gpd->cd", noisy_low, grad_embed)
 
-    every_modul = lax.all_gather(
-        jnp.concatenate(grad_moduls + [grad_modul_f], -1), AXES, axis=0, tiled=True
+    every_modul = gather_small(
+        jnp.concatenate(grad_moduls + [grad_modul_f], -1), count
     ).reshape(all_images, len(image_units), BLOCK)
     image_place = np.full((UNITS + 1,), -1, np.int32)
     image_place[image_units] = np.arange(len(image_units))
@@ -367,12 +811,26 @@
         jnp.zeros((), jnp.bfloat16),
     )
     cond_part = dot_low("gsc,dsc->gd", slot_grad_out, low_slots)
-    small_part = jnp.concatenate([cond_part, grad_patch, grad_head], 0)
-    small_sum, loss_sum = lax.psum((small_part, loss_part), AXES)
-    grad_cond_act = small_sum[:all_images]
-    grad_patch = small_sum[all_images : all_images + CHANNELS]
-    grad_head = small_sum[all_images + CHANNELS :]
-    grad_cond = local_back(jax.nn.silu, cond, grad_cond_act)
+    edge_rows = max(1, 2 * CHANNELS // count)
+    edge = jnp.concatenate([grad_patch, grad_head], 0)
+    edge = jnp.concatenate(
+        [edge, jnp.zeros((edge_rows * count - 2 * CHANNELS, D), jnp.float32)], 0
+    )
+    small_part = jnp.concatenate(
+        [
+            cond_part.reshape(count, images, D),
+            edge.reshape(count, edge_rows, D),
+            jnp.broadcast_to(loss_part, (count, 1, D)),
+        ],
+        1,
+    )
+    factor = local_back(jax.nn.silu, cond, jnp.ones_like(cond))
+    factor = jnp.concatenate([factor, jnp.ones((edge_rows + 1, D), jnp.float32)], 0)
+    small_sum = plan.share(lambda a, b: a * b, small_part, factor, 3)
+    grad_cond = small_sum[:, :images].reshape(all_images, D)
+    edge = small_sum[:, images : images + edge_rows].reshape(-1, D)
+    grad_patch, grad_head = edge[:CHANNELS], edge[CHANNELS : 2 * CHANNELS]
+    loss_sum = small_sum[0, images + edge_rows, 0]
     grad_time_out = grad_cond.astype(jnp.bfloat16)
     grad_time_act = dot_low("ge,de->gd", grad_time_out, time_two)
     grad_time_pre = local_back(jax.nn.silu, time_pre, grad_time_act).astype(jnp.bfloat16)
@@ -391,11 +849,16 @@
     dense_place[dense_units] = np.arange(len(dense_units))
     slot_place = jnp.asarray(dense_place)[unit_of_slot]
     all_rows = jnp.concatenate(
-        [rows_l.reshape(rows, DENSE_UNITS, BLOCK) for rows_l in grad_rows], 1
+        [
+            grad_rows[l, i].reshape(rows, -1, BLOCK)
+            for l in range(LAYERS)
+            for i in range(3)
+        ],
+        1,
     )
     slot_rows = jnp.take(all_rows, slot_place, axis=1)
-    dense_grad = lax.all_to_all(
-        slot_rows, AXES, split_axis=1, concat_axis=0, tiled=True
+    dense_grad = plan.restore_rows(
+        lax.all_to_all(slot_rows, AXES, split_axis=1, concat_axis=0, tiled=True)
     ).astype(jnp.float32)
 
     owned_grad = jnp.where(

time: 1120 us -> 877 us (0.78)
  waiting for transfers between devices: 593 us -> 127 us
  Pallas kernels: 0 us -> 365 us
  blocking collectives: 128 us -> 0 us
  matrix products: 186 us -> 163 us
  starting transfers between devices: 18 us -> 33.1 us
  between operations: 18.4 us -> 5.68 us
    pallas_call x0 -> x4, Pallas kernels: none -> 365 us  [the longest x1 146 us: gather(): pl.pallas_call(lambda *refs: gather_kernel(widths, *refs), out_shape=[jax...]
    reduce_scatter x2 -> x0, waiting for transfers between devices: 234 us -> none  [on_device(): lax.psum_scatter(weight_grad.astype(jnp.bfloat16), AXES, scatter_dimensio...]
    all_gather x4 -> x0, waiting for transfers between devices: 147 us -> none  [the longest x2 147 us: on_device(): lax.all_gather(unit_rows[:, l * DENSE_UNITS:(l + 1) * DENSE_UNITS].reshap...]
    psum x1 -> x0, waiting for transfers between devices: 122 us -> none  [on_device(): small_sum, loss_sum = lax.psum((small_part, loss_part), AXES)]
    psum x1 -> x0, blocking collectives: 89.7 us -> none  [on_device(): small_sum, loss_sum = lax.psum((small_part, loss_part), AXES)]
    dot_general x46 -> x39, matrix products: 183 us -> 132 us  [dot_low(): jnp.einsum(pattern, left_side, right_side, preferred_element_type=jnp.flo...]
    ppermute x0 -> x15, waiting for transfers between devices: none -> 49.8 us  [swap_bit(): return lax.ppermute(values, AXES, [(i, i ^ bit) for i in range(count)])]
    unnamed x1 -> x0, blocking collectives: 38.7 us -> none
  transfers between devices with their start and end apart: 10 -> 18, of which waited for: 7 -> 11; matrix products, arithmetic and copies ran while one was open for 17% -> 12% of each run, Pallas kernels for 0% -> 23%
where the time goes in v2:
time: 877 us; the launch traced here: 865 us
  Pallas kernels  365 us (42%)
  matrix products  163 us (19%)
  waiting for transfers between devices  127 us (14%)
  local copies, waits for them, and re-layouts  103 us (12%)
  other arithmetic  67.4 us (8%)
  starting transfers between devices  33.1 us (4%)
    pallas_call x1, Pallas kernels, gather(): pl.pallas_call(lambda *refs: gather_kernel(widths, *refs), out_shape=[jax...  146 us
    pallas_call x1, Pallas kernels, scatter(): pl.pallas_call(lambda *refs: scatter_kernel(widths, *refs), out_shape=[ja...  145 us
    dot_general x39, matrix products, dot_low(): jnp.einsum(pattern, left_side, right_side, preferred_element_type=jnp.flo...  132 us
    pallas_call x2, Pallas kernels, share(): pl.pallas_call(lambda *refs: share_kernel(finish, *refs), out_shape=jax.S...  73.7 us
    all_to_all x1, waiting for transfers between devices, on_device(): lax.all_to_all(plan.order_rows(low_slots), AXES, split_axis=0, concat_axi...  64.8 us
    ppermute x15, waiting for transfers between devices, swap_bit(): return lax.ppermute(values, AXES, [(i, i ^ bit) for i in range(count)])  49.8 us
    dot_general x8, matrix products, dot_rows(): lax.dot_general(left_side, right_side, (((0,), (0,)), ((), ())), preferre...  30.6 us
    unnamed x296, local copies, waits for them, and re-layouts  22 us
  transfers between devices with their start and end apart: 18, of which 11 were waited for; matrix products, arithmetic and copies ran while one was open for 12% of the time, Pallas kernels for 23%

profile of v2, /device:TPU:3, one launch (start us, length us, event | category | flops | bytes accessed | tf_op | source)
XLA Modules:
  0.0 865.2 jit_solution(2560132429328926268)
XLA Ops:
  55.1 20.6 %shard_map.242 = f32[32,2,768]{2,1,0:T(2,128)} custom-call(f32[32,2,768]{2,1,0:T(2,128)} %select_select_fusion.1.refs_0_, f32[2,768]{1,0:T(2,128)} %broadcast_select_fusion.20.refs_1_), custom_call_target="tpu_custom_call" | custom-call | bytes 20000000 | tf_op jit(solution)/shard_map/pallas_call | solution.py:577
  84.5 12.8 %all-to-all-done = f32[64,15,128]{2,1,0:T(8,128)S(1)} async-done(((f32[64,15,128]{2,1,0:T(8,128)}), f32[64,15,128]{2,1,0:T(8,128)S(1)}, u32[]{:S(2)}, u32[]{:S(2)}) %all-to-all-start) | async-done | bytes 491552 | tf_op jit(solution)/shard_map/all_to_all | solution.py:766
  107.3 64.8 %all-to-all-done.1 = bf16[768,15,128]{2,1,0:T(8,128)(2,1)} async-done(((bf16[768,15,128]{2,1,0:T(8,128)(2,1)}), bf16[768,15,128]{2,1,0:T(8,128)(2,1)}, u32[]{:S(2)}, u32[]{:S(2)}) %all-to-all-start.1) | async-done | bytes 2949152 | tf_op jit(solution)/shard_map/all_to_all | solution.py:717
  181.1 146.2 %shard_map.243 = (bf16[2,2,2,4,24,3072]{5,4,3,2,1,0:T(8,128)(2,1)}, bf16[2,2,2,4,24,3072]{5,4,3,2,1,0:T(8,128)(2,1)}, bf16[2,2,2,4,24,3072]{5,4,3,2,1,0:T(8,128)...) custom-call(bf16[24,3072]{1,0:T(8,128)(2,1)} %get-tuple-element.91.r, ...), custom_call_target="tpu_custom_call" | custom-call | bytes 56623104 | tf_op jit(solution)/shard_map/pallas_call | solution.py:607
  347.7 5.0 fusion.102
  371.5 6.5 fusion.100
  382.9 8.5 fusion.13
  402.1 5.3 convolution_convert_fusion.8
  423.1 4.9 multiply_reduce_fusion.15
  430.6 10.3 %fusion.6 = bf16[2,256,3072]{2,1,0:T(8,128)(2,1)S(1)} fusion(f32[2,256,3072]{2,1,0:T(8,128)} %copy-done.110, bf16[768,3072,1]{1,0,2:T(8,128)(2,1)} %bitcast.387, f32[2,256,768]{2,1,0:T(8,128)S(1)} %get-tuple-element.57, f32[2,768]{1,0:T(2,128)S(1)} %get-tuple-element.118), kind=kOutput, calls=%fused_computation.33 | convolution fusion | flops 2448162816 | bytes 15734784 | tf_op jit(solution)/shard_map/gpd,df->gpf/dot_general | solution.py:55
  453.4 5.3 convolution_convert_fusion.4
  467.8 8.2 bitcast_convert_fusion.3
  489.6 5.1 bitcast_convert_fusion
  501.8 5.0 multiply_reduce_fusion.4
  512.7 5.1 collective-permute-start.5
  527.2 145.3 %shard_map.245 = (bf16[24,3072]{1,0:T(8,128)(2,1)}, bf16[24,3072]{1,0:T(8,128)(2,1)}, bf16[24,3072]{1,0:T(8,128)(2,1)}, bf16[24,3072]{1,0:T(8,128)(2,1)}, bf16[2...) custom-call(bf16[2,2,2,4,24,3072]{5,4,3,2,1,0:T(8,128)(2,1)} %bitcast.338, bf16[2,2,2,4,24,3072]{5,4,3,2,1,0:T(8,128)(2,1)} %bitcast.339, ...), custom_call_target="tpu_custom_call" | custom-call | bytes 56623104 | tf_op jit(solution)/shard_map/pallas_call | solution.py:632
  688.9 5.6 collective-permute-done.11
  699.0 6.9 collective-permute-done.13
  707.1 6.3 collective-permute-done.8
  717.9 5.5 all-to-all-start.2
  726.6 25.0 %collective-permute-done.9 = bf16[32,10752]{1,0:T(8,128)(2,1)} collective-permute-done((bf16[32,10752]{1,0:T(8,128)(2,1)}, bf16[32,10752]{1,0:T(8,128)(2,1)}, u32[]{:S(2)}, u32[]{:S(2)}) %collective-permute-start.9) | collective-permute-done | bytes 688160 | tf_op jit(solution)/shard_map/ppermute | solution.py:233
  758.5 53.1 %shard_map.244 = f32[32,4,768]{2,1,0:T(4,128)} custom-call(f32[32,4,768]{2,1,0:T(4,128)} %maximum_maximum_fusion.refs_0_, f32[4,768]{1,0:T(4,128)} %concatenate.108.refs_1_), custom_call_target="tpu_custom_call" | custom-call | bytes 20000000 | tf_op jit(solution)/shard_map/pallas_call | solution.py:577
  830.2 10.0 %multiply_subtract_fusion = (f32[1288,768]{1,0:T(8,128)}, f32[1288,768]{1,0:T(8,128)}, f32[1288,768]{1,0:T(8,128)}) fusion(f32[1288,768]{1,0:T(8,128)S(1)} %copy-done.10, f32[1288]{0:T(1024)S(1)} %copy-done.80, f32[16,768]{1,0:T(8,128)S(1)} %bitcast.371, f32[1000,768]{1,0:T(8,128)S(1)} %scatter_custom_fusion.1, f32[256,768]{1,0:T(8,128)S(1)} %copy-done.45, ...), kind=kLoop, calls=%fused_computation.68 | loop fusion | flops 16816128 | bytes 27702304 | tf_op jit(solution)/shard_map/sub | solution.py:105
  846.0 17.6 %fusion.17 = (f32[768,15,128]{2,0,1:T(8,128)}, f32[768,15,128]{2,0,1:T(8,128)}, f32[768,15,128]{2,0,1:T(8,128)}) fusion(f32[768,15,128]{2,0,1:T(8,128)} %param.26, pred[15]{0:T(512)(128)(4,1)S(1)} %copy-done.102, f32[768,15,128]{2,0,1:T(8,128)S(1)} %bitcast.336, f32[768,15,128]{2,0,1:T(8,128)} %param.25, f32[15]{0:T(128)S(1)} %copy-done.109, ...), kind=kOutput, calls=%fused_computation.61 | convolution fusion | flops 217128960 | bytes 47628408 | tf_op jit(solution)/shard_map/gd,gsc->dsc/dot_general | solution.py:55
  (563 shorter events, 270.8 us)
Async XLA Ops:
  1.3 28.1 %collective-permute-start = (s32[2,2]{0,1:T(2,128)S(1)}, s32[2,2]{0,1:T(2,128)S(1)}, u32[]{:S(2)}, u32[]{:S(2)}) collective-permute-start(s32[2,2]{0,1:T(2,128)S(1)} %pad_add_fusion), channel_id=1, source_target_pairs={{0,1},{1,0},{2,3},{3,2},{4,5},{5,4},{6,7},{7,6},{8,9},{9,8},{10,11... | collective-permute-start | bytes 56 | tf_op jit(solution)/shard_map/ppermute | solution.py:233
  29.6 3.3 collective-permute-start.1
  33.0 2.9 collective-permute-start.2
  36.1 2.4 collective-permute-start.3
  38.7 9.1 %collective-permute-start.4 = (s32[32,2]{0,1:T(2,128)S(1)}, s32[32,2]{0,1:T(2,128)S(1)}, u32[]{:S(2)}, u32[]{:S(2)}) collective-permute-start(s32[32,2]{0,1:T(2,128)S(1)} %pad_add_fusion.4), channel_id=1, source_target_pairs={{0,16},{1,17},{2,18},{3,19},{4,20},{5,21},{6,22},{7,23},{8,24},{9,... | collective-permute-start | bytes 776 | tf_op jit(solution)/shard_map/ppermute | solution.py:233
  78.5 18.8 %all-to-all-start = ((f32[64,15,128]{2,1,0:T(8,128)}), f32[64,15,128]{2,1,0:T(8,128)S(1)}, u32[]{:S(2)}, u32[]{:S(2)}) async-start(f32[64,15,128]{2,1,0:T(8,128)} %copy.286), calls=%async_computation | async-start | bytes 1048576 | tf_op jit(solution)/shard_map/all_to_all | solution.py:766
  84.4 256.3 %copy-start.7 = (f32[2,256,768]{2,1,0:T(8,128)}, f32[2,256,768]{2,1,0:T(8,128)S(1)}, u32[]{:S(2)}) copy-start(f32[2,256,768]{2,1,0:T(8,128)S(1)} %get-tuple-element.152) | copy-start | bytes 4718596
  84.4 242.9 %copy-start.78 = (f32[2,256]{1,0:T(2,128)}, f32[2,256]{1,0:T(2,128)S(1)}, u32[]{:S(2)}) copy-start(f32[2,256]{1,0:T(2,128)S(1)} %broadcast_multiply_fusion.4) | copy-start | bytes 6148
  97.3 74.8 %all-to-all-start.1 = ((bf16[768,15,128]{2,1,0:T(8,128)(2,1)}), bf16[768,15,128]{2,1,0:T(8,128)(2,1)}, u32[]{:S(2)}, u32[]{:S(2)}) async-start(bf16[768,15,128]{2,1,0:T(8,128)(2,1)} %copy.289), calls=%async_computation.1 | async-start | bytes 6291456 | tf_op jit(solution)/shard_map/all_to_all | solution.py:717
  103.5 223.8 %copy-start.81 = (f32[2,256]{1,0:T(2,128)}, f32[2,256]{1,0:T(2,128)S(1)}, u32[]{:S(2)}) copy-start(f32[2,256]{1,0:T(2,128)S(1)} %fusion.67) | copy-start | bytes 6148
  107.3 220.1 %copy-start.76 = (f32[2,768]{1,0:T(2,128)}, f32[2,768]{1,0:T(2,128)S(1)}, u32[]{:S(2)}) copy-start(f32[2,768]{1,0:T(2,128)S(1)} %get-tuple-element.121) | copy-start | bytes 18436
  107.3 220.1 %copy-start.88 = (f32[2,768]{1,0:T(2,128)}, f32[2,768]{1,0:T(2,128)S(1)}, u32[]{:S(2)}) copy-start(f32[2,768]{1,0:T(2,128)S(1)} %get-tuple-element.120) | copy-start | bytes 18436
  512.7 173.6 %collective-permute-start.5 = (bf16[2,10752]{1,0:T(2,128)(2,1)S(1)}, bf16[2,10752]{1,0:T(2,128)(2,1)S(1)}, u32[]{:S(2)}, u32[]{:S(2)}) collective-permute-start(bf16[2,10752]{1,0:T(2,128)(2,1)S(1)} %constant_dynamic-update-slice_fusion), channel_id=1, source_target_pairs={{0,1},{1,0},{2,3},{3,2},{4,5},{5,4},{6,7},{7,6},{8,9},{9,8},{10,11... | collective-permute-start | bytes 129032 | tf_op jit(solution)/shard_map/ppermute | solution.py:233
  527.2 155.4 %copy-start.87 = (s32[1024]{0:T(1024)S(1)}, s32[1024]{0:T(1024)}, u32[]{:S(2)}) copy-start(s32[1024]{0:T(1024)} %get-tuple-element.178) | copy-start | bytes 12292
  673.5 11.9 %collective-permute-start.10 = (bf16[24,768]{1,0:T(8,128)(2,1)S(1)}, bf16[24,768]{1,0:T(8,128)(2,1)S(1)}, u32[]{:S(2)}, u32[]{:S(2)}) collective-permute-start(bf16[24,768]{1,0:T(8,128)(2,1)S(1)} %slice.185), channel_id=1, source_target_pairs={{0,1},{1,0},{2,3},{3,2},{4,5},{5,4},{6,7},{7,6},{8,9},{9,8},{10,11... | collective-permute-start | bytes 110600 | tf_op jit(solution)/shard_map/ppermute | solution.py:233
  686.2 8.3 collective-permute-start.11
  686.5 9.9 %collective-permute-start.6 = (bf16[4,10752]{1,0:T(4,128)(2,1)S(1)}, bf16[4,10752]{1,0:T(4,128)(2,1)S(1)}, u32[]{:S(2)}, u32[]{:S(2)}) collective-permute-start(bf16[4,10752]{1,0:T(4,128)(2,1)S(1)} %pad_maximum_fusion.18), channel_id=1, source_target_pairs={{0,2},{1,3},{2,0},{3,1},{4,6},{5,7},{6,4},{7,5},{8,10},{9,11},{10,... | collective-permute-start | bytes 258056 | tf_op jit(solution)/shard_map/ppermute | solution.py:233
  694.6 2.6 collective-permute-start.12
  696.6 1.6 collective-permute-start.7
  697.2 8.7 %collective-permute-start.13 = (bf16[192,768]{1,0:T(8,128)(2,1)S(1)}, bf16[192,768]{1,0:T(8,128)(2,1)S(1)}, u32[]{:S(2)}, u32[]{:S(2)}) collective-permute-start(bf16[192,768]{1,0:T(8,128)(2,1)S(1)} %pad_maximum_fusion.14), channel_id=1, source_target_pairs={{0,8},{1,9},{2,10},{3,11},{4,12},{5,13},{6,14},{7,15},{8,0},{9,1},... | collective-permute-start | bytes 884744 | tf_op jit(solution)/shard_map/ppermute | solution.py:233
  698.4 15.0 %collective-permute-start.8 = (bf16[16,10752]{1,0:T(8,128)(2,1)S(1)}, bf16[16,10752]{1,0:T(8,128)(2,1)S(1)}, u32[]{:S(2)}, u32[]{:S(2)}) collective-permute-start(bf16[16,10752]{1,0:T(8,128)(2,1)S(1)} %pad_maximum_fusion.13), channel_id=1, source_target_pairs={{0,8},{1,9},{2,10},{3,11},{4,12},{5,13},{6,14},{7,15},{8,0},{9,1},... | collective-permute-start | bytes 1032200 | tf_op jit(solution)/shard_map/ppermute | solution.py:233
  707.0 17.1 %collective-permute-start.14 = (bf16[384,768]{1,0:T(8,128)(2,1)}, bf16[384,768]{1,0:T(8,128)(2,1)}, u32[]{:S(2)}, u32[]{:S(2)}) collective-permute-start(bf16[384,768]{1,0:T(8,128)(2,1)} %pad_maximum_fusion.12), channel_id=1, source_target_pairs={{0,16},{1,17},{2,18},{3,19},{4,20},{5,21},{6,22},{7,23},{8,24},{9,... | collective-permute-start | bytes 1769480 | tf_op jit(solution)/shard_map/ppermute | solution.py:233
  715.1 36.4 %collective-permute-start.9 = (bf16[32,10752]{1,0:T(8,128)(2,1)}, bf16[32,10752]{1,0:T(8,128)(2,1)}, u32[]{:S(2)}, u32[]{:S(2)}) collective-permute-start(bf16[32,10752]{1,0:T(8,128)(2,1)} %pad_maximum_fusion.11), channel_id=1, source_target_pairs={{0,16},{1,17},{2,18},{3,19},{4,20},{5,21},{6,22},{7,23},{8,24},{9,... | collective-permute-start | bytes 2064392 | tf_op jit(solution)/shard_map/ppermute | solution.py:233
  717.9 122.3 %all-to-all-start.2 = ((bf16[24,480,128]{2,0,1:T(8,128)(2,1)}), bf16[24,480,128]{2,0,1:T(8,128)(2,1)}, u32[]{:S(2)}, u32[]{:S(2)}) async-start(bf16[24,480,128]{2,0,1:T(8,128)(2,1)} %select_bitcast_fusion), calls=%async_computation.2 | async-start | bytes 5898240 | tf_op jit(solution)/shard_map/all_to_all | solution.py:861
  (131 other events, 895.9 us)

commit v3 on v2

--- a/solution.py
+++ b/solution.py
@@ -264,6 +264,7 @@
 
 
 MESH = pl.DeviceIdType.MESH
+GATHER_VMEM = 40 * 2**20
 SCATTER_VMEM = 56 * 2**20
 
 
@@ -288,11 +289,22 @@
     return (y * 2 + x) * 2 + c
 
 
-def meet(targets):
+def device_at(j):
+    shards = lax.axis_size("shard")
+    devices = lax.axis_size("rep") * shards
+    me = lax.axis_index("rep") * shards + lax.axis_index("shard")
+    peer = lax.rem(me + j, devices)
+    return peer, (peer // shards, lax.rem(peer, shards))
+
+
+def meet_all(devices):
     barrier = pltpu.get_barrier_semaphore()
-    for target in targets:
-        pl.semaphore_signal(barrier, inc=1, device_id=target, device_id_type=MESH)
-    pl.semaphore_wait(barrier, len(targets))
+
+    @pl.loop(1, devices)
+    def _(j):
+        pl.semaphore_signal(barrier, inc=1, device_id=device_at(j)[1], device_id_type=MESH)
+
+    pl.semaphore_wait(barrier, devices - 1)
 
 
 def neighbours():
@@ -306,11 +318,17 @@
 
 def gather_kernel(widths, *refs):
     count = len(widths)
-    pieces, outs = refs[:count], refs[count : 2 * count]
-    own_sem, send_sem, recv_sem = refs[2 * count :]
+    pieces = refs[:count]
+    time_act, label_rows, low_slots = refs[count : count + 3]
+    outs = refs[count + 3 : 2 * count + 3]
+    cond_out, modul_out = refs[2 * count + 3 : 2 * count + 5]
+    time_two, parts, own_sem, send_sem, recv_sem, time_sem, modul_sem = refs[2 * count + 5 :]
+    devices, images = modul_out.shape[:2]
+    slots = low_slots.shape[0]
     y, x, c, z = place_of()
     to_x, to_y, to_core, to_z = neighbours()
-    meet([to_x, to_y, to_core] + to_z)
+    me = rep_of(y, x, c) * 4 + z
+    meet_all(devices)
 
     def remote(k, number, source, dest, target):
         return pltpu.make_async_remote_copy(
@@ -363,6 +381,35 @@
     def arrived(copies):
         for copy in copies:
             copy.wait_recv()
+
+    def modul_copy(j, arriving):
+        peer, where = device_at(devices - j if arriving else j)
+        return pltpu.make_async_remote_copy(
+            src_ref=parts.at[pl.ds(peer * images, images)],
+            dst_ref=modul_out.at[peer if arriving else me],
+            send_sem=modul_sem.at[0, j],
+            recv_sem=modul_sem.at[1, j],
+            device_id=where,
+            device_id_type=MESH,
+        )
+
+    def image_products():
+        copy = pltpu.make_async_copy(outs[0], time_two, time_sem)
+        copy.start()
+        copy.wait()
+        weight = time_two[...].reshape(D, D).astype(jnp.bfloat16)
+        cond = jnp.dot(time_act[...], weight, preferred_element_type=jnp.float32)
+        cond = cond + label_rows[...]
+        cond_out[...] = cond
+        act = (cond * jax.nn.sigmoid(cond)).astype(jnp.bfloat16)
+        for s in range(slots):
+            parts[:, s, :] = jnp.dot(act, low_slots[s], preferred_element_type=jnp.float32)
+        for i in range(images):
+            modul_out[me, i] = parts[me * images + i]
+
+        @pl.loop(1, devices)
+        def _(j):
+            modul_copy(j, False).start()
 
     for k in range(count):
         own_copy(k).start()
@@ -380,8 +427,17 @@
         if 0 <= t - 2 < count:
             arrived(second_copies(t - 2, True))
             start(core_copies(t - 2, False))
-    for k in range(count):
+        if t == 3:
+            arrived(core_copies(0, True))
+            image_products()
+    for k in range(1, count):
         arrived(core_copies(k, True))
+
+    @pl.loop(1, devices)
+    def _(j):
+        modul_copy(j, True).wait_recv()
+        modul_copy(j, False).wait_send()
+
     for k in range(count):
         for copies in (line_copies, first_copies, second_copies, core_copies):
             for copy in copies(k, False):
@@ -390,15 +446,29 @@
 
 def scatter_kernel(widths, *refs):
     count = len(widths)
-    grads, outs = refs[:count], refs[count : 2 * count]
-    scratch = refs[2 * count :]
+    grads, modul = refs[:count], refs[count]
+    outs, every_modul = refs[count + 1 : 2 * count + 1], refs[2 * count + 1]
+    scratch = refs[2 * count + 2 :]
+    devices = every_modul.shape[0]
     own, core_in, first_in, second_in, line_in = (
         scratch[i * count : (i + 1) * count] for i in range(5)
     )
-    own_sem, send_sem, recv_sem = scratch[5 * count :]
+    own_sem, send_sem, recv_sem, modul_sem = scratch[5 * count :]
     y, x, c, z = place_of()
     to_x, to_y, to_core, to_z = neighbours()
-    meet([to_x, to_y, to_core] + to_z)
+    me = rep_of(y, x, c) * 4 + z
+    meet_all(devices)
+
+    def modul_copy(j, arriving):
+        peer, where = device_at(devices - j if arriving else j)
+        return pltpu.make_async_remote_copy(
+            src_ref=modul,
+            dst_ref=every_modul.at[peer if arriving else me],
+            send_sem=modul_sem.at[0, j],
+            recv_sem=modul_sem.at[1, j],
+            device_id=where,
+            device_id_type=MESH,
+        )
 
     def remote(k, number, source, dest, target):
         return pltpu.make_async_remote_copy(
@@ -480,6 +550,12 @@
     for k in range(count):
         start(core_copies(k))
         own_copy(k).start()
+    every_modul[me] = modul[...]
+
+    @pl.loop(1, devices)
+    def _(j):
+        modul_copy(j, False).start()
+
     for t in range(count + 3):
         if t < count:
             own_copy(t).wait()
@@ -506,6 +582,11 @@
             for copy in copies(k):
                 copy.wait_send()
 
+    @pl.loop(1, devices)
+    def _(j):
+        modul_copy(j, True).wait_recv()
+        modul_copy(j, False).wait_send()
+
 
 def share_kernel(finish, parts, extra, out, landed, send_sem, recv_sem):
     devices = parts.shape[0]
@@ -600,28 +681,47 @@
         split = values.reshape((2, 2, 2, 4, D // 32) + shape[1:])
         return jnp.moveaxis(split, 2, 0).reshape(shape)
 
-    def gather(self, pieces):
+    def gather(self, pieces, time_piece, time_act, label_rows, low_slots):
+        pieces = [time_piece.astype(jnp.float32)] + list(pieces)
         widths = tuple(piece.shape[1] for piece in pieces)
         count, rows = len(pieces), D // 32
+        all_images = time_act.shape[0]
+        slots = low_slots.shape[1]
+        room = -(-slots // 8) * 8
         size = sum(4 * D * width for width in widths)
-        whole = pl.pallas_call(
+        whole_shape = [(2, 2, 2, 4, rows, width) for width in widths]
+        *whole, cond, modul = pl.pallas_call(
             lambda *refs: gather_kernel(widths, *refs),
             out_shape=[
-                jax.ShapeDtypeStruct((2, 2, 2, 4, rows, width), jnp.bfloat16) for width in widths
+                jax.ShapeDtypeStruct(shape, piece.dtype)
+                for shape, piece in zip(whole_shape, pieces)
+            ]
+            + [
+                jax.ShapeDtypeStruct((all_images, D), jnp.float32),
+                jax.ShapeDtypeStruct((32, all_images // 32, room, BLOCK), jnp.float32),
             ],
-            in_specs=[pl.BlockSpec(memory_space=pltpu.VMEM)] * count,
-            out_specs=[pl.BlockSpec(memory_space=pl.ANY)] * count,
+            in_specs=[pl.BlockSpec(memory_space=pltpu.VMEM)] * (count + 3),
+            out_specs=[pl.BlockSpec(memory_space=pl.ANY)] * count
+            + [pl.BlockSpec(memory_space=pltpu.VMEM)] * 2,
             scratch_shapes=[
+                pltpu.VMEM(whole_shape[0], jnp.float32),
+                pltpu.VMEM((all_images, room, BLOCK), jnp.float32),
                 pltpu.SemaphoreType.DMA((count,)),
                 pltpu.SemaphoreType.DMA((count, 8)),
                 pltpu.SemaphoreType.DMA((count, 8)),
+                pltpu.SemaphoreType.DMA,
+                pltpu.SemaphoreType.DMA((2, 32)),
             ],
-            compiler_params=pltpu.CompilerParams(collective_id=0, has_side_effects=True),
+            compiler_params=pltpu.CompilerParams(
+                collective_id=0, has_side_effects=True, vmem_limit_bytes=GATHER_VMEM
+            ),
             cost_estimate=pl.CostEstimate(flops=0, bytes_accessed=size, transcendentals=0),
-        )(*pieces)
-        return [part.reshape(D, -1) for part in whole]
-
-    def scatter(self, grads):
+        )(*pieces, time_act, label_rows, jnp.swapaxes(low_slots, 0, 1))
+        whole = [part.reshape(D, -1) for part in whole]
+        modul = jnp.swapaxes(modul[:, :, :slots], 0, 1).reshape(-1, 32 * slots, BLOCK)
+        return whole[1:], whole[0].astype(jnp.bfloat16), cond, modul
+
+    def scatter(self, grads, modul):
         widths = tuple(grad.shape[1] for grad in grads)
         count, rows = len(grads), D // 32
         size = sum(4 * D * width for width in widths)
@@ -629,22 +729,27 @@
         scratch += [pltpu.VMEM((2, 2, 4, rows, width // 2), jnp.bfloat16) for width in widths]
         scratch += [pltpu.VMEM((2, 4, rows, width // 2), jnp.bfloat16) for width in widths]
         scratch += [pltpu.VMEM((3, rows, width), jnp.bfloat16) for width in widths]
-        return pl.pallas_call(
+        piece = modul.reshape(-1, BLOCK)
+        *scattered, every_modul = pl.pallas_call(
             lambda *refs: scatter_kernel(widths, *refs),
-            out_shape=[jax.ShapeDtypeStruct((rows, width), jnp.bfloat16) for width in widths],
-            in_specs=[pl.BlockSpec(memory_space=pl.ANY)] * count,
-            out_specs=[pl.BlockSpec(memory_space=pltpu.VMEM)] * count,
+            out_shape=[jax.ShapeDtypeStruct((rows, width), jnp.bfloat16) for width in widths]
+            + [jax.ShapeDtypeStruct((32,) + piece.shape, jnp.bfloat16)],
+            in_specs=[pl.BlockSpec(memory_space=pl.ANY)] * count
+            + [pl.BlockSpec(memory_space=pltpu.VMEM)],
+            out_specs=[pl.BlockSpec(memory_space=pltpu.VMEM)] * (count + 1),
             scratch_shapes=scratch
             + [
                 pltpu.SemaphoreType.DMA((count,)),
                 pltpu.SemaphoreType.DMA((count, 8)),
                 pltpu.SemaphoreType.DMA((count, 8)),
+                pltpu.SemaphoreType.DMA((2, 32)),
             ],
             compiler_params=pltpu.CompilerParams(
                 collective_id=1, has_side_effects=True, vmem_limit_bytes=SCATTER_VMEM
             ),
             cost_estimate=pl.CostEstimate(flops=0, bytes_accessed=size, transcendentals=0),
-        )(*[grad.reshape(2, 2, 2, 4, rows, -1) for grad in grads])
+        )(*[grad.reshape(2, 2, 2, 4, rows, -1) for grad in grads], piece)
+        return scattered, every_modul.reshape(32 * modul.shape[0], -1)
 
     def share(self, finish, parts, extra, number):
         return share(finish, parts, extra, number)
@@ -657,13 +762,19 @@
     def restore_rows(self, values):
         return values
 
-    def gather(self, pieces):
-        return [lax.all_gather(piece, AXES, axis=0, tiled=True) for piece in pieces]
-
-    def scatter(self, grads):
-        return [
+    def gather(self, pieces, time_piece, time_act, label_rows, low_slots):
+        whole = [lax.all_gather(piece, AXES, axis=0, tiled=True) for piece in pieces]
+        time_two = lax.all_gather(time_piece, AXES, axis=0, tiled=True)
+        cond = jnp.dot(time_act, time_two, preferred_element_type=jnp.float32) + label_rows
+        modul = dot_low("gd,dsc->gsc", jax.nn.silu(cond).astype(jnp.bfloat16), low_slots)
+        modul = lax.all_to_all(modul, AXES, split_axis=0, concat_axis=1, tiled=True)
+        return whole, time_two, cond, modul
+
+    def scatter(self, grads, modul):
+        scattered = [
             lax.psum_scatter(grad, AXES, scatter_dimension=0, tiled=True) for grad in grads
         ]
+        return scattered, lax.all_gather(modul, AXES, axis=0, tiled=True)
 
     def share(self, finish, parts, extra, number):
         own = finish(scatter_small(parts, parts.shape[0]), extra)
@@ -724,13 +835,6 @@
         base = l * DENSE_COLS
         cuts = (base, base + 4 * D, base + 4 * D + FF, base + DENSE_COLS)
         pieces += [unit_rows[:, cuts[i] : cuts[i + 1]] for i in range(3)]
-    whole = plan.gather(pieces)
-    weights_all = [
-        (whole[3 * l][:, : 3 * D], whole[3 * l][:, 3 * D :], whole[3 * l + 1], whole[3 * l + 2])
-        for l in range(LAYERS)
-    ]
-    time_two = plan.restore_rows(gather_small(unit_rows[:, LAYERS * DENSE_COLS :], count))
-
     x_start = latents.astype(jnp.float32).reshape(-1, PATCHES, CHANNELS)
     noise_f = noise.astype(jnp.float32).reshape(-1, PATCHES, CHANNELS)
     times = (t_index.astype(jnp.float32) + 0.5) / TSTEPS
@@ -750,20 +854,16 @@
     freq_low = frequencies(every_time).astype(jnp.bfloat16)
     time_pre = jnp.dot(freq_low, time_w, preferred_element_type=jnp.float32)
     time_act = jax.nn.silu(time_pre).astype(jnp.bfloat16)
-    slot_cond = dot_low("gd,dsc->gsc", time_act, low_slots)
-    time_place = owner[time_units] - me * slot_dev
-    is_here = (time_place >= 0) & (time_place < slot_dev)
-    cond_part = jnp.where(
-        is_here[None, :, None],
-        jnp.take(slot_cond, jnp.clip(time_place, 0, slot_dev - 1), axis=1),
-        0.0,
-    ).reshape(count, images, D)
-    cond_all = plan.share(lambda a, b: a + b, cond_part, jnp.take(table, labels, axis=0), 2)
-    cond = lax.dynamic_index_in_dim(cond_all, me, 0, False)
-    cond_act = jax.nn.silu(cond_all.reshape(all_images, D)).astype(jnp.bfloat16)
-
-    slot_modul = dot_low("gd,dsc->gsc", cond_act, low_slots)
-    slot_modul = lax.all_to_all(slot_modul, AXES, split_axis=0, concat_axis=1, tiled=True)
+    label_rows = jnp.take(table, every_label, axis=0)
+    whole, time_two, cond_all, slot_modul = plan.gather(
+        pieces, unit_rows[:, LAYERS * DENSE_COLS :], time_act, label_rows, low_slots
+    )
+    weights_all = [
+        (whole[3 * l][:, : 3 * D], whole[3 * l][:, 3 * D :], whole[3 * l + 1], whole[3 * l + 2])
+        for l in range(LAYERS)
+    ]
+    cond = lax.dynamic_slice_in_dim(cond_all, me * images, images)
+    cond_act = jax.nn.silu(cond_all).astype(jnp.bfloat16)
     modul_all = jnp.take(slot_modul, owner[image_units], axis=1).reshape(images, -1)
 
     saved_all = []
@@ -792,16 +892,17 @@
             grad_hidden, weights_all[l], saved_all[l]
         )
     order = list(reversed(range(LAYERS)))
-    scattered = plan.scatter([grad for l in order for grad in reversed(layer_grads[l])])
+    scattered, every_modul = plan.scatter(
+        [grad for l in order for grad in reversed(layer_grads[l])],
+        jnp.concatenate(grad_moduls + [grad_modul_f], -1),
+    )
+    every_modul = every_modul.reshape(all_images, len(image_units), BLOCK)
     grad_rows = {
         (l, 2 - i): scattered[3 * n + i] for n, l in enumerate(order) for i in range(3)
     }
     grad_embed = grad_hidden.astype(jnp.bfloat16)
     grad_patch = dot_low("gpc,gpd->cd", noisy_low, grad_embed)
 
-    every_modul = gather_small(
-        jnp.concatenate(grad_moduls + [grad_modul_f], -1), count
-    ).reshape(all_images, len(image_units), BLOCK)
     image_place = np.full((UNITS + 1,), -1, np.int32)
     image_place[image_units] = np.arange(len(image_units))
     my_place = jnp.asarray(image_place)[my_unit]

time: 877 us -> 810 us (0.924)
  waiting for transfers between devices: 127 us -> 47.4 us
  Pallas kernels: 365 us -> 396 us
  starting transfers between devices: 33.1 us -> 21.9 us
    all_to_all x1, waiting for transfers between devices: 64.8 us -> 0.01 us  [on_device(): lax.all_to_all(plan.order_rows(low_slots), AXES, split_axis=0, concat_axi...]
    pallas_call x1, Pallas kernels: 146 us -> 164 us  [gather(): pl.pallas_call(lambda *refs: gather_kernel(widths, *refs), out_shape=[jax...]
    ppermute x15 -> x5, starting transfers between devices: 20.4 us -> 7.48 us  [swap_bit(): return lax.ppermute(values, AXES, [(i, i ^ bit) for i in range(count)])]
    pallas_call x1, Pallas kernels: 145 us -> 158 us  [scatter(): pl.pallas_call(lambda *refs: scatter_kernel(widths, *refs), out_shape=[ja...]
    all_to_all x1 -> x0, waiting for transfers between devices: 12.8 us -> none  [on_device(): lax.all_to_all(slot_modul, AXES, split_axis=0, concat_axis=1, tiled=True)]
    unnamed x296 -> x302, local copies, waits for them, and re-layouts: 22 us -> 19.5 us
    ppermute x15 -> x5, waiting for transfers between devices: 49.8 us -> 47.4 us  [swap_bit(): return lax.ppermute(values, AXES, [(i, i ^ bit) for i in range(count)])]
    dot_general x39 -> x37, matrix products: 132 us -> 131 us  [dot_low(): jnp.einsum(pattern, left_side, right_side, preferred_element_type=jnp.flo...]
  transfers between devices with their start and end apart: 18 -> 7, of which waited for: 11 -> 3; matrix products, arithmetic and copies ran while one was open for 12% -> 10% of each run, Pallas kernels for 23% -> 9%
where the time goes in v3:
time: 810 us; the launch traced here: 803 us
  Pallas kernels  396 us (49%)
  matrix products  167 us (21%)
  local copies, waits for them, and re-layouts  99.5 us (12%)
  other arithmetic  66.8 us (8%)
  waiting for transfers between devices  47.4 us (6%)
  starting transfers between devices  21.9 us (3%)
    pallas_call x1, Pallas kernels, gather(): pl.pallas_call(lambda *refs: gather_kernel(widths, *refs), out_shape=[jax...  164 us
    pallas_call x1, Pallas kernels, scatter(): pl.pallas_call(lambda *refs: scatter_kernel(widths, *refs), out_shape=[ja...  158 us
    dot_general x37, matrix products, dot_low(): jnp.einsum(pattern, left_side, right_side, preferred_element_type=jnp.flo...  131 us
    pallas_call x1, Pallas kernels, share(): pl.pallas_call(lambda *refs: share_kernel(finish, *refs), out_shape=jax.S...  73.3 us
    ppermute x5, waiting for transfers between devices, swap_bit(): return lax.ppermute(values, AXES, [(i, i ^ bit) for i in range(count)])  47.4 us
    dot_general x8, matrix products, dot_rows(): lax.dot_general(left_side, right_side, (((0,), (0,)), ((), ())), preferre...  33.6 us
    unnamed x302, local copies, waits for them, and re-layouts  19.5 us
  transfers between devices with their start and end apart: 7, of which 3 were waited for; matrix products, arithmetic and copies ran while one was open for 10% of the time, Pallas kernels for 9%

profile of v3, /device:TPU:3, one launch (start us, length us, event | category | flops | bytes accessed | tf_op | source)
XLA Modules:
  0.0 803.5 jit_solution(15938702775311656269)
XLA Ops:
  11.0 5.8 all-to-all-start
  41.4 45.6 %collective-permute-done.1 = s32[4,2]{0,1:T(2,128)S(1)} collective-permute-done((s32[4,2]{0,1:T(2,128)S(1)}, s32[4,2]{0,1:T(2,128)S(1)}, u32[]{:S(2)}, u32[]{:S(2)}) %collective-permute-start.1) | collective-permute-done | bytes 64 | tf_op jit(solution)/shard_map/ppermute | solution.py:233
  112.1 164.3 %shard_map.224 = (f32[2,2,2,4,24,768]{5,4,3,2,1,0:T(8,128)S(1)}, bf16[2,2,2,4,24,3072]{5,4,3,2,1,0:T(8,128)(2,1)S(1)}, bf16[2,2,2,4,24,3072]{5,4,3,2,1,0:T(8,128...) custom-call(f32[24,768]{1,0:T(8,128)S(1)} %slice_convert_fusion.refs, ...), custom_call_target="tpu_custom_call" | custom-call | bytes 58982400 | tf_op jit(solution)/shard_map/pallas_call | solution.py:693
  281.3 4.6 convolution_convert_fusion.1
  301.4 5.4 fusion.96
  326.6 4.8 fusion.58
  331.4 6.3 fusion.94
  343.8 7.6 fusion.13
  351.4 8.0 bitcast_convert_fusion.3
  362.1 5.1 bitcast_convert_fusion.2
  375.7 5.3 convolution_convert_fusion.8
  396.5 5.0 multiply_reduce_fusion.15
  408.9 6.3 fusion.6
  415.1 4.8 bitcast_convert_fusion.1
  422.8 4.8 bitcast_convert_fusion
  437.9 5.3 convolution_convert_fusion.4
  457.0 4.7 multiply_reduce_fusion.4
  472.4 5.0 pad_maximum_fusion
  481.4 158.2 %shard_map.225 = (bf16[24,3072]{1,0:T(8,128)(2,1)}, bf16[24,3072]{1,0:T(8,128)(2,1)}, bf16[24,3072]{1,0:T(8,128)(2,1)}, bf16[24,3072]{1,0:T(8,128)(2,1)}, bf16[2...) custom-call(bf16[2,2,2,4,24,3072]{5,4,3,2,1,0:T(8,128)(2,1)} %bitcast.314, ...), custom_call_target="tpu_custom_call" | custom-call | bytes 56623104 | tf_op jit(solution)/shard_map/pallas_call | solution.py:733
  652.5 8.6 %all-to-all-start.1 = ((bf16[24,480,128]{2,0,1:T(8,128)(2,1)}), bf16[24,480,128]{2,0,1:T(8,128)(2,1)}, u32[]{:S(2)}, u32[]{:S(2)}) async-start(bf16[24,480,128]{2,0,1:T(8,128)(2,1)} %select_bitcast_fusion), calls=%async_computation.1 | async-start | bytes 5898240 | tf_op jit(solution)/shard_map/all_to_all | solution.py:962
  676.0 73.3 %shard_map.226 = f32[32,4,768]{2,1,0:T(4,128)} custom-call(f32[32,4,768]{2,1,0:T(4,128)} %maximum_maximum_fusion.refs_0_, f32[4,768]{1,0:T(4,128)} %concatenate.75.refs_1_), custom_call_target="tpu_custom_call" | custom-call | bytes 20000000 | tf_op jit(solution)/shard_map/pallas_call | solution.py:658
  764.2 4.7 fusion.35
  768.8 9.9 %multiply_subtract_fusion = (f32[1288,768]{1,0:T(8,128)}, f32[1288,768]{1,0:T(8,128)}, f32[1288,768]{1,0:T(8,128)}) fusion(f32[1288,768]{1,0:T(8,128)S(1)} %copy-done.11, f32[1288]{0:T(1024)S(1)} %select_multiply_fusion, f32[16,768]{1,0:T(8,128)S(1)} %bitcast.341, f32[1000,768]{1,0:T(8,128)S(1)} %scatter_custom_fusion.1, f32[256,768]{1,0:T(8,128)S(1)} %copy-done.37, ...), kind=kLoop, calls=%fused_computation.66 | loop fusion | flops 16816128 | bytes 27702304 | tf_op jit(solution)/shard_map/sub | solution.py:105
  784.6 17.6 %fusion.17 = (f32[768,15,128]{2,0,1:T(8,128)}, f32[768,15,128]{2,0,1:T(8,128)}, f32[768,15,128]{2,0,1:T(8,128)}) fusion(f32[768,15,128]{2,0,1:T(8,128)} %param.24, pred[15]{0:T(512)(128)(4,1)S(1)} %copy-done.108, f32[768,15,128]{2,0,1:T(8,128)S(1)} %bitcast.288, f32[768,15,128]{2,0,1:T(8,128)} %param.23, f32[15]{0:T(128)S(1)} %copy-done.112, ...), kind=kOutput, calls=%fused_computation.59 | convolution fusion | flops 216883200 | bytes 47530104 | tf_op jit(solution)/shard_map/gd,gsc->dsc/dot_general | solution.py:55
  (519 shorter events, 227.1 us)
Async XLA Ops:
  1.3 37.8 %collective-permute-start = (s32[2,2]{0,1:T(2,128)S(1)}, s32[2,2]{0,1:T(2,128)S(1)}, u32[]{:S(2)}, u32[]{:S(2)}) collective-permute-start(s32[2,2]{0,1:T(2,128)S(1)} %pad_add_fusion), channel_id=1, source_target_pairs={{0,1},{1,0},{2,3},{3,2},{4,5},{5,4},{6,7},{7,6},{8,9},{9,8},{10,11... | collective-permute-start | bytes 56 | tf_op jit(solution)/shard_map/ppermute | solution.py:233
  11.0 14.0 %copy-start.5 = (s32[235]{0:T(256)S(1)}, s32[235]{0:T(256)}, u32[]{:S(2)}) copy-start(s32[235]{0:T(256)} %constant.319.clone) | copy-start | bytes 2824
  11.0 91.7 %all-to-all-start = ((bf16[768,15,128]{2,1,0:T(8,128)(2,1)}), bf16[768,15,128]{2,1,0:T(8,128)(2,1)}, u32[]{:S(2)}, u32[]{:S(2)}) async-start(bf16[768,15,128]{2,1,0:T(8,128)(2,1)} %copy.221), calls=%async_computation | async-start | bytes 6291456 | tf_op jit(solution)/shard_map/all_to_all | solution.py:828
  39.3 47.7 %collective-permute-start.1 = (s32[4,2]{0,1:T(2,128)S(1)}, s32[4,2]{0,1:T(2,128)S(1)}, u32[]{:S(2)}, u32[]{:S(2)}) collective-permute-start(s32[4,2]{0,1:T(2,128)S(1)} %pad_add_fusion.1), channel_id=1, source_target_pairs={{0,2},{1,3},{2,0},{3,1},{4,6},{5,7},{6,4},{7,5},{8,10},{9,11},{10,... | collective-permute-start | bytes 104 | tf_op jit(solution)/shard_map/ppermute | solution.py:233
  87.1 2.0 collective-permute-start.2
  89.3 2.7 collective-permute-start.3
  92.1 4.9 collective-permute-start.4
  112.1 169.2 %copy-start.67 = (f32[2,256]{1,0:T(2,128)S(1)}, f32[2,256]{1,0:T(2,128)}, u32[]{:S(2)}) copy-start(f32[2,256]{1,0:T(2,128)} %copy-done.66) | copy-start | bytes 6148
  112.1 169.2 %copy-start.75 = (f32[2,256]{1,0:T(2,128)S(1)}, f32[2,256]{1,0:T(2,128)}, u32[]{:S(2)}) copy-start(f32[2,256]{1,0:T(2,128)} %fusion.61) | copy-start | bytes 6148
  281.3 56.8 %copy-start.71 = (f32[2,768]{1,0:T(2,128)}, f32[2,768]{1,0:T(2,128)S(1)}, u32[]{:S(2)}) copy-start(f32[2,768]{1,0:T(2,128)S(1)} %get-tuple-element.97) | copy-start | bytes 18436
  281.3 61.8 %copy-start.56 = (f32[2,768]{1,0:T(2,128)}, f32[2,768]{1,0:T(2,128)S(1)}, u32[]{:S(2)}) copy-start(f32[2,768]{1,0:T(2,128)S(1)} %get-tuple-element.96) | copy-start | bytes 18436
  306.8 17.7 %copy-start.17 = (f32[2,256,768]{2,1,0:T(8,128)}, f32[2,256,768]{2,1,0:T(8,128)S(1)}, u32[]{:S(2)}) copy-start(f32[2,256,768]{2,1,0:T(8,128)S(1)} %get-tuple-element.75) | copy-start | bytes 4718596
  396.5 12.3 %slice-start.23 = ((s8[6291456]{0:T(1024)(128)(4,1)}), s8[4194304]{0:T(1024)(128)(4,1)S(1)}, s32[]{:S(2)}) async-start(s8[6291456]{0:T(1024)(128)(4,1)} %bitcast.370), calls=%async_computation.25 | async-start | bytes 8388608
  407.6 12.4 %slice-start.13 = ((s8[4718592]{0:T(1024)(128)(4,1)}), s8[4194304]{0:T(1024)(128)(4,1)S(1)}, s32[]{:S(2)}) async-start(s8[4718592]{0:T(1024)(128)(4,1)} %bitcast.353), calls=%async_computation.15 | async-start | bytes 8388608
  408.8 11.1 %slice-start.14 = ((s8[4718592]{0:T(1024)(128)(4,1)}), s8[524288]{0:T(1024)(128)(4,1)S(1)}, s32[]{:S(2)}) async-start(s8[4718592]{0:T(1024)(128)(4,1)} %bitcast.353), calls=%async_computation.16 | async-start | bytes 1048576
  481.4 163.9 %copy-start.92 = (s32[1024]{0:T(1024)S(1)}, s32[1024]{0:T(1024)}, u32[]{:S(2)}) copy-start(s32[1024]{0:T(1024)} %get-tuple-element.166) | copy-start | bytes 12292
  652.5 11.0 %copy-start.70 = (f32[2,256]{1,0:T(2,128)S(1)}, f32[2,256]{1,0:T(2,128)}, u32[]{:S(2)}) copy-start(f32[2,256]{1,0:T(2,128)} %copy-done.69) | copy-start | bytes 6148
  652.5 11.5 %copy-start.93 = (f32[2,256]{1,0:T(2,128)S(1)}, f32[2,256]{1,0:T(2,128)}, u32[]{:S(2)}) copy-start(f32[2,256]{1,0:T(2,128)} %get-tuple-element.47) | copy-start | bytes 6148
  652.5 11.5 %copy-start.55 = (bf16[2,256,16]{1,2,0:T(8,128)(2,1)S(1)}, bf16[2,256,16]{1,2,0:T(8,128)(2,1)}, u32[]{:S(2)}) copy-start(bf16[2,256,16]{1,2,0:T(8,128)(2,1)} %copy-done.54) | copy-start | bytes 49156
  652.5 11.5 %copy-start.74 = (f32[2,256]{1,0:T(2,128)S(1)}, f32[2,256]{1,0:T(2,128)}, u32[]{:S(2)}) copy-start(f32[2,256]{1,0:T(2,128)} %copy-done.73) | copy-start | bytes 6148
  652.5 11.5 %copy-start.77 = (f32[2,256]{1,0:T(2,128)S(1)}, f32[2,256]{1,0:T(2,128)}, u32[]{:S(2)}) copy-start(f32[2,256]{1,0:T(2,128)} %fusion.61) | copy-start | bytes 6148
  652.5 126.2 %all-to-all-start.1 = ((bf16[24,480,128]{2,0,1:T(8,128)(2,1)}), bf16[24,480,128]{2,0,1:T(8,128)(2,1)}, u32[]{:S(2)}, u32[]{:S(2)}) async-start(bf16[24,480,128]{2,0,1:T(8,128)(2,1)} %select_bitcast_fusion), calls=%async_computation.1 | async-start | bytes 5898240 | tf_op jit(solution)/shard_map/all_to_all | solution.py:962
  670.6 84.9 %copy-start.39 = (bf16[15,64,128]{2,1,0:T(8,128)(2,1)}, bf16[15,64,128]{2,1,0:T(8,128)(2,1)S(1)}, u32[]{:S(2)}) copy-start(bf16[15,64,128]{2,1,0:T(8,128)(2,1)S(1)} %gather_fusion.6) | copy-start | bytes 737284
  670.6 84.9 %copy-start.1 = (f32[2,2,2,4,24,768]{5,4,3,2,1,0:T(8,128)S(1)}, f32[2,2,2,4,24,768]{5,4,3,2,1,0:T(8,128)}, u32[]{:S(2)}) copy-start(f32[2,2,2,4,24,768]{5,4,3,2,1,0:T(8,128)} %copy-done) | copy-start | bytes 7077892
  (124 other events, 583.2 us)

commit v4 on v3

--- a/solution.py
+++ b/solution.py
@@ -179,10 +179,10 @@
     shift_a, scale_a, gate_a, shift_b, scale_b, gate_b = jnp.split(modul, 6, -1)
     grad_gate_b = jnp.sum(grad_out * branch_b, 1)
     grad_branch_b = (gate_b[:, None, :] * grad_out).astype(jnp.bfloat16)
-    grad_down = row_product(grad_branch_b, post_act)
+    grad_down = (grad_branch_b, post_act)
     grad_post = dot_low("gpd,df->gpf", grad_branch_b, w_down)
     grad_pre = local_back(gelu_tanh, pre_act, grad_post).astype(jnp.bfloat16)
-    grad_up = row_product(mlp_in, grad_pre)
+    grad_up = (mlp_in, grad_pre)
     grad_mlp_in = dot_low("gpf,df->gpd", grad_pre, w_up)
     normed_b = norm_rows(middle)
     grad_scale_b = jnp.sum(grad_mlp_in * normed_b, 1)
@@ -192,7 +192,7 @@
     )
     grad_gate_a = jnp.sum(grad_middle * branch_a, 1)
     grad_branch_a = (gate_a[:, None, :] * grad_middle).astype(jnp.bfloat16)
-    grad_out_w = row_product(heads_out, grad_branch_a)
+    grad_out_w = (heads_out, grad_branch_a)
     grad_heads = (
         dot_low("gpe,de->gpd", grad_branch_a, w_out)
         .astype(jnp.bfloat16)
@@ -215,7 +215,7 @@
         ],
         -1,
     ).astype(jnp.bfloat16)
-    grad_qkv_w = row_product(attn_in, grad_qkv)
+    grad_qkv_w = (attn_in, grad_qkv)
     grad_attn_in = dot_low("gpe,de->gpd", grad_qkv, w_qkv)
     normed_a = norm_rows(hidden)
     grad_scale_a = jnp.sum(grad_attn_in * normed_a, 1)
@@ -226,41 +226,7 @@
     grad_modul = jnp.concatenate(
         [grad_shift_a, grad_scale_a, grad_gate_a, grad_shift_b, grad_scale_b, grad_gate_b], -1
     ).astype(jnp.bfloat16)
-    return (grad_in, grad_modul, [jnp.concatenate([grad_qkv_w, grad_out_w], 1), grad_up, grad_down])
-
-
-def swap_bit(values, bit, count):
-    return lax.ppermute(values, AXES, [(i, i ^ bit) for i in range(count)])
-
-
-def gather_small(values, count):
-    if count & (count - 1):
-        return lax.all_gather(values, AXES, axis=0, tiled=True)
-    me = lax.axis_index(AXES)
-    bit = 1
-    while bit < count:
-        other = swap_bit(values, bit, count)
-        upper = (me & bit) > 0
-        values = jnp.concatenate(
-            [jnp.where(upper, other, values), jnp.where(upper, values, other)], 0
-        )
-        bit *= 2
-    return values
-
-
-def scatter_small(values, count):
-    if count & (count - 1):
-        return lax.psum_scatter(values, AXES, scatter_dimension=0, tiled=False)
-    me = lax.axis_index(AXES)
-    bit = count // 2
-    while bit:
-        half = values.shape[0] // 2
-        upper = (me & bit) > 0
-        low, high = values[:half], values[half:]
-        other = swap_bit(jnp.where(upper, low, high), bit, count)
-        values = jnp.where(upper, high, low) + other
-        bit //= 2
-    return values[0]
+    return (grad_in, grad_modul, [grad_qkv_w, grad_out_w, grad_up, grad_down])
 
 
 MESH = pl.DeviceIdType.MESH
@@ -319,10 +285,12 @@
 def gather_kernel(widths, *refs):
     count = len(widths)
     pieces = refs[:count]
-    time_act, label_rows, low_slots = refs[count : count + 3]
-    outs = refs[count + 3 : 2 * count + 3]
-    cond_out, modul_out = refs[2 * count + 3 : 2 * count + 5]
-    time_two, parts, own_sem, send_sem, recv_sem, time_sem, modul_sem = refs[2 * count + 5 :]
+    info, low_slots = refs[count : count + 2]
+    outs = refs[count + 2 : 2 * count + 2]
+    every_info, cond_out, modul_out = refs[2 * count + 2 : 2 * count + 5]
+    time_two, parts, own_sem, send_sem, recv_sem, time_sem, modul_sem, info_sem = refs[
+        2 * count + 5 :
+    ]
     devices, images = modul_out.shape[:2]
     slots = low_slots.shape[0]
     y, x, c, z = place_of()
@@ -393,13 +361,35 @@
             device_id_type=MESH,
         )
 
+    def info_copy(j, arriving):
+        peer, where = device_at(devices - j if arriving else j)
+        return pltpu.make_async_remote_copy(
+            src_ref=info,
+            dst_ref=every_info.at[pl.ds((peer if arriving else me) * images, images)],
+            send_sem=info_sem.at[0, j],
+            recv_sem=info_sem.at[1, j],
+            device_id=where,
+            device_id_type=MESH,
+        )
+
+    def info_rows(first):
+        return jnp.concatenate([every_info[:, first + j, :] for j in range(D // BLOCK)], -1)
+
     def image_products():
         copy = pltpu.make_async_copy(outs[0], time_two, time_sem)
         copy.start()
+
+        @pl.loop(1, devices)
+        def _(j):
+            info_copy(j, True).wait_recv()
+            info_copy(j, False).wait_send()
+
         copy.wait()
-        weight = time_two[...].reshape(D, D).astype(jnp.bfloat16)
-        cond = jnp.dot(time_act[...], weight, preferred_element_type=jnp.float32)
-        cond = cond + label_rows[...]
+        weight = time_two[...].astype(jnp.float32).reshape(D, D).astype(jnp.bfloat16)
+        cond = jnp.dot(
+            info_rows(0).astype(jnp.bfloat16), weight, preferred_element_type=jnp.float32
+        )
+        cond = cond + info_rows(8)
         cond_out[...] = cond
         act = (cond * jax.nn.sigmoid(cond)).astype(jnp.bfloat16)
         for s in range(slots):
@@ -411,6 +401,12 @@
         def _(j):
             modul_copy(j, False).start()
 
+    @pl.loop(1, devices)
+    def _(j):
+        info_copy(j, False).start()
+
+    for i in range(images):
+        every_info[me * images + i] = info[i]
     for k in range(count):
         own_copy(k).start()
     start(line_copies(0, False))
@@ -444,31 +440,97 @@
                 copy.wait_send()
 
 
-def scatter_kernel(widths, *refs):
+def scatter_kernel(widths, slots, *refs):
     count = len(widths)
-    grads, modul = refs[:count], refs[count]
-    outs, every_modul = refs[count + 1 : 2 * count + 1], refs[2 * count + 1]
-    scratch = refs[2 * count + 2 :]
-    devices = every_modul.shape[0]
-    own, core_in, first_in, second_in, line_in = (
-        scratch[i * count : (i + 1) * count] for i in range(5)
-    )
-    own_sem, send_sem, recv_sem, modul_sem = scratch[5 * count :]
+    lefts, rights = refs[:count], refs[count : 2 * count]
+    modul, pick, low_slots, edge, factor = refs[2 * count : 2 * count + 5]
+    outs = refs[2 * count + 5 : 3 * count + 5]
+    chosen, shared = refs[3 * count + 5 : 3 * count + 7]
+    scratch = refs[3 * count + 7 :]
+    own, first_in, second_in, line_in = (scratch[i * count : (i + 1) * count] for i in range(4))
+    (
+        left_in, right_in, away, every_modul, parts, landed,
+        load_sem, send_sem, recv_sem, modul_sem, part_sem, sum_sem,
+    ) = scratch[4 * count :]
+    devices, images = shared.shape[:2]
     y, x, c, z = place_of()
     to_x, to_y, to_core, to_z = neighbours()
     me = rep_of(y, x, c) * 4 + z
+    rows = D // 32
+    half_rows = D // 2
     meet_all(devices)
 
-    def modul_copy(j, arriving):
+    def exchange(source, dest, sem, j, arriving):
         peer, where = device_at(devices - j if arriving else j)
         return pltpu.make_async_remote_copy(
-            src_ref=modul,
-            dst_ref=every_modul.at[peer if arriving else me],
-            send_sem=modul_sem.at[0, j],
-            recv_sem=modul_sem.at[1, j],
+            src_ref=source(peer, me),
+            dst_ref=dest(peer if arriving else me),
+            send_sem=sem.at[0, j],
+            recv_sem=sem.at[1, j],
             device_id=where,
             device_id_type=MESH,
         )
+
+    def modul_copy(j, arriving):
+        return exchange(
+            lambda peer, mine: modul,
+            lambda owner: every_modul.at[pl.ds(owner * images, images)],
+            modul_sem, j, arriving,
+        )
+
+    def part_copy(j, arriving):
+        return exchange(
+            lambda peer, mine: parts.at[pl.ds(peer * images, images)],
+            lambda owner: landed.at[owner],
+            part_sem, j, arriving,
+        )
+
+    def sum_copy(j, arriving):
+        return exchange(
+            lambda peer, mine: shared.at[mine], lambda owner: shared.at[owner], sum_sem, j, arriving
+        )
+
+    def all_start(copy):
+        @pl.loop(1, devices)
+        def _(j):
+            copy(j, False).start()
+
+    def all_arrived(copy):
+        @pl.loop(1, devices)
+        def _(j):
+            copy(j, True).wait_recv()
+
+    def all_sent(copy):
+        @pl.loop(1, devices)
+        def _(j):
+            copy(j, False).wait_send()
+
+    def image_parts():
+        all_arrived(modul_copy)
+
+        @pl.loop(0, devices * images)
+        def _(i):
+            chosen[i] = jnp.dot(pick[...], every_modul[i], preferred_element_type=jnp.float32)
+
+        total = jnp.zeros((devices * images, D), jnp.float32)
+        for s in range(slots):
+            total = total + lax.dot_general(
+                chosen[:, s, :].astype(jnp.bfloat16),
+                low_slots[s],
+                (((1,), (1,)), ((), ())),
+                preferred_element_type=jnp.float32,
+            )
+        parts[...] = edge[...]
+        for j in range(D // BLOCK):
+            parts[:, j, :] = total[:, j * BLOCK : (j + 1) * BLOCK]
+        all_start(part_copy)
+        for i in range(images):
+            landed[me, i] = parts[me * images + i]
+
+    def image_sums():
+        all_arrived(part_copy)
+        shared[me] = jnp.sum(landed[...], 0) * factor[...]
+        all_start(sum_copy)
 
     def remote(k, number, source, dest, target):
         return pltpu.make_async_remote_copy(
@@ -480,11 +542,18 @@
             device_id_type=MESH,
         )
 
-    def own_copy(k):
-        return pltpu.make_async_copy(grads[k].at[c], own[k], own_sem.at[k])
+    def loads(k):
+        slot = k % 3
+        return [
+            pltpu.make_async_copy(lefts[k], left_in.at[slot], load_sem.at[0, slot]),
+            pltpu.make_async_copy(
+                rights[k], right_in.at[slot, :, pl.ds(0, widths[k])], load_sem.at[1, slot]
+            ),
+        ]
 
     def core_copies(k):
-        return [remote(k, 0, grads[k].at[1 - c], core_in[k], to_core)]
+        source = away.at[k % 3, :, :, :, :, pl.ds(0, widths[k])]
+        return [remote(k, 0, source, own[k], to_core)]
 
     def first_copies(k):
         half = widths[k] // 2
@@ -520,11 +589,37 @@
         for copy in copies:
             copy.wait_recv()
 
-    def core_sum(k):
-        @pl.loop(0, 16)
-        def _(i):
-            at = (i // 8, (i // 4) % 2, i % 4)
-            own[k][at] = own[k][at] + core_in[k][at]
+    def products(k, half, store):
+        slot = k % 3
+        tile = 256
+
+        @pl.loop(0, widths[k] // tile)
+        def _(n):
+            columns = pl.ds(pl.multiple_of(n * tile, tile), tile)
+            left = left_in[slot, :, pl.ds(pl.multiple_of(half * half_rows, BLOCK), half_rows)]
+            result = dot_rows(left, right_in[slot, :, columns])
+            for i in range(16):
+                at = (i // 8, (i // 4) % 2, i % 4, slice(None), columns)
+                store(at, result[i * rows : (i + 1) * rows])
+
+    def away_products(k):
+        for copy in loads(k):
+            copy.wait()
+        if k >= 3:
+            for copy in core_copies(k - 3):
+                copy.wait_send()
+
+        def store(at, value):
+            away[(k % 3,) + at] = value.astype(jnp.bfloat16)
+
+        products(k, 1 - c, store)
+        start(core_copies(k))
+
+    def own_products(k):
+        def store(at, value):
+            own[k][at] = (value + own[k][at].astype(jnp.float32)).astype(jnp.bfloat16)
+
+        products(k, c, store)
 
     def first_sum(k):
         half = widths[k] // 2
@@ -547,21 +642,21 @@
             own[k][a_at] = own[k][a_at] + second_in[k][0, at_z]
             own[k][b_at] = own[k][b_at] + second_in[k][1, at_z]
 
-    for k in range(count):
-        start(core_copies(k))
-        own_copy(k).start()
-    every_modul[me] = modul[...]
-
-    @pl.loop(1, devices)
-    def _(j):
-        modul_copy(j, False).start()
-
+    all_start(modul_copy)
+    for i in range(images):
+        every_modul[me * images + i] = modul[i]
+    for k in range(min(3, count)):
+        start(loads(k))
+    away_products(0)
     for t in range(count + 3):
+        if t + 1 < count:
+            away_products(t + 1)
         if t < count:
-            own_copy(t).wait()
             arrived(core_copies(t))
-            core_sum(t)
+            own_products(t)
             start(first_copies(t))
+            if t + 3 < count:
+                start(loads(t + 3))
         if 0 <= t - 1 < count:
             arrived(first_copies(t - 1))
             first_sum(t - 1)
@@ -577,97 +672,19 @@
             for step in (1, 2, 3):
                 total = total + line_in[k][step - 1].astype(jnp.float32)
             outs[k][...] = total.astype(jnp.bfloat16)
+        if t == 3:
+            image_parts()
+        if t == 6:
+            image_sums()
+    all_arrived(sum_copy)
+    for copy in (modul_copy, part_copy, sum_copy):
+        all_sent(copy)
     for k in range(count):
         for copies in (core_copies, first_copies, second_copies, line_copies):
+            if copies is core_copies and k + 3 < count:
+                continue
             for copy in copies(k):
                 copy.wait_send()
-
-    @pl.loop(1, devices)
-    def _(j):
-        modul_copy(j, True).wait_recv()
-        modul_copy(j, False).wait_send()
-
-
-def share_kernel(finish, parts, extra, out, landed, send_sem, recv_sem):
-    devices = parts.shape[0]
-    shards = lax.axis_size("shard")
-    me = lax.axis_index("rep") * shards + lax.axis_index("shard")
-
-    def target(j):
-        peer = lax.rem(me + j, devices)
-        return peer, (peer // shards, lax.rem(peer, shards))
-
-    barrier = pltpu.get_barrier_semaphore()
-
-    @pl.loop(1, devices)
-    def _(j):
-        pl.semaphore_signal(barrier, inc=1, device_id=target(j)[1], device_id_type=MESH)
-
-    pl.semaphore_wait(barrier, devices - 1)
-
-    def copy_part(j):
-        peer, where = target(j)
-        return pltpu.make_async_remote_copy(
-            src_ref=parts.at[peer],
-            dst_ref=landed.at[j],
-            send_sem=send_sem.at[0, j],
-            recv_sem=recv_sem.at[0, j],
-            device_id=where,
-            device_id_type=MESH,
-        )
-
-    def copy_sum(j, arriving):
-        owner = lax.rem(me + devices - j, devices) if arriving else me
-        return pltpu.make_async_remote_copy(
-            src_ref=out.at[owner],
-            dst_ref=out.at[owner],
-            send_sem=send_sem.at[1, j],
-            recv_sem=recv_sem.at[1, j],
-            device_id=target(j)[1],
-            device_id_type=MESH,
-        )
-
-    @pl.loop(1, devices)
-    def _(j):
-        copy_part(j).start()
-
-    landed[0] = parts[me]
-
-    @pl.loop(1, devices)
-    def _(j):
-        copy_part(j).wait_recv()
-
-    out[me] = finish(jnp.sum(landed[...], 0), extra[...])
-
-    @pl.loop(1, devices)
-    def _(j):
-        copy_sum(j, False).start()
-
-    @pl.loop(1, devices)
-    def _(j):
-        copy_sum(j, True).wait_recv()
-
-    @pl.loop(1, devices)
-    def _(j):
-        copy_part(j).wait_send()
-        copy_sum(j, False).wait_send()
-
-
-def share(finish, parts, extra, number):
-    devices = parts.shape[0]
-    return pl.pallas_call(
-        lambda *refs: share_kernel(finish, *refs),
-        out_shape=jax.ShapeDtypeStruct(parts.shape, jnp.float32),
-        in_specs=[pl.BlockSpec(memory_space=pltpu.VMEM)] * 2,
-        out_specs=pl.BlockSpec(memory_space=pltpu.VMEM),
-        scratch_shapes=[
-            pltpu.VMEM(parts.shape, jnp.float32),
-            pltpu.SemaphoreType.DMA((2, devices)),
-            pltpu.SemaphoreType.DMA((2, devices)),
-        ],
-        compiler_params=pltpu.CompilerParams(collective_id=number, has_side_effects=True),
-        cost_estimate=pl.CostEstimate(flops=0, bytes_accessed=20_000_000, transcendentals=0),
-    )(parts, extra)
 
 
 class RingPlan:
@@ -681,78 +698,91 @@
         split = values.reshape((2, 2, 2, 4, D // 32) + shape[1:])
         return jnp.moveaxis(split, 2, 0).reshape(shape)
 
-    def gather(self, pieces, time_piece, time_act, label_rows, low_slots):
-        pieces = [time_piece.astype(jnp.float32)] + list(pieces)
+    def gather(self, pieces, time_piece, info, low_slots):
+        pieces = [time_piece] + list(pieces)
         widths = tuple(piece.shape[1] for piece in pieces)
         count, rows = len(pieces), D // 32
-        all_images = time_act.shape[0]
+        all_images = 32 * info.shape[0]
         slots = low_slots.shape[1]
         room = -(-slots // 8) * 8
         size = sum(4 * D * width for width in widths)
         whole_shape = [(2, 2, 2, 4, rows, width) for width in widths]
-        *whole, cond, modul = pl.pallas_call(
+        *whole, every_info, cond, modul = pl.pallas_call(
             lambda *refs: gather_kernel(widths, *refs),
             out_shape=[
                 jax.ShapeDtypeStruct(shape, piece.dtype)
                 for shape, piece in zip(whole_shape, pieces)
             ]
             + [
+                jax.ShapeDtypeStruct((all_images,) + info.shape[1:], jnp.float32),
                 jax.ShapeDtypeStruct((all_images, D), jnp.float32),
                 jax.ShapeDtypeStruct((32, all_images // 32, room, BLOCK), jnp.float32),
             ],
-            in_specs=[pl.BlockSpec(memory_space=pltpu.VMEM)] * (count + 3),
+            in_specs=[pl.BlockSpec(memory_space=pltpu.VMEM)] * (count + 2),
             out_specs=[pl.BlockSpec(memory_space=pl.ANY)] * count
-            + [pl.BlockSpec(memory_space=pltpu.VMEM)] * 2,
+            + [pl.BlockSpec(memory_space=pltpu.VMEM)] * 3,
             scratch_shapes=[
-                pltpu.VMEM(whole_shape[0], jnp.float32),
+                pltpu.VMEM(whole_shape[0], jnp.bfloat16),
                 pltpu.VMEM((all_images, room, BLOCK), jnp.float32),
                 pltpu.SemaphoreType.DMA((count,)),
                 pltpu.SemaphoreType.DMA((count, 8)),
                 pltpu.SemaphoreType.DMA((count, 8)),
                 pltpu.SemaphoreType.DMA,
                 pltpu.SemaphoreType.DMA((2, 32)),
+                pltpu.SemaphoreType.DMA((2, 32)),
             ],
             compiler_params=pltpu.CompilerParams(
                 collective_id=0, has_side_effects=True, vmem_limit_bytes=GATHER_VMEM
             ),
             cost_estimate=pl.CostEstimate(flops=0, bytes_accessed=size, transcendentals=0),
-        )(*pieces, time_act, label_rows, jnp.swapaxes(low_slots, 0, 1))
+        )(*pieces, info, jnp.swapaxes(low_slots, 0, 1))
         whole = [part.reshape(D, -1) for part in whole]
         modul = jnp.swapaxes(modul[:, :, :slots], 0, 1).reshape(-1, 32 * slots, BLOCK)
-        return whole[1:], whole[0].astype(jnp.bfloat16), cond, modul
-
-    def scatter(self, grads, modul):
-        widths = tuple(grad.shape[1] for grad in grads)
-        count, rows = len(grads), D // 32
+        return whole[1:], whole[0], every_info, cond, modul
+
+    def scatter(self, grads, modul, pick, low_slots, edge, factor):
+        lefts = [left.reshape(-1, D) for left, _ in grads]
+        rights = [right.reshape(left.shape[0], -1) for (_, right), left in zip(grads, lefts)]
+        widths = tuple(right.shape[1] for right in rights)
+        count, rows, tokens = len(grads), D // 32, lefts[0].shape[0]
+        widest = max(widths)
+        images, slots = modul.shape[0], low_slots.shape[1]
         size = sum(4 * D * width for width in widths)
-        scratch = [pltpu.VMEM((2, 2, 4, rows, width), jnp.bfloat16) for width in widths] * 2
+        scratch = [pltpu.VMEM((2, 2, 4, rows, width), jnp.bfloat16) for width in widths]
         scratch += [pltpu.VMEM((2, 2, 4, rows, width // 2), jnp.bfloat16) for width in widths]
         scratch += [pltpu.VMEM((2, 4, rows, width // 2), jnp.bfloat16) for width in widths]
         scratch += [pltpu.VMEM((3, rows, width), jnp.bfloat16) for width in widths]
-        piece = modul.reshape(-1, BLOCK)
-        *scattered, every_modul = pl.pallas_call(
-            lambda *refs: scatter_kernel(widths, *refs),
+        *scattered, chosen, shared = pl.pallas_call(
+            lambda *refs: scatter_kernel(widths, slots, *refs),
             out_shape=[jax.ShapeDtypeStruct((rows, width), jnp.bfloat16) for width in widths]
-            + [jax.ShapeDtypeStruct((32,) + piece.shape, jnp.bfloat16)],
-            in_specs=[pl.BlockSpec(memory_space=pl.ANY)] * count
-            + [pl.BlockSpec(memory_space=pltpu.VMEM)],
-            out_specs=[pl.BlockSpec(memory_space=pltpu.VMEM)] * (count + 1),
+            + [
+                jax.ShapeDtypeStruct((32 * images, pick.shape[0], BLOCK), jnp.float32),
+                jax.ShapeDtypeStruct((32,) + factor.shape, jnp.float32),
+            ],
+            in_specs=[pl.BlockSpec(memory_space=pl.ANY)] * (2 * count)
+            + [pl.BlockSpec(memory_space=pltpu.VMEM)] * 5,
+            out_specs=[pl.BlockSpec(memory_space=pltpu.VMEM)] * (count + 2),
             scratch_shapes=scratch
             + [
-                pltpu.SemaphoreType.DMA((count,)),
+                pltpu.VMEM((3, tokens, D), jnp.bfloat16),
+                pltpu.VMEM((3, tokens, widest), jnp.bfloat16),
+                pltpu.VMEM((3, 2, 2, 4, rows, widest), jnp.bfloat16),
+                pltpu.VMEM((32 * images,) + modul.shape[1:], jnp.bfloat16),
+                pltpu.VMEM(edge.shape, jnp.float32),
+                pltpu.VMEM((32,) + factor.shape, jnp.float32),
+                pltpu.SemaphoreType.DMA((2, 3)),
                 pltpu.SemaphoreType.DMA((count, 8)),
                 pltpu.SemaphoreType.DMA((count, 8)),
+                pltpu.SemaphoreType.DMA((2, 32)),
+                pltpu.SemaphoreType.DMA((2, 32)),
                 pltpu.SemaphoreType.DMA((2, 32)),
             ],
             compiler_params=pltpu.CompilerParams(
                 collective_id=1, has_side_effects=True, vmem_limit_bytes=SCATTER_VMEM
             ),
             cost_estimate=pl.CostEstimate(flops=0, bytes_accessed=size, transcendentals=0),
-        )(*[grad.reshape(2, 2, 2, 4, rows, -1) for grad in grads], piece)
-        return scattered, every_modul.reshape(32 * modul.shape[0], -1)
-
-    def share(self, finish, parts, extra, number):
-        return share(finish, parts, extra, number)
+        )(*lefts, *rights, modul, pick, jnp.swapaxes(low_slots, 0, 1), edge, factor)
+        return scattered, chosen[:, :slots].astype(jnp.bfloat16), shared
 
 
 class PlainPlan:
@@ -762,23 +792,31 @@
     def restore_rows(self, values):
         return values
 
-    def gather(self, pieces, time_piece, time_act, label_rows, low_slots):
+    def gather(self, pieces, time_piece, info, low_slots):
         whole = [lax.all_gather(piece, AXES, axis=0, tiled=True) for piece in pieces]
         time_two = lax.all_gather(time_piece, AXES, axis=0, tiled=True)
-        cond = jnp.dot(time_act, time_two, preferred_element_type=jnp.float32) + label_rows
+        every_info = lax.all_gather(info, AXES, axis=0, tiled=True)
+        blocks = D // BLOCK
+        time_act = every_info[:, :blocks].reshape(-1, D).astype(jnp.bfloat16)
+        cond = jnp.dot(time_act, time_two, preferred_element_type=jnp.float32)
+        cond = cond + every_info[:, 8 : 8 + blocks].reshape(-1, D)
         modul = dot_low("gd,dsc->gsc", jax.nn.silu(cond).astype(jnp.bfloat16), low_slots)
         modul = lax.all_to_all(modul, AXES, split_axis=0, concat_axis=1, tiled=True)
-        return whole, time_two, cond, modul
-
-    def scatter(self, grads, modul):
+        return whole, time_two, every_info, cond, modul
+
+    def scatter(self, grads, modul, pick, low_slots, edge, factor):
         scattered = [
-            lax.psum_scatter(grad, AXES, scatter_dimension=0, tiled=True) for grad in grads
+            lax.psum_scatter(row_product(*pair), AXES, scatter_dimension=0, tiled=True)
+            for pair in grads
         ]
-        return scattered, lax.all_gather(modul, AXES, axis=0, tiled=True)
-
-    def share(self, finish, parts, extra, number):
-        own = finish(scatter_small(parts, parts.shape[0]), extra)
-        return gather_small(own[None], parts.shape[0])
+        slots = low_slots.shape[1]
+        every = lax.all_gather(modul, AXES, axis=0, tiled=True)
+        chosen = dot_low("su,guc->gsc", pick, every)[:, :slots].astype(jnp.bfloat16)
+        part = dot_low("gsc,dsc->gd", chosen, low_slots).reshape(-1, D // BLOCK, BLOCK)
+        parts = edge.at[:, : D // BLOCK].set(part)
+        own = lax.psum_scatter(parts, AXES, scatter_dimension=0, tiled=True) * factor
+        shared = lax.all_gather(own, AXES, axis=0, tiled=False)
+        return scattered, chosen, shared
 
 
 def unit_lists():
@@ -821,10 +859,6 @@
     low_slots = master.astype(jnp.bfloat16)
 
     plan = RingPlan() if (lax.axis_size("rep"), lax.axis_size("shard")) == (8, 4) else PlainPlan()
-    every_int = gather_small(jnp.stack([t_index, labels], 1), count)
-    every_t, every_label = every_int[:, 0], every_int[:, 1]
-    all_images = every_t.shape[0]
-
     spread = lax.all_to_all(
         plan.order_rows(low_slots), AXES, split_axis=0, concat_axis=1, tiled=True
     )
@@ -849,15 +883,32 @@
     noisy_low = noisy.astype(jnp.bfloat16)
     hidden = dot_low("gpc,cd->gpd", noisy_low, patch_w) + positions()
 
-    every_time = (every_t.astype(jnp.float32) + 0.5) / TSTEPS
+    blocks = D // BLOCK
+    freq_own = frequencies(times).astype(jnp.bfloat16)
+    time_own = jnp.dot(freq_own, time_w, preferred_element_type=jnp.float32)
+    act_own = jax.nn.silu(time_own).astype(jnp.bfloat16).astype(jnp.float32)
+    label_own = jnp.take(table, labels, axis=0)
+    numbers = jnp.stack([t_index, labels], 1).astype(jnp.float32)
+    info = jnp.concatenate(
+        [
+            act_own.reshape(images, blocks, BLOCK),
+            jnp.pad(numbers, ((0, 0), (0, BLOCK - 2)))[:, None],
+            jnp.zeros((images, 7 - blocks, BLOCK), jnp.float32),
+            label_own.reshape(images, blocks, BLOCK),
+            jnp.zeros((images, 8 - blocks, BLOCK), jnp.float32),
+        ],
+        1,
+    )
+    whole, time_two, every_info, cond_all, slot_modul = plan.gather(
+        pieces, unit_rows[:, LAYERS * DENSE_COLS :], info, low_slots
+    )
+    all_images = cond_all.shape[0]
+    every_time = (every_info[:, blocks, 0] + 0.5) / TSTEPS
+    every_label = every_info[:, blocks, 1].astype(jnp.int32)
     weight_total = jnp.sum(1.0 + 3.0 * every_time) * PATCHES
     freq_low = frequencies(every_time).astype(jnp.bfloat16)
     time_pre = jnp.dot(freq_low, time_w, preferred_element_type=jnp.float32)
-    time_act = jax.nn.silu(time_pre).astype(jnp.bfloat16)
-    label_rows = jnp.take(table, every_label, axis=0)
-    whole, time_two, cond_all, slot_modul = plan.gather(
-        pieces, unit_rows[:, LAYERS * DENSE_COLS :], time_act, label_rows, low_slots
-    )
+    time_act = every_info[:, :blocks].reshape(all_images, D).astype(jnp.bfloat16)
     weights_all = [
         (whole[3 * l][:, : 3 * D], whole[3 * l][:, 3 * D :], whole[3 * l + 1], whole[3 * l + 2])
         for l in range(LAYERS)
@@ -891,47 +942,37 @@
         grad_hidden, grad_moduls[l], layer_grads[l] = layer_backward(
             grad_hidden, weights_all[l], saved_all[l]
         )
-    order = list(reversed(range(LAYERS)))
-    scattered, every_modul = plan.scatter(
-        [grad for l in order for grad in reversed(layer_grads[l])],
-        jnp.concatenate(grad_moduls + [grad_modul_f], -1),
-    )
-    every_modul = every_modul.reshape(all_images, len(image_units), BLOCK)
-    grad_rows = {
-        (l, 2 - i): scattered[3 * n + i] for n, l in enumerate(order) for i in range(3)
-    }
     grad_embed = grad_hidden.astype(jnp.bfloat16)
     grad_patch = dot_low("gpc,gpd->cd", noisy_low, grad_embed)
 
     image_place = np.full((UNITS + 1,), -1, np.int32)
     image_place[image_units] = np.arange(len(image_units))
     my_place = jnp.asarray(image_place)[my_unit]
-    slot_grad_out = jnp.where(
-        (my_place >= 0)[None, :, None],
-        jnp.take(every_modul, jnp.maximum(my_place, 0), axis=1),
-        jnp.zeros((), jnp.bfloat16),
-    )
-    cond_part = dot_low("gsc,dsc->gd", slot_grad_out, low_slots)
-    edge_rows = max(1, 2 * CHANNELS // count)
+    room_slots, room_units = -(-slot_dev // 16) * 16, -(-len(image_units) // 16) * 16
+    pick = jnp.pad(my_place, (0, room_slots - slot_dev), constant_values=-1)[:, None]
+    pick = (pick == jnp.arange(room_units, dtype=jnp.int32)).astype(jnp.bfloat16)
+    modul_grad = jnp.concatenate(grad_moduls + [grad_modul_f], -1).reshape(images, -1, BLOCK)
+    modul_grad = jnp.pad(modul_grad, ((0, 0), (0, room_units - len(image_units)), (0, 0)))
     edge = jnp.concatenate([grad_patch, grad_head], 0)
-    edge = jnp.concatenate(
-        [edge, jnp.zeros((edge_rows * count - 2 * CHANNELS, D), jnp.float32)], 0
-    )
-    small_part = jnp.concatenate(
-        [
-            cond_part.reshape(count, images, D),
-            edge.reshape(count, edge_rows, D),
-            jnp.broadcast_to(loss_part, (count, 1, D)),
-        ],
-        1,
-    )
-    factor = local_back(jax.nn.silu, cond, jnp.ones_like(cond))
-    factor = jnp.concatenate([factor, jnp.ones((edge_rows + 1, D), jnp.float32)], 0)
-    small_sum = plan.share(lambda a, b: a * b, small_part, factor, 3)
-    grad_cond = small_sum[:, :images].reshape(all_images, D)
-    edge = small_sum[:, images : images + edge_rows].reshape(-1, D)
+    edge_room = max(all_images, 4 * CHANNELS)
+    edge = jnp.concatenate([edge, jnp.broadcast_to(loss_part, (2 * CHANNELS, D))], 0)
+    edge = jnp.pad(edge, ((0, edge_room - 4 * CHANNELS), (0, 0)))[:all_images]
+    edge = jnp.pad(edge.reshape(all_images, blocks, BLOCK), ((0, 0), (8, 8 - blocks), (0, 0)))
+    factor = local_back(jax.nn.silu, cond, jnp.ones_like(cond)).reshape(images, blocks, BLOCK)
+    factor = jnp.pad(factor, ((0, 0), (0, 16 - blocks), (0, 0)), constant_values=1.0)
+    order = list(reversed(range(LAYERS)))
+    scattered, slot_grad_out, shared = plan.scatter(
+        [grad for l in order for grad in reversed(layer_grads[l])],
+        modul_grad, pick, low_slots, edge, factor,
+    )
+    grad_rows = {
+        (l, 3 - i): scattered[4 * n + i] for n, l in enumerate(order) for i in range(4)
+    }
+    shared = shared.reshape(all_images, 16, BLOCK)
+    grad_cond = shared[:, :blocks].reshape(all_images, D)
+    edge = shared[:, 8 : 8 + blocks].reshape(all_images, D)
     grad_patch, grad_head = edge[:CHANNELS], edge[CHANNELS : 2 * CHANNELS]
-    loss_sum = small_sum[0, images + edge_rows, 0]
+    loss_sum = edge[2 * CHANNELS, 0]
     grad_time_out = grad_cond.astype(jnp.bfloat16)
     grad_time_act = dot_low("ge,de->gd", grad_time_out, time_two)
     grad_time_pre = local_back(jax.nn.silu, time_pre, grad_time_act).astype(jnp.bfloat16)
@@ -953,7 +994,7 @@
         [
             grad_rows[l, i].reshape(rows, -1, BLOCK)
             for l in range(LAYERS)
-            for i in range(3)
+            for i in range(4)
         ],
         1,
     )

time: 810 us -> 793 us (0.979)
  matrix products: 167 us -> 133 us
  waiting for transfers between devices: 47.4 us -> 80.6 us
  Pallas kernels: 396 us -> 364 us
  local copies, waits for them, and re-layouts: 99.5 us -> 122 us
    ppermute x5 -> x0, waiting for transfers between devices: 47.4 us -> none  [swap_bit(): return lax.ppermute(values, AXES, [(i, i ^ bit) for i in range(count)])]
    all_to_all x1, waiting for transfers between devices: 0.01 us -> 45.5 us  [on_device(): lax.all_to_all(plan.order_rows(low_slots), AXES, split_axis=0, concat_axi...]
    pallas_call x2 -> x1, Pallas kernels: 231 us -> 194 us  [scatter(): pl.pallas_call(lambda *refs: scatter_kernel(widths, slots, *refs), out_sh...]
    dot_general x9 -> x1, matrix products: 35.5 us -> 0.18 us  [on_device(): time_own = jnp.dot(freq_own, time_w, preferred_element_type=jnp.float32)]
    all_to_all x1, waiting for transfers between devices: 0.01 us -> 35.1 us  [on_device(): lax.all_to_all(slot_rows, AXES, split_axis=1, concat_axis=0, tiled=True)]
    unnamed x302 -> x288, local copies, waits for them, and re-layouts: 19.5 us -> 32.7 us
    concatenate x3 -> x9, local copies, waits for them, and re-layouts: 0.69 us -> 10.7 us  [the longest x6 10.6 us: layer_backward(): jnp.concatenate([grad_queries.reshape(groups, -1, D), grad_keys.reshape(g...]
    another operation x2 -> x10, local copies, waits for them, and re-layouts: 1.72 us -> 11 us  [on_device(): every_modul = every_modul.reshape(all_images, len(image_units), BLOCK)]
  transfers between devices with their start and end apart: 7 -> 2, of which waited for: 3 -> 2; matrix products, arithmetic and copies ran while one was open for 10% -> 7% of each run, Pallas kernels for 9% -> 0%
where the time goes in v4:
time: 793 us; the launch traced here: 788 us
  Pallas kernels  364 us (46%)
  matrix products  133 us (17%)
  local copies, waits for them, and re-layouts  122 us (15%)
  waiting for transfers between devices  80.6 us (10%)
  other arithmetic  67.5 us (9%)
  starting transfers between devices  15.1 us (2%)
    pallas_call x1, Pallas kernels, scatter(): pl.pallas_call(lambda *refs: scatter_kernel(widths, slots, *refs), out_sh...  194 us
    pallas_call x1, Pallas kernels, gather(): pl.pallas_call(lambda *refs: gather_kernel(widths, *refs), out_shape=[jax...  170 us
    dot_general x37, matrix products, dot_low(): jnp.einsum(pattern, left_side, right_side, preferred_element_type=jnp.flo...  133 us
    all_to_all x1, waiting for transfers between devices, on_device(): lax.all_to_all(plan.order_rows(low_slots), AXES, split_axis=0, concat_axi...  45.5 us
    all_to_all x1, waiting for transfers between devices, on_device(): lax.all_to_all(slot_rows, AXES, split_axis=1, concat_axis=0, tiled=True)  35.1 us
    unnamed x288, local copies, waits for them, and re-layouts  32.7 us
  transfers between devices with their start and end apart: 2, of which 2 were waited for; matrix products, arithmetic and copies ran while one was open for 7% of the time, Pallas kernels for 0%

profile of v4, /device:TPU:3, one launch (start us, length us, event | category | flops | bytes accessed | tf_op | source)
XLA Modules:
  0.0 787.6 jit_solution(957533680991547300)
XLA Ops:
  4.7 3.6 copy.260
  8.3 6.5 all-to-all-start
  40.7 45.5 %all-to-all-done = bf16[768,15,128]{2,1,0:T(8,128)(2,1)} async-done(((bf16[768,15,128]{2,1,0:T(8,128)(2,1)}), bf16[768,15,128]{2,1,0:T(8,128)(2,1)}, u32[]{:S(2)}, u32[]{:S(2)}) %all-to-all-start) | async-done | bytes 2949152 | tf_op jit(solution)/shard_map/all_to_all | solution.py:862
  86.2 4.3 copy.262
  95.6 170.2 %shard_map.224 = (bf16[2,2,2,4,24,768]{5,4,3,2,1,0:T(8,128)(2,1)S(1)}, bf16[2,2,2,4,24,3072]{5,4,3,2,1,0:T(8,128)(2,1)S(1)}, bf16[2,2,2,4,24,3072]{5,4,3,2,1,0:T...) custom-call(bf16[24,768]{1,0:T(8,128)(2,1)S(1)} %slice.177.refs_0_, ...), custom_call_target="tpu_custom_call" | custom-call | bytes 58982400 | tf_op jit(solution)/shard_map/pallas_call | solution.py:710
  271.8 4.3 convolution_convert_fusion.1
  291.3 6.1 multiply_convert_fusion.3
  297.4 3.8 fusion.123
  321.5 4.0 multiply_convert_fusion.2
  335.1 6.4 fusion.13
  352.3 5.3 convolution_convert_fusion.6
  357.7 7.1 multiply_reduce_fusion.1
  364.8 4.6 multiply_convert_fusion.1
  380.0 5.9 multiply_reduce_fusion.15
  389.5 9.2 %fusion.6 = bf16[2,256,3072]{2,1,0:T(8,128)(2,1)S(1)} fusion(f32[2,256,3072]{2,1,0:T(8,128)} %get-tuple-element.143, bf16[2,256,768]{2,1,0:T(8,128)(2,1)S(1)} %multiply_convert_fusion.5, bf16[768,3072,1]{1,0,2:T(8,128)(2,1)} %bitcast.420), kind=kOutput, calls=%fused_computation.24 | convolution fusion | flops 2447376384 | bytes 14942208 | tf_op jit(solution)/shard_map/gpd,df->gpf/dot_general | solution.py:55
  408.2 5.0 convolution_convert_fusion.2
  413.2 7.2 multiply_reduce_fusion
  420.4 4.6 multiply_convert_fusion
  460.5 4.6 multiply_reduce_fusion.4
  479.6 193.7 %shard_map.225 = (bf16[24,3072]{1,0:T(8,128)(2,1)}, bf16[24,3072]{1,0:T(8,128)(2,1)}, bf16[24,768]{1,0:T(8,128)(2,1)}, bf16[24,2304]{1,0:T(8,128)(2,1)}, bf16[24...) custom-call(bf16[512,768]{1,0:T(8,128)(2,1)} %bitcast.389, ...), custom_call_target="tpu_custom_call" | custom-call | bytes 56623104 | tf_op jit(solution)/shard_map/pallas_call | solution.py:755
  686.8 8.6 %all-to-all-start.1 = ((bf16[24,480,128]{2,0,1:T(8,128)(2,1)}), bf16[24,480,128]{2,0,1:T(8,128)(2,1)}, u32[]{:S(2)}, u32[]{:S(2)}) async-start(bf16[24,480,128]{2,0,1:T(8,128)(2,1)} %select_bitcast_fusion), calls=%async_computation.1 | async-start | bytes 5898240 | tf_op jit(solution)/shard_map/all_to_all | solution.py:1003
  717.7 9.7 %multiply_subtract_fusion = (f32[1288,768]{1,0:T(8,128)}, f32[1288,768]{1,0:T(8,128)}, f32[1288,768]{1,0:T(8,128)}) fusion(f32[1288,768]{1,0:T(8,128)S(1)} %copy-done.15, f32[1288]{0:T(1024)S(1)} %select_multiply_fusion, f32[16,768]{1,0:T(8,128)S(1)} %bitcast.406, f32[1000,768]{1,0:T(8,128)S(1)} %copy-done.20, f32[256,768]{1,0:T(8,128)S(1)} %copy-done.64, ...), kind=kLoop, calls=%fused_computation.57 | loop fusion | flops 16816128 | bytes 27702304 | tf_op jit(solution)/shard_map/sub | solution.py:105
  727.4 35.1 %all-to-all-done.1 = bf16[24,480,128]{2,0,1:T(8,128)(2,1)} async-done(((bf16[24,480,128]{2,0,1:T(8,128)(2,1)}), bf16[24,480,128]{2,0,1:T(8,128)(2,1)}, u32[]{:S(2)}, u32[]{:S(2)}) %all-to-all-start.1) | async-done | bytes 2949152 | tf_op jit(solution)/shard_map/all_to_all | solution.py:1003
  768.4 17.6 %fusion.17 = (f32[768,15,128]{2,0,1:T(8,128)}, f32[768,15,128]{2,0,1:T(8,128)}, f32[768,15,128]{2,0,1:T(8,128)}) fusion(f32[768,15,128]{2,0,1:T(8,128)} %param.24, pred[15]{0:T(512)(128)(4,1)S(1)} %copy-done.99, f32[768,15,128]{2,0,1:T(8,128)S(1)} %bitcast.325, f32[768,15,128]{2,0,1:T(8,128)} %param.23, f32[15]{0:T(128)S(1)} %copy-done.106, ...), kind=kOutput, calls=%fused_computation.50 | convolution fusion | flops 216883200 | bytes 47530104 | tf_op jit(solution)/shard_map/gd,gsc->dsc/dot_general | solution.py:55
  (501 shorter events, 209.2 us)
Async XLA Ops:
  8.2 8.7 %copy-start.98 = (s32[2]{0:T(128)S(1)}, s32[2]{0:T(128)}, u32[]{:S(2)}) copy-start(s32[2]{0:T(128)} %param.20) | copy-start | bytes 28
  8.2 9.3 %copy-start.97 = (s32[84]{0:T(128)S(1)}, s32[84]{0:T(128)}, u32[]{:S(2)}) copy-start(s32[84]{0:T(128)} %constant.329) | copy-start | bytes 1012
  8.3 10.5 %copy-start.96 = (s32[150]{0:T(256)S(1)}, s32[150]{0:T(256)}, u32[]{:S(2)}) copy-start(s32[150]{0:T(256)} %constant.330) | copy-start | bytes 1804
  8.3 78.0 %all-to-all-start = ((bf16[768,15,128]{2,1,0:T(8,128)(2,1)}), bf16[768,15,128]{2,1,0:T(8,128)(2,1)}, u32[]{:S(2)}, u32[]{:S(2)}) async-start(bf16[768,15,128]{2,1,0:T(8,128)(2,1)} %copy.260), calls=%async_computation | async-start | bytes 6291456 | tf_op jit(solution)/shard_map/all_to_all | solution.py:862
  14.8 8.0 %copy-start.92 = (f32[128]{0:T(128)}, f32[128]{0:T(128)S(1)}, u32[]{:S(2)}) copy-start(f32[128]{0:T(128)S(1)} %multiply_exponential_fusion.1) | copy-start | bytes 1540
  17.0 13.9 %copy-start.94 = (s32[15]{0:T(128)}, s32[15]{0:T(128)S(1)}, u32[]{:S(2)}) copy-start(s32[15]{0:T(128)S(1)} %get-tuple-element.67) | copy-start | bytes 184
  35.5 235.9 %copy-start.74 = (f32[2,256]{1,0:T(2,128)}, f32[2,256]{1,0:T(2,128)S(1)}, u32[]{:S(2)}) copy-start(f32[2,256]{1,0:T(2,128)S(1)} %broadcast_multiply_fusion.4) | copy-start | bytes 6148
  36.7 234.8 %copy-start.76 = (f32[2,256]{1,0:T(2,128)}, f32[2,256]{1,0:T(2,128)S(1)}, u32[]{:S(2)}) copy-start(f32[2,256]{1,0:T(2,128)S(1)} %fusion.88) | copy-start | bytes 6148
  40.5 55.1 %copy-start = (bf16[15,768,128]{2,1,0:T(8,128)(2,1)}, bf16[15,768,128]{2,1,0:T(8,128)(2,1)S(1)}, u32[]{:S(2)}) copy-start(bf16[15,768,128]{2,1,0:T(8,128)(2,1)S(1)} %convert_bitcast_fusion.refs_8_.refs_18_) | copy-start | bytes 8847364
  271.4 26.0 %copy-start.78 = (f32[2,768]{1,0:T(2,128)}, f32[2,768]{1,0:T(2,128)S(1)}, u32[]{:S(2)}) copy-start(f32[2,768]{1,0:T(2,128)S(1)} %get-tuple-element.116) | copy-start | bytes 18436
  352.3 12.5 %slice-start.2 = ((s8[6291456]{0:T(1024)(128)(4,1)}), s8[4194304]{0:T(1024)(128)(4,1)S(1)}, s32[]{:S(2)}) async-start(s8[6291456]{0:T(1024)(128)(4,1)} %bitcast.322), calls=%async_computation.4 | async-start | bytes 8388608
  387.8 10.9 %slice-start.13 = ((s8[4718592]{0:T(1024)(128)(4,1)}), s8[4194304]{0:T(1024)(128)(4,1)S(1)}, s32[]{:S(2)}) async-start(s8[4718592]{0:T(1024)(128)(4,1)} %bitcast.417), calls=%async_computation.15 | async-start | bytes 8388608
  389.5 9.2 %slice-start.14 = ((s8[4718592]{0:T(1024)(128)(4,1)}), s8[524288]{0:T(1024)(128)(4,1)S(1)}, s32[]{:S(2)}) async-start(s8[4718592]{0:T(1024)(128)(4,1)} %bitcast.417), calls=%async_computation.16 | async-start | bytes 1048576
  408.2 12.2 %slice-start = ((s8[6291456]{0:T(1024)(128)(4,1)}), s8[4194304]{0:T(1024)(128)(4,1)S(1)}, s32[]{:S(2)}) async-start(s8[6291456]{0:T(1024)(128)(4,1)} %bitcast.320), calls=%async_computation.2 | async-start | bytes 8388608
  466.5 8.8 %copy-start.44 = (bf16[512,768]{1,0:T(8,128)(2,1)S(1)}, bf16[512,768]{1,0:T(8,128)(2,1)}, u32[]{:S(2)}) copy-start(bf16[512,768]{1,0:T(8,128)(2,1)} %copy.295) | copy-start | bytes 2359300
  466.5 8.8 %copy-start.45 = (bf16[512,768]{1,0:T(8,128)(2,1)S(1)}, bf16[512,768]{1,0:T(8,128)(2,1)}, u32[]{:S(2)}) copy-start(bf16[512,768]{1,0:T(8,128)(2,1)} %copy.294) | copy-start | bytes 2359300
  479.6 201.8 %copy-start.89 = (s32[1024]{0:T(1024)S(1)}, s32[1024]{0:T(1024)}, u32[]{:S(2)}) copy-start(s32[1024]{0:T(1024)} %get-tuple-element.168) | copy-start | bytes 12292
  686.8 8.6 %copy-start.95 = (s32[15]{0:T(128)S(1)}, s32[15]{0:T(128)}, u32[]{:S(2)}) copy-start(s32[15]{0:T(128)} %copy-done.94) | copy-start | bytes 184
  686.8 9.2 %copy-start.104 = (s32[15]{0:T(128)S(1)}, s32[15]{0:T(128)}, u32[]{:S(2)}) copy-start(s32[15]{0:T(128)} %copy-done.103) | copy-start | bytes 184
  686.8 11.5 %copy-start.63 = (f32[32,2,16,128]{3,2,1,0:T(8,128)S(1)}, f32[32,2,16,128]{3,2,1,0:T(8,128)}, u32[]{:S(2)}) copy-start(f32[32,2,16,128]{3,2,1,0:T(8,128)} %get-tuple-element.36) | copy-start | bytes 1572868
  686.8 13.4 %copy-start.70 = (f32[64,16,128]{2,1,0:T(8,128)S(1)}, f32[64,16,128]{2,1,0:T(8,128)}, u32[]{:S(2)}) copy-start(f32[64,16,128]{2,1,0:T(8,128)} %get-tuple-element.38) | copy-start | bytes 1572868
  686.8 75.7 %all-to-all-start.1 = ((bf16[24,480,128]{2,0,1:T(8,128)(2,1)}), bf16[24,480,128]{2,0,1:T(8,128)(2,1)}, u32[]{:S(2)}, u32[]{:S(2)}) async-start(bf16[24,480,128]{2,0,1:T(8,128)(2,1)} %select_bitcast_fusion), calls=%async_computation.1 | async-start | bytes 5898240 | tf_op jit(solution)/shard_map/all_to_all | solution.py:1003
  699.6 10.0 %copy-start.93 = (f32[128]{0:T(128)S(1)}, f32[128]{0:T(128)}, u32[]{:S(2)}) copy-start(f32[128]{0:T(128)} %copy-done.92) | copy-start | bytes 1540
  699.6 10.8 %copy-start.2 = (bf16[2,2,2,4,24,768]{5,4,3,2,1,0:T(8,128)(2,1)S(1)}, bf16[2,2,2,4,24,768]{5,4,3,2,1,0:T(8,128)(2,1)}, u32[]{:S(2)}) copy-start(bf16[2,2,2,4,24,768]{5,4,3,2,1,0:T(8,128)(2,1)} %copy-done.1) | copy-start | bytes 3538948
  (107 other events, 379.0 us)

commit v5 on v4

--- a/solution.py
+++ b/solution.py
@@ -449,7 +449,7 @@
     scratch = refs[3 * count + 7 :]
     own, first_in, second_in, line_in = (scratch[i * count : (i + 1) * count] for i in range(4))
     (
-        left_in, right_in, away, every_modul, parts, landed,
+        left_in, left_turned, right_in, away, every_modul, parts, landed,
         load_sem, send_sem, recv_sem, modul_sem, part_sem, sum_sem,
     ) = scratch[4 * count :]
     devices, images = shared.shape[:2]
@@ -471,12 +471,33 @@
             device_id_type=MESH,
         )
 
-    def modul_copy(j, arriving):
-        return exchange(
-            lambda peer, mine: modul,
-            lambda owner: every_modul.at[pl.ds(owner * images, images)],
-            modul_sem, j, arriving,
-        )
+    def modul_copies(step, arriving):
+        if step == 0:
+            copies = []
+            for number in (1, 2, 3):
+                at_z = lax.rem(z + 4 - number, 4) if arriving else z
+                copies.append((modul, every_modul.at[y, x, c, at_z], to_z[number - 1]))
+        else:
+            at_x = 1 - x if arriving and step == 1 else x
+            at_y = 1 - y if arriving and step == 2 else y
+            at_c = 1 - c if arriving and step == 3 else c
+            block = (
+                every_modul.at[y, at_x, c],
+                every_modul.at[at_y, :, c],
+                every_modul.at[:, :, at_c],
+            )[step - 1]
+            copies = [(block, block, (to_x, to_y, to_core)[step - 1])]
+        return [
+            pltpu.make_async_remote_copy(
+                src_ref=source,
+                dst_ref=dest,
+                send_sem=modul_sem.at[0, step, number],
+                recv_sem=modul_sem.at[1, step, number],
+                device_id=target,
+                device_id_type=MESH,
+            )
+            for number, (source, dest, target) in enumerate(copies)
+        ]
 
     def part_copy(j, arriving):
         return exchange(
@@ -506,11 +527,16 @@
             copy(j, False).wait_send()
 
     def image_parts():
-        all_arrived(modul_copy)
-
-        @pl.loop(0, devices * images)
+        arrived(modul_copies(3, True))
+
+        @pl.loop(0, devices // 4)
         def _(i):
-            chosen[i] = jnp.dot(pick[...], every_modul[i], preferred_element_type=jnp.float32)
+            for n in range(4):
+                for m in range(images):
+                    block = every_modul[i // 4, (i // 2) % 2, i % 2, n, m]
+                    chosen[(i * 4 + n) * images + m] = jnp.dot(
+                        pick[...], block, preferred_element_type=jnp.float32
+                    )
 
         total = jnp.zeros((devices * images, D), jnp.float32)
         for s in range(slots):
@@ -542,14 +568,12 @@
             device_id_type=MESH,
         )
 
-    def loads(k):
-        slot = k % 3
-        return [
-            pltpu.make_async_copy(lefts[k], left_in.at[slot], load_sem.at[0, slot]),
-            pltpu.make_async_copy(
-                rights[k], right_in.at[slot, :, pl.ds(0, widths[k])], load_sem.at[1, slot]
-            ),
-        ]
+    def load_left(k):
+        return pltpu.make_async_copy(lefts[k], left_in.at[k % 2], load_sem.at[0, k % 2])
+
+    def load_right(k):
+        place = right_in.at[k % 3, :, pl.ds(0, widths[k])]
+        return pltpu.make_async_copy(rights[k], place, load_sem.at[1, k % 3])
 
     def core_copies(k):
         source = away.at[k % 3, :, :, :, :, pl.ds(0, widths[k])]
@@ -591,20 +615,23 @@
 
     def products(k, half, store):
         slot = k % 3
-        tile = 256
+        tile = D
 
         @pl.loop(0, widths[k] // tile)
         def _(n):
             columns = pl.ds(pl.multiple_of(n * tile, tile), tile)
-            left = left_in[slot, :, pl.ds(pl.multiple_of(half * half_rows, BLOCK), half_rows)]
-            result = dot_rows(left, right_in[slot, :, columns])
+            left = left_turned[slot, pl.ds(pl.multiple_of(half * half_rows, half_rows), half_rows)]
+            result = jnp.dot(left, right_in[slot, :, columns], preferred_element_type=jnp.float32)
             for i in range(16):
                 at = (i // 8, (i // 4) % 2, i % 4, slice(None), columns)
                 store(at, result[i * rows : (i + 1) * rows])
 
     def away_products(k):
-        for copy in loads(k):
-            copy.wait()
+        load_left(k).wait()
+        load_right(k).wait()
+        left_turned[k % 3] = left_in[k % 2].T
+        if k + 2 < count:
+            load_left(k + 2).start()
         if k >= 3:
             for copy in core_copies(k - 3):
                 copy.wait_send()
@@ -642,11 +669,12 @@
             own[k][a_at] = own[k][a_at] + second_in[k][0, at_z]
             own[k][b_at] = own[k][b_at] + second_in[k][1, at_z]
 
-    all_start(modul_copy)
-    for i in range(images):
-        every_modul[me * images + i] = modul[i]
+    start(modul_copies(0, False))
+    every_modul[y, x, c, z] = modul[...]
     for k in range(min(3, count)):
-        start(loads(k))
+        load_right(k).start()
+        if k < 2:
+            load_left(k).start()
     away_products(0)
     for t in range(count + 3):
         if t + 1 < count:
@@ -656,7 +684,7 @@
             own_products(t)
             start(first_copies(t))
             if t + 3 < count:
-                start(loads(t + 3))
+                load_right(t + 3).start()
         if 0 <= t - 1 < count:
             arrived(first_copies(t - 1))
             first_sum(t - 1)
@@ -672,13 +700,19 @@
             for step in (1, 2, 3):
                 total = total + line_in[k][step - 1].astype(jnp.float32)
             outs[k][...] = total.astype(jnp.bfloat16)
+        if t < 3:
+            arrived(modul_copies(t, True))
+            start(modul_copies(t + 1, False))
         if t == 3:
             image_parts()
         if t == 6:
             image_sums()
     all_arrived(sum_copy)
-    for copy in (modul_copy, part_copy, sum_copy):
+    for copy in (part_copy, sum_copy):
         all_sent(copy)
+    for step in range(4):
+        for copy in modul_copies(step, False):
+            copy.wait_send()
     for k in range(count):
         for copies in (core_copies, first_copies, second_copies, line_copies):
             if copies is core_copies and k + 3 < count:
@@ -764,16 +798,17 @@
             out_specs=[pl.BlockSpec(memory_space=pltpu.VMEM)] * (count + 2),
             scratch_shapes=scratch
             + [
-                pltpu.VMEM((3, tokens, D), jnp.bfloat16),
+                pltpu.VMEM((2, tokens, D), jnp.bfloat16),
+                pltpu.VMEM((3, D, tokens), jnp.bfloat16),
                 pltpu.VMEM((3, tokens, widest), jnp.bfloat16),
                 pltpu.VMEM((3, 2, 2, 4, rows, widest), jnp.bfloat16),
-                pltpu.VMEM((32 * images,) + modul.shape[1:], jnp.bfloat16),
+                pltpu.VMEM((2, 2, 2, 4) + modul.shape, jnp.bfloat16),
                 pltpu.VMEM(edge.shape, jnp.float32),
                 pltpu.VMEM((32,) + factor.shape, jnp.float32),
                 pltpu.SemaphoreType.DMA((2, 3)),
                 pltpu.SemaphoreType.DMA((count, 8)),
                 pltpu.SemaphoreType.DMA((count, 8)),
-                pltpu.SemaphoreType.DMA((2, 32)),
+                pltpu.SemaphoreType.DMA((2, 4, 3)),
                 pltpu.SemaphoreType.DMA((2, 32)),
                 pltpu.SemaphoreType.DMA((2, 32)),
             ],

time: 793 us -> 774 us (0.976)
  Pallas kernels: 364 us -> 343 us
    pallas_call x1, Pallas kernels: 194 us -> 173 us  [scatter(): pl.pallas_call(lambda *refs: scatter_kernel(widths, slots, *refs), out_sh...]
where the time goes in v5:
time: 774 us; the launch traced here: 769 us
  Pallas kernels  343 us (44%)
  matrix products  133 us (17%)
  local copies, waits for them, and re-layouts  122 us (16%)
  waiting for transfers between devices  80.7 us (10%)
  other arithmetic  67.6 us (9%)
  starting transfers between devices  17 us (2%)
    pallas_call x1, Pallas kernels, scatter(): pl.pallas_call(lambda *refs: scatter_kernel(widths, slots, *refs), out_sh...  173 us
    pallas_call x1, Pallas kernels, gather(): pl.pallas_call(lambda *refs: gather_kernel(widths, *refs), out_shape=[jax...  170 us
    dot_general x37, matrix products, dot_low(): jnp.einsum(pattern, left_side, right_side, preferred_element_type=jnp.flo...  133 us
    all_to_all x1, waiting for transfers between devices, on_device(): lax.all_to_all(plan.order_rows(low_slots), AXES, split_axis=0, concat_axi...  45.6 us
    all_to_all x1, waiting for transfers between devices, on_device(): lax.all_to_all(slot_rows, AXES, split_axis=1, concat_axis=0, tiled=True)  35.1 us
    unnamed x288, local copies, waits for them, and re-layouts  32.7 us
  transfers between devices with their start and end apart: 2, of which 2 were waited for; matrix products, arithmetic and copies ran while one was open for 7% of the time, Pallas kernels for 0%

profile of v5, /device:TPU:3, one launch (start us, length us, event | category | flops | bytes accessed | tf_op | source)
XLA Modules:
  0.0 768.8 jit_solution(16689281235344379228)
XLA Ops:
  4.7 3.6 copy.260
  8.3 6.5 all-to-all-start
  40.7 45.6 %all-to-all-done = bf16[768,15,128]{2,1,0:T(8,128)(2,1)} async-done(((bf16[768,15,128]{2,1,0:T(8,128)(2,1)}), bf16[768,15,128]{2,1,0:T(8,128)(2,1)}, u32[]{:S(2)}, u32[]{:S(2)}) %all-to-all-start) | async-done | bytes 2949152 | tf_op jit(solution)/shard_map/all_to_all | solution.py:897
  86.2 4.3 copy.262
  95.6 170.1 %shard_map.224 = (bf16[2,2,2,4,24,768]{5,4,3,2,1,0:T(8,128)(2,1)S(1)}, bf16[2,2,2,4,24,3072]{5,4,3,2,1,0:T(8,128)(2,1)S(1)}, bf16[2,2,2,4,24,3072]{5,4,3,2,1,0:T...) custom-call(bf16[24,768]{1,0:T(8,128)(2,1)S(1)} %slice.177.refs_0_, ...), custom_call_target="tpu_custom_call" | custom-call | bytes 58982400 | tf_op jit(solution)/shard_map/pallas_call | solution.py:744
  271.7 4.3 convolution_convert_fusion.1
  291.2 6.0 multiply_convert_fusion.3
  297.3 3.8 fusion.123
  321.4 4.0 multiply_convert_fusion.2
  335.0 6.4 fusion.13
  352.2 5.3 convolution_convert_fusion.6
  357.6 7.1 multiply_reduce_fusion.1
  364.7 4.6 multiply_convert_fusion.1
  379.9 5.9 multiply_reduce_fusion.15
  389.4 9.2 %fusion.6 = bf16[2,256,3072]{2,1,0:T(8,128)(2,1)S(1)} fusion(f32[2,256,3072]{2,1,0:T(8,128)} %get-tuple-element.143, bf16[2,256,768]{2,1,0:T(8,128)(2,1)S(1)} %multiply_convert_fusion.5, bf16[768,3072,1]{1,0,2:T(8,128)(2,1)} %bitcast.420), kind=kOutput, calls=%fused_computation.24 | convolution fusion | flops 2447376384 | bytes 14942208 | tf_op jit(solution)/shard_map/gpd,df->gpf/dot_general | solution.py:55
  408.1 5.0 convolution_convert_fusion.2
  413.1 7.2 multiply_reduce_fusion
  420.3 4.6 multiply_convert_fusion
  460.4 4.6 multiply_reduce_fusion.4
  479.5 173.2 %shard_map.225 = (bf16[24,3072]{1,0:T(8,128)(2,1)}, bf16[24,3072]{1,0:T(8,128)(2,1)}, bf16[24,768]{1,0:T(8,128)(2,1)}, bf16[24,2304]{1,0:T(8,128)(2,1)}, bf16[24...) custom-call(bf16[512,768]{1,0:T(8,128)(2,1)} %bitcast.389, ...), custom_call_target="tpu_custom_call" | custom-call | bytes 56623104 | tf_op jit(solution)/shard_map/pallas_call | solution.py:789
  666.2 10.5 %all-to-all-start.1 = ((bf16[24,480,128]{2,0,1:T(8,128)(2,1)}), bf16[24,480,128]{2,0,1:T(8,128)(2,1)}, u32[]{:S(2)}, u32[]{:S(2)}) async-start(bf16[24,480,128]{2,0,1:T(8,128)(2,1)} %select_bitcast_fusion), calls=%async_computation.1 | async-start | bytes 5898240 | tf_op jit(solution)/shard_map/all_to_all | solution.py:1038
  699.0 9.9 %multiply_subtract_fusion = (f32[1288,768]{1,0:T(8,128)}, f32[1288,768]{1,0:T(8,128)}, f32[1288,768]{1,0:T(8,128)}) fusion(f32[1288,768]{1,0:T(8,128)S(1)} %copy-done.15, f32[1288]{0:T(1024)S(1)} %select_multiply_fusion, f32[16,768]{1,0:T(8,128)S(1)} %bitcast.406, f32[1000,768]{1,0:T(8,128)S(1)} %copy-done.20, f32[256,768]{1,0:T(8,128)S(1)} %copy-done.64, ...), kind=kLoop, calls=%fused_computation.57 | loop fusion | flops 16816128 | bytes 27702304 | tf_op jit(solution)/shard_map/sub | solution.py:105
  709.0 35.1 %all-to-all-done.1 = bf16[24,480,128]{2,0,1:T(8,128)(2,1)} async-done(((bf16[24,480,128]{2,0,1:T(8,128)(2,1)}), bf16[24,480,128]{2,0,1:T(8,128)(2,1)}, u32[]{:S(2)}, u32[]{:S(2)}) %all-to-all-start.1) | async-done | bytes 2949152 | tf_op jit(solution)/shard_map/all_to_all | solution.py:1038
  749.9 17.6 %fusion.17 = (f32[768,15,128]{2,0,1:T(8,128)}, f32[768,15,128]{2,0,1:T(8,128)}, f32[768,15,128]{2,0,1:T(8,128)}) fusion(f32[768,15,128]{2,0,1:T(8,128)} %param.24, pred[15]{0:T(512)(128)(4,1)S(1)} %copy-done.99, f32[768,15,128]{2,0,1:T(8,128)S(1)} %bitcast.325, f32[768,15,128]{2,0,1:T(8,128)} %param.23, f32[15]{0:T(128)S(1)} %copy-done.106, ...), kind=kOutput, calls=%fused_computation.50 | convolution fusion | flops 216883200 | bytes 47530104 | tf_op jit(solution)/shard_map/gd,gsc->dsc/dot_general | solution.py:55
  (501 shorter events, 209.2 us)
Async XLA Ops:
  8.2 8.7 %copy-start.98 = (s32[2]{0:T(128)S(1)}, s32[2]{0:T(128)}, u32[]{:S(2)}) copy-start(s32[2]{0:T(128)} %param.20) | copy-start | bytes 28
  8.2 9.2 %copy-start.97 = (s32[84]{0:T(128)S(1)}, s32[84]{0:T(128)}, u32[]{:S(2)}) copy-start(s32[84]{0:T(128)} %constant.329) | copy-start | bytes 1012
  8.3 10.5 %copy-start.96 = (s32[150]{0:T(256)S(1)}, s32[150]{0:T(256)}, u32[]{:S(2)}) copy-start(s32[150]{0:T(256)} %constant.330) | copy-start | bytes 1804
  8.3 78.0 %all-to-all-start = ((bf16[768,15,128]{2,1,0:T(8,128)(2,1)}), bf16[768,15,128]{2,1,0:T(8,128)(2,1)}, u32[]{:S(2)}, u32[]{:S(2)}) async-start(bf16[768,15,128]{2,1,0:T(8,128)(2,1)} %copy.260), calls=%async_computation | async-start | bytes 6291456 | tf_op jit(solution)/shard_map/all_to_all | solution.py:897
  14.8 8.0 %copy-start.92 = (f32[128]{0:T(128)}, f32[128]{0:T(128)S(1)}, u32[]{:S(2)}) copy-start(f32[128]{0:T(128)S(1)} %multiply_exponential_fusion.1) | copy-start | bytes 1540
  16.9 13.9 %copy-start.94 = (s32[15]{0:T(128)}, s32[15]{0:T(128)S(1)}, u32[]{:S(2)}) copy-start(s32[15]{0:T(128)S(1)} %get-tuple-element.67) | copy-start | bytes 184
  35.5 235.9 %copy-start.74 = (f32[2,256]{1,0:T(2,128)}, f32[2,256]{1,0:T(2,128)S(1)}, u32[]{:S(2)}) copy-start(f32[2,256]{1,0:T(2,128)S(1)} %broadcast_multiply_fusion.4) | copy-start | bytes 6148
  36.6 234.8 %copy-start.76 = (f32[2,256]{1,0:T(2,128)}, f32[2,256]{1,0:T(2,128)S(1)}, u32[]{:S(2)}) copy-start(f32[2,256]{1,0:T(2,128)S(1)} %fusion.88) | copy-start | bytes 6148
  40.5 55.1 %copy-start = (bf16[15,768,128]{2,1,0:T(8,128)(2,1)}, bf16[15,768,128]{2,1,0:T(8,128)(2,1)S(1)}, u32[]{:S(2)}) copy-start(bf16[15,768,128]{2,1,0:T(8,128)(2,1)S(1)} %convert_bitcast_fusion.refs_8_.refs_18_) | copy-start | bytes 8847364
  271.4 25.9 %copy-start.78 = (f32[2,768]{1,0:T(2,128)}, f32[2,768]{1,0:T(2,128)S(1)}, u32[]{:S(2)}) copy-start(f32[2,768]{1,0:T(2,128)S(1)} %get-tuple-element.116) | copy-start | bytes 18436
  352.2 12.5 %slice-start.2 = ((s8[6291456]{0:T(1024)(128)(4,1)}), s8[4194304]{0:T(1024)(128)(4,1)S(1)}, s32[]{:S(2)}) async-start(s8[6291456]{0:T(1024)(128)(4,1)} %bitcast.322), calls=%async_computation.4 | async-start | bytes 8388608
  387.7 10.9 %slice-start.13 = ((s8[4718592]{0:T(1024)(128)(4,1)}), s8[4194304]{0:T(1024)(128)(4,1)S(1)}, s32[]{:S(2)}) async-start(s8[4718592]{0:T(1024)(128)(4,1)} %bitcast.417), calls=%async_computation.15 | async-start | bytes 8388608
  389.4 9.2 %slice-start.14 = ((s8[4718592]{0:T(1024)(128)(4,1)}), s8[524288]{0:T(1024)(128)(4,1)S(1)}, s32[]{:S(2)}) async-start(s8[4718592]{0:T(1024)(128)(4,1)} %bitcast.417), calls=%async_computation.16 | async-start | bytes 1048576
  408.1 12.2 %slice-start = ((s8[6291456]{0:T(1024)(128)(4,1)}), s8[4194304]{0:T(1024)(128)(4,1)S(1)}, s32[]{:S(2)}) async-start(s8[6291456]{0:T(1024)(128)(4,1)} %bitcast.320), calls=%async_computation.2 | async-start | bytes 8388608
  466.4 8.8 %copy-start.44 = (bf16[512,768]{1,0:T(8,128)(2,1)S(1)}, bf16[512,768]{1,0:T(8,128)(2,1)}, u32[]{:S(2)}) copy-start(bf16[512,768]{1,0:T(8,128)(2,1)} %copy.295) | copy-start | bytes 2359300
  466.4 8.8 %copy-start.45 = (bf16[512,768]{1,0:T(8,128)(2,1)S(1)}, bf16[512,768]{1,0:T(8,128)(2,1)}, u32[]{:S(2)}) copy-start(bf16[512,768]{1,0:T(8,128)(2,1)} %copy.294) | copy-start | bytes 2359300
  479.4 181.3 %copy-start.89 = (s32[1024]{0:T(1024)S(1)}, s32[1024]{0:T(1024)}, u32[]{:S(2)}) copy-start(s32[1024]{0:T(1024)} %get-tuple-element.168) | copy-start | bytes 12292
  666.2 10.5 %copy-start.95 = (s32[15]{0:T(128)S(1)}, s32[15]{0:T(128)}, u32[]{:S(2)}) copy-start(s32[15]{0:T(128)} %copy-done.94) | copy-start | bytes 184
  666.2 11.1 %copy-start.104 = (s32[15]{0:T(128)S(1)}, s32[15]{0:T(128)}, u32[]{:S(2)}) copy-start(s32[15]{0:T(128)} %copy-done.103) | copy-start | bytes 184
  666.2 13.4 %copy-start.63 = (f32[32,2,16,128]{3,2,1,0:T(8,128)S(1)}, f32[32,2,16,128]{3,2,1,0:T(8,128)}, u32[]{:S(2)}) copy-start(f32[32,2,16,128]{3,2,1,0:T(8,128)} %get-tuple-element.36) | copy-start | bytes 1572868
  666.2 15.3 %copy-start.70 = (f32[64,16,128]{2,1,0:T(8,128)S(1)}, f32[64,16,128]{2,1,0:T(8,128)}, u32[]{:S(2)}) copy-start(f32[64,16,128]{2,1,0:T(8,128)} %get-tuple-element.38) | copy-start | bytes 1572868
  666.2 77.8 %all-to-all-start.1 = ((bf16[24,480,128]{2,0,1:T(8,128)(2,1)}), bf16[24,480,128]{2,0,1:T(8,128)(2,1)}, u32[]{:S(2)}, u32[]{:S(2)}) async-start(bf16[24,480,128]{2,0,1:T(8,128)(2,1)} %select_bitcast_fusion), calls=%async_computation.1 | async-start | bytes 5898240 | tf_op jit(solution)/shard_map/all_to_all | solution.py:1038
  680.9 10.0 %copy-start.93 = (f32[128]{0:T(128)S(1)}, f32[128]{0:T(128)}, u32[]{:S(2)}) copy-start(f32[128]{0:T(128)} %copy-done.92) | copy-start | bytes 1540
  680.9 10.8 %copy-start.2 = (bf16[2,2,2,4,24,768]{5,4,3,2,1,0:T(8,128)(2,1)S(1)}, bf16[2,2,2,4,24,768]{5,4,3,2,1,0:T(8,128)(2,1)}, u32[]{:S(2)}) copy-start(bf16[2,2,2,4,24,768]{5,4,3,2,1,0:T(8,128)(2,1)} %copy-done.1) | copy-start | bytes 3538948
  (107 other events, 378.7 us)

commit v6 on v5

--- a/solution.py
+++ b/solution.py
@@ -105,34 +105,16 @@
     return (weight - rate * (ratio + decay_rate * weight), first_new, second_new)
 
 
-def split_heads(qkv_all):
-    groups, length = (qkv_all.shape[0], qkv_all.shape[1])
-    return tuple(
-        (
-            qkv_all[..., part_idx * D : (part_idx + 1) * D].reshape(groups, length, HEADS, HEAD_DIM)
-            for part_idx in range(3)
-        )
-    )
-
-
 def modulate(normed, shift, scale):
     return normed * (1.0 + scale[:, None, :]) + shift[:, None, :]
 
 
 def layer_forward(hidden, modul, weights):
     w_qkv, w_out, w_up, w_down = weights
-    groups = hidden.shape[0]
     shift_a, scale_a, gate_a, shift_b, scale_b, gate_b = jnp.split(modul, 6, -1)
     attn_in = modulate(norm_rows(hidden), shift_a, scale_a).astype(jnp.bfloat16)
     qkv_all = dot_low("gpd,de->gpe", attn_in, w_qkv).astype(jnp.bfloat16)
-    queries, keys_all, values = split_heads(qkv_all)
-    scores = dot_low("gqhe,gkhe->ghqk", queries, keys_all) * HEAD_DIM ** (-0.5)
-    top_score = jnp.max(scores, -1, keepdims=True)
-    log_total = top_score + jnp.log(jnp.sum(jnp.exp(scores - top_score), -1, keepdims=True))
-    attn_prob = jnp.exp(scores - log_total).astype(jnp.bfloat16)
-    heads_out = (
-        dot_low("ghqk,gkhe->gqhe", attn_prob, values).astype(jnp.bfloat16).reshape(groups, -1, D)
-    )
+    heads_out = attend(qkv_all)
     branch_a = dot_low("gpd,de->gpe", heads_out, w_out)
     middle = hidden + gate_a[:, None, :] * branch_a
     mlp_in = modulate(norm_rows(middle), shift_b, scale_b).astype(jnp.bfloat16)
@@ -147,7 +129,6 @@
             modul,
             attn_in,
             qkv_all,
-            log_total,
             heads_out,
             branch_a,
             middle,
@@ -166,7 +147,6 @@
         modul,
         attn_in,
         qkv_all,
-        log_total,
         heads_out,
         branch_a,
         middle,
@@ -175,7 +155,6 @@
         post_act,
         branch_b,
     ) = saved
-    groups = hidden.shape[0]
     shift_a, scale_a, gate_a, shift_b, scale_b, gate_b = jnp.split(modul, 6, -1)
     grad_gate_b = jnp.sum(grad_out * branch_b, 1)
     grad_branch_b = (gate_b[:, None, :] * grad_out).astype(jnp.bfloat16)
@@ -193,28 +172,8 @@
     grad_gate_a = jnp.sum(grad_middle * branch_a, 1)
     grad_branch_a = (gate_a[:, None, :] * grad_middle).astype(jnp.bfloat16)
     grad_out_w = (heads_out, grad_branch_a)
-    grad_heads = (
-        dot_low("gpe,de->gpd", grad_branch_a, w_out)
-        .astype(jnp.bfloat16)
-        .reshape(groups, -1, HEADS, HEAD_DIM)
-    )
-    queries, keys_all, values = split_heads(qkv_all)
-    scores = dot_low("gqhe,gkhe->ghqk", queries, keys_all) * HEAD_DIM ** (-0.5)
-    attn_prob = jnp.exp(scores - log_total)
-    grad_prob = dot_low("gqhe,gkhe->ghqk", grad_heads, values)
-    grad_values = dot_low("ghqk,gqhe->gkhe", attn_prob.astype(jnp.bfloat16), grad_heads)
-    inner_sum = jnp.sum(attn_prob * grad_prob, -1, keepdims=True)
-    grad_scores = (HEAD_DIM ** (-0.5) * attn_prob * (grad_prob - inner_sum)).astype(jnp.bfloat16)
-    grad_queries = dot_low("ghqk,gkhe->gqhe", grad_scores, keys_all)
-    grad_keys = dot_low("ghqk,gqhe->gkhe", grad_scores, queries)
-    grad_qkv = jnp.concatenate(
-        [
-            grad_queries.reshape(groups, -1, D),
-            grad_keys.reshape(groups, -1, D),
-            grad_values.reshape(groups, -1, D),
-        ],
-        -1,
-    ).astype(jnp.bfloat16)
+    grad_heads = dot_low("gpe,de->gpd", grad_branch_a, w_out).astype(jnp.bfloat16)
+    grad_qkv = attend_back(qkv_all, grad_heads)
     grad_qkv_w = (attn_in, grad_qkv)
     grad_attn_in = dot_low("gpe,de->gpd", grad_qkv, w_qkv)
     normed_a = norm_rows(hidden)
@@ -244,6 +203,94 @@
     left_side = left_side.reshape(-1, left_side.shape[-1])
     right_side = right_side.reshape(-1, right_side.shape[-1])
     return dot_rows(left_side, right_side).astype(jnp.bfloat16)
+
+
+def head_mask(number):
+    lane = lax.broadcasted_iota(jnp.int32, (PATCHES, 2 * HEAD_DIM), 1)
+    return (lane >= number * HEAD_DIM) & (lane < (number + 1) * HEAD_DIM)
+
+
+def dot_lanes(left_side, right_side):
+    return lax.dot_general(
+        left_side, right_side, (((1,), (1,)), ((), ())), preferred_element_type=jnp.float32
+    )
+
+
+def attend_kernel(queries, keys_all, values, out):
+    result = jnp.zeros((PATCHES, 2 * HEAD_DIM), jnp.float32)
+    for number in (0, 1):
+        mask = head_mask(number)
+        one = jnp.where(mask, queries[0], jnp.zeros((), jnp.bfloat16))
+        scores = dot_lanes(one, keys_all[0]) * HEAD_DIM ** (-0.5)
+        powers = jnp.exp(scores - jnp.max(scores, -1, keepdims=True))
+        prob = (powers * (1.0 / jnp.sum(powers, -1, keepdims=True))).astype(jnp.bfloat16)
+        mixed = jnp.dot(prob, values[0], preferred_element_type=jnp.float32)
+        result = jnp.where(mask, mixed, result)
+    out[0] = result.astype(jnp.bfloat16)
+
+
+def attend_back_kernel(queries, keys_all, values, grad, out):
+    pair = pl.program_id(1)
+    results = [jnp.zeros((PATCHES, 2 * HEAD_DIM), jnp.float32)] * 3
+    none = jnp.zeros((), jnp.bfloat16)
+    for number in (0, 1):
+        mask = head_mask(number)
+        scores = dot_lanes(keys_all[0], jnp.where(mask, queries[0], none)) * HEAD_DIM ** (-0.5)
+        powers = jnp.exp(scores - jnp.max(scores, 0, keepdims=True))
+        prob = powers * (1.0 / jnp.sum(powers, 0, keepdims=True))
+        grad_prob = dot_lanes(values[0], jnp.where(mask, grad[0], none))
+        inner = jnp.sum(prob * grad_prob, 0, keepdims=True)
+        grad_scores = (HEAD_DIM ** (-0.5) * prob * (grad_prob - inner)).astype(jnp.bfloat16)
+        parts = (
+            dot_rows(grad_scores, keys_all[0]),
+            jnp.dot(grad_scores, queries[0], preferred_element_type=jnp.float32),
+            jnp.dot(prob.astype(jnp.bfloat16), grad[0], preferred_element_type=jnp.float32),
+        )
+        results = [jnp.where(mask, part, result) for part, result in zip(parts, results)]
+    for third, result in enumerate(results):
+        first = pl.multiple_of(third * D + pair * 2 * HEAD_DIM, 2 * HEAD_DIM)
+        out[0, :, pl.ds(first, 2 * HEAD_DIM)] = result.astype(jnp.bfloat16)
+
+
+def pair_block(third):
+    pairs = HEADS // 2
+    return pl.BlockSpec(
+        (1, PATCHES, 2 * HEAD_DIM), lambda image, pair: (image, 0, third * pairs + pair)
+    )
+
+
+def attend(qkv_all):
+    images = qkv_all.shape[0]
+    pairs = HEADS // 2
+    return pl.pallas_call(
+        attend_kernel,
+        grid=(images, pairs),
+        out_shape=jax.ShapeDtypeStruct((images, PATCHES, D), jnp.bfloat16),
+        in_specs=[pair_block(0), pair_block(1), pair_block(2)],
+        out_specs=pair_block(0),
+        cost_estimate=pl.CostEstimate(
+            flops=4 * images * PATCHES * PATCHES * D,
+            bytes_accessed=8 * images * PATCHES * D,
+            transcendentals=images * HEADS * PATCHES * PATCHES,
+        ),
+    )(qkv_all, qkv_all, qkv_all)
+
+
+def attend_back(qkv_all, grad_heads):
+    images = qkv_all.shape[0]
+    pairs = HEADS // 2
+    return pl.pallas_call(
+        attend_back_kernel,
+        grid=(images, pairs),
+        out_shape=jax.ShapeDtypeStruct((images, PATCHES, 3 * D), jnp.bfloat16),
+        in_specs=[pair_block(0), pair_block(1), pair_block(2), pair_block(0)],
+        out_specs=pl.BlockSpec((1, PATCHES, 3 * D), lambda image, pair: (image, 0, 0)),
+        cost_estimate=pl.CostEstimate(
+            flops=10 * images * PATCHES * PATCHES * D,
+            bytes_accessed=14 * images * PATCHES * D,
+            transcendentals=images * HEADS * PATCHES * PATCHES,
+        ),
+    )(qkv_all, qkv_all, qkv_all, grad_heads)
 
 
 def place_of():
@@ -733,7 +780,8 @@
         return jnp.moveaxis(split, 2, 0).reshape(shape)
 
     def gather(self, pieces, time_piece, info, low_slots):
-        pieces = [time_piece] + list(pieces)
+        turn = sorted(range(len(pieces)), key=lambda n: (n % 4 == 1, n))
+        pieces = [time_piece] + [pieces[n] for n in turn]
         widths = tuple(piece.shape[1] for piece in pieces)
         count, rows = len(pieces), D // 32
         all_images = 32 * info.shape[0]
@@ -772,7 +820,8 @@
         )(*pieces, info, jnp.swapaxes(low_slots, 0, 1))
         whole = [part.reshape(D, -1) for part in whole]
         modul = jnp.swapaxes(modul[:, :, :slots], 0, 1).reshape(-1, 32 * slots, BLOCK)
-        return whole[1:], whole[0], every_info, cond, modul
+        ordered = [whole[1 + turn.index(n)] for n in range(len(turn))]
+        return ordered, whole[0], every_info, cond, modul
 
     def scatter(self, grads, modul, pick, low_slots, edge, factor):
         lefts = [left.reshape(-1, D) for left, _ in grads]
@@ -902,8 +951,8 @@
     pieces = []
     for l in range(LAYERS):
         base = l * DENSE_COLS
-        cuts = (base, base + 4 * D, base + 4 * D + FF, base + DENSE_COLS)
-        pieces += [unit_rows[:, cuts[i] : cuts[i + 1]] for i in range(3)]
+        cuts = (0, 3 * D, 4 * D, 4 * D + FF, DENSE_COLS)
+        pieces += [unit_rows[:, base + cuts[i] : base + cuts[i + 1]] for i in range(4)]
     x_start = latents.astype(jnp.float32).reshape(-1, PATCHES, CHANNELS)
     noise_f = noise.astype(jnp.float32).reshape(-1, PATCHES, CHANNELS)
     times = (t_index.astype(jnp.float32) + 0.5) / TSTEPS
@@ -944,10 +993,7 @@
     freq_low = frequencies(every_time).astype(jnp.bfloat16)
     time_pre = jnp.dot(freq_low, time_w, preferred_element_type=jnp.float32)
     time_act = every_info[:, :blocks].reshape(all_images, D).astype(jnp.bfloat16)
-    weights_all = [
-        (whole[3 * l][:, : 3 * D], whole[3 * l][:, 3 * D :], whole[3 * l + 1], whole[3 * l + 2])
-        for l in range(LAYERS)
-    ]
+    weights_all = [tuple(whole[4 * l : 4 * l + 4]) for l in range(LAYERS)]
     cond = lax.dynamic_slice_in_dim(cond_all, me * images, images)
     cond_act = jax.nn.silu(cond_all).astype(jnp.bfloat16)
     modul_all = jnp.take(slot_modul, owner[image_units], axis=1).reshape(images, -1)
@@ -995,14 +1041,13 @@
     edge = jnp.pad(edge.reshape(all_images, blocks, BLOCK), ((0, 0), (8, 8 - blocks), (0, 0)))
     factor = local_back(jax.nn.silu, cond, jnp.ones_like(cond)).reshape(images, blocks, BLOCK)
     factor = jnp.pad(factor, ((0, 0), (0, 16 - blocks), (0, 0)), constant_values=1.0)
-    order = list(reversed(range(LAYERS)))
+    order = [(l, i) for l in range(LAYERS) for i in (0, 2, 3)]
+    order = [(LAYERS - 1, 1)] + order + [(l, 1) for l in range(LAYERS - 1)]
     scattered, slot_grad_out, shared = plan.scatter(
-        [grad for l in order for grad in reversed(layer_grads[l])],
+        [layer_grads[l][i] for l, i in order],
         modul_grad, pick, low_slots, edge, factor,
     )
-    grad_rows = {
-        (l, 3 - i): scattered[4 * n + i] for n, l in enumerate(order) for i in range(4)
-    }
+    grad_rows = dict(zip(order, scattered))
     shared = shared.reshape(all_images, 16, BLOCK)
     grad_cond = shared[:, :blocks].reshape(all_images, D)
     edge = shared[:, 8 : 8 + blocks].reshape(all_images, D)

time: 774 us -> 719 us (0.929)
  local copies, waits for them, and re-layouts: 122 us -> 63.4 us
  Pallas kernels: 343 us -> 391 us
  matrix products: 133 us -> 106 us
  other arithmetic: 67.6 us -> 51 us
    pallas_call x0 -> x4, Pallas kernels: none -> 58 us  [the longest x2 31.8 us: attend_back(): pl.pallas_call(attend_back_kernel, grid=(images, pairs), out_shape=jax.Sh...]
    dot_general x37 -> x25, matrix products: 133 us -> 106 us  [dot_low(): jnp.einsum(pattern, left_side, right_side, preferred_element_type=jnp.flo...]
    slice x10 -> x3, local copies, waits for them, and re-layouts: 14.5 us -> 0.07 us  [on_device(): unit_rows[:, base + cuts[i]:base + cuts[i + 1]]]
    another operation x8 -> x0, local copies, waits for them, and re-layouts: 10.8 us -> none
    concatenate x6 -> x0, local copies, waits for them, and re-layouts: 10.6 us -> none  [layer_backward(): jnp.concatenate([grad_queries.reshape(groups, -1, D), grad_keys.reshape(g...]
    reshape x6 -> x0, local copies, waits for them, and re-layouts: 9.55 us -> none  [the longest x2 3.47 us: layer_backward(): grad_values.reshape(groups, -1, D)]
    convert_element_type x2 -> x0, other arithmetic: 9.29 us -> none  [layer_backward(): (HEAD_DIM ** (-0.5) * attn_prob * (grad_prob - inner_sum)).astype(jnp.bfl...]
    unnamed x288 -> x204, local copies, waits for them, and re-layouts: 32.7 us -> 28.2 us
where the time goes in v6:
time: 719 us; the launch traced here: 713 us
  Pallas kernels  391 us (54%)
  matrix products  106 us (15%)
  waiting for transfers between devices  81.5 us (11%)
  local copies, waits for them, and re-layouts  63.4 us (9%)
  other arithmetic  51 us (7%)
  starting transfers between devices  14.5 us (2%)
    pallas_call x1, Pallas kernels, scatter(): pl.pallas_call(lambda *refs: scatter_kernel(widths, slots, *refs), out_sh...  167 us
    pallas_call x1, Pallas kernels, gather(): pl.pallas_call(lambda *refs: gather_kernel(widths, *refs), out_shape=[jax...  166 us
    dot_general x25, matrix products, dot_low(): jnp.einsum(pattern, left_side, right_side, preferred_element_type=jnp.flo...  106 us
    all_to_all x1, waiting for transfers between devices, on_device(): lax.all_to_all(plan.order_rows(low_slots), AXES, split_axis=0, concat_axi...  46.2 us
    all_to_all x1, waiting for transfers between devices, on_device(): lax.all_to_all(slot_rows, AXES, split_axis=1, concat_axis=0, tiled=True)  35.3 us
    pallas_call x2, Pallas kernels, attend_back(): pl.pallas_call(attend_back_kernel, grid=(images, pairs), out_shape=jax.Sh...  31.8 us
    unnamed x204, local copies, waits for them, and re-layouts  28.2 us
    pallas_call x2, Pallas kernels, attend(): pl.pallas_call(attend_kernel, grid=(images, pairs), out_shape=jax.ShapeDt...  26.3 us
  transfers between devices with their start and end apart: 2, of which 2 were waited for; matrix products, arithmetic and copies ran while one was open for 7% of the time, Pallas kernels for 0%

profile of v6, /device:TPU:3, one launch (start us, length us, event | category | flops | bytes accessed | tf_op | source)
XLA Modules:
  0.0 712.5 jit_solution(4246593321054712687)
XLA Ops:
  4.7 3.6 copy.102
  8.3 6.5 all-to-all-start
  40.0 46.2 %all-to-all-done = bf16[768,15,128]{2,1,0:T(8,128)(2,1)} async-done(((bf16[768,15,128]{2,1,0:T(8,128)(2,1)}), bf16[768,15,128]{2,1,0:T(8,128)(2,1)}, u32[]{:S(2)}, u32[]{:S(2)}) %all-to-all-start) | async-done | bytes 2949152 | tf_op jit(solution)/shard_map/all_to_all | solution.py:946
  86.2 4.3 copy.104
  95.6 166.2 %shard_map.224 = (bf16[2,2,2,4,24,768]{5,4,3,2,1,0:T(8,128)(2,1)S(1)}, bf16[2,2,2,4,24,2304]{5,4,3,2,1,0:T(8,128)(2,1)S(1)}, bf16[2,2,2,4,24,3072]{5,4,3,2,1,0:T...) custom-call(bf16[24,768]{1,0:T(8,128)(2,1)S(1)} %get-tuple-element.9, ...), custom_call_target="tpu_custom_call" | custom-call | bytes 58982400 | tf_op jit(solution)/shard_map/pallas_call | solution.py:792
  269.8 5.5 convolution_convert_fusion.1.queries.keys_all.values
  275.3 13.2 %shard_map.225 = bf16[2,256,768]{2,1,0:T(8,128)(2,1)} custom-call(bf16[2,256,2304]{2,1,0:T(8,128)(2,1)} %convolution_convert_fusion.1.queries.keys_all.values, bf16[2,256,2304]{2,1,0:T(8,128)(2,1)} %convolution_convert_fusion.1.queries.keys_all.values, bf16[2,256,2304]{2,1,0:T(8,128)(2,1)} %convolution_convert_fusion.1.queries.keys_all.values), custom_call_target="tpu_custom_call" | custom-call | flops 402653184 | bytes 3145728 | tf_op jit(solution)/shard_map/pallas_call | solution.py:265
  292.3 8.9 %multiply_convert_fusion.1 = (bf16[2,256,3072]{2,1,0:T(8,128)(2,1)S(1)}, f32[2,256,3072]{2,1,0:T(8,128)}) fusion(bf16[2,256,768]{2,1,0:T(8,128)(2,1)S(1)} %add_convert_fusion.4, bf16[768,3072,1]{1,0,2:T(8,128)(2,1)} %bitcast.268), kind=kOutput, calls=%fused_computation.33 | convolution fusion | flops 2430074880 | bytes 14942208 | tf_op jit(solution)/shard_map/gpd,df->gpf/dot_general | solution.py:55
  301.3 3.8 fusion.97
  311.3 13.0 %shard_map.226 = bf16[2,256,768]{2,1,0:T(8,128)(2,1)} custom-call(bf16[2,256,2304]{2,1,0:T(8,128)(2,1)} %convolution_convert_fusion.queries.keys_all.values, bf16[2,256,2304]{2,1,0:T(8,128)(2,1)} %convolution_convert_fusion.queries.keys_all.values, bf16[2,256,2304]{2,1,0:T(8,128)(2,1)} %convolution_convert_fusion.queries.keys_all.values), custom_call_target="tpu_custom_call" | custom-call | flops 402653184 | bytes 3145728 | tf_op jit(solution)/shard_map/pallas_call | solution.py:265
  324.4 3.6 fusion.96
  328.7 9.2 %multiply_convert_fusion = (bf16[2,256,3072]{2,1,0:T(8,128)(2,1)S(1)}, f32[2,256,3072]{2,1,0:T(8,128)}) fusion(bf16[2,256,768]{2,1,0:T(8,128)(2,1)S(1)} %add_convert_fusion.2, bf16[768,3072,1]{1,0,2:T(8,128)(2,1)} %bitcast.278), kind=kOutput, calls=%fused_computation.32 | convolution fusion | flops 2430074880 | bytes 14942208 | tf_op jit(solution)/shard_map/gpd,df->gpf/dot_general | solution.py:55
  338.0 3.8 fusion.95
  352.2 7.6 %fusion.13 = bf16[2,256,3072]{2,1,0:T(8,128)(2,1)S(1)} fusion(f32[2,256,3072]{2,1,0:T(8,128)S(1)} %copy-done.75, bf16[2,256,768]{2,1,0:T(8,128)(2,1)S(1)} %get-tuple-element.94, bf16[768,3072,1]{1,0,2:T(8,128)(2,1)} %bitcast.282), kind=kOutput, calls=%fused_computation.31 | convolution fusion | flops 2447376384 | bytes 14942208 | tf_op jit(solution)/shard_map/gpd,df->gpf/dot_general | solution.py:55
  368.6 15.9 %shard_map.227 = bf16[2,256,2304]{2,1,0:T(8,128)(2,1)} custom-call(bf16[2,256,2304]{2,1,0:T(8,128)(2,1)} %convolution_convert_fusion.queries.keys_all.values, bf16[2,256,2304]{2,1,0:T(8,128)(2,1)} %convolution_convert_fusion.queries.keys_all.values, bf16[2,256,2304]{2,1,0:T(8,128)(2,1)} %convolution_convert_fusion.queries.keys_all.values, ...), custom_call_target="tpu_custom_call" | custom-call | flops 1006632960 | bytes 5505024 | tf_op jit(solution)/shard_map/pallas_call | solution.py:282
  384.6 5.0 multiply_reduce_fusion.11
  393.2 6.1 fusion.6
  407.1 15.9 %shard_map.228 = bf16[2,256,2304]{2,1,0:T(8,128)(2,1)} custom-call(bf16[2,256,2304]{2,1,0:T(8,128)(2,1)} %convolution_convert_fusion.1.queries.keys_all.values, bf16[2,256,2304]{2,1,0:T(8,128)(2,1)} %convolution_convert_fusion.1.queries.keys_all.values, bf16[2,256,2304]{2,1,0:T(8,128)(2,1)} %convolution_convert_fusion.1.queries.keys_all.values, ...), custom_call_target="tpu_custom_call" | custom-call | flops 1006632960 | bytes 5505024 | tf_op jit(solution)/shard_map/pallas_call | solution.py:282
  423.0 4.9 multiply_reduce_fusion
  432.5 167.2 %shard_map.229 = (bf16[24,768]{1,0:T(8,128)(2,1)}, bf16[24,2304]{1,0:T(8,128)(2,1)}, bf16[24,3072]{1,0:T(8,128)(2,1)}, bf16[24,3072]{1,0:T(8,128)(2,1)}, bf16[24...) custom-call(bf16[512,768]{1,0:T(8,128)(2,1)} %bitcast.238, ...), custom_call_target="tpu_custom_call" | custom-call | bytes 56623104 | tf_op jit(solution)/shard_map/pallas_call | solution.py:838
  612.5 8.0 %all-to-all-start.1 = ((bf16[24,480,128]{2,0,1:T(8,128)(2,1)}), bf16[24,480,128]{2,0,1:T(8,128)(2,1)}, u32[]{:S(2)}, u32[]{:S(2)}) async-start(bf16[24,480,128]{2,0,1:T(8,128)(2,1)} %select_bitcast_fusion), calls=%async_computation.1 | async-start | bytes 5898240 | tf_op jit(solution)/shard_map/all_to_all | solution.py:1083
  642.5 9.9 %multiply_subtract_fusion = (f32[1288,768]{1,0:T(8,128)}, f32[1288,768]{1,0:T(8,128)}, f32[1288,768]{1,0:T(8,128)}) fusion(f32[1288,768]{1,0:T(8,128)S(1)} %copy-done.21, f32[1288]{0:T(1024)S(1)} %select_multiply_fusion, f32[16,768]{1,0:T(8,128)S(1)} %bitcast.260, f32[1000,768]{1,0:T(8,128)S(1)} %copy-done.25, f32[256,768]{1,0:T(8,128)S(1)} %copy-done.45, ...), kind=kLoop, calls=%fused_computation.45 | loop fusion | flops 16816128 | bytes 27702304 | tf_op jit(solution)/shard_map/sub | solution.py:105
  652.5 35.3 %all-to-all-done.1 = bf16[24,480,128]{2,0,1:T(8,128)(2,1)} async-done(((bf16[24,480,128]{2,0,1:T(8,128)(2,1)}), bf16[24,480,128]{2,0,1:T(8,128)(2,1)}, u32[]{:S(2)}, u32[]{:S(2)}) %all-to-all-start.1) | async-done | bytes 2949152 | tf_op jit(solution)/shard_map/all_to_all | solution.py:1083
  693.7 17.6 %fusion.17 = (f32[768,15,128]{2,0,1:T(8,128)}, f32[768,15,128]{2,0,1:T(8,128)}, f32[768,15,128]{2,0,1:T(8,128)}) fusion(f32[768,15,128]{2,0,1:T(8,128)} %param.24, pred[15]{0:T(512)(128)(4,1)S(1)} %copy-done.65, f32[768,15,128]{2,0,1:T(8,128)S(1)} %bitcast.231, f32[768,15,128]{2,0,1:T(8,128)} %param.23, f32[15]{0:T(128)S(1)} %copy-done.73, ...), kind=kOutput, calls=%fused_computation.40 | convolution fusion | flops 216883200 | bytes 47530104 | tf_op jit(solution)/shard_map/gd,gsc->dsc/dot_general | solution.py:55
  (367 shorter events, 126.5 us)
Async XLA Ops:
  8.2 8.7 %copy-start.64 = (s32[2]{0:T(128)S(1)}, s32[2]{0:T(128)}, u32[]{:S(2)}) copy-start(s32[2]{0:T(128)} %param.20) | copy-start | bytes 28
  8.2 9.3 %copy-start.63 = (s32[84]{0:T(128)S(1)}, s32[84]{0:T(128)}, u32[]{:S(2)}) copy-start(s32[84]{0:T(128)} %constant.325) | copy-start | bytes 1012
  8.3 10.5 %copy-start.62 = (s32[150]{0:T(256)S(1)}, s32[150]{0:T(256)}, u32[]{:S(2)}) copy-start(s32[150]{0:T(256)} %constant.326) | copy-start | bytes 1804
  8.3 78.0 %all-to-all-start = ((bf16[768,15,128]{2,1,0:T(8,128)(2,1)}), bf16[768,15,128]{2,1,0:T(8,128)(2,1)}, u32[]{:S(2)}, u32[]{:S(2)}) async-start(bf16[768,15,128]{2,1,0:T(8,128)(2,1)} %copy.102), calls=%async_computation | async-start | bytes 6291456 | tf_op jit(solution)/shard_map/all_to_all | solution.py:946
  17.0 13.8 %copy-start.60 = (s32[15]{0:T(128)}, s32[15]{0:T(128)S(1)}, u32[]{:S(2)}) copy-start(s32[15]{0:T(128)S(1)} %get-tuple-element.71) | copy-start | bytes 184
  39.8 55.8 %copy-start = (bf16[15,768,128]{2,1,0:T(8,128)(2,1)}, bf16[15,768,128]{2,1,0:T(8,128)(2,1)S(1)}, u32[]{:S(2)}) copy-start(bf16[15,768,128]{2,1,0:T(8,128)(2,1)S(1)} %convert_bitcast_fusion.refs_10_.refs_18_) | copy-start | bytes 8847364
  275.3 13.2 %copy-start.2 = (bf16[2,2,2,4,24,768]{5,4,3,2,1,0:T(8,128)(2,1)S(1)}, bf16[2,2,2,4,24,768]{5,4,3,2,1,0:T(8,128)(2,1)}, u32[]{:S(2)}) copy-start(bf16[2,2,2,4,24,768]{5,4,3,2,1,0:T(8,128)(2,1)} %copy-done.1) | copy-start | bytes 3538948
  291.6 9.6 %copy-start.15 = (f32[2,256,768]{2,1,0:T(8,128)}, f32[2,256,768]{2,1,0:T(8,128)S(1)}, u32[]{:S(2)}) copy-start(f32[2,256,768]{2,1,0:T(8,128)S(1)} %get-tuple-element.89) | copy-start | bytes 4718596
  292.0 9.3 %slice-start.5 = ((s8[4718592]{0:T(1024)(128)(4,1)}), s8[4194304]{0:T(1024)(128)(4,1)S(1)}, s32[]{:S(2)}) async-start(s8[4718592]{0:T(1024)(128)(4,1)} %bitcast.272), calls=%async_computation.7 | async-start | bytes 8388608
  292.3 8.9 %copy-start.34 = (bf16[2,256,768]{2,1,0:T(8,128)(2,1)}, bf16[2,256,768]{2,1,0:T(8,128)(2,1)S(1)}, u32[]{:S(2)}) copy-start(bf16[2,256,768]{2,1,0:T(8,128)(2,1)S(1)} %add_convert_fusion.4) | copy-start | bytes 2359300
  292.3 8.9 %slice-start.6 = ((s8[4718592]{0:T(1024)(128)(4,1)}), s8[524288]{0:T(1024)(128)(4,1)S(1)}, s32[]{:S(2)}) async-start(s8[4718592]{0:T(1024)(128)(4,1)} %bitcast.272), calls=%async_computation.8 | async-start | bytes 1048576
  311.3 13.0 %copy-start.4 = (bf16[2,2,2,4,24,768]{5,4,3,2,1,0:T(8,128)(2,1)S(1)}, bf16[2,2,2,4,24,768]{5,4,3,2,1,0:T(8,128)(2,1)}, u32[]{:S(2)}) copy-start(bf16[2,2,2,4,24,768]{5,4,3,2,1,0:T(8,128)(2,1)} %copy-done.3) | copy-start | bytes 3538948
  328.0 10.0 %copy-start.19 = (f32[2,256,768]{2,1,0:T(8,128)}, f32[2,256,768]{2,1,0:T(8,128)S(1)}, u32[]{:S(2)}) copy-start(f32[2,256,768]{2,1,0:T(8,128)S(1)} %get-tuple-element.85) | copy-start | bytes 4718596
  328.3 9.6 %slice-start.11 = ((s8[4718592]{0:T(1024)(128)(4,1)}), s8[4194304]{0:T(1024)(128)(4,1)S(1)}, s32[]{:S(2)}) async-start(s8[4718592]{0:T(1024)(128)(4,1)} %bitcast.283), calls=%async_computation.13 | async-start | bytes 8388608
  328.7 9.3 %copy-start.36 = (bf16[2,256,768]{2,1,0:T(8,128)(2,1)}, bf16[2,256,768]{2,1,0:T(8,128)(2,1)S(1)}, u32[]{:S(2)}) copy-start(bf16[2,256,768]{2,1,0:T(8,128)(2,1)S(1)} %add_convert_fusion.2) | copy-start | bytes 2359300
  328.7 9.3 %slice-start.12 = ((s8[4718592]{0:T(1024)(128)(4,1)}), s8[524288]{0:T(1024)(128)(4,1)S(1)}, s32[]{:S(2)}) async-start(s8[4718592]{0:T(1024)(128)(4,1)} %bitcast.283), calls=%async_computation.14 | async-start | bytes 1048576
  350.3 9.5 %slice-start.9 = ((s8[4718592]{0:T(1024)(128)(4,1)}), s8[4194304]{0:T(1024)(128)(4,1)S(1)}, s32[]{:S(2)}) async-start(s8[4718592]{0:T(1024)(128)(4,1)} %bitcast.279), calls=%async_computation.11 | async-start | bytes 8388608
  368.6 15.9 %copy-start.18 = (f32[2,256,768]{2,1,0:T(8,128)S(1)}, f32[2,256,768]{2,1,0:T(8,128)}, u32[]{:S(2)}) copy-start(f32[2,256,768]{2,1,0:T(8,128)} %copy-done.17) | copy-start | bytes 4718596
  384.6 8.6 %slice-start.7 = ((s8[4718592]{0:T(1024)(128)(4,1)}), s8[4194304]{0:T(1024)(128)(4,1)S(1)}, s32[]{:S(2)}) async-start(s8[4718592]{0:T(1024)(128)(4,1)} %bitcast.275), calls=%async_computation.9 | async-start | bytes 8388608
  384.6 8.6 %slice-start.13 = ((s8[6291456]{0:T(1024)(128)(4,1)}), s8[4194304]{0:T(1024)(128)(4,1)S(1)}, s32[]{:S(2)}) async-start(s8[6291456]{0:T(1024)(128)(4,1)} %bitcast.289), calls=%async_computation.15 | async-start | bytes 8388608
  407.1 15.9 %copy-start.14 = (f32[2,256,768]{2,1,0:T(8,128)S(1)}, f32[2,256,768]{2,1,0:T(8,128)}, u32[]{:S(2)}) copy-start(f32[2,256,768]{2,1,0:T(8,128)} %copy-done.12) | copy-start | bytes 4718596
  612.5 8.5 %copy-start.70 = (s32[15]{0:T(128)S(1)}, s32[15]{0:T(128)}, u32[]{:S(2)}) copy-start(s32[15]{0:T(128)} %copy-done.69) | copy-start | bytes 184
  612.5 10.8 %copy-start.44 = (f32[32,2,16,128]{3,2,1,0:T(8,128)S(1)}, f32[32,2,16,128]{3,2,1,0:T(8,128)}, u32[]{:S(2)}) copy-start(f32[32,2,16,128]{3,2,1,0:T(8,128)} %get-tuple-element.40) | copy-start | bytes 1572868
  612.5 75.3 %all-to-all-start.1 = ((bf16[24,480,128]{2,0,1:T(8,128)(2,1)}), bf16[24,480,128]{2,0,1:T(8,128)(2,1)}, u32[]{:S(2)}, u32[]{:S(2)}) async-start(bf16[24,480,128]{2,0,1:T(8,128)(2,1)} %select_bitcast_fusion), calls=%async_computation.1 | async-start | bytes 5898240 | tf_op jit(solution)/shard_map/all_to_all | solution.py:1083
  (69 other events, 221.9 us)

commit v7 on v6

--- a/solution.py
+++ b/solution.py
@@ -133,7 +133,7 @@
             branch_a,
             middle,
             mlp_in,
-            pre_act,
+            pre_act.astype(jnp.bfloat16),
             post_act,
             branch_b,
         ),
@@ -160,7 +160,7 @@
     grad_branch_b = (gate_b[:, None, :] * grad_out).astype(jnp.bfloat16)
     grad_down = (grad_branch_b, post_act)
     grad_post = dot_low("gpd,df->gpf", grad_branch_b, w_down)
-    grad_pre = local_back(gelu_tanh, pre_act, grad_post).astype(jnp.bfloat16)
+    grad_pre = local_back(gelu_tanh, pre_act.astype(jnp.float32), grad_post).astype(jnp.bfloat16)
     grad_up = (mlp_in, grad_pre)
     grad_mlp_in = dot_low("gpf,df->gpd", grad_pre, w_up)
     normed_b = norm_rows(middle)
@@ -205,6 +205,14 @@
     return dot_rows(left_side, right_side).astype(jnp.bfloat16)
 
 
+def unit_groups():
+    groups, place = [], 0
+    for number in (3 * D, D, FF, FF) * LAYERS + (D,):
+        groups.append((place, number // BLOCK))
+        place += number // BLOCK
+    return groups
+
+
 def head_mask(number):
     lane = lax.broadcasted_iota(jnp.int32, (PATCHES, 2 * HEAD_DIM), 1)
     return (lane >= number * HEAD_DIM) & (lane < (number + 1) * HEAD_DIM)
@@ -217,37 +225,42 @@
 
 
 def attend_kernel(queries, keys_all, values, out):
-    result = jnp.zeros((PATCHES, 2 * HEAD_DIM), jnp.float32)
+    row = lax.broadcasted_iota(jnp.int32, (2 * HEAD_DIM, PATCHES), 0)
+    scaled = queries[0] * HEAD_DIM ** (-0.5)
+    result = jnp.zeros((2 * HEAD_DIM, PATCHES), jnp.float32)
     for number in (0, 1):
-        mask = head_mask(number)
-        one = jnp.where(mask, queries[0], jnp.zeros((), jnp.bfloat16))
-        scores = dot_lanes(one, keys_all[0]) * HEAD_DIM ** (-0.5)
-        powers = jnp.exp(scores - jnp.max(scores, -1, keepdims=True))
-        prob = (powers * (1.0 / jnp.sum(powers, -1, keepdims=True))).astype(jnp.bfloat16)
-        mixed = jnp.dot(prob, values[0], preferred_element_type=jnp.float32)
-        result = jnp.where(mask, mixed, result)
-    out[0] = result.astype(jnp.bfloat16)
+        one = jnp.where(head_mask(number), scaled, jnp.zeros((), jnp.bfloat16))
+        scores = dot_lanes(keys_all[0], one)
+        powers = jnp.exp(scores - jnp.max(scores, 0, keepdims=True))
+        prob = (powers * (1.0 / jnp.sum(powers, 0, keepdims=True))).astype(jnp.bfloat16)
+        result = jnp.where(row // HEAD_DIM == number, dot_rows(values[0], prob), result)
+    out[0] = result.T.astype(jnp.bfloat16)
 
 
 def attend_back_kernel(queries, keys_all, values, grad, out):
     pair = pl.program_id(1)
-    results = [jnp.zeros((PATCHES, 2 * HEAD_DIM), jnp.float32)] * 3
+    row = lax.broadcasted_iota(jnp.int32, (2 * HEAD_DIM, PATCHES), 0)
+    scaled = queries[0] * HEAD_DIM ** (-0.5)
+    grad_queries = jnp.zeros((2 * HEAD_DIM, PATCHES), jnp.float32)
+    grad_keys = jnp.zeros((PATCHES, 2 * HEAD_DIM), jnp.float32)
+    grad_values = grad_keys
     none = jnp.zeros((), jnp.bfloat16)
     for number in (0, 1):
         mask = head_mask(number)
-        scores = dot_lanes(keys_all[0], jnp.where(mask, queries[0], none)) * HEAD_DIM ** (-0.5)
+        scores = dot_lanes(keys_all[0], jnp.where(mask, scaled, none))
         powers = jnp.exp(scores - jnp.max(scores, 0, keepdims=True))
         prob = powers * (1.0 / jnp.sum(powers, 0, keepdims=True))
         grad_prob = dot_lanes(values[0], jnp.where(mask, grad[0], none))
         inner = jnp.sum(prob * grad_prob, 0, keepdims=True)
-        grad_scores = (HEAD_DIM ** (-0.5) * prob * (grad_prob - inner)).astype(jnp.bfloat16)
-        parts = (
-            dot_rows(grad_scores, keys_all[0]),
-            jnp.dot(grad_scores, queries[0], preferred_element_type=jnp.float32),
-            jnp.dot(prob.astype(jnp.bfloat16), grad[0], preferred_element_type=jnp.float32),
-        )
-        results = [jnp.where(mask, part, result) for part, result in zip(parts, results)]
-    for third, result in enumerate(results):
+        grad_scores = (prob * (grad_prob - inner)).astype(jnp.bfloat16)
+        part = dot_rows(keys_all[0], grad_scores)
+        grad_queries = jnp.where(row // HEAD_DIM == number, part, grad_queries)
+        part = jnp.dot(grad_scores, scaled, preferred_element_type=jnp.float32)
+        grad_keys = jnp.where(mask, part, grad_keys)
+        part = jnp.dot(prob.astype(jnp.bfloat16), grad[0], preferred_element_type=jnp.float32)
+        grad_values = jnp.where(mask, part, grad_values)
+    grad_queries = grad_queries.T * HEAD_DIM ** (-0.5)
+    for third, result in enumerate((grad_queries, grad_keys, grad_values)):
         first = pl.multiple_of(third * D + pair * 2 * HEAD_DIM, 2 * HEAD_DIM)
         out[0, :, pl.ds(first, 2 * HEAD_DIM)] = result.astype(jnp.bfloat16)
 
@@ -329,14 +342,14 @@
     return to_x, to_y, to_core, to_z
 
 
-def gather_kernel(widths, *refs):
+def gather_kernel(widths, bases, *refs):
     count = len(widths)
-    pieces = refs[:count]
-    info, low_slots = refs[count : count + 2]
-    outs = refs[count + 2 : 2 * count + 2]
-    every_info, cond_out, modul_out = refs[2 * count + 2 : 2 * count + 5]
+    units, info, low_slots = refs[:3]
+    outs = refs[3 : count + 3]
+    every_info, cond_out, modul_out = refs[count + 3 : count + 6]
+    pieces = refs[count + 6 : 2 * count + 6]
     time_two, parts, own_sem, send_sem, recv_sem, time_sem, modul_sem, info_sem = refs[
-        2 * count + 5 :
+        2 * count + 6 :
     ]
     devices, images = modul_out.shape[:2]
     slots = low_slots.shape[0]
@@ -454,12 +467,16 @@
 
     for i in range(images):
         every_info[me * images + i] = info[i]
-    for k in range(count):
+    def send_piece(k):
+        for n in range(widths[k] // BLOCK):
+            pieces[k][:, n * BLOCK : (n + 1) * BLOCK] = units[bases[k] + n]
+        start(line_copies(k, False))
         own_copy(k).start()
-    start(line_copies(0, False))
+
+    send_piece(0)
     for t in range(count + 2):
         if t + 1 < count:
-            start(line_copies(t + 1, False))
+            send_piece(t + 1)
         if t < count:
             own_copy(t).wait()
             arrived(line_copies(t, True))
@@ -487,13 +504,12 @@
                 copy.wait_send()
 
 
-def scatter_kernel(widths, slots, *refs):
+def scatter_kernel(widths, bases, slots, *refs):
     count = len(widths)
     lefts, rights = refs[:count], refs[count : 2 * count]
     modul, pick, low_slots, edge, factor = refs[2 * count : 2 * count + 5]
-    outs = refs[2 * count + 5 : 3 * count + 5]
-    chosen, shared = refs[3 * count + 5 : 3 * count + 7]
-    scratch = refs[3 * count + 7 :]
+    units, chosen, shared = refs[2 * count + 5 : 2 * count + 8]
+    scratch = refs[2 * count + 8 :]
     own, first_in, second_in, line_in = (scratch[i * count : (i + 1) * count] for i in range(4))
     (
         left_in, left_turned, right_in, away, every_modul, parts, landed,
@@ -746,7 +762,9 @@
             total = own[k][y, x, z].astype(jnp.float32)
             for step in (1, 2, 3):
                 total = total + line_in[k][step - 1].astype(jnp.float32)
-            outs[k][...] = total.astype(jnp.bfloat16)
+            for n in range(widths[k] // BLOCK):
+                part = total[:, n * BLOCK : (n + 1) * BLOCK]
+                units[bases[k] + n] = part.astype(jnp.bfloat16)
         if t < 3:
             arrived(modul_copies(t, True))
             start(modul_copies(t + 1, False))
@@ -769,41 +787,42 @@
 
 
 class RingPlan:
-    def order_rows(self, values):
-        shape = values.shape
-        split = values.reshape((2, 2, 2, 4, D // 32) + shape[1:])
-        return jnp.moveaxis(split, 0, 2).reshape(shape)
-
-    def restore_rows(self, values):
-        shape = values.shape
-        split = values.reshape((2, 2, 2, 4, D // 32) + shape[1:])
-        return jnp.moveaxis(split, 2, 0).reshape(shape)
-
-    def gather(self, pieces, time_piece, info, low_slots):
-        turn = sorted(range(len(pieces)), key=lambda n: (n % 4 == 1, n))
-        pieces = [time_piece] + [pieces[n] for n in turn]
-        widths = tuple(piece.shape[1] for piece in pieces)
-        count, rows = len(pieces), D // 32
+    def split_rows(self, values):
+        slots = values.shape[0]
+        split = values.reshape(slots, 2, 2, 2, 4, D // 32, BLOCK)
+        return split.transpose(2, 3, 1, 4, 0, 5, 6).reshape(32, slots, D // 32, BLOCK)
+
+    def join_rows(self, values):
+        slots = values.shape[1]
+        split = values.reshape(2, 2, 2, 4, slots, D // 32, BLOCK)
+        return split.transpose(4, 2, 0, 1, 3, 5, 6).reshape(slots, D, BLOCK)
+
+    def gather(self, units, info, low_slots):
+        names = unit_groups()
+        turn = [len(names) - 1] + sorted(range(len(names) - 1), key=lambda n: (n % 4 == 1, n))
+        bases = tuple(names[n][0] for n in turn)
+        widths = tuple(names[n][1] * BLOCK for n in turn)
+        count, rows = len(turn), D // 32
         all_images = 32 * info.shape[0]
-        slots = low_slots.shape[1]
+        slots = low_slots.shape[0]
         room = -(-slots // 8) * 8
         size = sum(4 * D * width for width in widths)
         whole_shape = [(2, 2, 2, 4, rows, width) for width in widths]
         *whole, every_info, cond, modul = pl.pallas_call(
-            lambda *refs: gather_kernel(widths, *refs),
+            lambda *refs: gather_kernel(widths, bases, *refs),
             out_shape=[
-                jax.ShapeDtypeStruct(shape, piece.dtype)
-                for shape, piece in zip(whole_shape, pieces)
+                jax.ShapeDtypeStruct(shape, jnp.bfloat16) for shape in whole_shape
             ]
             + [
                 jax.ShapeDtypeStruct((all_images,) + info.shape[1:], jnp.float32),
                 jax.ShapeDtypeStruct((all_images, D), jnp.float32),
                 jax.ShapeDtypeStruct((32, all_images // 32, room, BLOCK), jnp.float32),
             ],
-            in_specs=[pl.BlockSpec(memory_space=pltpu.VMEM)] * (count + 2),
+            in_specs=[pl.BlockSpec(memory_space=pltpu.VMEM)] * 3,
             out_specs=[pl.BlockSpec(memory_space=pl.ANY)] * count
             + [pl.BlockSpec(memory_space=pltpu.VMEM)] * 3,
-            scratch_shapes=[
+            scratch_shapes=[pltpu.VMEM((rows, width), jnp.bfloat16) for width in widths]
+            + [
                 pltpu.VMEM(whole_shape[0], jnp.bfloat16),
                 pltpu.VMEM((all_images, room, BLOCK), jnp.float32),
                 pltpu.SemaphoreType.DMA((count,)),
@@ -817,34 +836,39 @@
                 collective_id=0, has_side_effects=True, vmem_limit_bytes=GATHER_VMEM
             ),
             cost_estimate=pl.CostEstimate(flops=0, bytes_accessed=size, transcendentals=0),
-        )(*pieces, info, jnp.swapaxes(low_slots, 0, 1))
+        )(units, info, low_slots)
         whole = [part.reshape(D, -1) for part in whole]
         modul = jnp.swapaxes(modul[:, :, :slots], 0, 1).reshape(-1, 32 * slots, BLOCK)
-        ordered = [whole[1 + turn.index(n)] for n in range(len(turn))]
-        return ordered, whole[0], every_info, cond, modul
-
-    def scatter(self, grads, modul, pick, low_slots, edge, factor):
+        ordered = [whole[turn.index(n)] for n in range(count)]
+        return ordered[:-1], ordered[-1], every_info, cond, modul
+
+    def scatter(self, layer_grads, modul, pick, low_slots, edge, factor):
+        turn = [(l, n) for l in range(LAYERS) for n in (0, 2, 3)]
+        turn = [(LAYERS - 1, 1)] + turn + [(l, 1) for l in range(LAYERS - 1)]
+        grads = [layer_grads[l][n] for l, n in turn]
+        names = unit_groups()
+        bases = tuple(names[4 * l + n][0] for l, n in turn)
         lefts = [left.reshape(-1, D) for left, _ in grads]
         rights = [right.reshape(left.shape[0], -1) for (_, right), left in zip(grads, lefts)]
         widths = tuple(right.shape[1] for right in rights)
         count, rows, tokens = len(grads), D // 32, lefts[0].shape[0]
         widest = max(widths)
-        images, slots = modul.shape[0], low_slots.shape[1]
+        images, slots = modul.shape[0], low_slots.shape[0]
         size = sum(4 * D * width for width in widths)
         scratch = [pltpu.VMEM((2, 2, 4, rows, width), jnp.bfloat16) for width in widths]
         scratch += [pltpu.VMEM((2, 2, 4, rows, width // 2), jnp.bfloat16) for width in widths]
         scratch += [pltpu.VMEM((2, 4, rows, width // 2), jnp.bfloat16) for width in widths]
         scratch += [pltpu.VMEM((3, rows, width), jnp.bfloat16) for width in widths]
-        *scattered, chosen, shared = pl.pallas_call(
-            lambda *refs: scatter_kernel(widths, slots, *refs),
-            out_shape=[jax.ShapeDtypeStruct((rows, width), jnp.bfloat16) for width in widths]
-            + [
+        units, chosen, shared = pl.pallas_call(
+            lambda *refs: scatter_kernel(widths, bases, slots, *refs),
+            out_shape=[
+                jax.ShapeDtypeStruct((sum(widths) // BLOCK, rows, BLOCK), jnp.bfloat16),
                 jax.ShapeDtypeStruct((32 * images, pick.shape[0], BLOCK), jnp.float32),
                 jax.ShapeDtypeStruct((32,) + factor.shape, jnp.float32),
             ],
             in_specs=[pl.BlockSpec(memory_space=pl.ANY)] * (2 * count)
             + [pl.BlockSpec(memory_space=pltpu.VMEM)] * 5,
-            out_specs=[pl.BlockSpec(memory_space=pltpu.VMEM)] * (count + 2),
+            out_specs=[pl.BlockSpec(memory_space=pltpu.VMEM)] * 3,
             scratch_shapes=scratch
             + [
                 pltpu.VMEM((2, tokens, D), jnp.bfloat16),
@@ -865,42 +889,46 @@
                 collective_id=1, has_side_effects=True, vmem_limit_bytes=SCATTER_VMEM
             ),
             cost_estimate=pl.CostEstimate(flops=0, bytes_accessed=size, transcendentals=0),
-        )(*lefts, *rights, modul, pick, jnp.swapaxes(low_slots, 0, 1), edge, factor)
-        return scattered, chosen[:, :slots].astype(jnp.bfloat16), shared
+        )(*lefts, *rights, modul, pick, low_slots, edge, factor)
+        return units, chosen[:, :slots].astype(jnp.bfloat16), shared
 
 
 class PlainPlan:
-    def order_rows(self, values):
-        return values
-
-    def restore_rows(self, values):
-        return values
-
-    def gather(self, pieces, time_piece, info, low_slots):
-        whole = [lax.all_gather(piece, AXES, axis=0, tiled=True) for piece in pieces]
-        time_two = lax.all_gather(time_piece, AXES, axis=0, tiled=True)
+    def split_rows(self, values):
+        slots, devices = values.shape[0], lax.axis_size("rep") * lax.axis_size("shard")
+        return jnp.swapaxes(values.reshape(slots, devices, -1, BLOCK), 0, 1)
+
+    def join_rows(self, values):
+        return jnp.swapaxes(values, 0, 1).reshape(-1, D, BLOCK)
+
+    def gather(self, units, info, low_slots):
+        whole = []
+        for first, number in unit_groups():
+            piece = jnp.swapaxes(units[first : first + number], 0, 1)
+            piece = piece.reshape(-1, number * BLOCK)
+            whole.append(lax.all_gather(piece, AXES, axis=0, tiled=True))
         every_info = lax.all_gather(info, AXES, axis=0, tiled=True)
         blocks = D // BLOCK
         time_act = every_info[:, :blocks].reshape(-1, D).astype(jnp.bfloat16)
-        cond = jnp.dot(time_act, time_two, preferred_element_type=jnp.float32)
+        cond = jnp.dot(time_act, whole[-1], preferred_element_type=jnp.float32)
         cond = cond + every_info[:, 8 : 8 + blocks].reshape(-1, D)
-        modul = dot_low("gd,dsc->gsc", jax.nn.silu(cond).astype(jnp.bfloat16), low_slots)
+        modul = dot_low("gd,sdc->gsc", jax.nn.silu(cond).astype(jnp.bfloat16), low_slots)
         modul = lax.all_to_all(modul, AXES, split_axis=0, concat_axis=1, tiled=True)
-        return whole, time_two, every_info, cond, modul
-
-    def scatter(self, grads, modul, pick, low_slots, edge, factor):
-        scattered = [
-            lax.psum_scatter(row_product(*pair), AXES, scatter_dimension=0, tiled=True)
-            for pair in grads
-        ]
-        slots = low_slots.shape[1]
+        return whole[:-1], whole[-1], every_info, cond, modul
+
+    def scatter(self, layer_grads, modul, pick, low_slots, edge, factor):
+        units = []
+        for pair in (pair for grads in layer_grads for pair in grads):
+            own = lax.psum_scatter(row_product(*pair), AXES, scatter_dimension=0, tiled=True)
+            units.append(jnp.swapaxes(own.reshape(own.shape[0], -1, BLOCK), 0, 1))
+        slots = low_slots.shape[0]
         every = lax.all_gather(modul, AXES, axis=0, tiled=True)
         chosen = dot_low("su,guc->gsc", pick, every)[:, :slots].astype(jnp.bfloat16)
-        part = dot_low("gsc,dsc->gd", chosen, low_slots).reshape(-1, D // BLOCK, BLOCK)
+        part = dot_low("gsc,sdc->gd", chosen, low_slots).reshape(-1, D // BLOCK, BLOCK)
         parts = edge.at[:, : D // BLOCK].set(part)
         own = lax.psum_scatter(parts, AXES, scatter_dimension=0, tiled=True) * factor
         shared = lax.all_gather(own, AXES, axis=0, tiled=False)
-        return scattered, chosen, shared
+        return jnp.concatenate(units, 0), chosen, shared
 
 
 def unit_lists():
@@ -940,19 +968,15 @@
         jnp.full((slot_total,), -1, jnp.int32).at[owner].set(jnp.arange(UNITS, dtype=jnp.int32))
     )
     my_unit = lax.dynamic_slice_in_dim(unit_of_slot, me * slot_dev, slot_dev)
-    low_slots = master.astype(jnp.bfloat16)
+    low_slots = jnp.swapaxes(master.astype(jnp.bfloat16), 0, 1)
 
     plan = RingPlan() if (lax.axis_size("rep"), lax.axis_size("shard")) == (8, 4) else PlainPlan()
     spread = lax.all_to_all(
-        plan.order_rows(low_slots), AXES, split_axis=0, concat_axis=1, tiled=True
-    )
+        plan.split_rows(low_slots), AXES, split_axis=0, concat_axis=0, tiled=True
+    ).reshape(slot_total, rows, BLOCK)
     moved = np.concatenate([dense_units, time_units])
-    unit_rows = jnp.take(spread, owner[moved], axis=1).reshape(rows, -1)
-    pieces = []
-    for l in range(LAYERS):
-        base = l * DENSE_COLS
-        cuts = (0, 3 * D, 4 * D, 4 * D + FF, DENSE_COLS)
-        pieces += [unit_rows[:, base + cuts[i] : base + cuts[i + 1]] for i in range(4)]
+    units = jnp.take(spread, owner[moved], axis=0, mode="clip")
+
     x_start = latents.astype(jnp.float32).reshape(-1, PATCHES, CHANNELS)
     noise_f = noise.astype(jnp.float32).reshape(-1, PATCHES, CHANNELS)
     times = (t_index.astype(jnp.float32) + 0.5) / TSTEPS
@@ -984,7 +1008,7 @@
         1,
     )
     whole, time_two, every_info, cond_all, slot_modul = plan.gather(
-        pieces, unit_rows[:, LAYERS * DENSE_COLS :], info, low_slots
+        units, info, low_slots
     )
     all_images = cond_all.shape[0]
     every_time = (every_info[:, blocks, 0] + 0.5) / TSTEPS
@@ -996,7 +1020,7 @@
     weights_all = [tuple(whole[4 * l : 4 * l + 4]) for l in range(LAYERS)]
     cond = lax.dynamic_slice_in_dim(cond_all, me * images, images)
     cond_act = jax.nn.silu(cond_all).astype(jnp.bfloat16)
-    modul_all = jnp.take(slot_modul, owner[image_units], axis=1).reshape(images, -1)
+    modul_all = jnp.take(slot_modul, owner[image_units], axis=1, mode="clip").reshape(images, -1)
 
     saved_all = []
     for l in range(LAYERS):
@@ -1041,13 +1065,9 @@
     edge = jnp.pad(edge.reshape(all_images, blocks, BLOCK), ((0, 0), (8, 8 - blocks), (0, 0)))
     factor = local_back(jax.nn.silu, cond, jnp.ones_like(cond)).reshape(images, blocks, BLOCK)
     factor = jnp.pad(factor, ((0, 0), (0, 16 - blocks), (0, 0)), constant_values=1.0)
-    order = [(l, i) for l in range(LAYERS) for i in (0, 2, 3)]
-    order = [(LAYERS - 1, 1)] + order + [(l, 1) for l in range(LAYERS - 1)]
-    scattered, slot_grad_out, shared = plan.scatter(
-        [layer_grads[l][i] for l, i in order],
-        modul_grad, pick, low_slots, edge, factor,
-    )
-    grad_rows = dict(zip(order, scattered))
+    unit_grads, slot_grad_out, shared = plan.scatter(
+        layer_grads, modul_grad, pick, low_slots, edge, factor
+    )
     shared = shared.reshape(all_images, 16, BLOCK)
     grad_cond = shared[:, :blocks].reshape(all_images, D)
     edge = shared[:, 8 : 8 + blocks].reshape(all_images, D)
@@ -1070,18 +1090,17 @@
     dense_place = np.full((UNITS + 1,), 0, np.int32)
     dense_place[dense_units] = np.arange(len(dense_units))
     slot_place = jnp.asarray(dense_place)[unit_of_slot]
-    all_rows = jnp.concatenate(
-        [
-            grad_rows[l, i].reshape(rows, -1, BLOCK)
-            for l in range(LAYERS)
-            for i in range(4)
-        ],
-        1,
-    )
-    slot_rows = jnp.take(all_rows, slot_place, axis=1)
-    dense_grad = plan.restore_rows(
-        lax.all_to_all(slot_rows, AXES, split_axis=1, concat_axis=0, tiled=True)
-    ).astype(jnp.float32)
+    slot_rows = jnp.take(unit_grads, slot_place, axis=0, mode="clip")
+    dense_grad = plan.join_rows(
+        lax.all_to_all(
+            slot_rows.reshape(count, slot_dev, rows, BLOCK),
+            AXES,
+            split_axis=0,
+            concat_axis=0,
+            tiled=True,
+        )
+    )
+    dense_grad = jnp.swapaxes(dense_grad, 0, 1).astype(jnp.float32)
 
     owned_grad = jnp.where(
         is_image[None, :, None],

time: 719 us -> 695 us (0.967)
  local copies, waits for them, and re-layouts: 63.4 us -> 52.8 us
    unnamed x204 -> x181, local copies, waits for them, and re-layouts: 28.2 us -> 21 us
  transfers between devices with their start and end apart: 2 -> 2, of which waited for: 2 -> 2; matrix products, arithmetic and copies ran while one was open for 7% -> 8% of each run, Pallas kernels for 0% -> 0%
where the time goes in v7:
time: 695 us; the launch traced here: 690 us
  Pallas kernels  388 us (56%)
  matrix products  108 us (16%)
  waiting for transfers between devices  75.8 us (11%)
  local copies, waits for them, and re-layouts  52.8 us (8%)
  other arithmetic  45.9 us (7%)
  starting transfers between devices  14.5 us (2%)
    pallas_call x1, Pallas kernels, scatter(): pl.pallas_call(lambda *refs: scatter_kernel(widths, bases, slots, *refs),...  167 us
    pallas_call x1, Pallas kernels, gather(): pl.pallas_call(lambda *refs: gather_kernel(widths, bases, *refs), out_sha...  166 us
    dot_general x25, matrix products, dot_low(): jnp.einsum(pattern, left_side, right_side, preferred_element_type=jnp.flo...  106 us
    all_to_all x1, waiting for transfers between devices, on_device(): lax.all_to_all(plan.split_rows(low_slots), AXES, split_axis=0, concat_axi...  41.2 us
    all_to_all x1, waiting for transfers between devices, on_device(): lax.all_to_all(slot_rows.reshape(count, slot_dev, rows, BLOCK), AXES, spl...  34.6 us
    pallas_call x2, Pallas kernels, attend_back(): pl.pallas_call(attend_back_kernel, grid=(images, pairs), out_shape=jax.Sh...  30.4 us
    pallas_call x2, Pallas kernels, attend(): pl.pallas_call(attend_kernel, grid=(images, pairs), out_shape=jax.ShapeDt...  25.2 us
    unnamed x181, local copies, waits for them, and re-layouts  21 us
  transfers between devices with their start and end apart: 2, of which 2 were waited for; matrix products, arithmetic and copies ran while one was open for 8% of the time, Pallas kernels for 0%

profile of v7, /device:TPU:3, one launch (start us, length us, event | category | flops | bytes accessed | tf_op | source)
XLA Modules:
  0.0 689.8 jit_solution(4585246275866368391)
XLA Ops:
  6.0 6.5 all-to-all-start
  38.6 41.2 %all-to-all-done = bf16[32,15,24,128]{3,2,1,0:T(8,128)(2,1)} async-done(((bf16[32,15,24,128]{3,2,1,0:T(8,128)(2,1)}), bf16[32,15,24,128]{3,2,1,0:T(8,128)(2,1)}, u32[]{:S(2)}, u32[]{:S(2)}) %all-to-all-start) | async-done | bytes 2949152 | tf_op jit(solution)/shard_map/all_to_all | solution.py:974
  84.5 165.7 %shard_map.224 = (bf16[2,2,2,4,24,768]{5,4,3,2,1,0:T(8,128)(2,1)S(1)}, bf16[2,2,2,4,24,2304]{5,4,3,2,1,0:T(8,128)(2,1)S(1)}, bf16[2,2,2,4,24,3072]{5,4,3,2,1,0:T...) custom-call(bf16[150,24,128]{2,1,0:T(8,128)(2,1)S(1)} %copy-done.1, ...), custom_call_target="tpu_custom_call" | custom-call | bytes 58982400 | tf_op jit(solution)/shard_map/pallas_call | solution.py:811
  258.1 5.4 convolution_convert_fusion.1.queries.keys_all.values
  263.5 12.6 %shard_map.225 = bf16[2,256,768]{2,1,0:T(8,128)(2,1)} custom-call(bf16[2,256,2304]{2,1,0:T(8,128)(2,1)} %convolution_convert_fusion.1.queries.keys_all.values, bf16[2,256,2304]{2,1,0:T(8,128)(2,1)} %convolution_convert_fusion.1.queries.keys_all.values, bf16[2,256,2304]{2,1,0:T(8,128)(2,1)} %convolution_convert_fusion.1.queries.keys_all.values), custom_call_target="tpu_custom_call" | custom-call | flops 402653184 | bytes 3145728 | tf_op jit(solution)/shard_map/pallas_call | solution.py:278
  279.9 8.8 %fusion.15 = (bf16[2,256,3072]{2,1,0:T(8,128)(2,1)S(1)}, bf16[2,256,3072]{2,1,0:T(8,128)(2,1)}) fusion(bf16[2,256,768]{2,1,0:T(8,128)(2,1)S(1)} %add_convert_fusion.4, bf16[768,3072,1]{1,0,2:T(8,128)(2,1)} %bitcast.197), kind=kOutput, calls=%fused_computation.39 | convolution fusion | flops 2431647744 | bytes 11796480 | tf_op jit(solution)/shard_map/gpd,df->gpf/dot_general | solution.py:55
  288.8 3.8 fusion.116
  298.9 12.6 %shard_map.226 = bf16[2,256,768]{2,1,0:T(8,128)(2,1)} custom-call(bf16[2,256,2304]{2,1,0:T(8,128)(2,1)} %convolution_convert_fusion.queries.keys_all.values, bf16[2,256,2304]{2,1,0:T(8,128)(2,1)} %convolution_convert_fusion.queries.keys_all.values, bf16[2,256,2304]{2,1,0:T(8,128)(2,1)} %convolution_convert_fusion.queries.keys_all.values), custom_call_target="tpu_custom_call" | custom-call | flops 402653184 | bytes 3145728 | tf_op jit(solution)/shard_map/pallas_call | solution.py:278
  311.6 3.6 fusion.115
  315.9 8.9 %fusion.23 = (bf16[2,256,3072]{2,1,0:T(8,128)(2,1)S(1)}, bf16[2,256,3072]{2,1,0:T(8,128)(2,1)}) fusion(bf16[2,256,768]{2,1,0:T(8,128)(2,1)S(1)} %add_convert_fusion.2, bf16[768,3072,1]{1,0,2:T(8,128)(2,1)} %bitcast.207), kind=kOutput, calls=%fused_computation.47 | convolution fusion | flops 2431647744 | bytes 11796480 | tf_op jit(solution)/shard_map/gpd,df->gpf/dot_general | solution.py:55
  324.8 3.8 fusion.114
  337.9 8.7 %fusion.7 = bf16[2,256,3072]{2,1,0:T(8,128)(2,1)S(1)} fusion(bf16[2,256,768]{2,1,0:T(8,128)(2,1)S(1)} %get-tuple-element.80, bf16[768,3072,1]{1,0,2:T(8,128)(2,1)} %bitcast.211, bf16[2,256,3072]{2,1,0:T(8,128)(2,1)S(1)} %copy-done.71), kind=kOutput, calls=%fused_computation.31 | convolution fusion | flops 2448949248 | bytes 11796480 | tf_op jit(solution)/shard_map/gpd,df->gpf/dot_general | solution.py:55
  355.5 15.2 %shard_map.227 = bf16[2,256,2304]{2,1,0:T(8,128)(2,1)} custom-call(bf16[2,256,2304]{2,1,0:T(8,128)(2,1)} %convolution_convert_fusion.queries.keys_all.values, bf16[2,256,2304]{2,1,0:T(8,128)(2,1)} %convolution_convert_fusion.queries.keys_all.values, bf16[2,256,2304]{2,1,0:T(8,128)(2,1)} %convolution_convert_fusion.queries.keys_all.values, ...), custom_call_target="tpu_custom_call" | custom-call | flops 1006632960 | bytes 5505024 | tf_op jit(solution)/shard_map/pallas_call | solution.py:295
  370.6 5.0 multiply_reduce_fusion.11
  379.8 6.3 fusion.4
  393.8 15.2 %shard_map.228 = bf16[2,256,2304]{2,1,0:T(8,128)(2,1)} custom-call(bf16[2,256,2304]{2,1,0:T(8,128)(2,1)} %convolution_convert_fusion.1.queries.keys_all.values, bf16[2,256,2304]{2,1,0:T(8,128)(2,1)} %convolution_convert_fusion.1.queries.keys_all.values, bf16[2,256,2304]{2,1,0:T(8,128)(2,1)} %convolution_convert_fusion.1.queries.keys_all.values, ...), custom_call_target="tpu_custom_call" | custom-call | flops 1006632960 | bytes 5505024 | tf_op jit(solution)/shard_map/pallas_call | solution.py:295
  409.0 4.9 multiply_reduce_fusion
  418.6 167.1 %shard_map.229 = (bf16[144,24,128]{2,1,0:T(8,128)(2,1)}, f32[64,16,128]{2,1,0:T(8,128)}, f32[32,2,16,128]{3,2,1,0:T(8,128)}) custom-call(bf16[512,768]{1,0:T(8,128)(2,1)} %bitcast.171, bf16[512,768]{1,0:T(8,128)(2,1)} %bitcast.176, bf16[512,768]{1,0:T(8,128)(2,1)} %bitcast.177, bf16[512,768]{1,0:T(8,128)(2,1)} %bitcast.181, bf16[512,768]{1,0:T(8,128)(2,1)} %bitcast.178, ...), custom_call_target="tpu_custom_call" | custom-call | bytes 56623104 | tf_op jit(solution)/shard_map/pallas_call | solution.py:862
  585.7 4.2 gather_fusion.8
  589.9 8.0 %all-to-all-start.1 = ((bf16[32,15,24,128]{3,2,1,0:T(8,128)(2,1)}), bf16[32,15,24,128]{3,2,1,0:T(8,128)(2,1)}, u32[]{:S(2)}, u32[]{:S(2)}) async-start(bf16[32,15,24,128]{3,2,1,0:T(8,128)(2,1)} %bitcast.61), calls=%async_computation.1 | async-start | bytes 5898240 | tf_op jit(solution)/shard_map/all_to_all | solution.py:1095
  620.5 10.0 %multiply_subtract_fusion = (f32[1288,768]{1,0:T(8,128)}, f32[1288,768]{1,0:T(8,128)}, f32[1288,768]{1,0:T(8,128)}) fusion(f32[1288,768]{1,0:T(8,128)S(1)} %copy-done.22, f32[1288]{0:T(1024)S(1)} %select_multiply_fusion, f32[16,768]{1,0:T(8,128)S(1)} %bitcast.193, f32[1000,768]{1,0:T(8,128)S(1)} %copy-done.26, f32[256,768]{1,0:T(8,128)S(1)} %copy-done.45, ...), kind=kLoop, calls=%fused_computation.69 | loop fusion | flops 16816128 | bytes 27702304 | tf_op jit(solution)/shard_map/sub | solution.py:105
  630.6 34.6 %all-to-all-done.1 = bf16[32,15,24,128]{3,2,1,0:T(8,128)(2,1)} async-done(((bf16[32,15,24,128]{3,2,1,0:T(8,128)(2,1)}), bf16[32,15,24,128]{3,2,1,0:T(8,128)(2,1)}, u32[]{:S(2)}, u32[]{:S(2)}) %all-to-all-start.1) | async-done | bytes 2949152 | tf_op jit(solution)/shard_map/all_to_all | solution.py:1095
  665.2 5.3 copy.52
  670.6 17.6 %fusion.37 = (f32[768,15,128]{2,0,1:T(8,128)}, f32[768,15,128]{2,0,1:T(8,128)}, f32[768,15,128]{2,0,1:T(8,128)}) fusion(f32[768,15,128]{2,0,1:T(8,128)} %param.24, pred[15]{0:T(512)(128)(4,1)S(1)} %copy-done.61, f32[768,15,128]{2,0,1:T(8,128)} %param.22, f32[768,15,128]{2,0,1:T(8,128)} %param.23, f32[15]{0:T(128)S(1)} %copy-done.68, ...), kind=kOutput, calls=%fused_computation.64 | convolution fusion | flops 216883200 | bytes 47530104 | tf_op jit(solution)/shard_map/gd,gsc->dsc/dot_general | solution.py:55
  (325 shorter events, 110.1 us)
Async XLA Ops:
  6.0 73.8 %all-to-all-start = ((bf16[32,15,24,128]{3,2,1,0:T(8,128)(2,1)}), bf16[32,15,24,128]{3,2,1,0:T(8,128)(2,1)}, u32[]{:S(2)}, u32[]{:S(2)}) async-start(bf16[32,15,24,128]{3,2,1,0:T(8,128)(2,1)} %bitcast.4), calls=%async_computation | async-start | bytes 5898240 | tf_op jit(solution)/shard_map/all_to_all | solution.py:974
  18.5 8.8 %copy-start.51 = (bf16[2,4096]{1,0:T(2,128)(2,1)S(1)}, bf16[2,4096]{1,0:T(2,128)(2,1)}, u32[]{:S(2)}) copy-start(bf16[2,4096]{1,0:T(2,128)(2,1)} %param.17) | copy-start | bytes 49156
  38.6 211.7 %copy-start = (bf16[15,768,128]{2,1,0:T(8,128)(2,1)}, bf16[15,768,128]{2,1,0:T(8,128)(2,1)S(1)}, u32[]{:S(2)}) copy-start(bf16[15,768,128]{2,1,0:T(8,128)(2,1)S(1)} %convert_bitcast_fusion.refs_2_.refs_18_) | copy-start | bytes 8847364
  263.5 12.6 %copy-start.3 = (bf16[2,2,2,4,24,768]{5,4,3,2,1,0:T(8,128)(2,1)S(1)}, bf16[2,2,2,4,24,768]{5,4,3,2,1,0:T(8,128)(2,1)}, u32[]{:S(2)}) copy-start(bf16[2,2,2,4,24,768]{5,4,3,2,1,0:T(8,128)(2,1)} %copy-done.2) | copy-start | bytes 3538948
  279.2 9.5 %copy-start.16 = (f32[2,256,768]{2,1,0:T(8,128)}, f32[2,256,768]{2,1,0:T(8,128)S(1)}, u32[]{:S(2)}) copy-start(f32[2,256,768]{2,1,0:T(8,128)S(1)} %get-tuple-element.75) | copy-start | bytes 4718596
  279.6 9.2 %slice-start.3 = ((s8[4718592]{0:T(1024)(128)(4,1)}), s8[4194304]{0:T(1024)(128)(4,1)S(1)}, s32[]{:S(2)}) async-start(s8[4718592]{0:T(1024)(128)(4,1)} %bitcast.201), calls=%async_computation.5 | async-start | bytes 8388608
  279.9 8.8 %copy-start.35 = (bf16[2,256,768]{2,1,0:T(8,128)(2,1)}, bf16[2,256,768]{2,1,0:T(8,128)(2,1)S(1)}, u32[]{:S(2)}) copy-start(bf16[2,256,768]{2,1,0:T(8,128)(2,1)S(1)} %add_convert_fusion.4) | copy-start | bytes 2359300
  279.9 8.9 %slice-start.4 = ((s8[4718592]{0:T(1024)(128)(4,1)}), s8[524288]{0:T(1024)(128)(4,1)S(1)}, s32[]{:S(2)}) async-start(s8[4718592]{0:T(1024)(128)(4,1)} %bitcast.201), calls=%async_computation.6 | async-start | bytes 1048576
  298.9 12.6 %copy-start.5 = (bf16[2,2,2,4,24,768]{5,4,3,2,1,0:T(8,128)(2,1)S(1)}, bf16[2,2,2,4,24,768]{5,4,3,2,1,0:T(8,128)(2,1)}, u32[]{:S(2)}) copy-start(bf16[2,2,2,4,24,768]{5,4,3,2,1,0:T(8,128)(2,1)} %copy-done.4) | copy-start | bytes 3538948
  315.2 9.6 %copy-start.20 = (f32[2,256,768]{2,1,0:T(8,128)}, f32[2,256,768]{2,1,0:T(8,128)S(1)}, u32[]{:S(2)}) copy-start(f32[2,256,768]{2,1,0:T(8,128)S(1)} %get-tuple-element.71) | copy-start | bytes 4718596
  315.5 9.3 %slice-start.9 = ((s8[4718592]{0:T(1024)(128)(4,1)}), s8[4194304]{0:T(1024)(128)(4,1)S(1)}, s32[]{:S(2)}) async-start(s8[4718592]{0:T(1024)(128)(4,1)} %bitcast.212), calls=%async_computation.11 | async-start | bytes 8388608
  315.8 8.9 %copy-start.37 = (bf16[2,256,768]{2,1,0:T(8,128)(2,1)}, bf16[2,256,768]{2,1,0:T(8,128)(2,1)S(1)}, u32[]{:S(2)}) copy-start(bf16[2,256,768]{2,1,0:T(8,128)(2,1)S(1)} %add_convert_fusion.2) | copy-start | bytes 2359300
  315.9 9.0 %slice-start.10 = ((s8[4718592]{0:T(1024)(128)(4,1)}), s8[524288]{0:T(1024)(128)(4,1)S(1)}, s32[]{:S(2)}) async-start(s8[4718592]{0:T(1024)(128)(4,1)} %bitcast.212), calls=%async_computation.12 | async-start | bytes 1048576
  336.6 9.9 %slice-start.7 = ((s8[4718592]{0:T(1024)(128)(4,1)}), s8[4194304]{0:T(1024)(128)(4,1)S(1)}, s32[]{:S(2)}) async-start(s8[4718592]{0:T(1024)(128)(4,1)} %bitcast.208), calls=%async_computation.9 | async-start | bytes 8388608
  337.9 8.7 %copy-start.21 = (f32[2,256,768]{2,1,0:T(8,128)S(1)}, f32[2,256,768]{2,1,0:T(8,128)}, u32[]{:S(2)}) copy-start(f32[2,256,768]{2,1,0:T(8,128)} %copy-done.20) | copy-start | bytes 4718596
  337.9 8.7 %slice-start.8 = ((s8[4718592]{0:T(1024)(128)(4,1)}), s8[524288]{0:T(1024)(128)(4,1)S(1)}, s32[]{:S(2)}) async-start(s8[4718592]{0:T(1024)(128)(4,1)} %bitcast.208), calls=%async_computation.10 | async-start | bytes 1048576
  355.5 15.2 %copy-start.19 = (f32[2,256,768]{2,1,0:T(8,128)S(1)}, f32[2,256,768]{2,1,0:T(8,128)}, u32[]{:S(2)}) copy-start(f32[2,256,768]{2,1,0:T(8,128)} %copy-done.18) | copy-start | bytes 4718596
  370.6 8.6 %slice-start.5 = ((s8[4718592]{0:T(1024)(128)(4,1)}), s8[4194304]{0:T(1024)(128)(4,1)S(1)}, s32[]{:S(2)}) async-start(s8[4718592]{0:T(1024)(128)(4,1)} %bitcast.204), calls=%async_computation.7 | async-start | bytes 8388608
  377.5 8.5 %slice-start.1 = ((s8[4718592]{0:T(1024)(128)(4,1)}), s8[4194304]{0:T(1024)(128)(4,1)S(1)}, s32[]{:S(2)}) async-start(s8[4718592]{0:T(1024)(128)(4,1)} %bitcast.198), calls=%async_computation.3 | async-start | bytes 8388608
  393.8 15.2 %copy-start.15 = (f32[2,256,768]{2,1,0:T(8,128)S(1)}, f32[2,256,768]{2,1,0:T(8,128)}, u32[]{:S(2)}) copy-start(f32[2,256,768]{2,1,0:T(8,128)} %copy-done.13) | copy-start | bytes 4718596
  418.6 167.1 %copy-start.53 = (s32[1024]{0:T(1024)S(1)}, s32[1024]{0:T(1024)}, u32[]{:S(2)}) copy-start(s32[1024]{0:T(1024)} %get-tuple-element.138) | copy-start | bytes 12292
  589.9 9.1 %copy-start.65 = (s32[15]{0:T(128)S(1)}, s32[15]{0:T(128)}, u32[]{:S(2)}) copy-start(s32[15]{0:T(128)} %copy-done.64) | copy-start | bytes 184
  589.9 11.4 %copy-start.44 = (f32[32,2,16,128]{3,2,1,0:T(8,128)S(1)}, f32[32,2,16,128]{3,2,1,0:T(8,128)}, u32[]{:S(2)}) copy-start(f32[32,2,16,128]{3,2,1,0:T(8,128)} %get-tuple-element.33) | copy-start | bytes 1572868
  589.9 75.3 %all-to-all-start.1 = ((bf16[32,15,24,128]{3,2,1,0:T(8,128)(2,1)}), bf16[32,15,24,128]{3,2,1,0:T(8,128)(2,1)}, u32[]{:S(2)}, u32[]{:S(2)}) async-start(bf16[32,15,24,128]{3,2,1,0:T(8,128)(2,1)} %bitcast.61), calls=%async_computation.1 | async-start | bytes 5898240 | tf_op jit(solution)/shard_map/all_to_all | solution.py:1095
  (61 other events, 189.1 us)

commit v8 on v7

--- a/solution.py
+++ b/solution.py
@@ -213,8 +213,12 @@
     return groups
 
 
+PAIR = 2 * HEAD_DIM
+SPAN = 3
+
+
 def head_mask(number):
-    lane = lax.broadcasted_iota(jnp.int32, (PATCHES, 2 * HEAD_DIM), 1)
+    lane = lax.broadcasted_iota(jnp.int32, (PATCHES, PAIR), 1)
     return (lane >= number * HEAD_DIM) & (lane < (number + 1) * HEAD_DIM)
 
 
@@ -225,59 +229,65 @@
 
 
 def attend_kernel(queries, keys_all, values, out):
-    row = lax.broadcasted_iota(jnp.int32, (2 * HEAD_DIM, PATCHES), 0)
-    scaled = queries[0] * HEAD_DIM ** (-0.5)
-    result = jnp.zeros((2 * HEAD_DIM, PATCHES), jnp.float32)
-    for number in (0, 1):
-        one = jnp.where(head_mask(number), scaled, jnp.zeros((), jnp.bfloat16))
-        scores = dot_lanes(keys_all[0], one)
-        powers = jnp.exp(scores - jnp.max(scores, 0, keepdims=True))
-        prob = (powers * (1.0 / jnp.sum(powers, 0, keepdims=True))).astype(jnp.bfloat16)
-        result = jnp.where(row // HEAD_DIM == number, dot_rows(values[0], prob), result)
-    out[0] = result.T.astype(jnp.bfloat16)
-
-
-def attend_back_kernel(queries, keys_all, values, grad, out):
-    pair = pl.program_id(1)
-    row = lax.broadcasted_iota(jnp.int32, (2 * HEAD_DIM, PATCHES), 0)
-    scaled = queries[0] * HEAD_DIM ** (-0.5)
-    grad_queries = jnp.zeros((2 * HEAD_DIM, PATCHES), jnp.float32)
-    grad_keys = jnp.zeros((PATCHES, 2 * HEAD_DIM), jnp.float32)
-    grad_values = grad_keys
+    row = lax.broadcasted_iota(jnp.int32, (PAIR, PATCHES), 0)
+    for pair in range(SPAN):
+        lanes = slice(pair * PAIR, (pair + 1) * PAIR)
+        scaled = queries[0, :, lanes] * HEAD_DIM ** (-0.5)
+        keys, vals = keys_all[0, :, lanes], values[0, :, lanes]
+        result = jnp.zeros((PAIR, PATCHES), jnp.float32)
+        for number in (0, 1):
+            one = jnp.where(head_mask(number), scaled, jnp.zeros((), jnp.bfloat16))
+            scores = dot_lanes(keys, one)
+            powers = jnp.exp(scores - jnp.max(scores, 0, keepdims=True))
+            prob = (powers * (1.0 / jnp.sum(powers, 0, keepdims=True))).astype(jnp.bfloat16)
+            result = jnp.where(row // HEAD_DIM == number, dot_rows(vals, prob), result)
+        out[0, :, lanes] = result.T.astype(jnp.bfloat16)
+
+
+def attend_back_kernel(queries, keys_all, values, grads, out):
+    step = pl.program_id(1)
+    row = lax.broadcasted_iota(jnp.int32, (PAIR, PATCHES), 0)
     none = jnp.zeros((), jnp.bfloat16)
-    for number in (0, 1):
-        mask = head_mask(number)
-        scores = dot_lanes(keys_all[0], jnp.where(mask, scaled, none))
-        powers = jnp.exp(scores - jnp.max(scores, 0, keepdims=True))
-        prob = powers * (1.0 / jnp.sum(powers, 0, keepdims=True))
-        grad_prob = dot_lanes(values[0], jnp.where(mask, grad[0], none))
-        inner = jnp.sum(prob * grad_prob, 0, keepdims=True)
-        grad_scores = (prob * (grad_prob - inner)).astype(jnp.bfloat16)
-        part = dot_rows(keys_all[0], grad_scores)
-        grad_queries = jnp.where(row // HEAD_DIM == number, part, grad_queries)
-        part = jnp.dot(grad_scores, scaled, preferred_element_type=jnp.float32)
-        grad_keys = jnp.where(mask, part, grad_keys)
-        part = jnp.dot(prob.astype(jnp.bfloat16), grad[0], preferred_element_type=jnp.float32)
-        grad_values = jnp.where(mask, part, grad_values)
-    grad_queries = grad_queries.T * HEAD_DIM ** (-0.5)
-    for third, result in enumerate((grad_queries, grad_keys, grad_values)):
-        first = pl.multiple_of(third * D + pair * 2 * HEAD_DIM, 2 * HEAD_DIM)
-        out[0, :, pl.ds(first, 2 * HEAD_DIM)] = result.astype(jnp.bfloat16)
+    for pair in range(SPAN):
+        lanes = slice(pair * PAIR, (pair + 1) * PAIR)
+        scaled = queries[0, :, lanes] * HEAD_DIM ** (-0.5)
+        keys, vals, grad = (ref[0, :, lanes] for ref in (keys_all, values, grads))
+        grad_queries = jnp.zeros((PAIR, PATCHES), jnp.float32)
+        grad_keys = jnp.zeros((PATCHES, PAIR), jnp.float32)
+        grad_values = grad_keys
+        for number in (0, 1):
+            mask = head_mask(number)
+            scores = dot_lanes(keys, jnp.where(mask, scaled, none))
+            powers = jnp.exp(scores - jnp.max(scores, 0, keepdims=True))
+            prob = powers * (1.0 / jnp.sum(powers, 0, keepdims=True))
+            grad_prob = dot_lanes(vals, jnp.where(mask, grad, none))
+            inner = jnp.sum(prob * grad_prob, 0, keepdims=True)
+            grad_scores = (prob * (grad_prob - inner)).astype(jnp.bfloat16)
+            part = dot_rows(keys, grad_scores)
+            grad_queries = jnp.where(row // HEAD_DIM == number, part, grad_queries)
+            part = jnp.dot(grad_scores, scaled, preferred_element_type=jnp.float32)
+            grad_keys = jnp.where(mask, part, grad_keys)
+            part = jnp.dot(prob.astype(jnp.bfloat16), grad, preferred_element_type=jnp.float32)
+            grad_values = jnp.where(mask, part, grad_values)
+        grad_queries = grad_queries.T * HEAD_DIM ** (-0.5)
+        for third, result in enumerate((grad_queries, grad_keys, grad_values)):
+            first = pl.multiple_of(third * D + (step * SPAN + pair) * PAIR, PAIR)
+            out[0, :, pl.ds(first, PAIR)] = result.astype(jnp.bfloat16)
 
 
 def pair_block(third):
-    pairs = HEADS // 2
+    steps = HEADS // 2 // SPAN
     return pl.BlockSpec(
-        (1, PATCHES, 2 * HEAD_DIM), lambda image, pair: (image, 0, third * pairs + pair)
+        (1, PATCHES, SPAN * PAIR), lambda image, step: (image, 0, third * steps + step)
     )
 
 
 def attend(qkv_all):
     images = qkv_all.shape[0]
-    pairs = HEADS // 2
+    steps = HEADS // 2 // SPAN
     return pl.pallas_call(
         attend_kernel,
-        grid=(images, pairs),
+        grid=(images, steps),
         out_shape=jax.ShapeDtypeStruct((images, PATCHES, D), jnp.bfloat16),
         in_specs=[pair_block(0), pair_block(1), pair_block(2)],
         out_specs=pair_block(0),
@@ -291,19 +301,59 @@
 
 def attend_back(qkv_all, grad_heads):
     images = qkv_all.shape[0]
-    pairs = HEADS // 2
+    steps = HEADS // 2 // SPAN
     return pl.pallas_call(
         attend_back_kernel,
-        grid=(images, pairs),
+        grid=(images, steps),
         out_shape=jax.ShapeDtypeStruct((images, PATCHES, 3 * D), jnp.bfloat16),
         in_specs=[pair_block(0), pair_block(1), pair_block(2), pair_block(0)],
-        out_specs=pl.BlockSpec((1, PATCHES, 3 * D), lambda image, pair: (image, 0, 0)),
+        out_specs=pl.BlockSpec((1, PATCHES, 3 * D), lambda image, step: (image, 0, 0)),
         cost_estimate=pl.CostEstimate(
             flops=10 * images * PATCHES * PATCHES * D,
             bytes_accessed=14 * images * PATCHES * D,
             transcendentals=images * HEADS * PATCHES * PATCHES,
         ),
     )(qkv_all, qkv_all, qkv_all, grad_heads)
+
+
+def adam_kernel(starts, flags, dense, left, right, master, first, second, *refs):
+    new_master, new_first, new_second, image_grad = refs
+    slot = pl.program_id(0)
+    rate, used, is_dense = flags[slot, 0], flags[slot, 1], flags[slot, 2]
+    image_grad[...] = jnp.dot(left[0], right[0], preferred_element_type=jnp.float32)
+    rows = dense.shape[2]
+    for n, start in enumerate(starts):
+        at = (0, slice(start, start + rows))
+        grad = jnp.where(is_dense > 0.0, dense[n, 0].astype(jnp.float32), image_grad[at[1]])
+        old = (master[at], first[at], second[at])
+        new = adam_update(*old, grad, rate)
+        for ref, value, kept in zip((new_master, new_first, new_second), new, old):
+            ref[at] = jnp.where(used > 0.0, value, kept)
+
+
+def adam_slots(dense, starts, flags, left, right, *state):
+    slots = state[0].shape[0]
+    block = pl.BlockSpec((1, D, BLOCK), lambda slot: (slot, 0, 0))
+    side = left.shape[2]
+    return pl.pallas_call(
+        lambda *refs: adam_kernel(starts, *refs),
+        grid=(slots,),
+        out_shape=[jax.ShapeDtypeStruct((slots, D, BLOCK), jnp.float32)] * 3,
+        in_specs=[
+            pl.BlockSpec(memory_space=pltpu.SMEM),
+            pl.BlockSpec(
+                (dense.shape[0], 1) + dense.shape[2:], lambda slot: (0, slot, 0, 0)
+            ),
+            pl.BlockSpec((1, D, side), lambda slot: (slot, 0, 0)),
+            pl.BlockSpec((1, side, BLOCK), lambda slot: (slot, 0, 0)),
+        ]
+        + [block] * 3,
+        out_specs=[block] * 3,
+        scratch_shapes=[pltpu.VMEM((D, BLOCK), jnp.float32)],
+        cost_estimate=pl.CostEstimate(
+            flops=40 * slots * D * BLOCK, bytes_accessed=26 * slots * D * BLOCK, transcendentals=0
+        ),
+    )(flags, dense, left, right, *state)
 
 
 def place_of():
@@ -793,9 +843,11 @@
         return split.transpose(2, 3, 1, 4, 0, 5, 6).reshape(32, slots, D // 32, BLOCK)
 
     def join_rows(self, values):
-        slots = values.shape[1]
-        split = values.reshape(2, 2, 2, 4, slots, D // 32, BLOCK)
-        return split.transpose(4, 2, 0, 1, 3, 5, 6).reshape(slots, D, BLOCK)
+        starts = []
+        for device in range(32):
+            y, x, c, z = device // 16, device // 8 % 2, device // 4 % 2, device % 4
+            starts.append(((((c * 2 + y) * 2 + x) * 4) + z) * (D // 32))
+        return values, starts
 
     def gather(self, units, info, low_slots):
         names = unit_groups()
@@ -899,7 +951,7 @@
         return jnp.swapaxes(values.reshape(slots, devices, -1, BLOCK), 0, 1)
 
     def join_rows(self, values):
-        return jnp.swapaxes(values, 0, 1).reshape(-1, D, BLOCK)
+        return jnp.swapaxes(values, 0, 1).reshape(1, -1, D, BLOCK), [0]
 
     def gather(self, units, info, low_slots):
         whole = []
@@ -1083,15 +1135,11 @@
     my_time = jnp.clip(my_unit - TAIL_FIRST, 0, TIME_UNITS - 1)
     is_time = (my_unit >= TAIL_FIRST) & (my_unit < TAIL_FIRST + TIME_UNITS)
     time_cols = jnp.take(grad_time_out.reshape(all_images, TIME_UNITS, BLOCK), my_time, axis=1)
-    is_image = my_place >= 0
-    image_grad = dot_low("gd,gsc->dsc", cond_act, slot_grad_out)
-    time_grad = dot_low("gd,gsc->dsc", time_act, time_cols)
-
     dense_place = np.full((UNITS + 1,), 0, np.int32)
     dense_place[dense_units] = np.arange(len(dense_units))
     slot_place = jnp.asarray(dense_place)[unit_of_slot]
     slot_rows = jnp.take(unit_grads, slot_place, axis=0, mode="clip")
-    dense_grad = plan.join_rows(
+    dense_grad, starts = plan.join_rows(
         lax.all_to_all(
             slot_rows.reshape(count, slot_dev, rows, BLOCK),
             AXES,
@@ -1100,21 +1148,20 @@
             tiled=True,
         )
     )
-    dense_grad = jnp.swapaxes(dense_grad, 0, 1).astype(jnp.float32)
-
-    owned_grad = jnp.where(
-        is_image[None, :, None],
-        image_grad,
-        jnp.where(is_time[None, :, None], time_grad, dense_grad),
-    )
-    used = (my_unit >= 0)[None, :, None]
-    rate = rate_factor * unit_scale(jnp.maximum(my_unit, 0))[None, :, None]
-    new_w, new_first, new_second = adam_update(
-        master, first_moment, second_moment, owned_grad, rate
-    )
-    new_master = jnp.where(used, new_w, master)
-    new_first = jnp.where(used, new_first, first_moment)
-    new_second = jnp.where(used, new_second, second_moment)
+    is_dense = (my_unit >= 0) & (my_place < 0) & ~is_time
+    right = jnp.where(is_time[None, :, None], time_cols, slot_grad_out)
+    left = jnp.where(is_time[:, None, None], time_act.T[None], cond_act.T[None])
+    flags = [rate_factor * unit_scale(jnp.maximum(my_unit, 0)), my_unit >= 0, is_dense]
+    flags = jnp.stack([flag.astype(jnp.float32) for flag in flags], 1)
+    new_slots = adam_slots(
+        dense_grad,
+        starts,
+        flags,
+        left,
+        jnp.swapaxes(right, 0, 1),
+        *[jnp.swapaxes(values, 0, 1) for values in (master, first_moment, second_moment)],
+    )
+    new_master, new_first, new_second = [jnp.swapaxes(values, 0, 1) for values in new_slots]
     small_rate = rate_factor * table_scale(jnp.arange(small.shape[0], dtype=jnp.int32))[:, None]
     new_small, new_small_first, new_small_second = adam_update(
         small, small_first, small_second, small_grad, small_rate

time: 695 us -> 678 us (0.976)
  matrix products: 108 us -> 79.2 us
  Pallas kernels: 388 us -> 403 us
    dot_general x25 -> x23, matrix products: 106 us -> 78 us  [dot_low(): jnp.einsum(pattern, left_side, right_side, preferred_element_type=jnp.flo...]
    pallas_call x4 -> x5, Pallas kernels: 55.6 us -> 70.1 us  [the longest x2 26.1 us: attend_back(): pl.pallas_call(attend_back_kernel, grid=(images, steps), out_shape=jax.Sh...]
    unnamed x181 -> x148, local copies, waits for them, and re-layouts: 21 us -> 20.5 us
  transfers between devices with their start and end apart: 2 -> 2, of which waited for: 2 -> 2; matrix products, arithmetic and copies ran while one was open for 8% -> 7% of each run, Pallas kernels for 0% -> 0%
where the time goes in v8:
time: 678 us; the launch traced here: 674 us
  Pallas kernels  403 us (59%)
  waiting for transfers between devices  80.4 us (12%)
  matrix products  79.2 us (12%)
  local copies, waits for them, and re-layouts  46.8 us (7%)
  other arithmetic  45.1 us (7%)
  starting transfers between devices  14.5 us (2%)
    pallas_call x1, Pallas kernels, scatter(): pl.pallas_call(lambda *refs: scatter_kernel(widths, bases, slots, *refs),...  167 us
    pallas_call x1, Pallas kernels, gather(): pl.pallas_call(lambda *refs: gather_kernel(widths, bases, *refs), out_sha...  166 us
    dot_general x23, matrix products, dot_low(): jnp.einsum(pattern, left_side, right_side, preferred_element_type=jnp.flo...  78 us
    all_to_all x1, waiting for transfers between devices, on_device(): lax.all_to_all(plan.split_rows(low_slots), AXES, split_axis=0, concat_axi...  41.2 us
    all_to_all x1, waiting for transfers between devices, on_device(): lax.all_to_all(slot_rows.reshape(count, slot_dev, rows, BLOCK), AXES, spl...  39.2 us
    pallas_call x2, Pallas kernels, attend_back(): pl.pallas_call(attend_back_kernel, grid=(images, steps), out_shape=jax.Sh...  26.1 us
    pallas_call x1, Pallas kernels, adam_slots(): pl.pallas_call(lambda *refs: adam_kernel(starts, *refs), grid=(slots,), o...  22.2 us
    pallas_call x2, Pallas kernels, attend(): pl.pallas_call(attend_kernel, grid=(images, steps), out_shape=jax.ShapeDt...  21.7 us
  transfers between devices with their start and end apart: 2, of which 2 were waited for; matrix products, arithmetic and copies ran while one was open for 7% of the time, Pallas kernels for 0%

profile of v8, /device:TPU:3, one launch (start us, length us, event | category | flops | bytes accessed | tf_op | source)
XLA Modules:
  0.0 673.5 jit_solution(2845167662904877712)
XLA Ops:
  6.0 6.5 all-to-all-start
  12.4 3.6 convert_element_type.157
  25.7 3.5 gather_fusion.6
  38.6 41.2 %all-to-all-done = bf16[32,15,24,128]{3,2,1,0:T(8,128)(2,1)} async-done(((bf16[32,15,24,128]{3,2,1,0:T(8,128)(2,1)}), bf16[32,15,24,128]{3,2,1,0:T(8,128)(2,1)}, u32[]{:S(2)}, u32[]{:S(2)}) %all-to-all-start) | async-done | bytes 2949152 | tf_op jit(solution)/shard_map/all_to_all | solution.py:1026
  79.8 3.6 gather_fusion.1
  84.5 165.7 %shard_map.224 = (bf16[2,2,2,4,24,768]{5,4,3,2,1,0:T(8,128)(2,1)S(1)}, bf16[2,2,2,4,24,2304]{5,4,3,2,1,0:T(8,128)(2,1)S(1)}, bf16[2,2,2,4,24,3072]{5,4,3,2,1,0:T...) custom-call(bf16[150,24,128]{2,1,0:T(8,128)(2,1)S(1)} %copy-done.1, ...), custom_call_target="tpu_custom_call" | custom-call | bytes 58982400 | tf_op jit(solution)/shard_map/pallas_call | solution.py:863
  258.2 5.4 convolution_convert_fusion.1.queries.keys_all.values
  263.6 10.8 %shard_map.225 = bf16[2,256,768]{2,1,0:T(8,128)(2,1)} custom-call(bf16[2,256,2304]{2,1,0:T(8,128)(2,1)} %convolution_convert_fusion.1.queries.keys_all.values, bf16[2,256,2304]{2,1,0:T(8,128)(2,1)} %convolution_convert_fusion.1.queries.keys_all.values, bf16[2,256,2304]{2,1,0:T(8,128)(2,1)} %convolution_convert_fusion.1.queries.keys_all.values), custom_call_target="tpu_custom_call" | custom-call | flops 402653184 | bytes 3145728 | tf_op jit(solution)/shard_map/pallas_call | solution.py:288
  278.2 8.8 %fusion.15 = (bf16[2,256,3072]{2,1,0:T(8,128)(2,1)S(1)}, bf16[2,256,3072]{2,1,0:T(8,128)(2,1)}) fusion(bf16[2,256,768]{2,1,0:T(8,128)(2,1)S(1)} %add_convert_fusion.4, bf16[768,3072,1]{1,0,2:T(8,128)(2,1)} %bitcast.210), kind=kOutput, calls=%fused_computation.36 | convolution fusion | flops 2431647744 | bytes 11796480 | tf_op jit(solution)/shard_map/gpd,df->gpf/dot_general | solution.py:55
  287.0 3.8 fusion.107
  297.2 10.9 %shard_map.226 = bf16[2,256,768]{2,1,0:T(8,128)(2,1)} custom-call(bf16[2,256,2304]{2,1,0:T(8,128)(2,1)} %convolution_convert_fusion.queries.keys_all.values, bf16[2,256,2304]{2,1,0:T(8,128)(2,1)} %convolution_convert_fusion.queries.keys_all.values, bf16[2,256,2304]{2,1,0:T(8,128)(2,1)} %convolution_convert_fusion.queries.keys_all.values), custom_call_target="tpu_custom_call" | custom-call | flops 402653184 | bytes 3145728 | tf_op jit(solution)/shard_map/pallas_call | solution.py:288
  311.2 7.5 %fusion.23 = (bf16[2,256,3072]{2,1,0:T(8,128)(2,1)S(1)}, bf16[2,256,3072]{2,1,0:T(8,128)(2,1)S(1)}) fusion(bf16[2,256,768]{2,1,0:T(8,128)(2,1)S(1)} %add_convert_fusion.2, bf16[768,3072,1]{1,0,2:T(8,128)(2,1)} %bitcast.220), kind=kOutput, calls=%fused_computation.44 | convolution fusion | flops 2431647744 | bytes 11796480 | tf_op jit(solution)/shard_map/gpd,df->gpf/dot_general | solution.py:55
  327.7 6.3 fusion.7
  342.3 13.0 %shard_map.227 = bf16[2,256,2304]{2,1,0:T(8,128)(2,1)} custom-call(bf16[2,256,2304]{2,1,0:T(8,128)(2,1)} %convolution_convert_fusion.queries.keys_all.values, bf16[2,256,2304]{2,1,0:T(8,128)(2,1)} %convolution_convert_fusion.queries.keys_all.values, bf16[2,256,2304]{2,1,0:T(8,128)(2,1)} %convolution_convert_fusion.queries.keys_all.values, ...), custom_call_target="tpu_custom_call" | custom-call | flops 1006632960 | bytes 5505024 | tf_op jit(solution)/shard_map/pallas_call | solution.py:305
  355.4 5.0 multiply_reduce_fusion.11
  364.5 6.3 fusion.4
  378.6 13.1 %shard_map.228 = bf16[2,256,2304]{2,1,0:T(8,128)(2,1)} custom-call(bf16[2,256,2304]{2,1,0:T(8,128)(2,1)} %convolution_convert_fusion.1.queries.keys_all.values, bf16[2,256,2304]{2,1,0:T(8,128)(2,1)} %convolution_convert_fusion.1.queries.keys_all.values, bf16[2,256,2304]{2,1,0:T(8,128)(2,1)} %convolution_convert_fusion.1.queries.keys_all.values, ...), custom_call_target="tpu_custom_call" | custom-call | flops 1006632960 | bytes 5505024 | tf_op jit(solution)/shard_map/pallas_call | solution.py:305
  391.7 4.9 multiply_reduce_fusion
  403.1 167.1 %shard_map.229 = (bf16[144,24,128]{2,1,0:T(8,128)(2,1)}, f32[64,16,128]{2,1,0:T(8,128)}, f32[32,2,16,128]{3,2,1,0:T(8,128)}) custom-call(bf16[512,768]{1,0:T(8,128)(2,1)} %bitcast.177, bf16[512,768]{1,0:T(8,128)(2,1)} %bitcast.184, bf16[512,768]{1,0:T(8,128)(2,1)} %bitcast.185, bf16[512,768]{1,0:T(8,128)(2,1)} %bitcast.189, bf16[512,768]{1,0:T(8,128)(2,1)} %bitcast.186, ...), custom_call_target="tpu_custom_call" | custom-call | bytes 56623104 | tf_op jit(solution)/shard_map/pallas_call | solution.py:914
  570.1 4.2 gather_fusion.7
  574.3 8.0 %all-to-all-start.1 = ((bf16[32,15,24,128]{3,2,1,0:T(8,128)(2,1)}), bf16[32,15,24,128]{3,2,1,0:T(8,128)(2,1)}, u32[]{:S(2)}, u32[]{:S(2)}) async-start(bf16[32,15,24,128]{3,2,1,0:T(8,128)(2,1)} %bitcast.62), calls=%async_computation.1 | async-start | bytes 5898240 | tf_op jit(solution)/shard_map/all_to_all | solution.py:1143
  599.9 10.6 %multiply_subtract_fusion = (f32[1288,768]{1,0:T(8,128)}, f32[1288,768]{1,0:T(8,128)}, f32[1288,768]{1,0:T(8,128)}) fusion(f32[1288,768]{1,0:T(8,128)} %param.25, f32[1288]{0:T(1024)S(1)} %select_multiply_fusion, f32[16,768]{1,0:T(8,128)S(1)} %bitcast.202, f32[1000,768]{1,0:T(8,128)S(1)} %copy-done.22, f32[256,768]{1,0:T(8,128)S(1)} %fusion.56, ...), kind=kLoop, calls=%fused_computation.61 | loop fusion | flops 16816128 | bytes 27702304 | tf_op jit(solution)/shard_map/sub | solution.py:105
  610.5 39.2 %all-to-all-done.1.refs_1_ = bf16[32,15,24,128]{3,2,1,0:T(8,128)(2,1)} async-done(((bf16[32,15,24,128]{3,2,1,0:T(8,128)(2,1)}), bf16[32,15,24,128]{3,2,1,0:T(8,128)(2,1)}, u32[]{:S(2)}, u32[]{:S(2)}) %all-to-all-start.1) | async-done | bytes 2949152 | tf_op jit(solution)/shard_map/all_to_all | solution.py:1143
  649.7 22.2 %shard_map.230 = (f32[15,768,128]{2,1,0:T(8,128)}, f32[15,768,128]{2,1,0:T(8,128)}, f32[15,768,128]{2,1,0:T(8,128)}) custom-call(f32[15,3]{1,0:T(8,128)} %copy.77.refs_0_, bf16[32,15,24,128]{3,2,1,0:T(8,128)(2,1)} %all-to-all-done.1.refs_1_, bf16[15,768,64]{2,1,0:T(8,128)(2,1)} %broadcast_select_fusion.refs_2_, bf16[15,64,128]{2,1,0:T(8,128)(2,1)} %fusion.43.refs_3_, ...), custom_call_target="tpu_custom_call" | custom-call | flops 58982400 | bytes 38338560 | tf_op jit(solution)/shard_map/pallas_call | solution.py:338
  (294 shorter events, 97.8 us)
Async XLA Ops:
  6.0 73.8 %all-to-all-start = ((bf16[32,15,24,128]{3,2,1,0:T(8,128)(2,1)}), bf16[32,15,24,128]{3,2,1,0:T(8,128)(2,1)}, u32[]{:S(2)}, u32[]{:S(2)}) async-start(bf16[32,15,24,128]{3,2,1,0:T(8,128)(2,1)} %bitcast.4), calls=%async_computation | async-start | bytes 5898240 | tf_op jit(solution)/shard_map/all_to_all | solution.py:1026
  16.9 8.1 %copy-start.12 = (s32[235]{0:T(256)S(1)}, s32[235]{0:T(256)}, u32[]{:S(2)}) copy-start(s32[235]{0:T(256)} %constant.259.clone) | copy-start | bytes 2824
  17.1 8.6 %copy-start.10 = (s32[235]{0:T(256)S(1)}, s32[235]{0:T(256)}, u32[]{:S(2)}) copy-start(s32[235]{0:T(256)} %constant.260.clone) | copy-start | bytes 2824
  38.6 211.7 %copy-start = (bf16[15,768,128]{2,1,0:T(8,128)(2,1)}, bf16[15,768,128]{2,1,0:T(8,128)(2,1)S(1)}, u32[]{:S(2)}) copy-start(bf16[15,768,128]{2,1,0:T(8,128)(2,1)S(1)} %convert_bitcast_fusion.refs_2_.refs_18_) | copy-start | bytes 8847364
  263.6 10.8 %copy-start.3 = (bf16[2,2,2,4,24,768]{5,4,3,2,1,0:T(8,128)(2,1)S(1)}, bf16[2,2,2,4,24,768]{5,4,3,2,1,0:T(8,128)(2,1)}, u32[]{:S(2)}) copy-start(bf16[2,2,2,4,24,768]{5,4,3,2,1,0:T(8,128)(2,1)} %copy-done.2) | copy-start | bytes 3538948
  277.5 9.5 %copy-start.16 = (f32[2,256,768]{2,1,0:T(8,128)}, f32[2,256,768]{2,1,0:T(8,128)S(1)}, u32[]{:S(2)}) copy-start(f32[2,256,768]{2,1,0:T(8,128)S(1)} %get-tuple-element.80) | copy-start | bytes 4718596
  277.8 9.1 %slice-start.3 = ((s8[4718592]{0:T(1024)(128)(4,1)}), s8[4194304]{0:T(1024)(128)(4,1)S(1)}, s32[]{:S(2)}) async-start(s8[4718592]{0:T(1024)(128)(4,1)} %bitcast.214), calls=%async_computation.5 | async-start | bytes 8388608
  278.2 8.8 %copy-start.30 = (bf16[2,256,768]{2,1,0:T(8,128)(2,1)}, bf16[2,256,768]{2,1,0:T(8,128)(2,1)S(1)}, u32[]{:S(2)}) copy-start(bf16[2,256,768]{2,1,0:T(8,128)(2,1)S(1)} %add_convert_fusion.4) | copy-start | bytes 2359300
  278.2 8.8 %slice-start.4 = ((s8[4718592]{0:T(1024)(128)(4,1)}), s8[524288]{0:T(1024)(128)(4,1)S(1)}, s32[]{:S(2)}) async-start(s8[4718592]{0:T(1024)(128)(4,1)} %bitcast.214), calls=%async_computation.6 | async-start | bytes 1048576
  297.2 10.9 %copy-start.5 = (bf16[2,2,2,4,24,768]{5,4,3,2,1,0:T(8,128)(2,1)S(1)}, bf16[2,2,2,4,24,768]{5,4,3,2,1,0:T(8,128)(2,1)}, u32[]{:S(2)}) copy-start(bf16[2,2,2,4,24,768]{5,4,3,2,1,0:T(8,128)(2,1)} %copy-done.4) | copy-start | bytes 3538948
  310.9 7.9 %slice-start.9 = ((s8[4718592]{0:T(1024)(128)(4,1)}), s8[4194304]{0:T(1024)(128)(4,1)S(1)}, s32[]{:S(2)}) async-start(s8[4718592]{0:T(1024)(128)(4,1)} %bitcast.224), calls=%async_computation.11 | async-start | bytes 8388608
  311.2 7.6 %copy-start.32 = (bf16[2,256,768]{2,1,0:T(8,128)(2,1)}, bf16[2,256,768]{2,1,0:T(8,128)(2,1)S(1)}, u32[]{:S(2)}) copy-start(bf16[2,256,768]{2,1,0:T(8,128)(2,1)S(1)} %add_convert_fusion.2) | copy-start | bytes 2359300
  311.2 7.6 %slice-start.10 = ((s8[4718592]{0:T(1024)(128)(4,1)}), s8[524288]{0:T(1024)(128)(4,1)S(1)}, s32[]{:S(2)}) async-start(s8[4718592]{0:T(1024)(128)(4,1)} %bitcast.224), calls=%async_computation.12 | async-start | bytes 1048576
  326.4 7.5 %slice-start.7 = ((s8[4718592]{0:T(1024)(128)(4,1)}), s8[524288]{0:T(1024)(128)(4,1)S(1)}, s32[]{:S(2)}) async-start(s8[4718592]{0:T(1024)(128)(4,1)} %bitcast.221), calls=%async_computation.9 | async-start | bytes 1048576
  327.7 6.3 slice-start.8
  342.3 13.0 %copy-start.19 = (f32[2,256,768]{2,1,0:T(8,128)S(1)}, f32[2,256,768]{2,1,0:T(8,128)}, u32[]{:S(2)}) copy-start(f32[2,256,768]{2,1,0:T(8,128)} %copy-done.18) | copy-start | bytes 4718596
  355.4 8.6 %slice-start.5 = ((s8[4718592]{0:T(1024)(128)(4,1)}), s8[4194304]{0:T(1024)(128)(4,1)S(1)}, s32[]{:S(2)}) async-start(s8[4718592]{0:T(1024)(128)(4,1)} %bitcast.217), calls=%async_computation.7 | async-start | bytes 8388608
  362.3 8.5 %slice-start.1 = ((s8[4718592]{0:T(1024)(128)(4,1)}), s8[4194304]{0:T(1024)(128)(4,1)S(1)}, s32[]{:S(2)}) async-start(s8[4718592]{0:T(1024)(128)(4,1)} %bitcast.211), calls=%async_computation.3 | async-start | bytes 8388608
  364.5 6.3 slice-start.2
  378.6 13.1 %copy-start.15 = (f32[2,256,768]{2,1,0:T(8,128)S(1)}, f32[2,256,768]{2,1,0:T(8,128)}, u32[]{:S(2)}) copy-start(f32[2,256,768]{2,1,0:T(8,128)} %copy-done.13) | copy-start | bytes 4718596
  574.3 8.0 %copy-start.45 = (s32[15]{0:T(128)S(1)}, s32[15]{0:T(128)}, u32[]{:S(2)}) copy-start(s32[15]{0:T(128)} %copy-done.44) | copy-start | bytes 184
  574.3 8.1 %copy-start.48 = (s32[15]{0:T(128)S(1)}, s32[15]{0:T(128)}, u32[]{:S(2)}) copy-start(s32[15]{0:T(128)} %copy-done.47) | copy-start | bytes 184
  574.3 8.8 %copy-start.38 = (f32[32,2,16,128]{3,2,1,0:T(8,128)S(1)}, f32[32,2,16,128]{3,2,1,0:T(8,128)}, u32[]{:S(2)}) copy-start(f32[32,2,16,128]{3,2,1,0:T(8,128)} %get-tuple-element.36) | copy-start | bytes 1572868
  574.3 75.3 %all-to-all-start.1 = ((bf16[32,15,24,128]{3,2,1,0:T(8,128)(2,1)}), bf16[32,15,24,128]{3,2,1,0:T(8,128)(2,1)}, u32[]{:S(2)}, u32[]{:S(2)}) async-start(bf16[32,15,24,128]{3,2,1,0:T(8,128)(2,1)} %bitcast.62), calls=%async_computation.1 | async-start | bytes 5898240 | tf_op jit(solution)/shard_map/all_to_all | solution.py:1143
  (44 other events, 92.7 us)

commit v9 on v8

--- a/solution.py
+++ b/solution.py
@@ -189,7 +189,7 @@
 
 
 MESH = pl.DeviceIdType.MESH
-GATHER_VMEM = 40 * 2**20
+GATHER_VMEM = 60 * 2**20
 SCATTER_VMEM = 56 * 2**20
 
 
@@ -326,7 +326,11 @@
         at = (0, slice(start, start + rows))
         grad = jnp.where(is_dense > 0.0, dense[n, 0].astype(jnp.float32), image_grad[at[1]])
         old = (master[at], first[at], second[at])
-        new = adam_update(*old, grad, rate)
+        first_new = beta_one * old[1] + (1.0 - beta_one) * grad
+        second_new = beta_two * old[2] + (1.0 - beta_two) * grad * grad
+        root = jnp.sqrt(second_new * (1.0 / (1.0 - beta_two**STEP))) + adam_eps
+        ratio = first_new * (1.0 / (1.0 - beta_one**STEP)) / root
+        new = (old[0] - rate * (ratio + decay_rate * old[0]), first_new, second_new)
         for ref, value, kept in zip((new_master, new_first, new_second), new, old):
             ref[at] = jnp.where(used > 0.0, value, kept)
 
@@ -392,14 +396,41 @@
     return to_x, to_y, to_core, to_z
 
 
+def round_copies(step, source, held, sem, arriving):
+    y, x, c, z = place_of()
+    to_x, to_y, to_core, to_z = neighbours()
+    if step == 0:
+        copies = []
+        for number in (1, 2, 3):
+            at_z = lax.rem(z + 4 - number, 4) if arriving else z
+            copies.append((source, held.at[y, x, c, at_z], to_z[number - 1]))
+    else:
+        at_x = 1 - x if arriving and step == 1 else x
+        at_y = 1 - y if arriving and step == 2 else y
+        at_c = 1 - c if arriving and step == 3 else c
+        block = (held.at[y, at_x, c], held.at[at_y, :, c], held.at[:, :, at_c])[step - 1]
+        copies = [(block, block, (to_x, to_y, to_core)[step - 1])]
+    return [
+        pltpu.make_async_remote_copy(
+            src_ref=start,
+            dst_ref=dest,
+            send_sem=sem.at[0, step, number],
+            recv_sem=sem.at[1, step, number],
+            device_id=target,
+            device_id_type=MESH,
+        )
+        for number, (start, dest, target) in enumerate(copies)
+    ]
+
+
 def gather_kernel(widths, bases, *refs):
     count = len(widths)
-    units, info, low_slots = refs[:3]
-    outs = refs[3 : count + 3]
-    every_info, cond_out, modul_out = refs[count + 3 : count + 6]
-    pieces = refs[count + 6 : 2 * count + 6]
+    places, spread, info, low_slots = refs[:4]
+    outs = refs[4 : count + 4]
+    every_info, cond_out, modul_out = refs[count + 4 : count + 7]
+    pieces = refs[count + 7 : 2 * count + 7]
     time_two, parts, own_sem, send_sem, recv_sem, time_sem, modul_sem, info_sem = refs[
-        2 * count + 6 :
+        2 * count + 7 :
     ]
     devices, images = modul_out.shape[:2]
     slots = low_slots.shape[0]
@@ -471,29 +502,20 @@
             device_id_type=MESH,
         )
 
-    def info_copy(j, arriving):
-        peer, where = device_at(devices - j if arriving else j)
-        return pltpu.make_async_remote_copy(
-            src_ref=info,
-            dst_ref=every_info.at[pl.ds((peer if arriving else me) * images, images)],
-            send_sem=info_sem.at[0, j],
-            recv_sem=info_sem.at[1, j],
-            device_id=where,
-            device_id_type=MESH,
-        )
+    def info_copies(step, arriving):
+        return round_copies(step, info, every_info, info_sem, arriving)
 
     def info_rows(first):
-        return jnp.concatenate([every_info[:, first + j, :] for j in range(D // BLOCK)], -1)
+        rows = [every_info[:, :, :, :, :, first + j, :] for j in range(D // BLOCK)]
+        return jnp.concatenate([row.reshape(devices * images, BLOCK) for row in rows], -1)
 
     def image_products():
         copy = pltpu.make_async_copy(outs[0], time_two, time_sem)
         copy.start()
-
-        @pl.loop(1, devices)
-        def _(j):
-            info_copy(j, True).wait_recv()
-            info_copy(j, False).wait_send()
-
+        arrived(info_copies(3, True))
+        for step in range(4):
+            for sent in info_copies(step, False):
+                sent.wait_send()
         copy.wait()
         weight = time_two[...].astype(jnp.float32).reshape(D, D).astype(jnp.bfloat16)
         cond = jnp.dot(
@@ -511,15 +533,11 @@
         def _(j):
             modul_copy(j, False).start()
 
-    @pl.loop(1, devices)
-    def _(j):
-        info_copy(j, False).start()
-
-    for i in range(images):
-        every_info[me * images + i] = info[i]
+    start(info_copies(0, False))
+    every_info[y, x, c, z] = info[...]
     def send_piece(k):
         for n in range(widths[k] // BLOCK):
-            pieces[k][:, n * BLOCK : (n + 1) * BLOCK] = units[bases[k] + n]
+            pieces[k][:, n * BLOCK : (n + 1) * BLOCK] = spread[places[bases[k] + n]]
         start(line_copies(k, False))
         own_copy(k).start()
 
@@ -537,6 +555,9 @@
         if 0 <= t - 2 < count:
             arrived(second_copies(t - 2, True))
             start(core_copies(t - 2, False))
+        if t < 3:
+            arrived(info_copies(t, True))
+            start(info_copies(t + 1, False))
         if t == 3:
             arrived(core_copies(0, True))
             image_products()
@@ -565,7 +586,7 @@
         left_in, left_turned, right_in, away, every_modul, parts, landed,
         load_sem, send_sem, recv_sem, modul_sem, part_sem, sum_sem,
     ) = scratch[4 * count :]
-    devices, images = shared.shape[:2]
+    devices, images = 32, shared.shape[4]
     y, x, c, z = place_of()
     to_x, to_y, to_core, to_z = neighbours()
     me = rep_of(y, x, c) * 4 + z
@@ -585,43 +606,16 @@
         )
 
     def modul_copies(step, arriving):
-        if step == 0:
-            copies = []
-            for number in (1, 2, 3):
-                at_z = lax.rem(z + 4 - number, 4) if arriving else z
-                copies.append((modul, every_modul.at[y, x, c, at_z], to_z[number - 1]))
-        else:
-            at_x = 1 - x if arriving and step == 1 else x
-            at_y = 1 - y if arriving and step == 2 else y
-            at_c = 1 - c if arriving and step == 3 else c
-            block = (
-                every_modul.at[y, at_x, c],
-                every_modul.at[at_y, :, c],
-                every_modul.at[:, :, at_c],
-            )[step - 1]
-            copies = [(block, block, (to_x, to_y, to_core)[step - 1])]
-        return [
-            pltpu.make_async_remote_copy(
-                src_ref=source,
-                dst_ref=dest,
-                send_sem=modul_sem.at[0, step, number],
-                recv_sem=modul_sem.at[1, step, number],
-                device_id=target,
-                device_id_type=MESH,
-            )
-            for number, (source, dest, target) in enumerate(copies)
-        ]
+        return round_copies(step, modul, every_modul, modul_sem, arriving)
+
+    def sum_copies(step, arriving):
+        return round_copies(step, shared.at[y, x, c, z], shared, sum_sem, arriving)
 
     def part_copy(j, arriving):
         return exchange(
             lambda peer, mine: parts.at[pl.ds(peer * images, images)],
             lambda owner: landed.at[owner],
             part_sem, j, arriving,
-        )
-
-    def sum_copy(j, arriving):
-        return exchange(
-            lambda peer, mine: shared.at[mine], lambda owner: shared.at[owner], sum_sem, j, arriving
         )
 
     def all_start(copy):
@@ -668,8 +662,8 @@
 
     def image_sums():
         all_arrived(part_copy)
-        shared[me] = jnp.sum(landed[...], 0) * factor[...]
-        all_start(sum_copy)
+        shared[y, x, c, z] = jnp.sum(landed[...], 0) * factor[...]
+        start(sum_copies(0, False))
 
     def remote(k, number, source, dest, target):
         return pltpu.make_async_remote_copy(
@@ -822,11 +816,13 @@
             image_parts()
         if t == 6:
             image_sums()
-    all_arrived(sum_copy)
-    for copy in (part_copy, sum_copy):
-        all_sent(copy)
+        if 7 <= t < 10:
+            arrived(sum_copies(t - 7, True))
+            start(sum_copies(t - 6, False))
+    arrived(sum_copies(3, True))
+    all_sent(part_copy)
     for step in range(4):
-        for copy in modul_copies(step, False):
+        for copy in modul_copies(step, False) + sum_copies(step, False):
             copy.wait_send()
     for k in range(count):
         for copies in (core_copies, first_copies, second_copies, line_copies):
@@ -849,7 +845,7 @@
             starts.append(((((c * 2 + y) * 2 + x) * 4) + z) * (D // 32))
         return values, starts
 
-    def gather(self, units, info, low_slots):
+    def gather(self, places, spread, info, low_slots):
         names = unit_groups()
         turn = [len(names) - 1] + sorted(range(len(names) - 1), key=lambda n: (n % 4 == 1, n))
         bases = tuple(names[n][0] for n in turn)
@@ -866,11 +862,12 @@
                 jax.ShapeDtypeStruct(shape, jnp.bfloat16) for shape in whole_shape
             ]
             + [
-                jax.ShapeDtypeStruct((all_images,) + info.shape[1:], jnp.float32),
+                jax.ShapeDtypeStruct((2, 2, 2, 4) + info.shape, jnp.float32),
                 jax.ShapeDtypeStruct((all_images, D), jnp.float32),
                 jax.ShapeDtypeStruct((32, all_images // 32, room, BLOCK), jnp.float32),
             ],
-            in_specs=[pl.BlockSpec(memory_space=pltpu.VMEM)] * 3,
+            in_specs=[pl.BlockSpec(memory_space=pltpu.SMEM)]
+            + [pl.BlockSpec(memory_space=pltpu.VMEM)] * 3,
             out_specs=[pl.BlockSpec(memory_space=pl.ANY)] * count
             + [pl.BlockSpec(memory_space=pltpu.VMEM)] * 3,
             scratch_shapes=[pltpu.VMEM((rows, width), jnp.bfloat16) for width in widths]
@@ -882,16 +879,17 @@
                 pltpu.SemaphoreType.DMA((count, 8)),
                 pltpu.SemaphoreType.DMA,
                 pltpu.SemaphoreType.DMA((2, 32)),
-                pltpu.SemaphoreType.DMA((2, 32)),
+                pltpu.SemaphoreType.DMA((2, 4, 3)),
             ],
             compiler_params=pltpu.CompilerParams(
                 collective_id=0, has_side_effects=True, vmem_limit_bytes=GATHER_VMEM
             ),
             cost_estimate=pl.CostEstimate(flops=0, bytes_accessed=size, transcendentals=0),
-        )(units, info, low_slots)
+        )(places, spread, info, low_slots)
         whole = [part.reshape(D, -1) for part in whole]
         modul = jnp.swapaxes(modul[:, :, :slots], 0, 1).reshape(-1, 32 * slots, BLOCK)
         ordered = [whole[turn.index(n)] for n in range(count)]
+        every_info = every_info.reshape((all_images,) + info.shape[1:])
         return ordered[:-1], ordered[-1], every_info, cond, modul
 
     def scatter(self, layer_grads, modul, pick, low_slots, edge, factor):
@@ -916,7 +914,7 @@
             out_shape=[
                 jax.ShapeDtypeStruct((sum(widths) // BLOCK, rows, BLOCK), jnp.bfloat16),
                 jax.ShapeDtypeStruct((32 * images, pick.shape[0], BLOCK), jnp.float32),
-                jax.ShapeDtypeStruct((32,) + factor.shape, jnp.float32),
+                jax.ShapeDtypeStruct((2, 2, 2, 4) + factor.shape, jnp.float32),
             ],
             in_specs=[pl.BlockSpec(memory_space=pl.ANY)] * (2 * count)
             + [pl.BlockSpec(memory_space=pltpu.VMEM)] * 5,
@@ -935,7 +933,7 @@
                 pltpu.SemaphoreType.DMA((count, 8)),
                 pltpu.SemaphoreType.DMA((2, 4, 3)),
                 pltpu.SemaphoreType.DMA((2, 32)),
-                pltpu.SemaphoreType.DMA((2, 32)),
+                pltpu.SemaphoreType.DMA((2, 4, 3)),
             ],
             compiler_params=pltpu.CompilerParams(
                 collective_id=1, has_side_effects=True, vmem_limit_bytes=SCATTER_VMEM
@@ -953,7 +951,8 @@
     def join_rows(self, values):
         return jnp.swapaxes(values, 0, 1).reshape(1, -1, D, BLOCK), [0]
 
-    def gather(self, units, info, low_slots):
+    def gather(self, places, spread, info, low_slots):
+        units = jnp.take(spread, places, axis=0, mode="clip")
         whole = []
         for first, number in unit_groups():
             piece = jnp.swapaxes(units[first : first + number], 0, 1)
@@ -1027,7 +1026,7 @@
         plan.split_rows(low_slots), AXES, split_axis=0, concat_axis=0, tiled=True
     ).reshape(slot_total, rows, BLOCK)
     moved = np.concatenate([dense_units, time_units])
-    units = jnp.take(spread, owner[moved], axis=0, mode="clip")
+    places = owner[moved]
 
     x_start = latents.astype(jnp.float32).reshape(-1, PATCHES, CHANNELS)
     noise_f = noise.astype(jnp.float32).reshape(-1, PATCHES, CHANNELS)
@@ -1060,7 +1059,7 @@
         1,
     )
     whole, time_two, every_info, cond_all, slot_modul = plan.gather(
-        units, info, low_slots
+        places, spread, info, low_slots
     )
     all_images = cond_all.shape[0]
     every_time = (every_info[:, blocks, 0] + 0.5) / TSTEPS

time: 678 us -> 660 us (0.973)
  Pallas kernels: 403 us -> 392 us
  waiting for transfers between devices: 80.4 us -> 73 us
    unnamed x148 -> x129, local copies, waits for them, and re-layouts: 20.5 us -> 14.5 us
  transfers between devices with their start and end apart: 2 -> 2, of which waited for: 2 -> 2; matrix products, arithmetic and copies ran while one was open for 7% -> 9% of each run, Pallas kernels for 0% -> 0%
where the time goes in v9:
time: 660 us; the launch traced here: 656 us
  Pallas kernels  392 us (59%)
  matrix products  83.1 us (13%)
  waiting for transfers between devices  73 us (11%)
  other arithmetic  45.7 us (7%)
  local copies, waits for them, and re-layouts  43.3 us (7%)
  starting transfers between devices  14 us (2%)
    pallas_call x1, Pallas kernels, scatter(): pl.pallas_call(lambda *refs: scatter_kernel(widths, bases, slots, *refs),...  162 us
    pallas_call x1, Pallas kernels, gather(): pl.pallas_call(lambda *refs: gather_kernel(widths, bases, *refs), out_sha...  160 us
    dot_general x23, matrix products, dot_low(): jnp.einsum(pattern, left_side, right_side, preferred_element_type=jnp.flo...  81.9 us
    all_to_all x1, waiting for transfers between devices, on_device(): lax.all_to_all(plan.split_rows(low_slots), AXES, split_axis=0, concat_axi...  39.1 us
    all_to_all x1, waiting for transfers between devices, on_device(): lax.all_to_all(slot_rows.reshape(count, slot_dev, rows, BLOCK), AXES, spl...  33.9 us
    pallas_call x2, Pallas kernels, attend_back(): pl.pallas_call(attend_back_kernel, grid=(images, steps), out_shape=jax.Sh...  26 us
    pallas_call x1, Pallas kernels, adam_slots(): pl.pallas_call(lambda *refs: adam_kernel(starts, *refs), grid=(slots,), o...  22.2 us
    pallas_call x2, Pallas kernels, attend(): pl.pallas_call(attend_kernel, grid=(images, steps), out_shape=jax.ShapeDt...  21.5 us
  transfers between devices with their start and end apart: 2, of which 2 were waited for; matrix products, arithmetic and copies ran while one was open for 9% of the time, Pallas kernels for 0%

profile of v9, /device:TPU:3, one launch (start us, length us, event | category | flops | bytes accessed | tf_op | source)
XLA Modules:
  0.0 655.7 jit_solution(18238812061698534726)
XLA Ops:
  6.0 6.5 all-to-all-start
  12.4 3.7 convert_element_type.157
  26.0 3.5 gather_fusion.5
  35.9 4.8 convert_bitcast_fusion.refs_3_.refs_18_
  40.7 39.1 %all-to-all-done = bf16[32,15,24,128]{3,2,1,0:T(8,128)(2,1)} async-done(((bf16[32,15,24,128]{3,2,1,0:T(8,128)(2,1)}), bf16[32,15,24,128]{3,2,1,0:T(8,128)(2,1)}, u32[]{:S(2)}, u32[]{:S(2)}) %all-to-all-start) | async-done | bytes 2949152 | tf_op jit(solution)/shard_map/all_to_all | solution.py:1025
  79.8 160.2 %shard_map.224 = (bf16[2,2,2,4,24,768]{5,4,3,2,1,0:T(8,128)(2,1)}, bf16[2,2,2,4,24,2304]{5,4,3,2,1,0:T(8,128)(2,1)}, bf16[2,2,2,4,24,3072]{5,4,3,2,1,0:T(8,128)(...) custom-call(s32[150]{0:T(256)} %gather_fusion, ...), custom_call_target="tpu_custom_call" | custom-call | bytes 58982400 | tf_op jit(solution)/shard_map/pallas_call | solution.py:859
  243.3 5.4 convolution_convert_fusion.1.queries.keys_all.values
  248.8 10.7 %shard_map.225 = bf16[2,256,768]{2,1,0:T(8,128)(2,1)} custom-call(bf16[2,256,2304]{2,1,0:T(8,128)(2,1)} %convolution_convert_fusion.1.queries.keys_all.values, bf16[2,256,2304]{2,1,0:T(8,128)(2,1)} %convolution_convert_fusion.1.queries.keys_all.values, bf16[2,256,2304]{2,1,0:T(8,128)(2,1)} %convolution_convert_fusion.1.queries.keys_all.values), custom_call_target="tpu_custom_call" | custom-call | flops 402653184 | bytes 3145728 | tf_op jit(solution)/shard_map/pallas_call | solution.py:288
  263.6 8.6 %fusion.15 = (bf16[2,256,3072]{2,1,0:T(8,128)(2,1)S(1)}, bf16[2,256,3072]{2,1,0:T(8,128)(2,1)}) fusion(bf16[2,256,768]{2,1,0:T(8,128)(2,1)S(1)} %add_convert_fusion.4, bf16[768,3072,1]{1,0,2:T(8,128)(2,1)} %bitcast.210), kind=kOutput, calls=%fused_computation.35 | convolution fusion | flops 2431647744 | bytes 11796480 | tf_op jit(solution)/shard_map/gpd,df->gpf/dot_general | solution.py:55
  272.2 3.8 fusion.107
  282.4 10.8 %shard_map.226 = bf16[2,256,768]{2,1,0:T(8,128)(2,1)} custom-call(bf16[2,256,2304]{2,1,0:T(8,128)(2,1)} %convolution_convert_fusion.queries.keys_all.values, bf16[2,256,2304]{2,1,0:T(8,128)(2,1)} %convolution_convert_fusion.queries.keys_all.values, bf16[2,256,2304]{2,1,0:T(8,128)(2,1)} %convolution_convert_fusion.queries.keys_all.values), custom_call_target="tpu_custom_call" | custom-call | flops 402653184 | bytes 3145728 | tf_op jit(solution)/shard_map/pallas_call | solution.py:288
  296.7 7.6 %fusion.23 = (bf16[2,256,3072]{2,1,0:T(8,128)(2,1)S(1)}, bf16[2,256,3072]{2,1,0:T(8,128)(2,1)S(1)}) fusion(bf16[2,256,768]{2,1,0:T(8,128)(2,1)S(1)} %add_convert_fusion.2, bf16[768,3072,1]{1,0,2:T(8,128)(2,1)} %bitcast.220), kind=kOutput, calls=%fused_computation.43 | convolution fusion | flops 2431647744 | bytes 11796480 | tf_op jit(solution)/shard_map/gpd,df->gpf/dot_general | solution.py:55
  313.2 6.3 fusion.7
  328.0 13.0 %shard_map.227 = bf16[2,256,2304]{2,1,0:T(8,128)(2,1)} custom-call(bf16[2,256,2304]{2,1,0:T(8,128)(2,1)} %convolution_convert_fusion.queries.keys_all.values, bf16[2,256,2304]{2,1,0:T(8,128)(2,1)} %convolution_convert_fusion.queries.keys_all.values, bf16[2,256,2304]{2,1,0:T(8,128)(2,1)} %convolution_convert_fusion.queries.keys_all.values, ...), custom_call_target="tpu_custom_call" | custom-call | flops 1006632960 | bytes 5505024 | tf_op jit(solution)/shard_map/pallas_call | solution.py:305
  341.0 5.4 multiply_reduce_fusion.11
  350.5 6.3 fusion.4
  365.7 13.0 %shard_map.228 = bf16[2,256,2304]{2,1,0:T(8,128)(2,1)} custom-call(bf16[2,256,2304]{2,1,0:T(8,128)(2,1)} %convolution_convert_fusion.1.queries.keys_all.values, bf16[2,256,2304]{2,1,0:T(8,128)(2,1)} %convolution_convert_fusion.1.queries.keys_all.values, bf16[2,256,2304]{2,1,0:T(8,128)(2,1)} %convolution_convert_fusion.1.queries.keys_all.values, ...), custom_call_target="tpu_custom_call" | custom-call | flops 1006632960 | bytes 5505024 | tf_op jit(solution)/shard_map/pallas_call | solution.py:305
  378.7 4.9 multiply_reduce_fusion
  390.7 162.3 %shard_map.229 = (bf16[144,24,128]{2,1,0:T(8,128)(2,1)}, f32[64,16,128]{2,1,0:T(8,128)}, f32[2,2,2,4,2,16,128]{6,5,4,3,2,1,0:T(8,128)}) custom-call(bf16[512,768]{1,0:T(8,128)(2,1)} %bitcast.171, bf16[512,768]{1,0:T(8,128)(2,1)} %bitcast.178, bf16[512,768]{1,0:T(8,128)(2,1)} %bitcast.179, bf16[512,768]{1,0:T(8,128)(2,1)} %bitcast.183, ...), custom_call_target="tpu_custom_call" | custom-call | bytes 56623104 | tf_op jit(solution)/shard_map/pallas_call | solution.py:912
  552.9 4.2 gather_fusion.6
  557.1 7.5 %all-to-all-start.1 = ((bf16[32,15,24,128]{3,2,1,0:T(8,128)(2,1)}), bf16[32,15,24,128]{3,2,1,0:T(8,128)(2,1)}, u32[]{:S(2)}, u32[]{:S(2)}) async-start(bf16[32,15,24,128]{3,2,1,0:T(8,128)(2,1)} %bitcast.64), calls=%async_computation.1 | async-start | bytes 5898240 | tf_op jit(solution)/shard_map/all_to_all | solution.py:1142
  587.7 10.3 %multiply_subtract_fusion = (f32[1288,768]{1,0:T(8,128)}, f32[1288,768]{1,0:T(8,128)}, f32[1288,768]{1,0:T(8,128)}) fusion(f32[1288,768]{1,0:T(8,128)} %param.25, f32[1288]{0:T(1024)S(1)} %select_multiply_fusion, f32[16,768]{1,0:T(8,128)S(1)} %bitcast.200, f32[1000,768]{1,0:T(8,128)S(1)} %scatter_custom_fusion.1, f32[256,768]{1,0:T(8,128)S(1)} %copy-done.27, ...), kind=kLoop, calls=%fused_computation.60 | loop fusion | flops 16816128 | bytes 27702304 | tf_op jit(solution)/shard_map/sub | solution.py:105
  598.0 33.9 %all-to-all-done.1.refs_1_ = bf16[32,15,24,128]{3,2,1,0:T(8,128)(2,1)} async-done(((bf16[32,15,24,128]{3,2,1,0:T(8,128)(2,1)}), bf16[32,15,24,128]{3,2,1,0:T(8,128)(2,1)}, u32[]{:S(2)}, u32[]{:S(2)}) %all-to-all-start.1) | async-done | bytes 2949152 | tf_op jit(solution)/shard_map/all_to_all | solution.py:1142
  632.0 22.2 %shard_map.230 = (f32[15,768,128]{2,1,0:T(8,128)}, f32[15,768,128]{2,1,0:T(8,128)}, f32[15,768,128]{2,1,0:T(8,128)}) custom-call(f32[15,3]{1,0:T(8,128)} %copy.84.refs_0_, bf16[32,15,24,128]{3,2,1,0:T(8,128)(2,1)} %all-to-all-done.1.refs_1_, bf16[15,768,64]{2,1,0:T(8,128)(2,1)} %broadcast_select_fusion.refs_2_, bf16[15,64,128]{2,1,0:T(8,128)(2,1)} %fusion.43.refs_3_, ...), custom_call_target="tpu_custom_call" | custom-call | flops 58982400 | bytes 38338560 | tf_op jit(solution)/shard_map/pallas_call | solution.py:342
  (274 shorter events, 97.3 us)
Async XLA Ops:
  6.0 73.8 %all-to-all-start = ((bf16[32,15,24,128]{3,2,1,0:T(8,128)(2,1)}), bf16[32,15,24,128]{3,2,1,0:T(8,128)(2,1)}, u32[]{:S(2)}, u32[]{:S(2)}) async-start(bf16[32,15,24,128]{3,2,1,0:T(8,128)(2,1)} %bitcast.4), calls=%async_computation | async-start | bytes 5898240 | tf_op jit(solution)/shard_map/all_to_all | solution.py:1025
  16.2 5.5 copy-start.40
  17.0 8.2 %copy-start.2 = (s32[235]{0:T(256)S(1)}, s32[235]{0:T(256)}, u32[]{:S(2)}) copy-start(s32[235]{0:T(256)} %constant.259.clone) | copy-start | bytes 2824
  17.2 8.7 %copy-start = (s32[235]{0:T(256)S(1)}, s32[235]{0:T(256)}, u32[]{:S(2)}) copy-start(s32[235]{0:T(256)} %constant.260.clone) | copy-start | bytes 2824
  17.4 7.8 %copy-start.34 = (f32[128]{0:T(128)}, f32[128]{0:T(128)S(1)}, u32[]{:S(2)}) copy-start(f32[128]{0:T(128)S(1)} %multiply_exponential_fusion.1) | copy-start | bytes 1540
  25.8 5.0 copy-start.37
  263.3 8.9 %slice-start.3 = ((s8[4718592]{0:T(1024)(128)(4,1)}), s8[4194304]{0:T(1024)(128)(4,1)S(1)}, s32[]{:S(2)}) async-start(s8[4718592]{0:T(1024)(128)(4,1)} %bitcast.214), calls=%async_computation.5 | async-start | bytes 8388608
  263.6 8.6 %copy-start.16 = (bf16[2,256,768]{2,1,0:T(8,128)(2,1)}, bf16[2,256,768]{2,1,0:T(8,128)(2,1)S(1)}, u32[]{:S(2)}) copy-start(bf16[2,256,768]{2,1,0:T(8,128)(2,1)S(1)} %add_convert_fusion.4) | copy-start | bytes 2359300
  263.6 8.6 %slice-start.4 = ((s8[4718592]{0:T(1024)(128)(4,1)}), s8[524288]{0:T(1024)(128)(4,1)S(1)}, s32[]{:S(2)}) async-start(s8[4718592]{0:T(1024)(128)(4,1)} %bitcast.214), calls=%async_computation.6 | async-start | bytes 1048576
  272.2 3.9 copy-start.11
  296.3 8.0 %slice-start.9 = ((s8[4718592]{0:T(1024)(128)(4,1)}), s8[4194304]{0:T(1024)(128)(4,1)S(1)}, s32[]{:S(2)}) async-start(s8[4718592]{0:T(1024)(128)(4,1)} %bitcast.224), calls=%async_computation.11 | async-start | bytes 8388608
  296.7 7.6 %copy-start.18 = (bf16[2,256,768]{2,1,0:T(8,128)(2,1)}, bf16[2,256,768]{2,1,0:T(8,128)(2,1)S(1)}, u32[]{:S(2)}) copy-start(bf16[2,256,768]{2,1,0:T(8,128)(2,1)S(1)} %add_convert_fusion.2) | copy-start | bytes 2359300
  296.7 7.6 %slice-start.10 = ((s8[4718592]{0:T(1024)(128)(4,1)}), s8[524288]{0:T(1024)(128)(4,1)S(1)}, s32[]{:S(2)}) async-start(s8[4718592]{0:T(1024)(128)(4,1)} %bitcast.224), calls=%async_computation.12 | async-start | bytes 1048576
  312.0 7.6 %slice-start.7 = ((s8[4718592]{0:T(1024)(128)(4,1)}), s8[524288]{0:T(1024)(128)(4,1)S(1)}, s32[]{:S(2)}) async-start(s8[4718592]{0:T(1024)(128)(4,1)} %bitcast.221), calls=%async_computation.9 | async-start | bytes 1048576
  313.2 6.3 slice-start.8
  340.9 5.5 copy-start.4
  341.0 9.1 %slice-start.5 = ((s8[4718592]{0:T(1024)(128)(4,1)}), s8[4194304]{0:T(1024)(128)(4,1)S(1)}, s32[]{:S(2)}) async-start(s8[4718592]{0:T(1024)(128)(4,1)} %bitcast.217), calls=%async_computation.7 | async-start | bytes 8388608
  348.3 8.5 %slice-start.1 = ((s8[4718592]{0:T(1024)(128)(4,1)}), s8[4194304]{0:T(1024)(128)(4,1)S(1)}, s32[]{:S(2)}) async-start(s8[4718592]{0:T(1024)(128)(4,1)} %bitcast.211), calls=%async_computation.3 | async-start | bytes 8388608
  350.5 6.3 slice-start.2
  557.1 7.5 %copy-start.36 = (s32[15]{0:T(128)S(1)}, s32[15]{0:T(128)}, u32[]{:S(2)}) copy-start(s32[15]{0:T(128)} %copy-done.35) | copy-start | bytes 184
  557.1 7.6 %copy-start.38 = (s32[15]{0:T(128)S(1)}, s32[15]{0:T(128)}, u32[]{:S(2)}) copy-start(s32[15]{0:T(128)} %copy-done.37) | copy-start | bytes 184
  557.1 8.9 %copy-start.26 = (f32[2,2,2,4,2,16,128]{6,5,4,3,2,1,0:T(8,128)S(1)}, f32[2,2,2,4,2,16,128]{6,5,4,3,2,1,0:T(8,128)}, u32[]{:S(2)}) copy-start(f32[2,2,2,4,2,16,128]{6,5,4,3,2,1,0:T(8,128)} %get-tuple-element.36) | copy-start | bytes 1572868
  557.1 74.8 %all-to-all-start.1 = ((bf16[32,15,24,128]{3,2,1,0:T(8,128)(2,1)}), bf16[32,15,24,128]{3,2,1,0:T(8,128)(2,1)}, u32[]{:S(2)}, u32[]{:S(2)}) async-start(bf16[32,15,24,128]{3,2,1,0:T(8,128)(2,1)} %bitcast.64), calls=%async_computation.1 | async-start | bytes 5898240 | tf_op jit(solution)/shard_map/all_to_all | solution.py:1142
  564.6 5.2 copy-start.28
  (34 other events, 66.7 us)

commit v10 on v9

--- a/solution.py
+++ b/solution.py
@@ -214,7 +214,7 @@
 
 
 PAIR = 2 * HEAD_DIM
-SPAN = 3
+SPAN = 6
 
 
 def head_mask(number):
@@ -316,48 +316,62 @@
     )(qkv_all, qkv_all, qkv_all, grad_heads)
 
 
-def adam_kernel(starts, flags, dense, left, right, master, first, second, *refs):
+def adam_kernel(starts, flags, picks, dense, extra, left, right, master, first, second, *refs):
     new_master, new_first, new_second, image_grad = refs
-    slot = pl.program_id(0)
-    rate, used, is_dense = flags[slot, 0], flags[slot, 1], flags[slot, 2]
-    image_grad[...] = jnp.dot(left[0], right[0], preferred_element_type=jnp.float32)
-    rows = dense.shape[2]
-    for n, start in enumerate(starts):
-        at = (0, slice(start, start + rows))
-        grad = jnp.where(is_dense > 0.0, dense[n, 0].astype(jnp.float32), image_grad[at[1]])
-        old = (master[at], first[at], second[at])
-        first_new = beta_one * old[1] + (1.0 - beta_one) * grad
-        second_new = beta_two * old[2] + (1.0 - beta_two) * grad * grad
-        root = jnp.sqrt(second_new * (1.0 / (1.0 - beta_two**STEP))) + adam_eps
-        ratio = first_new * (1.0 / (1.0 - beta_one**STEP)) / root
-        new = (old[0] - rate * (ratio + decay_rate * old[0]), first_new, second_new)
-        for ref, value, kept in zip((new_master, new_first, new_second), new, old):
-            ref[at] = jnp.where(used > 0.0, value, kept)
-
-
-def adam_slots(dense, starts, flags, left, right, *state):
+    group = pl.program_id(0)
+    size, rows = master.shape[0], dense.shape[2]
+
+    @pl.loop(0, size)
+    def _(s):
+        slot = group * size + s
+        rate, used = flags[slot, 0], flags[slot, 1]
+        from_dense, from_extra, from_images = (flags[slot, n] for n in (2, 3, 4))
+        image_grad[...] = jnp.dot(left[s], right[s], preferred_element_type=jnp.float32)
+        for n, start in enumerate(starts):
+            at = (s, slice(start, start + rows))
+            grad = jnp.where(from_images > 0.0, image_grad[at[1]], 0.0)
+            part = dense[n, picks[slot, 0]].astype(jnp.float32)
+            grad = jnp.where(from_dense > 0.0, part, grad)
+            part = extra[n, picks[slot, 1]].astype(jnp.float32)
+            grad = jnp.where(from_extra > 0.0, part, grad)
+            old = (master[at], first[at], second[at])
+            first_new = beta_one * old[1] + (1.0 - beta_one) * grad
+            second_new = beta_two * old[2] + (1.0 - beta_two) * grad * grad
+            root = jnp.sqrt(second_new * (1.0 / (1.0 - beta_two**STEP))) + adam_eps
+            turned = pl.reciprocal(root, approx=True)
+            turned = turned * (2.0 - root * turned)
+            turned = turned * (2.0 - root * turned)
+            ratio = first_new * (1.0 / (1.0 - beta_one**STEP)) * turned
+            new = (old[0] - rate * (ratio + decay_rate * old[0]), first_new, second_new)
+            for ref, value, kept in zip((new_master, new_first, new_second), new, old):
+                ref[at] = jnp.where(used > 0.0, value, kept)
+
+
+def adam_slots(dense, extra, starts, flags, picks, left, right, *state):
     slots = state[0].shape[0]
-    block = pl.BlockSpec((1, D, BLOCK), lambda slot: (slot, 0, 0))
+    size = next(size for size in (3, 2, 1) if slots % size == 0)
+    block = pl.BlockSpec((size, D, BLOCK), lambda group: (group, 0, 0))
     side = left.shape[2]
     return pl.pallas_call(
         lambda *refs: adam_kernel(starts, *refs),
-        grid=(slots,),
+        grid=(slots // size,),
         out_shape=[jax.ShapeDtypeStruct((slots, D, BLOCK), jnp.float32)] * 3,
         in_specs=[
             pl.BlockSpec(memory_space=pltpu.SMEM),
-            pl.BlockSpec(
-                (dense.shape[0], 1) + dense.shape[2:], lambda slot: (0, slot, 0, 0)
-            ),
-            pl.BlockSpec((1, D, side), lambda slot: (slot, 0, 0)),
-            pl.BlockSpec((1, side, BLOCK), lambda slot: (slot, 0, 0)),
+            pl.BlockSpec(memory_space=pltpu.SMEM),
+            pl.BlockSpec(memory_space=pltpu.VMEM),
+            pl.BlockSpec(memory_space=pltpu.VMEM),
+            pl.BlockSpec((size, D, side), lambda group: (group, 0, 0)),
+            pl.BlockSpec((size, side, BLOCK), lambda group: (group, 0, 0)),
         ]
         + [block] * 3,
         out_specs=[block] * 3,
         scratch_shapes=[pltpu.VMEM((D, BLOCK), jnp.float32)],
+        compiler_params=pltpu.CompilerParams(vmem_limit_bytes=40 * 2**20),
         cost_estimate=pl.CostEstimate(
             flops=40 * slots * D * BLOCK, bytes_accessed=26 * slots * D * BLOCK, transcendentals=0
         ),
-    )(flags, dense, left, right, *state)
+    )(flags, picks, dense, extra, left, right, *state)
 
 
 def place_of():
@@ -425,12 +439,12 @@
 
 def gather_kernel(widths, bases, *refs):
     count = len(widths)
-    places, spread, info, low_slots = refs[:4]
-    outs = refs[4 : count + 4]
-    every_info, cond_out, modul_out = refs[count + 4 : count + 7]
-    pieces = refs[count + 7 : 2 * count + 7]
+    places, share, spread, extra, info, low_slots = refs[:6]
+    outs = refs[6 : count + 6]
+    every_info, cond_out, modul_out = refs[count + 6 : count + 9]
+    pieces = refs[count + 9 : 2 * count + 9]
     time_two, parts, own_sem, send_sem, recv_sem, time_sem, modul_sem, info_sem = refs[
-        2 * count + 7 :
+        2 * count + 9 :
     ]
     devices, images = modul_out.shape[:2]
     slots = low_slots.shape[0]
@@ -537,7 +551,10 @@
     every_info[y, x, c, z] = info[...]
     def send_piece(k):
         for n in range(widths[k] // BLOCK):
-            pieces[k][:, n * BLOCK : (n + 1) * BLOCK] = spread[places[bases[k] + n]]
+            unit = bases[k] + n
+            value = spread[places[0, unit]].astype(jnp.float32) * share[0, unit]
+            value = value + extra[places[1, unit]].astype(jnp.float32) * share[1, unit]
+            pieces[k][:, n * BLOCK : (n + 1) * BLOCK] = value.astype(jnp.bfloat16)
         start(line_copies(k, False))
         own_copy(k).start()
 
@@ -845,7 +862,7 @@
             starts.append(((((c * 2 + y) * 2 + x) * 4) + z) * (D // 32))
         return values, starts
 
-    def gather(self, places, spread, info, low_slots):
+    def gather(self, places, share, spread, extra, info, low_slots):
         names = unit_groups()
         turn = [len(names) - 1] + sorted(range(len(names) - 1), key=lambda n: (n % 4 == 1, n))
         bases = tuple(names[n][0] for n in turn)
@@ -866,8 +883,8 @@
                 jax.ShapeDtypeStruct((all_images, D), jnp.float32),
                 jax.ShapeDtypeStruct((32, all_images // 32, room, BLOCK), jnp.float32),
             ],
-            in_specs=[pl.BlockSpec(memory_space=pltpu.SMEM)]
-            + [pl.BlockSpec(memory_space=pltpu.VMEM)] * 3,
+            in_specs=[pl.BlockSpec(memory_space=pltpu.SMEM)] * 2
+            + [pl.BlockSpec(memory_space=pltpu.VMEM)] * 4,
             out_specs=[pl.BlockSpec(memory_space=pl.ANY)] * count
             + [pl.BlockSpec(memory_space=pltpu.VMEM)] * 3,
             scratch_shapes=[pltpu.VMEM((rows, width), jnp.bfloat16) for width in widths]
@@ -885,7 +902,7 @@
                 collective_id=0, has_side_effects=True, vmem_limit_bytes=GATHER_VMEM
             ),
             cost_estimate=pl.CostEstimate(flops=0, bytes_accessed=size, transcendentals=0),
-        )(places, spread, info, low_slots)
+        )(places, share, spread, extra, info, low_slots)
         whole = [part.reshape(D, -1) for part in whole]
         modul = jnp.swapaxes(modul[:, :, :slots], 0, 1).reshape(-1, 32 * slots, BLOCK)
         ordered = [whole[turn.index(n)] for n in range(count)]
@@ -951,8 +968,10 @@
     def join_rows(self, values):
         return jnp.swapaxes(values, 0, 1).reshape(1, -1, D, BLOCK), [0]
 
-    def gather(self, places, spread, info, low_slots):
-        units = jnp.take(spread, places, axis=0, mode="clip")
+    def gather(self, places, share, spread, extra, info, low_slots):
+        units = jnp.take(spread, places[0], axis=0, mode="clip") * share[0, :, None, None]
+        units = units + jnp.take(extra, places[1], axis=0, mode="clip") * share[1, :, None, None]
+        units = units.astype(jnp.bfloat16)
         whole = []
         for first, number in unit_groups():
             piece = jnp.swapaxes(units[first : first + number], 0, 1)
@@ -1022,11 +1041,40 @@
     low_slots = jnp.swapaxes(master.astype(jnp.bfloat16), 0, 1)
 
     plan = RingPlan() if (lax.axis_size("rep"), lax.axis_size("shard")) == (8, 4) else PlainPlan()
-    spread = lax.all_to_all(
-        plan.split_rows(low_slots), AXES, split_axis=0, concat_axis=0, tiled=True
-    ).reshape(slot_total, rows, BLOCK)
     moved = np.concatenate([dense_units, time_units])
-    places = owner[moved]
+    is_moved = np.zeros((UNITS + 1,), np.int32)
+    is_moved[moved] = 1
+    needed = jnp.asarray(is_moved)[unit_of_slot].reshape(count, slot_dev)
+    total_needed = jnp.sum(needed, 1, keepdims=True)
+    before = jnp.cumsum(needed, 1)
+    turn = jnp.arange(slot_dev, dtype=jnp.int32)[None]
+    rank = jnp.where(needed > 0, before - 1, total_needed + turn - before)
+    first_slots = max(1, 3 * slot_dev // 4)
+    last_slots = slot_dev - first_slots
+    overflow = jnp.max(total_needed) > first_slots
+    by_rank = (rank[:, :, None] == turn[:, None]).astype(jnp.int32)
+    my_rank = lax.dynamic_index_in_dim(rank, me, 0, False)
+    my_order = jnp.sum(lax.dynamic_index_in_dim(by_rank, me, 0, False) * turn.T, 0)
+
+    def exchange(blocks):
+        return lax.all_to_all(blocks, AXES, split_axis=0, concat_axis=0, tiled=True)
+
+    def exchange_last(blocks):
+        return lax.cond(overflow, exchange, jnp.zeros_like, blocks)
+
+    sorted_rows = plan.split_rows(jnp.take(low_slots, my_order, axis=0, mode="clip"))
+    spread = exchange(sorted_rows[:, :first_slots]).reshape(-1, rows, BLOCK)
+    extra = exchange_last(sorted_rows[:, first_slots:]).reshape(-1, rows, BLOCK)
+    moved_rank = rank.reshape(-1)[owner[moved]]
+    moved_device = owner[moved] // slot_dev
+    in_first = moved_rank < first_slots
+    places = jnp.stack(
+        [
+            moved_device * first_slots + jnp.minimum(moved_rank, first_slots - 1),
+            moved_device * last_slots + jnp.maximum(moved_rank - first_slots, 0),
+        ]
+    )
+    share = jnp.stack([in_first, ~in_first]).astype(jnp.float32)
 
     x_start = latents.astype(jnp.float32).reshape(-1, PATCHES, CHANNELS)
     noise_f = noise.astype(jnp.float32).reshape(-1, PATCHES, CHANNELS)
@@ -1059,7 +1107,7 @@
         1,
     )
     whole, time_two, every_info, cond_all, slot_modul = plan.gather(
-        places, spread, info, low_slots
+        places, share, spread, extra, info, low_slots
     )
     all_images = cond_all.shape[0]
     every_time = (every_info[:, blocks, 0] + 0.5) / TSTEPS
@@ -1137,25 +1185,28 @@
     dense_place = np.full((UNITS + 1,), 0, np.int32)
     dense_place[dense_units] = np.arange(len(dense_units))
     slot_place = jnp.asarray(dense_place)[unit_of_slot]
-    slot_rows = jnp.take(unit_grads, slot_place, axis=0, mode="clip")
-    dense_grad, starts = plan.join_rows(
-        lax.all_to_all(
-            slot_rows.reshape(count, slot_dev, rows, BLOCK),
-            AXES,
-            split_axis=0,
-            concat_axis=0,
-            tiled=True,
-        )
-    )
+    packed = jnp.sum(by_rank * slot_place.reshape(count, slot_dev, 1), 1)
+
+    def rows_of(places_of):
+        picked = jnp.take(unit_grads, places_of.reshape(-1), axis=0, mode="clip")
+        return picked.reshape(count, -1, rows, BLOCK)
+
+    dense_grad, starts = plan.join_rows(exchange(rows_of(packed[:, :first_slots])))
+    extra_grad, starts = plan.join_rows(exchange_last(rows_of(packed[:, first_slots:])))
     is_dense = (my_unit >= 0) & (my_place < 0) & ~is_time
     right = jnp.where(is_time[None, :, None], time_cols, slot_grad_out)
     left = jnp.where(is_time[:, None, None], time_act.T[None], cond_act.T[None])
-    flags = [rate_factor * unit_scale(jnp.maximum(my_unit, 0)), my_unit >= 0, is_dense]
+    in_first = my_rank < first_slots
+    flags = [rate_factor * unit_scale(jnp.maximum(my_unit, 0)), my_unit >= 0]
+    flags += [is_dense & in_first, is_dense & ~in_first, ~is_dense]
+    picks = [jnp.minimum(my_rank, first_slots - 1), jnp.maximum(my_rank - first_slots, 0)]
     flags = jnp.stack([flag.astype(jnp.float32) for flag in flags], 1)
     new_slots = adam_slots(
         dense_grad,
+        extra_grad,
         starts,
         flags,
+        jnp.stack(picks, 1),
         left,
         jnp.swapaxes(right, 0, 1),
         *[jnp.swapaxes(values, 0, 1) for values in (master, first_moment, second_moment)],

time: 660 us -> 636 us (0.964)
  waiting for transfers between devices: 73 us -> 49.2 us
  local copies, waits for them, and re-layouts: 43.3 us -> 55.7 us
  Pallas kernels: 392 us -> 385 us
    all_to_all x2, waiting for transfers between devices: 73 us -> 49.2 us  [exchange(): return lax.all_to_all(blocks, AXES, split_axis=0, concat_axis=0, tiled=True)]
    unnamed x129 -> x138, local copies, waits for them, and re-layouts: 14.5 us -> 17.6 us
  transfers between devices with their start and end apart: 2 -> 2, of which waited for: 2 -> 2; matrix products, arithmetic and copies ran while one was open for 9% -> 8% of each run, Pallas kernels for 0% -> 0%
where the time goes in v10:
time: 636 us; the launch traced here: 631 us
  Pallas kernels  385 us (61%)
  matrix products  80.9 us (13%)
  local copies, waits for them, and re-layouts  55.7 us (9%)
  waiting for transfers between devices  49.2 us (8%)
  other arithmetic  40.9 us (6%)
  starting transfers between devices  13.8 us (2%)
    pallas_call x1, Pallas kernels, scatter(): pl.pallas_call(lambda *refs: scatter_kernel(widths, bases, slots, *refs),...  163 us
    pallas_call x1, Pallas kernels, gather(): pl.pallas_call(lambda *refs: gather_kernel(widths, bases, *refs), out_sha...  160 us
    dot_general x23, matrix products, dot_low(): jnp.einsum(pattern, left_side, right_side, preferred_element_type=jnp.flo...  79.7 us
    all_to_all x2, waiting for transfers between devices, exchange(): return lax.all_to_all(blocks, AXES, split_axis=0, concat_axis=0, tiled=True)  49.2 us
    pallas_call x2, Pallas kernels, attend_back(): pl.pallas_call(attend_back_kernel, grid=(images, steps), out_shape=jax.Sh...  24.6 us
    pallas_call x2, Pallas kernels, attend(): pl.pallas_call(attend_kernel, grid=(images, steps), out_shape=jax.ShapeDt...  21.4 us
    unnamed x138, local copies, waits for them, and re-layouts  17.6 us
    pallas_call x1, Pallas kernels, adam_slots(): pl.pallas_call(lambda *refs: adam_kernel(starts, *refs), grid=(slots // s...  16.2 us
  transfers between devices with their start and end apart: 2, of which 2 were waited for; matrix products, arithmetic and copies ran while one was open for 8% of the time, Pallas kernels for 0%

profile of v10, /device:TPU:3, one launch (start us, length us, event | category | flops | bytes accessed | tf_op | source)
XLA Modules:
  0.0 630.6 jit_solution(6806572738649244868)
XLA Ops:
  2.7 3.6 gather_fusion.2
  19.1 7.0 %all-to-all-start.2 = ((bf16[32,11,24,128]{3,2,1,0:T(8,128)(2,1)}), bf16[32,11,24,128]{3,2,1,0:T(8,128)(2,1)}, u32[]{:S(2)}, u32[]{:S(2)}) async-start(bf16[32,11,24,128]{3,2,1,0:T(8,128)(2,1)} %slice.129), calls=%async_computation.2 | async-start | bytes 4325376 | tf_op jit(solution)/shard_map/all_to_all | solution.py:1060
  26.1 3.7 convert_element_type.169
  40.4 3.5 gather_fusion.9
  52.3 23.9 %all-to-all-done.2 = bf16[32,11,24,128]{3,2,1,0:T(8,128)(2,1)} async-done(((bf16[32,11,24,128]{3,2,1,0:T(8,128)(2,1)}), bf16[32,11,24,128]{3,2,1,0:T(8,128)(2,1)}, u32[]{:S(2)}, u32[]{:S(2)}) %all-to-all-start.2) | async-done | bytes 2162720 | tf_op jit(solution)/shard_map/all_to_all | solution.py:1060
  76.2 160.0 %shard_map.242 = (bf16[2,2,2,4,24,768]{5,4,3,2,1,0:T(8,128)(2,1)}, bf16[2,2,2,4,24,2304]{5,4,3,2,1,0:T(8,128)(2,1)}, bf16[2,2,2,4,24,3072]{5,4,3,2,1,0:T(8,128)(...) custom-call(s32[2,150]{1,0:T(2,128)} %pad_add_fusion.refs_0_, ...), custom_call_target="tpu_custom_call" | custom-call | bytes 58982400 | tf_op jit(solution)/shard_map/pallas_call | solution.py:876
  239.5 5.4 convolution_convert_fusion.1.queries.keys_all.values
  244.9 10.9 %shard_map.243 = bf16[2,256,768]{2,1,0:T(8,128)(2,1)} custom-call(bf16[2,256,2304]{2,1,0:T(8,128)(2,1)} %convolution_convert_fusion.1.queries.keys_all.values, bf16[2,256,2304]{2,1,0:T(8,128)(2,1)} %convolution_convert_fusion.1.queries.keys_all.values, bf16[2,256,2304]{2,1,0:T(8,128)(2,1)} %convolution_convert_fusion.1.queries.keys_all.values), custom_call_target="tpu_custom_call" | custom-call | flops 402653184 | bytes 3145728 | tf_op jit(solution)/shard_map/pallas_call | solution.py:288
  255.8 3.4 fusion.114
  259.9 8.2 %fusion.15 = (bf16[2,256,3072]{2,1,0:T(8,128)(2,1)S(1)}, bf16[2,256,3072]{2,1,0:T(8,128)(2,1)}) fusion(bf16[2,256,768]{2,1,0:T(8,128)(2,1)S(1)} %add_convert_fusion.4, bf16[768,3072,1]{1,0,2:T(8,128)(2,1)} %bitcast.252), kind=kOutput, calls=%fused_computation.40 | convolution fusion | flops 2431647744 | bytes 11796480 | tf_op jit(solution)/shard_map/gpd,df->gpf/dot_general | solution.py:55
  268.1 3.8 fusion.113
  278.2 10.6 %shard_map.244 = bf16[2,256,768]{2,1,0:T(8,128)(2,1)} custom-call(bf16[2,256,2304]{2,1,0:T(8,128)(2,1)} %convolution_convert_fusion.queries.keys_all.values, bf16[2,256,2304]{2,1,0:T(8,128)(2,1)} %convolution_convert_fusion.queries.keys_all.values, bf16[2,256,2304]{2,1,0:T(8,128)(2,1)} %convolution_convert_fusion.queries.keys_all.values), custom_call_target="tpu_custom_call" | custom-call | flops 402653184 | bytes 3145728 | tf_op jit(solution)/shard_map/pallas_call | solution.py:288
  292.4 7.1 %fusion.23 = (bf16[2,256,3072]{2,1,0:T(8,128)(2,1)S(1)}, bf16[2,256,3072]{2,1,0:T(8,128)(2,1)S(1)}) fusion(bf16[2,256,768]{2,1,0:T(8,128)(2,1)S(1)} %add_convert_fusion.2, bf16[768,3072,1]{1,0,2:T(8,128)(2,1)} %bitcast.262), kind=kOutput, calls=%fused_computation.48 | convolution fusion | flops 2431647744 | bytes 11796480 | tf_op jit(solution)/shard_map/gpd,df->gpf/dot_general | solution.py:55
  308.4 6.5 %fusion.7 = bf16[2,256,3072]{2,1,0:T(8,128)(2,1)S(1)} fusion(bf16[2,256,768]{2,1,0:T(8,128)(2,1)S(1)} %get-tuple-element.113, bf16[768,3072,1]{1,0,2:T(8,128)(2,1)S(1)} %bitcast.269, bf16[2,256,3072]{2,1,0:T(8,128)(2,1)S(1)} %get-tuple-element.168), kind=kOutput, calls=%fused_computation.32 | convolution fusion | flops 2448949248 | bytes 11796480 | tf_op jit(solution)/shard_map/gpd,df->gpf/dot_general | solution.py:55
  323.4 12.2 %shard_map.245 = bf16[2,256,2304]{2,1,0:T(8,128)(2,1)} custom-call(bf16[2,256,2304]{2,1,0:T(8,128)(2,1)} %convolution_convert_fusion.queries.keys_all.values, bf16[2,256,2304]{2,1,0:T(8,128)(2,1)} %convolution_convert_fusion.queries.keys_all.values, bf16[2,256,2304]{2,1,0:T(8,128)(2,1)} %convolution_convert_fusion.queries.keys_all.values, ...), custom_call_target="tpu_custom_call" | custom-call | flops 1006632960 | bytes 5505024 | tf_op jit(solution)/shard_map/pallas_call | solution.py:305
  335.6 5.4 multiply_reduce_fusion.11
  345.2 6.7 %fusion.4 = bf16[2,256,3072]{2,1,0:T(8,128)(2,1)S(1)} fusion(bf16[2,256,768]{2,1,0:T(8,128)(2,1)S(1)} %multiply_convert_fusion.1, bf16[768,3072,1]{1,0,2:T(8,128)(2,1)S(1)} %bitcast.261, bf16[2,256,3072]{2,1,0:T(8,128)(2,1)S(1)} %copy-done.48), kind=kOutput, calls=%fused_computation.29 | convolution fusion | flops 2448949248 | bytes 11796480 | tf_op jit(solution)/shard_map/gpd,df->gpf/dot_general | solution.py:55
  360.8 12.4 %shard_map.246 = bf16[2,256,2304]{2,1,0:T(8,128)(2,1)} custom-call(bf16[2,256,2304]{2,1,0:T(8,128)(2,1)} %convolution_convert_fusion.1.queries.keys_all.values, bf16[2,256,2304]{2,1,0:T(8,128)(2,1)} %convolution_convert_fusion.1.queries.keys_all.values, bf16[2,256,2304]{2,1,0:T(8,128)(2,1)} %convolution_convert_fusion.1.queries.keys_all.values, ...), custom_call_target="tpu_custom_call" | custom-call | flops 1006632960 | bytes 5505024 | tf_op jit(solution)/shard_map/pallas_call | solution.py:305
  373.1 4.9 multiply_reduce_fusion
  385.1 162.7 %shard_map.247 = (bf16[144,24,128]{2,1,0:T(8,128)(2,1)S(1)}, f32[64,16,128]{2,1,0:T(8,128)}, f32[2,2,2,4,2,16,128]{6,5,4,3,2,1,0:T(8,128)}) custom-call(bf16[512,768]{1,0:T(8,128)(2,1)} %bitcast.205, bf16[512,768]{1,0:T(8,128)(2,1)} %bitcast.214, bf16[512,768]{1,0:T(8,128)(2,1)} %bitcast.215, bf16[512,768]{1,0:T(8,128)(2,1)} %bitcast.219, ...), custom_call_target="tpu_custom_call" | custom-call | bytes 56623104 | tf_op jit(solution)/shard_map/pallas_call | solution.py:929
  553.3 6.8 %all-to-all-start.3 = ((bf16[32,11,24,128]{3,2,1,0:T(8,128)(2,1)}), bf16[32,11,24,128]{3,2,1,0:T(8,128)(2,1)}, u32[]{:S(2)}, u32[]{:S(2)}) async-start(bf16[32,11,24,128]{3,2,1,0:T(8,128)(2,1)} %bitcast.77), calls=%async_computation.3 | async-start | bytes 4325376 | tf_op jit(solution)/shard_map/all_to_all | solution.py:1060
  574.6 10.5 %multiply_subtract_fusion = (f32[1288,768]{1,0:T(8,128)}, f32[1288,768]{1,0:T(8,128)}, f32[1288,768]{1,0:T(8,128)}) fusion(f32[1288,768]{1,0:T(8,128)} %param.31, f32[1288]{0:T(1024)S(1)} %copy-done.35, f32[16,768]{1,0:T(8,128)S(1)} %bitcast.236, f32[1000,768]{1,0:T(8,128)S(1)} %copy-done.11, f32[256,768]{1,0:T(8,128)} %fusion.56, ...), kind=kLoop, calls=%fused_computation.65 | loop fusion | flops 16816128 | bytes 27702304 | tf_op jit(solution)/shard_map/sub | solution.py:105
  585.1 25.3 %all-to-all-done.3.refs_2_ = bf16[32,11,24,128]{3,2,1,0:T(8,128)(2,1)} async-done(((bf16[32,11,24,128]{3,2,1,0:T(8,128)(2,1)}), bf16[32,11,24,128]{3,2,1,0:T(8,128)(2,1)}, u32[]{:S(2)}, u32[]{:S(2)}) %all-to-all-start.3) | async-done | bytes 2162720 | tf_op jit(solution)/shard_map/all_to_all | solution.py:1060
  613.1 16.2 %shard_map.248 = (f32[15,768,128]{2,1,0:T(8,128)}, f32[15,768,128]{2,1,0:T(8,128)}, f32[15,768,128]{2,1,0:T(8,128)}) custom-call(f32[15,5]{1,0:T(8,128)S(1)} %stack.68.refs_0_, s32[15,2]{1,0:T(8,128)S(1)} %copy.159.refs_1_, bf16[32,11,24,128]{3,2,1,0:T(8,128)(2,1)} %all-to-all-done.3.refs_2_, bf16[32,4,24,128]{3,2,1,0:T(8,128)(2,1)} %copy-done.14, ...), custom_call_target="tpu_custom_call" | custom-call | flops 58982400 | bytes 38338560 | tf_op jit(solution)/shard_map/pallas_call | solution.py:355
  (324 shorter events, 105.0 us)
Async XLA Ops:
  19.1 57.1 %all-to-all-start.2 = ((bf16[32,11,24,128]{3,2,1,0:T(8,128)(2,1)}), bf16[32,11,24,128]{3,2,1,0:T(8,128)(2,1)}, u32[]{:S(2)}, u32[]{:S(2)}) async-start(bf16[32,11,24,128]{3,2,1,0:T(8,128)(2,1)} %slice.129), calls=%async_computation.2 | async-start | bytes 4325376 | tf_op jit(solution)/shard_map/all_to_all | solution.py:1060
  26.1 11.6 %copy-start.39 = (f32[128]{0:T(128)}, f32[128]{0:T(128)S(1)}, u32[]{:S(2)}) copy-start(f32[128]{0:T(128)S(1)} %multiply_exponential_fusion.1) | copy-start | bytes 1540
  29.8 3.8 copy-start.36
  29.8 4.0 copy-start.37
  29.8 4.3 copy-start.45
  29.9 4.5 copy-start.42
  33.9 5.3 slice-start
  34.0 6.4 %copy-start.1 = (s32[235]{0:T(256)S(1)}, s32[235]{0:T(256)}, u32[]{:S(2)}) copy-start(s32[235]{0:T(256)} %constant.304.clone) | copy-start | bytes 2824
  50.1 26.2 %copy-start.16 = (bf16[128,24,128]{2,1,0:T(8,128)(2,1)S(1)}, bf16[128,24,128]{2,1,0:T(8,128)(2,1)}, u32[]{:S(2)}) copy-start(bf16[128,24,128]{2,1,0:T(8,128)(2,1)} %copy-done.15) | copy-start | bytes 2359300
  259.5 8.6 %slice-start.3 = ((s8[4718592]{0:T(1024)(128)(4,1)}), s8[4194304]{0:T(1024)(128)(4,1)S(1)}, s32[]{:S(2)}) async-start(s8[4718592]{0:T(1024)(128)(4,1)} %bitcast.256), calls=%async_computation.7 | async-start | bytes 8388608
  259.9 8.2 %copy-start.22 = (bf16[2,256,768]{2,1,0:T(8,128)(2,1)}, bf16[2,256,768]{2,1,0:T(8,128)(2,1)S(1)}, u32[]{:S(2)}) copy-start(bf16[2,256,768]{2,1,0:T(8,128)(2,1)S(1)} %add_convert_fusion.4) | copy-start | bytes 2359300
  259.9 8.2 %slice-start.4 = ((s8[4718592]{0:T(1024)(128)(4,1)}), s8[524288]{0:T(1024)(128)(4,1)S(1)}, s32[]{:S(2)}) async-start(s8[4718592]{0:T(1024)(128)(4,1)} %bitcast.256), calls=%async_computation.8 | async-start | bytes 1048576
  268.1 3.8 copy-start.17
  292.0 7.5 %slice-start.9 = ((s8[4718592]{0:T(1024)(128)(4,1)}), s8[4194304]{0:T(1024)(128)(4,1)S(1)}, s32[]{:S(2)}) async-start(s8[4718592]{0:T(1024)(128)(4,1)} %bitcast.266), calls=%async_computation.13 | async-start | bytes 8388608
  292.3 7.1 %copy-start.24 = (bf16[2,256,768]{2,1,0:T(8,128)(2,1)}, bf16[2,256,768]{2,1,0:T(8,128)(2,1)S(1)}, u32[]{:S(2)}) copy-start(bf16[2,256,768]{2,1,0:T(8,128)(2,1)S(1)} %add_convert_fusion.2) | copy-start | bytes 2359300
  292.3 7.2 %slice-start.10 = ((s8[4718592]{0:T(1024)(128)(4,1)}), s8[524288]{0:T(1024)(128)(4,1)S(1)}, s32[]{:S(2)}) async-start(s8[4718592]{0:T(1024)(128)(4,1)} %bitcast.266), calls=%async_computation.14 | async-start | bytes 1048576
  307.2 7.8 %slice-start.7 = ((s8[4718592]{0:T(1024)(128)(4,1)}), s8[524288]{0:T(1024)(128)(4,1)S(1)}, s32[]{:S(2)}) async-start(s8[4718592]{0:T(1024)(128)(4,1)} %bitcast.263), calls=%async_computation.11 | async-start | bytes 1048576
  308.4 6.5 %slice-start.8 = ((s8[4718592]{0:T(1024)(128)(4,1)}), s8[4194304]{0:T(1024)(128)(4,1)S(1)}, s32[]{:S(2)}) async-start(s8[4718592]{0:T(1024)(128)(4,1)} %bitcast.263), calls=%async_computation.12 | async-start | bytes 8388608
  335.6 5.5 copy-start.6
  335.6 9.1 %slice-start.5 = ((s8[4718592]{0:T(1024)(128)(4,1)}), s8[4194304]{0:T(1024)(128)(4,1)S(1)}, s32[]{:S(2)}) async-start(s8[4718592]{0:T(1024)(128)(4,1)} %bitcast.259), calls=%async_computation.9 | async-start | bytes 8388608
  343.0 8.9 %slice-start.1 = ((s8[4718592]{0:T(1024)(128)(4,1)}), s8[4194304]{0:T(1024)(128)(4,1)S(1)}, s32[]{:S(2)}) async-start(s8[4718592]{0:T(1024)(128)(4,1)} %bitcast.253), calls=%async_computation.5 | async-start | bytes 8388608
  345.2 6.7 %slice-start.2 = ((s8[4718592]{0:T(1024)(128)(4,1)}), s8[524288]{0:T(1024)(128)(4,1)S(1)}, s32[]{:S(2)}) async-start(s8[4718592]{0:T(1024)(128)(4,1)} %bitcast.253), calls=%async_computation.6 | async-start | bytes 1048576
  380.0 3.8 copy-start.34
  553.3 57.1 %all-to-all-start.3 = ((bf16[32,11,24,128]{3,2,1,0:T(8,128)(2,1)}), bf16[32,11,24,128]{3,2,1,0:T(8,128)(2,1)}, u32[]{:S(2)}, u32[]{:S(2)}) async-start(bf16[32,11,24,128]{3,2,1,0:T(8,128)(2,1)} %bitcast.77), calls=%async_computation.3 | async-start | bytes 4325376 | tf_op jit(solution)/shard_map/all_to_all | solution.py:1060
  (38 other events, 73.3 us)

commit v11 on v10

--- a/solution.py
+++ b/solution.py
@@ -1042,14 +1042,17 @@
 
     plan = RingPlan() if (lax.axis_size("rep"), lax.axis_size("shard")) == (8, 4) else PlainPlan()
     moved = np.concatenate([dense_units, time_units])
-    is_moved = np.zeros((UNITS + 1,), np.int32)
-    is_moved[moved] = 1
-    needed = jnp.asarray(is_moved)[unit_of_slot].reshape(count, slot_dev)
+    in_layers = (unit_of_slot >= 0) & (unit_of_slot < TAIL_FIRST)
+    needed = in_layers & (unit_of_slot % LAYER_UNITS >= ADA_UNITS)
+    slot_place = unit_of_slot // LAYER_UNITS * DENSE_UNITS + unit_of_slot % LAYER_UNITS
+    slot_place = jnp.where(needed, slot_place - ADA_UNITS, 0)
+    needed = needed | (unit_of_slot >= TAIL_FIRST) & (unit_of_slot < TAIL_FIRST + TIME_UNITS)
+    needed = needed.astype(jnp.int32).reshape(count, slot_dev)
     total_needed = jnp.sum(needed, 1, keepdims=True)
     before = jnp.cumsum(needed, 1)
     turn = jnp.arange(slot_dev, dtype=jnp.int32)[None]
     rank = jnp.where(needed > 0, before - 1, total_needed + turn - before)
-    first_slots = max(1, 3 * slot_dev // 4)
+    first_slots = max(1, 2 * slot_dev // 3)
     last_slots = slot_dev - first_slots
     overflow = jnp.max(total_needed) > first_slots
     by_rank = (rank[:, :, None] == turn[:, None]).astype(jnp.int32)
@@ -1182,9 +1185,6 @@
     my_time = jnp.clip(my_unit - TAIL_FIRST, 0, TIME_UNITS - 1)
     is_time = (my_unit >= TAIL_FIRST) & (my_unit < TAIL_FIRST + TIME_UNITS)
     time_cols = jnp.take(grad_time_out.reshape(all_images, TIME_UNITS, BLOCK), my_time, axis=1)
-    dense_place = np.full((UNITS + 1,), 0, np.int32)
-    dense_place[dense_units] = np.arange(len(dense_units))
-    slot_place = jnp.asarray(dense_place)[unit_of_slot]
     packed = jnp.sum(by_rank * slot_place.reshape(count, slot_dev, 1), 1)
 
     def rows_of(places_of):

time: 636 us -> 624 us (0.981)
  local copies, waits for them, and re-layouts: 55.7 us -> 48.2 us
    gather x2 -> x0, local copies, waits for them, and re-layouts: 7.12 us -> none  [the longest x1 3.62 us: on_device(): needed = jnp.asarray(is_moved)[unit_of_slot].reshape(count, slot_dev)]
    unnamed x138 -> x136, local copies, waits for them, and re-layouts: 17.6 us -> 17.2 us
  transfers between devices with their start and end apart: 2 -> 2, of which waited for: 2 -> 2; matrix products, arithmetic and copies ran while one was open for 8% -> 7% of each run, Pallas kernels for 0% -> 0%
where the time goes in v11:
time: 624 us; the launch traced here: 618 us
  Pallas kernels  385 us (62%)
  matrix products  80.9 us (13%)
  local copies, waits for them, and re-layouts  48.2 us (8%)
  waiting for transfers between devices  43.4 us (7%)
  other arithmetic  41.8 us (7%)
  starting transfers between devices  13.4 us (2%)
    pallas_call x1, Pallas kernels, scatter(): pl.pallas_call(lambda *refs: scatter_kernel(widths, bases, slots, *refs),...  163 us
    pallas_call x1, Pallas kernels, gather(): pl.pallas_call(lambda *refs: gather_kernel(widths, bases, *refs), out_sha...  160 us
    dot_general x23, matrix products, dot_low(): jnp.einsum(pattern, left_side, right_side, preferred_element_type=jnp.flo...  79.7 us
    all_to_all x2, waiting for transfers between devices, exchange(): return lax.all_to_all(blocks, AXES, split_axis=0, concat_axis=0, tiled=True)  43.4 us
    pallas_call x2, Pallas kernels, attend_back(): pl.pallas_call(attend_back_kernel, grid=(images, steps), out_shape=jax.Sh...  24.8 us
    pallas_call x2, Pallas kernels, attend(): pl.pallas_call(attend_kernel, grid=(images, steps), out_shape=jax.ShapeDt...  21.4 us
    unnamed x136, local copies, waits for them, and re-layouts  17.2 us
    pallas_call x1, Pallas kernels, adam_slots(): pl.pallas_call(lambda *refs: adam_kernel(starts, *refs), grid=(slots // s...  16.2 us
  transfers between devices with their start and end apart: 2, of which 2 were waited for; matrix products, arithmetic and copies ran while one was open for 7% of the time, Pallas kernels for 0%

profile of v11, /device:TPU:3, one launch (start us, length us, event | category | flops | bytes accessed | tf_op | source)
XLA Modules:
  0.0 618.3 jit_solution(411805222999381035)
XLA Ops:
  3.1 3.2 convert_bitcast_fusion.refs_5_.refs_18_
  15.5 6.8 %all-to-all-start.2 = ((bf16[32,10,24,128]{3,2,1,0:T(8,128)(2,1)}), bf16[32,10,24,128]{3,2,1,0:T(8,128)(2,1)}, u32[]{:S(2)}, u32[]{:S(2)}) async-start(bf16[32,10,24,128]{3,2,1,0:T(8,128)(2,1)} %slice.125), calls=%async_computation.2 | async-start | bytes 3932160 | tf_op jit(solution)/shard_map/all_to_all | solution.py:1063
  22.4 3.7 convert_element_type.172
  44.6 23.3 %all-to-all-done.2 = bf16[32,10,24,128]{3,2,1,0:T(8,128)(2,1)} async-done(((bf16[32,10,24,128]{3,2,1,0:T(8,128)(2,1)}), bf16[32,10,24,128]{3,2,1,0:T(8,128)(2,1)}, u32[]{:S(2)}, u32[]{:S(2)}) %all-to-all-start.2) | async-done | bytes 1966112 | tf_op jit(solution)/shard_map/all_to_all | solution.py:1063
  67.9 160.2 %shard_map.224 = (bf16[2,2,2,4,24,768]{5,4,3,2,1,0:T(8,128)(2,1)}, bf16[2,2,2,4,24,2304]{5,4,3,2,1,0:T(8,128)(2,1)}, bf16[2,2,2,4,24,3072]{5,4,3,2,1,0:T(8,128)(...) custom-call(s32[2,150]{1,0:T(2,128)} %pad_add_fusion.refs_0_, ...), custom_call_target="tpu_custom_call" | custom-call | bytes 58982400 | tf_op jit(solution)/shard_map/pallas_call | solution.py:876
  230.6 5.7 convolution_convert_fusion.1.queries.keys_all.values
  236.2 10.6 %shard_map.225 = bf16[2,256,768]{2,1,0:T(8,128)(2,1)} custom-call(bf16[2,256,2304]{2,1,0:T(8,128)(2,1)} %convolution_convert_fusion.1.queries.keys_all.values, bf16[2,256,2304]{2,1,0:T(8,128)(2,1)} %convolution_convert_fusion.1.queries.keys_all.values, bf16[2,256,2304]{2,1,0:T(8,128)(2,1)} %convolution_convert_fusion.1.queries.keys_all.values), custom_call_target="tpu_custom_call" | custom-call | flops 402653184 | bytes 3145728 | tf_op jit(solution)/shard_map/pallas_call | solution.py:288
  246.8 3.4 fusion.115
  250.9 8.2 %fusion.15 = (bf16[2,256,3072]{2,1,0:T(8,128)(2,1)S(1)}, bf16[2,256,3072]{2,1,0:T(8,128)(2,1)}) fusion(bf16[2,256,768]{2,1,0:T(8,128)(2,1)S(1)} %add_convert_fusion.4, bf16[768,3072,1]{1,0,2:T(8,128)(2,1)} %bitcast.252), kind=kOutput, calls=%fused_computation.38 | convolution fusion | flops 2431647744 | bytes 11796480 | tf_op jit(solution)/shard_map/gpd,df->gpf/dot_general | solution.py:55
  259.2 3.8 fusion.114
  265.8 3.4 convolution_convert_fusion.queries.keys_all.values
  269.3 10.8 %shard_map.226 = bf16[2,256,768]{2,1,0:T(8,128)(2,1)} custom-call(bf16[2,256,2304]{2,1,0:T(8,128)(2,1)} %convolution_convert_fusion.queries.keys_all.values, bf16[2,256,2304]{2,1,0:T(8,128)(2,1)} %convolution_convert_fusion.queries.keys_all.values, bf16[2,256,2304]{2,1,0:T(8,128)(2,1)} %convolution_convert_fusion.queries.keys_all.values), custom_call_target="tpu_custom_call" | custom-call | flops 402653184 | bytes 3145728 | tf_op jit(solution)/shard_map/pallas_call | solution.py:288
  283.6 7.1 %fusion.23 = (bf16[2,256,3072]{2,1,0:T(8,128)(2,1)S(1)}, bf16[2,256,3072]{2,1,0:T(8,128)(2,1)S(1)}) fusion(bf16[2,256,768]{2,1,0:T(8,128)(2,1)S(1)} %add_convert_fusion.2, bf16[768,3072,1]{1,0,2:T(8,128)(2,1)} %bitcast.262), kind=kOutput, calls=%fused_computation.46 | convolution fusion | flops 2431647744 | bytes 11796480 | tf_op jit(solution)/shard_map/gpd,df->gpf/dot_general | solution.py:55
  299.7 6.5 %fusion.7 = bf16[2,256,3072]{2,1,0:T(8,128)(2,1)S(1)} fusion(bf16[2,256,768]{2,1,0:T(8,128)(2,1)S(1)} %get-tuple-element.113, bf16[768,3072,1]{1,0,2:T(8,128)(2,1)S(1)} %bitcast.269, bf16[2,256,3072]{2,1,0:T(8,128)(2,1)S(1)} %get-tuple-element.170), kind=kOutput, calls=%fused_computation.30 | convolution fusion | flops 2448949248 | bytes 11796480 | tf_op jit(solution)/shard_map/gpd,df->gpf/dot_general | solution.py:55
  314.7 12.2 %shard_map.227 = bf16[2,256,2304]{2,1,0:T(8,128)(2,1)} custom-call(bf16[2,256,2304]{2,1,0:T(8,128)(2,1)} %convolution_convert_fusion.queries.keys_all.values, bf16[2,256,2304]{2,1,0:T(8,128)(2,1)} %convolution_convert_fusion.queries.keys_all.values, bf16[2,256,2304]{2,1,0:T(8,128)(2,1)} %convolution_convert_fusion.queries.keys_all.values, ...), custom_call_target="tpu_custom_call" | custom-call | flops 1006632960 | bytes 5505024 | tf_op jit(solution)/shard_map/pallas_call | solution.py:305
  326.9 5.4 multiply_reduce_fusion.11
  336.5 6.5 %fusion.4 = bf16[2,256,3072]{2,1,0:T(8,128)(2,1)S(1)} fusion(bf16[2,256,768]{2,1,0:T(8,128)(2,1)S(1)} %multiply_convert_fusion.1, bf16[768,3072,1]{1,0,2:T(8,128)(2,1)S(1)} %bitcast.261, bf16[2,256,3072]{2,1,0:T(8,128)(2,1)S(1)} %copy-done.47), kind=kOutput, calls=%fused_computation.27 | convolution fusion | flops 2448949248 | bytes 11796480 | tf_op jit(solution)/shard_map/gpd,df->gpf/dot_general | solution.py:55
  351.5 12.6 %shard_map.228 = bf16[2,256,2304]{2,1,0:T(8,128)(2,1)} custom-call(bf16[2,256,2304]{2,1,0:T(8,128)(2,1)} %convolution_convert_fusion.1.queries.keys_all.values, bf16[2,256,2304]{2,1,0:T(8,128)(2,1)} %convolution_convert_fusion.1.queries.keys_all.values, bf16[2,256,2304]{2,1,0:T(8,128)(2,1)} %convolution_convert_fusion.1.queries.keys_all.values, ...), custom_call_target="tpu_custom_call" | custom-call | flops 1006632960 | bytes 5505024 | tf_op jit(solution)/shard_map/pallas_call | solution.py:305
  364.1 4.9 multiply_reduce_fusion
  376.8 162.9 %shard_map.229 = (bf16[144,24,128]{2,1,0:T(8,128)(2,1)S(1)}, f32[64,16,128]{2,1,0:T(8,128)}, f32[2,2,2,4,2,16,128]{6,5,4,3,2,1,0:T(8,128)}) custom-call(bf16[512,768]{1,0:T(8,128)(2,1)} %bitcast.205, bf16[512,768]{1,0:T(8,128)(2,1)} %bitcast.214, bf16[512,768]{1,0:T(8,128)(2,1)} %bitcast.215, bf16[512,768]{1,0:T(8,128)(2,1)} %bitcast.219, ...), custom_call_target="tpu_custom_call" | custom-call | bytes 56623104 | tf_op jit(solution)/shard_map/pallas_call | solution.py:929
  545.8 6.6 %all-to-all-start.3 = ((bf16[32,10,24,128]{3,2,1,0:T(8,128)(2,1)}), bf16[32,10,24,128]{3,2,1,0:T(8,128)(2,1)}, u32[]{:S(2)}, u32[]{:S(2)}) async-start(bf16[32,10,24,128]{3,2,1,0:T(8,128)(2,1)} %bitcast.77), calls=%async_computation.3 | async-start | bytes 3932160 | tf_op jit(solution)/shard_map/all_to_all | solution.py:1063
  567.6 10.5 %multiply_subtract_fusion = (f32[1288,768]{1,0:T(8,128)}, f32[1288,768]{1,0:T(8,128)}, f32[1288,768]{1,0:T(8,128)}) fusion(f32[1288,768]{1,0:T(8,128)} %param.29, f32[1288]{0:T(1024)S(1)} %copy-done.35, f32[16,768]{1,0:T(8,128)S(1)} %bitcast.236, f32[1000,768]{1,0:T(8,128)S(1)} %copy-done.10, f32[256,768]{1,0:T(8,128)} %fusion.56, ...), kind=kLoop, calls=%fused_computation.63 | loop fusion | flops 16816128 | bytes 27702304 | tf_op jit(solution)/shard_map/sub | solution.py:105
  578.1 20.1 %all-to-all-done.3.refs_2_ = bf16[32,10,24,128]{3,2,1,0:T(8,128)(2,1)} async-done(((bf16[32,10,24,128]{3,2,1,0:T(8,128)(2,1)}), bf16[32,10,24,128]{3,2,1,0:T(8,128)(2,1)}, u32[]{:S(2)}, u32[]{:S(2)}) %all-to-all-start.3) | async-done | bytes 1966112 | tf_op jit(solution)/shard_map/all_to_all | solution.py:1063
  600.8 16.2 %shard_map.230 = (f32[15,768,128]{2,1,0:T(8,128)}, f32[15,768,128]{2,1,0:T(8,128)}, f32[15,768,128]{2,1,0:T(8,128)}) custom-call(f32[15,5]{1,0:T(8,128)S(1)} %stack.68.refs_0_, s32[15,2]{1,0:T(8,128)S(1)} %copy.157.refs_1_, bf16[32,10,24,128]{3,2,1,0:T(8,128)(2,1)} %all-to-all-done.3.refs_2_, bf16[32,5,24,128]{3,2,1,0:T(8,128)(2,1)} %copy-done.15, ...), custom_call_target="tpu_custom_call" | custom-call | flops 58982400 | bytes 38338560 | tf_op jit(solution)/shard_map/pallas_call | solution.py:355
  (319 shorter events, 98.8 us)
Async XLA Ops:
  15.5 52.4 %all-to-all-start.2 = ((bf16[32,10,24,128]{3,2,1,0:T(8,128)(2,1)}), bf16[32,10,24,128]{3,2,1,0:T(8,128)(2,1)}, u32[]{:S(2)}, u32[]{:S(2)}) async-start(bf16[32,10,24,128]{3,2,1,0:T(8,128)(2,1)} %slice.125), calls=%async_computation.2 | async-start | bytes 3932160 | tf_op jit(solution)/shard_map/all_to_all | solution.py:1063
  22.3 11.1 %copy-start.39 = (f32[128]{0:T(128)}, f32[128]{0:T(128)S(1)}, u32[]{:S(2)}) copy-start(f32[128]{0:T(128)S(1)} %multiply_exponential_fusion.1) | copy-start | bytes 1540
  26.1 3.5 copy-start.37
  26.1 3.8 copy-start.44
  26.1 4.0 copy-start.42
  29.6 5.3 slice-start
  42.3 25.6 %copy-start.14 = (bf16[160,24,128]{2,1,0:T(8,128)(2,1)S(1)}, bf16[160,24,128]{2,1,0:T(8,128)(2,1)}, u32[]{:S(2)}) copy-start(bf16[160,24,128]{2,1,0:T(8,128)(2,1)} %copy-done.13) | copy-start | bytes 2949124
  230.5 5.7 copy-start.20
  250.6 8.6 %slice-start.3 = ((s8[4718592]{0:T(1024)(128)(4,1)}), s8[4194304]{0:T(1024)(128)(4,1)S(1)}, s32[]{:S(2)}) async-start(s8[4718592]{0:T(1024)(128)(4,1)} %bitcast.256), calls=%async_computation.7 | async-start | bytes 8388608
  250.9 8.2 %copy-start.21 = (bf16[2,256,768]{2,1,0:T(8,128)(2,1)}, bf16[2,256,768]{2,1,0:T(8,128)(2,1)S(1)}, u32[]{:S(2)}) copy-start(bf16[2,256,768]{2,1,0:T(8,128)(2,1)S(1)} %add_convert_fusion.4) | copy-start | bytes 2359300
  250.9 8.2 %slice-start.4 = ((s8[4718592]{0:T(1024)(128)(4,1)}), s8[524288]{0:T(1024)(128)(4,1)S(1)}, s32[]{:S(2)}) async-start(s8[4718592]{0:T(1024)(128)(4,1)} %bitcast.256), calls=%async_computation.8 | async-start | bytes 1048576
  259.1 3.8 copy-start.16
  283.3 7.5 %slice-start.9 = ((s8[4718592]{0:T(1024)(128)(4,1)}), s8[4194304]{0:T(1024)(128)(4,1)S(1)}, s32[]{:S(2)}) async-start(s8[4718592]{0:T(1024)(128)(4,1)} %bitcast.266), calls=%async_computation.13 | async-start | bytes 8388608
  283.6 7.2 %copy-start.23 = (bf16[2,256,768]{2,1,0:T(8,128)(2,1)}, bf16[2,256,768]{2,1,0:T(8,128)(2,1)S(1)}, u32[]{:S(2)}) copy-start(bf16[2,256,768]{2,1,0:T(8,128)(2,1)S(1)} %add_convert_fusion.2) | copy-start | bytes 2359300
  283.6 7.2 %slice-start.10 = ((s8[4718592]{0:T(1024)(128)(4,1)}), s8[524288]{0:T(1024)(128)(4,1)S(1)}, s32[]{:S(2)}) async-start(s8[4718592]{0:T(1024)(128)(4,1)} %bitcast.266), calls=%async_computation.14 | async-start | bytes 1048576
  298.5 7.7 %slice-start.7 = ((s8[4718592]{0:T(1024)(128)(4,1)}), s8[524288]{0:T(1024)(128)(4,1)S(1)}, s32[]{:S(2)}) async-start(s8[4718592]{0:T(1024)(128)(4,1)} %bitcast.263), calls=%async_computation.11 | async-start | bytes 1048576
  299.7 6.5 %slice-start.8 = ((s8[4718592]{0:T(1024)(128)(4,1)}), s8[4194304]{0:T(1024)(128)(4,1)S(1)}, s32[]{:S(2)}) async-start(s8[4718592]{0:T(1024)(128)(4,1)} %bitcast.263), calls=%async_computation.12 | async-start | bytes 8388608
  326.9 5.5 copy-start.5
  326.9 9.1 %slice-start.5 = ((s8[4718592]{0:T(1024)(128)(4,1)}), s8[4194304]{0:T(1024)(128)(4,1)S(1)}, s32[]{:S(2)}) async-start(s8[4718592]{0:T(1024)(128)(4,1)} %bitcast.259), calls=%async_computation.9 | async-start | bytes 8388608
  332.4 3.6 slice-start.6
  334.3 8.7 %slice-start.1 = ((s8[4718592]{0:T(1024)(128)(4,1)}), s8[4194304]{0:T(1024)(128)(4,1)S(1)}, s32[]{:S(2)}) async-start(s8[4718592]{0:T(1024)(128)(4,1)} %bitcast.253), calls=%async_computation.5 | async-start | bytes 8388608
  336.5 6.5 %slice-start.2 = ((s8[4718592]{0:T(1024)(128)(4,1)}), s8[524288]{0:T(1024)(128)(4,1)S(1)}, s32[]{:S(2)}) async-start(s8[4718592]{0:T(1024)(128)(4,1)} %bitcast.253), calls=%async_computation.6 | async-start | bytes 1048576
  544.8 7.5 %copy-start.33 = (f32[64,768]{1,0:T(8,128)S(1)}, f32[64,768]{1,0:T(8,128)}, u32[]{:S(2)}) copy-start(f32[64,768]{1,0:T(8,128)} %get-tuple-element.54) | copy-start | bytes 589828
  545.8 52.4 %all-to-all-start.3 = ((bf16[32,10,24,128]{3,2,1,0:T(8,128)(2,1)}), bf16[32,10,24,128]{3,2,1,0:T(8,128)(2,1)}, u32[]{:S(2)}, u32[]{:S(2)}) async-start(bf16[32,10,24,128]{3,2,1,0:T(8,128)(2,1)} %bitcast.77), calls=%async_computation.3 | async-start | bytes 3932160 | tf_op jit(solution)/shard_map/all_to_all | solution.py:1063
  (37 other events, 73.5 us)

commit v12 on v11

--- a/solution.py
+++ b/solution.py
@@ -1062,12 +1062,21 @@
     def exchange(blocks):
         return lax.all_to_all(blocks, AXES, split_axis=0, concat_axis=0, tiled=True)
 
-    def exchange_last(blocks):
-        return lax.cond(overflow, exchange, jnp.zeros_like, blocks)
-
-    sorted_rows = plan.split_rows(jnp.take(low_slots, my_order, axis=0, mode="clip"))
-    spread = exchange(sorted_rows[:, :first_slots]).reshape(-1, rows, BLOCK)
-    extra = exchange_last(sorted_rows[:, first_slots:]).reshape(-1, rows, BLOCK)
+    def exchange_last(blocks_of, values, places_of):
+        return lax.cond(
+            overflow,
+            lambda *given: exchange(blocks_of(*given)),
+            lambda *given: jnp.zeros((count, last_slots, rows, BLOCK), jnp.bfloat16),
+            values,
+            places_of,
+        )
+
+    def slot_blocks(values, places_of):
+        return plan.split_rows(jnp.take(values, places_of, axis=0, mode="clip"))
+
+    spread = exchange(slot_blocks(low_slots, my_order[:first_slots])).reshape(-1, rows, BLOCK)
+    extra = exchange_last(slot_blocks, low_slots, my_order[first_slots:])
+    extra = extra.reshape(-1, rows, BLOCK)
     moved_rank = rank.reshape(-1)[owner[moved]]
     moved_device = owner[moved] // slot_dev
     in_first = moved_rank < first_slots
@@ -1187,12 +1196,13 @@
     time_cols = jnp.take(grad_time_out.reshape(all_images, TIME_UNITS, BLOCK), my_time, axis=1)
     packed = jnp.sum(by_rank * slot_place.reshape(count, slot_dev, 1), 1)
 
-    def rows_of(places_of):
-        picked = jnp.take(unit_grads, places_of.reshape(-1), axis=0, mode="clip")
+    def unit_blocks(values, places_of):
+        picked = jnp.take(values, places_of.reshape(-1), axis=0, mode="clip")
         return picked.reshape(count, -1, rows, BLOCK)
 
-    dense_grad, starts = plan.join_rows(exchange(rows_of(packed[:, :first_slots])))
-    extra_grad, starts = plan.join_rows(exchange_last(rows_of(packed[:, first_slots:])))
+    dense_grad, starts = plan.join_rows(exchange(unit_blocks(unit_grads, packed[:, :first_slots])))
+    extra_grad = exchange_last(unit_blocks, unit_grads, packed[:, first_slots:])
+    extra_grad, starts = plan.join_rows(extra_grad)
     is_dense = (my_unit >= 0) & (my_place < 0) & ~is_time
     right = jnp.where(is_time[None, :, None], time_cols, slot_grad_out)
     left = jnp.where(is_time[:, None, None], time_act.T[None], cond_act.T[None])

time: 624 us -> 623 us (level)
    unnamed x136 -> x134, local copies, waits for them, and re-layouts: 17.2 us -> 17.7 us
where the time goes in v12:
time: 623 us; the launch traced here: 618 us
  Pallas kernels  385 us (62%)
  matrix products  80.9 us (13%)
  local copies, waits for them, and re-layouts  46.9 us (8%)
  waiting for transfers between devices  44.8 us (7%)
  other arithmetic  41.7 us (7%)
  starting transfers between devices  13.8 us (2%)
    pallas_call x1, Pallas kernels, scatter(): pl.pallas_call(lambda *refs: scatter_kernel(widths, bases, slots, *refs),...  163 us
    pallas_call x1, Pallas kernels, gather(): pl.pallas_call(lambda *refs: gather_kernel(widths, bases, *refs), out_sha...  160 us
    dot_general x23, matrix products, dot_low(): jnp.einsum(pattern, left_side, right_side, preferred_element_type=jnp.flo...  79.7 us
    all_to_all x2, waiting for transfers between devices, exchange(): return lax.all_to_all(blocks, AXES, split_axis=0, concat_axis=0, tiled=True)  44.8 us
    pallas_call x2, Pallas kernels, attend_back(): pl.pallas_call(attend_back_kernel, grid=(images, steps), out_shape=jax.Sh...  24.6 us
    pallas_call x2, Pallas kernels, attend(): pl.pallas_call(attend_kernel, grid=(images, steps), out_shape=jax.ShapeDt...  21.1 us
    unnamed x134, local copies, waits for them, and re-layouts  17.7 us
    pallas_call x1, Pallas kernels, adam_slots(): pl.pallas_call(lambda *refs: adam_kernel(starts, *refs), grid=(slots // s...  16.2 us
  transfers between devices with their start and end apart: 2, of which 2 were waited for; matrix products, arithmetic and copies ran while one was open for 7% of the time, Pallas kernels for 0%

profile of v12, /device:TPU:3, one launch (start us, length us, event | category | flops | bytes accessed | tf_op | source)
XLA Modules:
  0.0 618.4 jit_solution(13443057416862387870)
XLA Ops:
  3.1 3.2 convert_bitcast_fusion.refs_5_.refs_18_
  14.3 7.2 %all-to-all-start.2 = ((bf16[32,10,24,128]{3,2,1,0:T(8,128)(2,1)}), bf16[32,10,24,128]{3,2,1,0:T(8,128)(2,1)}, u32[]{:S(2)}, u32[]{:S(2)}) async-start(bf16[32,10,24,128]{3,2,1,0:T(8,128)(2,1)} %bitcast.206), calls=%async_computation.2 | async-start | bytes 3932160 | tf_op jit(solution)/shard_map/all_to_all | solution.py:1063
  21.6 3.7 convert_element_type.172
  43.8 23.3 %all-to-all-done.2 = bf16[32,10,24,128]{3,2,1,0:T(8,128)(2,1)} async-done(((bf16[32,10,24,128]{3,2,1,0:T(8,128)(2,1)}), bf16[32,10,24,128]{3,2,1,0:T(8,128)(2,1)}, u32[]{:S(2)}, u32[]{:S(2)}) %all-to-all-start.2) | async-done | bytes 1966112 | tf_op jit(solution)/shard_map/all_to_all | solution.py:1063
  67.1 160.2 %shard_map.224 = (bf16[2,2,2,4,24,768]{5,4,3,2,1,0:T(8,128)(2,1)}, bf16[2,2,2,4,24,2304]{5,4,3,2,1,0:T(8,128)(2,1)}, bf16[2,2,2,4,24,3072]{5,4,3,2,1,0:T(8,128)(...) custom-call(s32[2,150]{1,0:T(2,128)} %pad_add_fusion.refs_0_, ...), custom_call_target="tpu_custom_call" | custom-call | bytes 58982400 | tf_op jit(solution)/shard_map/pallas_call | solution.py:876
  230.6 5.4 convolution_convert_fusion.1.queries.keys_all.values
  236.0 10.5 %shard_map.225 = bf16[2,256,768]{2,1,0:T(8,128)(2,1)} custom-call(bf16[2,256,2304]{2,1,0:T(8,128)(2,1)} %convolution_convert_fusion.1.queries.keys_all.values, bf16[2,256,2304]{2,1,0:T(8,128)(2,1)} %convolution_convert_fusion.1.queries.keys_all.values, bf16[2,256,2304]{2,1,0:T(8,128)(2,1)} %convolution_convert_fusion.1.queries.keys_all.values), custom_call_target="tpu_custom_call" | custom-call | flops 402653184 | bytes 3145728 | tf_op jit(solution)/shard_map/pallas_call | solution.py:288
  246.6 3.4 fusion.115
  250.7 8.2 %fusion.15 = (bf16[2,256,3072]{2,1,0:T(8,128)(2,1)S(1)}, bf16[2,256,3072]{2,1,0:T(8,128)(2,1)}) fusion(bf16[2,256,768]{2,1,0:T(8,128)(2,1)S(1)} %add_convert_fusion.4, bf16[768,3072,1]{1,0,2:T(8,128)(2,1)} %bitcast.259), kind=kOutput, calls=%fused_computation.40 | convolution fusion | flops 2431647744 | bytes 11796480 | tf_op jit(solution)/shard_map/gpd,df->gpf/dot_general | solution.py:55
  258.9 3.8 fusion.114
  265.6 3.4 convolution_convert_fusion.queries.keys_all.values
  269.0 10.6 %shard_map.226 = bf16[2,256,768]{2,1,0:T(8,128)(2,1)} custom-call(bf16[2,256,2304]{2,1,0:T(8,128)(2,1)} %convolution_convert_fusion.queries.keys_all.values, bf16[2,256,2304]{2,1,0:T(8,128)(2,1)} %convolution_convert_fusion.queries.keys_all.values, bf16[2,256,2304]{2,1,0:T(8,128)(2,1)} %convolution_convert_fusion.queries.keys_all.values), custom_call_target="tpu_custom_call" | custom-call | flops 402653184 | bytes 3145728 | tf_op jit(solution)/shard_map/pallas_call | solution.py:288
  283.2 7.1 %fusion.23 = (bf16[2,256,3072]{2,1,0:T(8,128)(2,1)S(1)}, bf16[2,256,3072]{2,1,0:T(8,128)(2,1)S(1)}) fusion(bf16[2,256,768]{2,1,0:T(8,128)(2,1)S(1)} %add_convert_fusion.2, bf16[768,3072,1]{1,0,2:T(8,128)(2,1)} %bitcast.269), kind=kOutput, calls=%fused_computation.48 | convolution fusion | flops 2431647744 | bytes 11796480 | tf_op jit(solution)/shard_map/gpd,df->gpf/dot_general | solution.py:55
  299.3 6.7 %fusion.7 = bf16[2,256,3072]{2,1,0:T(8,128)(2,1)S(1)} fusion(bf16[2,256,768]{2,1,0:T(8,128)(2,1)S(1)} %get-tuple-element.115, bf16[768,3072,1]{1,0,2:T(8,128)(2,1)S(1)} %bitcast.276, bf16[2,256,3072]{2,1,0:T(8,128)(2,1)S(1)} %get-tuple-element.172), kind=kOutput, calls=%fused_computation.32 | convolution fusion | flops 2448949248 | bytes 11796480 | tf_op jit(solution)/shard_map/gpd,df->gpf/dot_general | solution.py:55
  314.5 12.2 %shard_map.227 = bf16[2,256,2304]{2,1,0:T(8,128)(2,1)} custom-call(bf16[2,256,2304]{2,1,0:T(8,128)(2,1)} %convolution_convert_fusion.queries.keys_all.values, bf16[2,256,2304]{2,1,0:T(8,128)(2,1)} %convolution_convert_fusion.queries.keys_all.values, bf16[2,256,2304]{2,1,0:T(8,128)(2,1)} %convolution_convert_fusion.queries.keys_all.values, ...), custom_call_target="tpu_custom_call" | custom-call | flops 1006632960 | bytes 5505024 | tf_op jit(solution)/shard_map/pallas_call | solution.py:305
  326.7 5.4 multiply_reduce_fusion.11
  336.3 6.4 %fusion.4 = bf16[2,256,3072]{2,1,0:T(8,128)(2,1)S(1)} fusion(bf16[2,256,768]{2,1,0:T(8,128)(2,1)S(1)} %multiply_convert_fusion.1, bf16[768,3072,1]{1,0,2:T(8,128)(2,1)S(1)} %bitcast.268, bf16[2,256,3072]{2,1,0:T(8,128)(2,1)S(1)} %copy-done.46), kind=kOutput, calls=%fused_computation.29 | convolution fusion | flops 2448949248 | bytes 11796480 | tf_op jit(solution)/shard_map/gpd,df->gpf/dot_general | solution.py:55
  351.6 12.4 %shard_map.228 = bf16[2,256,2304]{2,1,0:T(8,128)(2,1)} custom-call(bf16[2,256,2304]{2,1,0:T(8,128)(2,1)} %convolution_convert_fusion.1.queries.keys_all.values, bf16[2,256,2304]{2,1,0:T(8,128)(2,1)} %convolution_convert_fusion.1.queries.keys_all.values, bf16[2,256,2304]{2,1,0:T(8,128)(2,1)} %convolution_convert_fusion.1.queries.keys_all.values, ...), custom_call_target="tpu_custom_call" | custom-call | flops 1006632960 | bytes 5505024 | tf_op jit(solution)/shard_map/pallas_call | solution.py:305
  364.1 4.9 multiply_reduce_fusion
  376.7 162.9 %shard_map.229 = (bf16[144,24,128]{2,1,0:T(8,128)(2,1)S(1)}, f32[64,16,128]{2,1,0:T(8,128)}, f32[2,2,2,4,2,16,128]{6,5,4,3,2,1,0:T(8,128)}) custom-call(bf16[512,768]{1,0:T(8,128)(2,1)} %bitcast.209, bf16[512,768]{1,0:T(8,128)(2,1)} %bitcast.220, bf16[512,768]{1,0:T(8,128)(2,1)} %bitcast.221, bf16[512,768]{1,0:T(8,128)(2,1)} %bitcast.225, ...), custom_call_target="tpu_custom_call" | custom-call | bytes 56623104 | tf_op jit(solution)/shard_map/pallas_call | solution.py:929
  545.7 6.6 %all-to-all-start.3 = ((bf16[32,10,24,128]{3,2,1,0:T(8,128)(2,1)}), bf16[32,10,24,128]{3,2,1,0:T(8,128)(2,1)}, u32[]{:S(2)}, u32[]{:S(2)}) async-start(bf16[32,10,24,128]{3,2,1,0:T(8,128)(2,1)} %bitcast.80), calls=%async_computation.3 | async-start | bytes 3932160 | tf_op jit(solution)/shard_map/all_to_all | solution.py:1063
  566.2 10.5 %multiply_subtract_fusion = (f32[1288,768]{1,0:T(8,128)}, f32[1288,768]{1,0:T(8,128)}, f32[1288,768]{1,0:T(8,128)}) fusion(f32[1288,768]{1,0:T(8,128)} %param.29, f32[1288]{0:T(1024)S(1)} %copy-done.34, f32[16,768]{1,0:T(8,128)S(1)} %bitcast.242, f32[1000,768]{1,0:T(8,128)S(1)} %copy-done.10, f32[256,768]{1,0:T(8,128)} %fusion.56, ...), kind=kLoop, calls=%fused_computation.65 | loop fusion | flops 16816128 | bytes 27702304 | tf_op jit(solution)/shard_map/sub | solution.py:105
  576.7 21.4 %all-to-all-done.3.refs_2_ = bf16[32,10,24,128]{3,2,1,0:T(8,128)(2,1)} async-done(((bf16[32,10,24,128]{3,2,1,0:T(8,128)(2,1)}), bf16[32,10,24,128]{3,2,1,0:T(8,128)(2,1)}, u32[]{:S(2)}, u32[]{:S(2)}) %all-to-all-start.3) | async-done | bytes 1966112 | tf_op jit(solution)/shard_map/all_to_all | solution.py:1063
  600.8 16.2 %shard_map.230 = (f32[15,768,128]{2,1,0:T(8,128)}, f32[15,768,128]{2,1,0:T(8,128)}, f32[15,768,128]{2,1,0:T(8,128)}) custom-call(f32[15,5]{1,0:T(8,128)S(1)} %stack.68.refs_0_, s32[15,2]{1,0:T(8,128)S(1)} %copy.162.refs_1_, bf16[32,10,24,128]{3,2,1,0:T(8,128)(2,1)} %all-to-all-done.3.refs_2_, bf16[32,5,24,128]{3,2,1,0:T(8,128)(2,1)} %copy-done.15, ...), custom_call_target="tpu_custom_call" | custom-call | flops 58982400 | bytes 38338560 | tf_op jit(solution)/shard_map/pallas_call | solution.py:355
  (316 shorter events, 97.5 us)
Async XLA Ops:
  6.3 6.9 %copy-start.3 = (bf16[15,768,128]{2,1,0:T(8,128)(2,1)}, bf16[15,768,128]{2,1,0:T(8,128)(2,1)S(1)}, u32[]{:S(2)}) copy-start(bf16[15,768,128]{2,1,0:T(8,128)(2,1)S(1)} %convert_bitcast_fusion.refs_5_.refs_18_) | copy-start | bytes 8847364
  14.3 52.8 %all-to-all-start.2 = ((bf16[32,10,24,128]{3,2,1,0:T(8,128)(2,1)}), bf16[32,10,24,128]{3,2,1,0:T(8,128)(2,1)}, u32[]{:S(2)}, u32[]{:S(2)}) async-start(bf16[32,10,24,128]{3,2,1,0:T(8,128)(2,1)} %bitcast.206), calls=%async_computation.2 | async-start | bytes 3932160 | tf_op jit(solution)/shard_map/all_to_all | solution.py:1063
  21.6 11.1 %copy-start.38 = (f32[128]{0:T(128)}, f32[128]{0:T(128)S(1)}, u32[]{:S(2)}) copy-start(f32[128]{0:T(128)S(1)} %multiply_exponential_fusion.1) | copy-start | bytes 1540
  25.3 3.5 copy-start.36
  25.3 3.8 copy-start.43
  25.3 4.0 copy-start.41
  28.8 5.3 slice-start
  41.5 25.6 %copy-start.14 = (bf16[160,24,128]{2,1,0:T(8,128)(2,1)S(1)}, bf16[160,24,128]{2,1,0:T(8,128)(2,1)}, u32[]{:S(2)}) copy-start(bf16[160,24,128]{2,1,0:T(8,128)(2,1)} %copy-done.13) | copy-start | bytes 2949124
  250.3 8.6 %slice-start.3 = ((s8[4718592]{0:T(1024)(128)(4,1)}), s8[4194304]{0:T(1024)(128)(4,1)S(1)}, s32[]{:S(2)}) async-start(s8[4718592]{0:T(1024)(128)(4,1)} %bitcast.263), calls=%async_computation.7 | async-start | bytes 8388608
  250.7 8.2 %copy-start.21 = (bf16[2,256,768]{2,1,0:T(8,128)(2,1)}, bf16[2,256,768]{2,1,0:T(8,128)(2,1)S(1)}, u32[]{:S(2)}) copy-start(bf16[2,256,768]{2,1,0:T(8,128)(2,1)S(1)} %add_convert_fusion.4) | copy-start | bytes 2359300
  250.7 8.2 %slice-start.4 = ((s8[4718592]{0:T(1024)(128)(4,1)}), s8[524288]{0:T(1024)(128)(4,1)S(1)}, s32[]{:S(2)}) async-start(s8[4718592]{0:T(1024)(128)(4,1)} %bitcast.263), calls=%async_computation.8 | async-start | bytes 1048576
  258.9 3.8 copy-start.16
  282.8 7.5 %slice-start.9 = ((s8[4718592]{0:T(1024)(128)(4,1)}), s8[4194304]{0:T(1024)(128)(4,1)S(1)}, s32[]{:S(2)}) async-start(s8[4718592]{0:T(1024)(128)(4,1)} %bitcast.273), calls=%async_computation.13 | async-start | bytes 8388608
  283.2 7.2 %copy-start.23 = (bf16[2,256,768]{2,1,0:T(8,128)(2,1)}, bf16[2,256,768]{2,1,0:T(8,128)(2,1)S(1)}, u32[]{:S(2)}) copy-start(bf16[2,256,768]{2,1,0:T(8,128)(2,1)S(1)} %add_convert_fusion.2) | copy-start | bytes 2359300
  283.2 7.2 %slice-start.10 = ((s8[4718592]{0:T(1024)(128)(4,1)}), s8[524288]{0:T(1024)(128)(4,1)S(1)}, s32[]{:S(2)}) async-start(s8[4718592]{0:T(1024)(128)(4,1)} %bitcast.273), calls=%async_computation.14 | async-start | bytes 1048576
  298.0 8.0 %slice-start.7 = ((s8[4718592]{0:T(1024)(128)(4,1)}), s8[4194304]{0:T(1024)(128)(4,1)S(1)}, s32[]{:S(2)}) async-start(s8[4718592]{0:T(1024)(128)(4,1)} %bitcast.270), calls=%async_computation.11 | async-start | bytes 8388608
  299.3 6.7 %slice-start.8 = ((s8[4718592]{0:T(1024)(128)(4,1)}), s8[524288]{0:T(1024)(128)(4,1)S(1)}, s32[]{:S(2)}) async-start(s8[4718592]{0:T(1024)(128)(4,1)} %bitcast.270), calls=%async_computation.12 | async-start | bytes 1048576
  326.7 5.5 copy-start.5
  326.7 9.1 %slice-start.5 = ((s8[4718592]{0:T(1024)(128)(4,1)}), s8[4194304]{0:T(1024)(128)(4,1)S(1)}, s32[]{:S(2)}) async-start(s8[4718592]{0:T(1024)(128)(4,1)} %bitcast.266), calls=%async_computation.9 | async-start | bytes 8388608
  332.2 3.6 slice-start.6
  334.1 8.7 %slice-start.1 = ((s8[4718592]{0:T(1024)(128)(4,1)}), s8[4194304]{0:T(1024)(128)(4,1)S(1)}, s32[]{:S(2)}) async-start(s8[4718592]{0:T(1024)(128)(4,1)} %bitcast.260), calls=%async_computation.5 | async-start | bytes 8388608
  336.3 6.5 %slice-start.2 = ((s8[4718592]{0:T(1024)(128)(4,1)}), s8[524288]{0:T(1024)(128)(4,1)S(1)}, s32[]{:S(2)}) async-start(s8[4718592]{0:T(1024)(128)(4,1)} %bitcast.260), calls=%async_computation.6 | async-start | bytes 1048576
  544.8 7.5 %copy-start.33 = (f32[64,768]{1,0:T(8,128)S(1)}, f32[64,768]{1,0:T(8,128)}, u32[]{:S(2)}) copy-start(f32[64,768]{1,0:T(8,128)} %get-tuple-element.56) | copy-start | bytes 589828
  545.7 52.4 %all-to-all-start.3 = ((bf16[32,10,24,128]{3,2,1,0:T(8,128)(2,1)}), bf16[32,10,24,128]{3,2,1,0:T(8,128)(2,1)}, u32[]{:S(2)}, u32[]{:S(2)}) async-start(bf16[32,10,24,128]{3,2,1,0:T(8,128)(2,1)} %bitcast.80), calls=%async_computation.3 | async-start | bytes 3932160 | tf_op jit(solution)/shard_map/all_to_all | solution.py:1063
  (36 other events, 68.2 us)
